TPU v7x, 32 devices: a whole 2x2x4 slice. The times are simulated.
32 devices in a mesh: seq: 8 (over y, x, core), head: 4 (over z).
Axes of the slice: x: 2, y: 2, z: 4, core: 2. Of those that a mesh axis runs over, the one named last changes fastest.
Arguments:
- hidden: bfloat16 [768, 4096], P('seq'), may hold values from -6 to 6
- norm_gain: float32 [4096], replicated, may hold values from 0.5 to 1.5
- w_query: bfloat16 [4096, 4096], P(None, 'head'), may hold values from -0.09375 to 0.09375
- w_key: bfloat16 [4096, 1024], P(None, 'head'), may hold values from -0.25 to 0.25
- w_value: bfloat16 [4096, 1024], P(None, 'head'), may hold values from -0.09375 to 0.09375
- w_out: bfloat16 [4096, 4096], P('head'), may hold values from -0.09375 to 0.09375
- stored_kv: bfloat16 [8192, 2, 8, 128], P('seq', None, 'head'), may hold values from -720 to 720
- selected: int32 [768], replicated, may hold values from 0 to 8191, as said below
- prompt_order: int32 [2], replicated, may hold values from 0 to 1, each once
- store_slot: int32 [2], replicated, may hold values from 0 to 1, each once
Outputs:
- attn_out: bfloat16 [768, 4096], P('seq', 'head')
- new_kv: bfloat16 [768, 2, 8, 128], P('seq', None, 'head')
Inputs may be any that keep to these rules, and one draw needn't show every extreme that they name: `selected`: each block of 1024 prompt positions holds exactly 96 distinct entries, which stand together in that block's place of the list, increasing.
All inputs are finite; a program needn't handle non-finite values.
Results may differ from a plain program's by a relative error of at most 0.02.
The roundings to bfloat16 on the way count: a program that leaves them out, or rounds other values in their place, can miss the bound.
Values may be sent and summed in bfloat16 or wider, within the bound.
No kernel may reach another device: no remote copies, remote signals or barrier semaphores. Data moves between devices by JAX's collectives and lax.ppermute only.
A program may use at most 192 MiB of HBM per device.

v0:
```python
import jax
import jax.numpy as jnp
from jax import lax
from jax.sharding import PartitionSpec as P

HEADS = 32
KV_HEADS = 8
HEAD_DIM = 128
PASSAGE = 4096


def rope(x, pos):
    half = HEAD_DIM // 2
    freq = 500000.0 ** (-(jnp.arange(half, dtype=jnp.float32) * 2.0 / HEAD_DIM))
    angle = pos.astype(jnp.float32)[:, None] * freq[None, :]
    cosine = jnp.cos(angle)[:, None, :]
    sine = jnp.sin(angle)[:, None, :]
    first = x[..., :half]
    second = x[..., half:]
    return jnp.concatenate([first * cosine - second * sine, second * cosine + first * sine], -1)


def attend(query, query_pos, keys, values, key_pos, keep):
    scale = 1.0 / HEAD_DIM**0.5
    scores = jnp.einsum("qkgd,nkd->qkgn", query, keys, preferred_element_type=jnp.float32) * scale
    valid = (key_pos[None, :] <= query_pos[:, None]) & keep[None, :]
    valid = valid[:, None, None, :]
    scores = jnp.where(valid, scores, -1e30)
    top = jnp.max(scores, -1)
    weights = jnp.where(valid, jnp.exp(scores - top[..., None]), 0.0)
    total = jnp.sum(weights, -1)
    summed = jnp.einsum(
        "qkgn,nkd->qkgd", weights.astype(jnp.bfloat16), values, preferred_element_type=jnp.float32
    )
    return (top, total, summed)


def combine(left, right):
    top = jnp.maximum(left[0], right[0])
    left_factor = jnp.exp(left[0] - top)
    right_factor = jnp.exp(right[0] - top)
    total = left[1] * left_factor + right[1] * right_factor
    summed = left[2] * left_factor[..., None] + right[2] * right_factor[..., None]
    return (top, total, summed)


def body(
    hidden, norm_gain, w_query, w_key, w_value, w_out, stored_kv, selected, prompt_order, store_slot
):
    seq_index = lax.axis_index("seq")
    seq_count = lax.axis_size("seq")
    rows_all = selected.shape[0]
    own_rows = hidden.shape[0]
    shard_rows = stored_kv.shape[0]
    local_kv = w_key.shape[1] // HEAD_DIM
    group = HEADS // KV_HEADS
    passages = prompt_order.shape[0]
    positions = lax.dynamic_slice_in_dim(selected, seq_index * own_rows, own_rows)
    widened = hidden.astype(jnp.float32)
    normed = (
        widened * lax.rsqrt(jnp.mean(widened * widened, -1, keepdims=True) + 1e-05) * norm_gain
    ).astype(jnp.bfloat16)
    query = rope(
        jnp.dot(normed, w_query, preferred_element_type=jnp.float32).reshape(
            own_rows, local_kv * group, HEAD_DIM
        ),
        positions,
    )
    query = query.astype(jnp.bfloat16).reshape(own_rows, local_kv, group, HEAD_DIM)
    fresh_key = rope(
        jnp.dot(normed, w_key, preferred_element_type=jnp.float32).reshape(
            own_rows, local_kv, HEAD_DIM
        ),
        positions,
    )
    fresh_value = jnp.dot(normed, w_value, preferred_element_type=jnp.float32).reshape(
        own_rows, local_kv, HEAD_DIM
    )
    new_kv = jnp.stack([fresh_key, fresh_value], 1).astype(jnp.bfloat16)
    every_kv = lax.all_gather(new_kv, "seq", axis=0, tiled=True)
    always = jnp.ones((rows_all,), jnp.bool_)
    fresh_part = attend(query, positions, every_kv[:, 0], every_kv[:, 1], selected, always)
    slots = jnp.arange(passages, dtype=jnp.int32)
    picker = (prompt_order[:, None] == slots[None, :]).astype(jnp.int32)
    slot_of_prompt = jnp.sum(picker * store_slot[None, :], 1)
    prompt_of_slot = jnp.sum(
        (slot_of_prompt[:, None] == slots[None, :]).astype(jnp.int32) * slots[:, None], 0
    )
    marked = jnp.zeros((shard_rows * seq_count,), jnp.int32).at[selected].set(1)
    every_query = lax.all_gather(query, "seq", axis=0, tiled=True)
    rows = seq_index * shard_rows + jnp.arange(shard_rows, dtype=jnp.int32)
    slot = rows // PASSAGE
    offset = rows % PASSAGE
    place = jnp.sum(
        (slot[:, None] == slots[None, :]).astype(jnp.int32) * prompt_of_slot[None, :], 1
    )
    stored_pos = place * PASSAGE + offset
    stored_keep = marked[stored_pos] == 0
    keys = stored_kv[:, 0]
    values = stored_kv[:, 1]
    factor = max(1, min(seq_count, 512 // own_rows))
    while seq_count % factor != 0:
        factor = factor - 1
    per_block = own_rows * factor
    blocks = rows_all // per_block
    grouped = every_query.reshape(blocks, per_block, local_kv, group, HEAD_DIM)
    grouped_pos = selected.reshape(blocks, per_block)

    def local_block(item):
        return attend(item[0], item[1], keys, values, stored_pos, stored_keep)

    tops, totals, sums = lax.map(local_block, (grouped, grouped_pos))
    tops = tops.reshape(rows_all, local_kv, group)
    totals = totals.reshape(rows_all, local_kv, group)
    sums = sums.reshape(rows_all, local_kv, group, HEAD_DIM)
    highest = lax.pmax(tops.astype(jnp.bfloat16), "seq").astype(tops.dtype)
    shrink = jnp.exp(tops - highest)
    own_sums, own_totals = (
        lax.psum_scatter(
            (sums * shrink[..., None]).astype(jnp.bfloat16), "seq", scatter_dimension=0, tiled=True
        ).astype(jnp.float32),
        lax.psum_scatter(
            (totals * shrink).astype(jnp.bfloat16), "seq", scatter_dimension=0, tiled=True
        ).astype(jnp.float32),
    )
    own_top = lax.dynamic_slice_in_dim(highest, seq_index * own_rows, own_rows, 0)
    stored_part = (own_top, own_totals, own_sums)
    merged = combine(stored_part, fresh_part)
    context = (
        (merged[2] / merged[1][..., None])
        .astype(jnp.bfloat16)
        .reshape(own_rows, local_kv * group * HEAD_DIM)
    )
    partial_value = jnp.dot(context, w_out, preferred_element_type=jnp.float32)
    attn_out = lax.psum_scatter(
        partial_value.astype(jnp.bfloat16), "head", scatter_dimension=1, tiled=True
    )
    return (attn_out, new_kv)


def solution(mesh):
    in_specs = (
        P("seq", None),
        P(),
        P(None, "head"),
        P(None, "head"),
        P(None, "head"),
        P("head", None),
        P("seq", None, "head", None),
        P(),
        P(),
        P(),
    )
    out_specs = (P("seq", "head"), P("seq", None, "head", None))
    return jax.shard_map(body, mesh=mesh, in_specs=in_specs, out_specs=out_specs, check_vma=False)
```

profile of v0, /device:TPU:8, one launch (start us, length us, event | category | flops | bytes accessed | tf_op | source)
XLA Modules:
  0.0 205.8 jit_solution(1188854971722527360)
XLA Ops:
  7.2 1.5 fusion.23
  8.8 5.2 %convolution_bitcast_fusion.1 = f32[12,8,8,128]{3,1,2,0:T(8,128)S(1)} fusion(bf16[4096,1024]{1,0:T(8,128)(2,1)} %param.14, bf16[96,4096]{1,0:T(8,128)(2,1)} %param.12, f32[4096]{0:T(1024)} %param.13, f32[96]{0:T(128)S(1)} %add_rsqrt_fusion), kind=kOutput, calls=%fused_computation.38 | convolution fusion | flops 806879232 | bytes 9585024 | tf_op jit(solution)/shard_map/dot_general | solution.py:64
  14.7 0.8 pad_maximum_fusion
  15.7 3.4 %scatter_custom_fusion = s32[8192]{0:T(1024)S(1)} fusion(s32[768]{0:T(1024)S(1)} %compare_select_fusion.4, s32[768]{0:T(1024)S(1)} %broadcast.237, s32[]{:T(128)} %constant.46.clone.1), kind=kCustom, calls=%fused_computation.68 | custom fusion | bytes 32772 | tf_op jit(solution)/shard_map/scatter | solution.py:89
  19.6 6.2 %gather_fusion = s32[1024]{0:T(1024)S(1)} fusion(s32[8192]{0:T(1024)S(1)} %scatter_custom_fusion, s32[1024]{0:T(1024)S(1)} %broadcast_clamp_fusion), kind=kCustom, calls=%fused_computation | custom fusion | bytes 12288 | tf_op jit(solution)/shard_map/gather | solution.py:98
  25.8 0.7 fusion.63
  26.6 16.0 %all-gather.2.cloned.1.call-done = bf16[768,2,4,128]{3,0,2,1:T(8,128)(2,1)} async-done(((bf16[96,2,4,128]{3,0,2,1:T(8,128)(2,1)}), bf16[768,2,4,128]{3,0,2,1:T(8,128)(2,1)}) %all-gather.2.cloned.1.call-update) | async-done | bytes 1572880 | tf_op jit(solution)/shard_map/all_gather | solution.py:90
  42.6 26.4 %while.14 = (s32[]{:T(128)}, f32[2,384,2,4]{1,0,3,2:T(2,128)S(1)}, f32[2,384,2,4]{1,0,3,2:T(2,128)S(1)}, f32[2,384,2,4,128]{4,1,0,3,2:T(8,128)}, s32[1024]{0:T(1...) while((s32[]{:T(128)}, f32[2,384,2,4]{1,0,3,2:T(2,128)S(1)}, ...), condition=%wide.region_8.9_spmd, body=%wide.region_5.8_spmd.sunk | while | flops 1652287488 | bytes 68446392 | solution.py:112
  42.6 0.3 compare_and_fusion.2
  42.9 3.7 %bitcast_reduce_fusion.2 = (f32[384,2,4]{0,2,1:T(4,128)S(1)}, f32[2,384,4,1024]{3,1,2,0:T(8,128)S(1)}) fusion(pred[384,1024]{1,0:T(8,128)(4,1)S(1)} %compare_and_fusion.2, bf16[1024,2,128]{2,0,1:T(8,128)(2,1)S(1)} %get-tuple-element.249, bf16[2,384,2,4,128]{4,1,0,3,2:T(8,128)(2,1)} %get-tuple-element.248, s32[]{:T(128)} %get-tuple-element.229), kind=kOutput, calls=%fused_computation.3.clone.1 | convolution fusion | flops 814740480 | bytes 14299648 | tf_op jit(solution)/shard_map/while/body/eval_jaxpr/qkgd,nkd->qkgn/dot_general | solution.py:25
  46.6 4.8 %bitcast_dynamic-update-slice_fusion.2 = f32[2,384,2,4,128]{4,1,0,3,2:T(8,128)S(1)} fusion(f32[2,384,2,4,128]{4,1,0,3,2:T(8,128)S(1)} %copy-done.3, s32[]{:T(128)} %get-tuple-element.229, f32[2,384,4,1024]{3,1,2,0:T(8,128)S(1)} %get-tuple-element.216, f32[384,2,4]{0,2,1:T(4,128)S(1)} %get-tuple-element.215, ...), kind=kOutput, calls=%fused_computation.12.clone.1 | convolution fusion | flops 821035008 | bytes 15478788 | tf_op jit(solution)/shard_map/while/body/eval_jaxpr/qkgn,nkd->qkgd/dot_general | solution.py:32
  51.4 4.1 %fusion.76 = f32[384,2,4]{0,2,1:T(4,128)S(1)} fusion(f32[2,384,4,1024]{3,1,2,0:T(8,128)S(1)} %get-tuple-element.216, f32[384,2,4]{0,2,1:T(4,128)S(1)} %get-tuple-element.215, pred[384,1024]{1,0:T(8,128)(4,1)S(1)} %compare_and_fusion.2), kind=kLoop, calls=%fused_computation.8.clone.1 | loop fusion | flops 15725568 | bytes 13000704 | tf_op jit(solution)/shard_map/while/body/eval_jaxpr/reduce_sum | solution.py:31
  55.8 0.3 compare_and_fusion.2
  56.1 3.7 %bitcast_reduce_fusion.2 = (f32[384,2,4]{0,2,1:T(4,128)S(1)}, f32[2,384,4,1024]{3,1,2,0:T(8,128)S(1)}) fusion(pred[384,1024]{1,0:T(8,128)(4,1)S(1)} %compare_and_fusion.2, bf16[1024,2,128]{2,0,1:T(8,128)(2,1)S(1)} %get-tuple-element.249, bf16[2,384,2,4,128]{4,1,0,3,2:T(8,128)(2,1)} %get-tuple-element.248, s32[]{:T(128)} %get-tuple-element.229), kind=kOutput, calls=%fused_computation.3.clone.1 | convolution fusion | flops 814740480 | bytes 14299648 | tf_op jit(solution)/shard_map/while/body/eval_jaxpr/qkgd,nkd->qkgn/dot_general | solution.py:25
  59.8 4.8 %bitcast_dynamic-update-slice_fusion.2 = f32[2,384,2,4,128]{4,1,0,3,2:T(8,128)S(1)} fusion(f32[2,384,2,4,128]{4,1,0,3,2:T(8,128)S(1)} %copy-done.3, s32[]{:T(128)} %get-tuple-element.229, f32[2,384,4,1024]{3,1,2,0:T(8,128)S(1)} %get-tuple-element.216, f32[384,2,4]{0,2,1:T(4,128)S(1)} %get-tuple-element.215, ...), kind=kOutput, calls=%fused_computation.12.clone.1 | convolution fusion | flops 821035008 | bytes 15478788 | tf_op jit(solution)/shard_map/while/body/eval_jaxpr/qkgn,nkd->qkgd/dot_general | solution.py:32
  64.6 4.1 %fusion.76 = f32[384,2,4]{0,2,1:T(4,128)S(1)} fusion(f32[2,384,4,1024]{3,1,2,0:T(8,128)S(1)} %get-tuple-element.216, f32[384,2,4]{0,2,1:T(4,128)S(1)} %get-tuple-element.215, pred[384,1024]{1,0:T(8,128)(4,1)S(1)} %compare_and_fusion.2), kind=kLoop, calls=%fused_computation.8.clone.1 | loop fusion | flops 15725568 | bytes 13000704 | tf_op jit(solution)/shard_map/while/body/eval_jaxpr/reduce_sum | solution.py:31
  69.0 23.5 %pmax.7 = bf16[768,2,4]{0,2,1:T(4,128)(2,1)S(1)} all-reduce(bf16[768,2,4]{0,2,1:T(4,128)(2,1)S(1)} %convert_element_type.49), channel_id=1, replica_groups=mesh['seq'=8,'head'=4] {'seq'}, use_global_device_ids=true, to_apply=%region_9.10 | all-reduce | flops 6144 | bytes 24576 | tf_op jit(solution)/shard_map/pmax | solution.py:116
  92.6 0.8 copy.67
  93.5 3.3 %fusion.19 = bf16[768,2,4,128]{3,0,2,1:T(8,128)(2,1)} fusion(f32[2,384,2,4,128]{4,1,0,3,2:T(8,128)} %get-tuple-element.56, f32[768,2,4]{0,2,1:T(4,128)S(1)} %get-tuple-element.131), kind=kLoop, calls=%fused_computation.26 | loop fusion | flops 1572864 | bytes 4743168 | tf_op jit(solution)/shard_map/convert_element_type | solution.py:120
  97.1 0.5 fusion.57
  97.7 2.2 %convolution_convert_fusion.1 = bf16[96,256]{1,0:T(8,128)(2,1)S(1)} fusion(bf16[4096,256]{1,0:T(8,128)(2,1)} %param.16, bf16[96,4096]{1,0:T(8,128)(2,1)S(1)} %copy-done.2, f32[4096]{0:T(1024)S(1)} %copy-done.7, f32[96]{0:T(128)S(1)} %add_rsqrt_fusion), kind=kOutput, calls=%fused_computation.47 | convolution fusion | flops 202924032 | bytes 2949504 | tf_op jit(solution)/shard_map/dot_general | solution.py:76
  100.3 10.4 %all_gather.7 = bf16[768,2,2,128]{3,0,2,1:T(8,128)(2,1)S(1)} all-gather(bf16[96,2,2,128]{3,0,2,1:T(8,128)(2,1)S(1)} %pad_maximum_fusion.1), channel_id=1, replica_groups=mesh['seq'=8,'head'=4] {'seq'}, dimensions={0}, use_global_device_ids=true | all-gather | bytes 884736 | tf_op jit(solution)/shard_map/all_gather | solution.py:80
  110.8 0.6 fusion.20
  111.4 1.4 copy-done.1
  112.8 0.8 fusion.21
  113.6 13.5 %reduce-scatter.10.cloned.1.call-done = bf16[96,8]{1,0:T(8,128)(2,1)} async-done(((bf16[768,8]{1,0:T(8,128)(2,1)}), bf16[96,8]{1,0:T(8,128)(2,1)}) %reduce-scatter.10.cloned.1.call-update) | async-done | bytes 1552
  127.1 0.8 copy.68
  128.0 41.2 %reduce-scatter.6.cloned.1.call-done = bf16[96,2,4,128]{3,0,2,1:T(8,128)(2,1)} async-done(((bf16[768,2,4,128]{3,0,2,1:T(8,128)(2,1)}), bf16[96,2,4,128]{3,0,2,1:T(8,128)(2,1)}) %reduce-scatter.6.cloned.1.call-update) | async-done | bytes 196624 | tf_op jit(solution)/shard_map/reduce_scatter | solution.py:119
  169.2 2.4 %fusion.34 = bf16[96,2,4,128]{3,0,2,1:T(8,128)(2,1)S(1)} fusion(f32[2,768,96,4]{1,2,3,0:T(8,128)} %copy-done.1, f32[96,2,4]{0,2,1:T(4,128)S(1)} %get-tuple-element.148, pred[96,768]{1,0:T(8,128)(4,1)S(1)} %broadcast_compare_fusion, bf16[768,2,2,128]{3,0,2,1:T(8,128)(2,1)S(1)} %all_gather.7, bf16[96,2,4,128]{3,0,2,1:T(8,128)(2,1)} %reduce-scatter.6.cloned.1.call-done, ...), kind=kOutput, calls=%fused_computation.46 | convolution fusion | flops 154533888 | bytes 3235840 | tf_op jit(solution)/shard_map/qkgn,nkd->qkgd/dot_general | solution.py:32
  171.9 5.7 %convolution_convert_fusion = bf16[96,4096]{1,0:T(8,128)(2,1)} fusion(bf16[96,1024]{1,0:T(8,128)(2,1)S(1)} %reshape.250, bf16[1024,4096]{1,0:T(8,128)(2,1)} %param.17), kind=kOutput, calls=%fused_computation.24 | convolution fusion | flops 805699584 | bytes 9371648 | tf_op jit(solution)/shard_map/dot_general | solution.py:134
  177.7 0.7 copy.60
  178.4 20.9 %reduce-scatter.8.cloned.1.call-done = bf16[96,1024]{1,0:T(8,128)(2,1)} async-done(((bf16[96,4096]{1,0:T(8,128)(2,1)}), bf16[96,1024]{1,0:T(8,128)(2,1)}) %reduce-scatter.8.cloned.1.call-update) | async-done | bytes 196624 | tf_op jit(solution)/shard_map/reduce_scatter | solution.py:135
  (83 shorter events, 3.1 us)
Async XLA Ops:
  7.2 89.9 %copy-start = (bf16[4096,256]{1,0:T(8,128)(2,1)S(1)}, bf16[4096,256]{1,0:T(8,128)(2,1)}, u32[]{:S(2)}) copy-start(bf16[4096,256]{1,0:T(8,128)(2,1)} %param.15) | copy-start | bytes 6291460
  7.2 35.4 %all-gather.2.cloned.1.call-start = ((), (), s32[]{:S(2)}) async-start(), calls=%async_computation.3 | async-start | bytes 1769472 | tf_op jit(solution)/shard_map/all_gather | solution.py:90
  8.8 5.3 %copy-start.8 = (s32[768]{0:T(1024)S(1)}, s32[768]{0:T(1024)}, u32[]{:S(2)}) copy-start(s32[768]{0:T(1024)} %param.19) | copy-start | bytes 9220
  14.0 5.1 %copy-start.9 = (s32[2]{0:T(128)S(1)}, s32[2]{0:T(128)}, u32[]{:S(2)}) copy-start(s32[2]{0:T(128)} %param.21) | copy-start | bytes 28
  14.0 5.1 %copy-start.10 = (s32[2]{0:T(128)S(1)}, s32[2]{0:T(128)}, u32[]{:S(2)}) copy-start(s32[2]{0:T(128)} %param.20) | copy-start | bytes 28
  15.5 10.2 %copy-start.6 = (bf16[1024,2,2,128]{3,2,1,0:T(2,128)(2,1)S(1)}, bf16[1024,2,2,128]{3,2,1,0:T(2,128)(2,1)}, u32[]{:S(2)}) copy-start(bf16[1024,2,2,128]{3,2,1,0:T(2,128)(2,1)} %param.18) | copy-start | bytes 3145732
  15.6 111.5 %reduce-scatter.10.cloned.1.call-start = ((), (), s32[]{:S(2)}) async-start(), calls=%async_computation.6 | async-start | bytes 221184
  42.9 3.7 %copy-start.3 = (f32[2,384,2,4,128]{4,1,0,3,2:T(8,128)S(1)}, f32[2,384,2,4,128]{4,1,0,3,2:T(8,128)}, u32[]{:S(2)}) copy-start(f32[2,384,2,4,128]{4,1,0,3,2:T(8,128)} %get-tuple-element.232) | copy-start | bytes 9437188 | tf_op jit(solution)/shard_map/while
  51.4 4.1 %copy-start.4 = (f32[2,384,2,4,128]{4,1,0,3,2:T(8,128)}, f32[2,384,2,4,128]{4,1,0,3,2:T(8,128)S(1)}, u32[]{:S(2)}) copy-start(f32[2,384,2,4,128]{4,1,0,3,2:T(8,128)S(1)} %bitcast_dynamic-update-slice_fusion.2) | copy-start | bytes 9437188 | tf_op jit(solution)/shard_map/while
  56.1 3.7 %copy-start.3 = (f32[2,384,2,4,128]{4,1,0,3,2:T(8,128)S(1)}, f32[2,384,2,4,128]{4,1,0,3,2:T(8,128)}, u32[]{:S(2)}) copy-start(f32[2,384,2,4,128]{4,1,0,3,2:T(8,128)} %get-tuple-element.232) | copy-start | bytes 9437188 | tf_op jit(solution)/shard_map/while
  64.6 4.1 %copy-start.4 = (f32[2,384,2,4,128]{4,1,0,3,2:T(8,128)}, f32[2,384,2,4,128]{4,1,0,3,2:T(8,128)S(1)}, u32[]{:S(2)}) copy-start(f32[2,384,2,4,128]{4,1,0,3,2:T(8,128)S(1)} %bitcast_dynamic-update-slice_fusion.2) | copy-start | bytes 9437188 | tf_op jit(solution)/shard_map/while
  93.4 75.8 %reduce-scatter.6.cloned.1.call-start = ((), (), s32[]{:S(2)}) async-start(), calls=%async_computation.4 | async-start | bytes 1769472 | tf_op jit(solution)/shard_map/reduce_scatter | solution.py:119
  93.5 3.6 %copy-start.2 = (bf16[96,4096]{1,0:T(8,128)(2,1)S(1)}, bf16[96,4096]{1,0:T(8,128)(2,1)}, u32[]{:S(2)}) copy-start(bf16[96,4096]{1,0:T(8,128)(2,1)} %param.12) | copy-start | bytes 2359300
  93.5 3.6 %copy-start.7 = (f32[4096]{0:T(1024)S(1)}, f32[4096]{0:T(1024)}, u32[]{:S(2)}) copy-start(f32[4096]{0:T(1024)} %param.13) | copy-start | bytes 49156
  96.9 102.4 %reduce-scatter.8.cloned.1.call-start = ((), (), s32[]{:S(2)}) async-start(), calls=%async_computation.5 | async-start | bytes 983040 | tf_op jit(solution)/shard_map/reduce_scatter | solution.py:135
  97.7 13.0 %copy-start.5 = (bf16[96,2,4,128]{3,0,2,1:T(8,128)(2,1)S(1)}, bf16[96,2,4,128]{3,0,2,1:T(8,128)(2,1)}, u32[]{:S(2)}) copy-start(bf16[96,2,4,128]{3,0,2,1:T(8,128)(2,1)} %pad_maximum_fusion) | copy-start | bytes 589828
  111.4 1.4 copy-start.1
Sparse Core Ops, SparseCore 0:
  15.7 26.8 all-gather.1
  93.6 33.5 reduce-scatter.9
  130.8 38.4 reduce-scatter.5
  177.8 21.4 reduce-scatter.7
where the time goes:
time: 210 us; the launch traced here: 206 us
  waiting for transfers between devices  91.6 us (44%)
  blocking collectives  33.9 us (16%)
  matrix products  33.6 us (16%)
  other arithmetic  16.7 us (8%)
  local copies, waits for them, and re-layouts  15.3 us (7%)
  between operations  14.2 us (7%)
    reduce_scatter x1, waiting for transfers between devices, body(): lax.psum_scatter((sums * shrink[..., None]).astype(jnp.bfloat16), 'seq',...  41.2 us
    pmax x1, blocking collectives, body(): highest = lax.pmax(tops.astype(jnp.bfloat16), 'seq').astype(tops.dtype)  23.5 us
    reduce_scatter x1, waiting for transfers between devices, body(): lax.psum_scatter(partial_value.astype(jnp.bfloat16), 'head', scatter_dime...  20.9 us
    all_gather x1, waiting for transfers between devices, body(): every_query = lax.all_gather(query, 'seq', axis=0, tiled=True)  16 us
    unnamed x5, waiting for transfers between devices  13.6 us
    dot_general x3, matrix products, attend(): jnp.einsum('qkgn,nkd->qkgd', weights.astype(jnp.bfloat16), values, prefer...  12 us
    all_gather x1, blocking collectives, body(): every_kv = lax.all_gather(new_kv, 'seq', axis=0, tiled=True)  10.4 us
    reduce_sum x3, other arithmetic, attend(): total = jnp.sum(weights, -1)  9 us
  transfers between devices with their start and end apart: 4, of which 4 were waited for; matrix products, arithmetic and copies ran while one was open for 10% of the time, Pallas kernels for 0%

commit v1 on v0

v1 whole, which is shorter than its diff:
```python
import functools
import math

import jax
import jax.numpy as jnp
import numpy as np
from jax import lax
from jax.experimental import pallas as pl
from jax.experimental.pallas import tpu as pltpu
from jax.sharding import PartitionSpec as P

HEADS = 32
KV_HEADS = 8
HEAD_DIM = 128
PASSAGE = 4096
GROUP = HEADS // KV_HEADS
MASKED = -1e30
LANES = 128
MIB = 1024 * 1024

bf16 = jnp.bfloat16
f32 = jnp.float32
NT = (((1,), (1,)), ((), ()))


def iota(shape, dim):
    return lax.broadcasted_iota(jnp.int32, shape, dim)


def column_of(row):
    n = row.shape[1]
    eye = iota((n, n), 0) == iota((n, n), 1)
    return jnp.sum(jnp.where(eye, row.astype(f32), 0.0), 1, keepdims=True)


def project_kernel(
    width, hidden_any, gain, selected, freq, wq_any, wk_any, wv_any, query, kv,
    hidden, normed, weights, sem,
):
    rows, feat = hidden.shape
    q_cols, k_cols, v_cols = wq_any.shape[1], wk_any.shape[1], wv_any.shape[1]
    first = pltpu.make_async_copy(hidden_any, hidden, sem.at[0])
    first.start()
    chunks = []
    for source, count, base in ((wk_any, k_cols, 0), (wq_any, q_cols, k_cols), (wv_any, v_cols, k_cols + q_cols)):
        for at in range(0, count, width):
            chunks.append((source, at, base + at))
    copies = []
    for number, (source, at, place) in enumerate(chunks):
        copy = pltpu.make_async_copy(
            source.at[:, at : at + width], weights.at[:, place : place + width], sem.at[number + 1]
        )
        copy.start()
        copies.append(copy)
    total = selected.shape[1]
    me = lax.axis_index("seq")
    mine = iota((rows, total), 1) == iota((rows, total), 0) + me * rows
    positions = jnp.sum(jnp.where(mine, selected[...].astype(f32), 0.0), 1, keepdims=True)
    angle = positions * freq[...]
    cosine = jnp.cos(angle)
    sine = jnp.sin(angle)
    sine = jnp.where(iota(sine.shape, 1) < HEAD_DIM // 2, -sine, sine)
    first.wait()
    step = 16
    for at in range(0, rows, step):
        wide = hidden[at : at + step, :].astype(f32)
        mean = jnp.sum(wide * wide, 1, keepdims=True) * (1.0 / feat)
        normed[at : at + step, :] = (wide * lax.rsqrt(mean + 1e-5) * gain[...]).astype(bf16)
    for (source, at, place), copy in zip(chunks, copies):
        copy.wait()
        out = jnp.dot(normed[...], weights[:, place : place + width], preferred_element_type=f32)
        for head in range(0, width, HEAD_DIM):
            part = out[:, head : head + HEAD_DIM]
            if source is not wv_any:
                part = part * cosine + pltpu.roll(part, HEAD_DIM // 2, 1) * sine
            part = part.astype(bf16)
            if source is wq_any:
                query[:, at + head : at + head + HEAD_DIM] = part
            else:
                col = at + head + (0 if source is wk_any else k_cols)
                kv[:, col : col + HEAD_DIM] = part


def project(hidden, gain, selected, wq, wk, wv):
    rows, feat = hidden.shape
    cols = wq.shape[1] + wk.shape[1] + wv.shape[1]
    width = math.gcd(math.gcd(wq.shape[1], wk.shape[1]), 256)
    freq = 500000.0 ** (-(np.arange(HEAD_DIM // 2, dtype=np.float32) * np.float32(2.0 / HEAD_DIM)))
    freq = jnp.asarray(np.concatenate([freq, freq])[None, :].astype(np.float32))
    vmem = pl.BlockSpec(memory_space=pltpu.VMEM)
    hbm = pl.BlockSpec(memory_space=pl.ANY)
    return pl.pallas_call(
        functools.partial(project_kernel, width),
        out_shape=(
            jax.ShapeDtypeStruct((rows, wq.shape[1]), bf16),
            jax.ShapeDtypeStruct((rows, wk.shape[1] + wv.shape[1]), bf16),
        ),
        in_specs=[hbm, vmem, vmem, vmem, hbm, hbm, hbm],
        out_specs=(vmem, vmem),
        scratch_shapes=[
            pltpu.VMEM((rows, feat), bf16),
            pltpu.VMEM((rows, feat), bf16),
            pltpu.VMEM((feat, cols), bf16),
            pltpu.SemaphoreType.DMA((1 + cols // width,)),
        ],
        compiler_params=pltpu.CompilerParams(vmem_limit_bytes=28 * MIB),
        cost_estimate=pl.CostEstimate(
            flops=2 * rows * feat * cols, bytes_accessed=2 * feat * (cols + rows), transcendentals=0
        ),
        name="project",
    )(hidden, gain.reshape(1, feat), selected.reshape(1, -1), freq, wq, wk, wv)


def block_of(index, shard, order, slot):
    per = PASSAGE // shard
    own = index // per
    place = jnp.int32(0)
    for at in range(order.shape[0]):
        place = jnp.where(slot[order[at]] == own, at, place)
    return place * per + lax.rem(index, per)


def merge_kernel(order, slot, selected, stored, kv, cache, key_pos):
    shard, cols = stored.shape
    rows = kv.shape[0]
    me = lax.axis_index("seq")
    for half in range(2):
        index = me if half == 0 else me ^ 1
        block = block_of(index, shard, order, slot)
        holes = selected[pl.ds(block, 1), :] - block * shard
        offsets = column_of(selected[pl.ds(index, 1), :] - index * shard)
        high = jnp.floor(offsets * (1.0 / 32))
        low = offsets - 32 * high
        wide = (LANES, LANES)
        given = iota((LANES, 1), 0) < rows
        sources = [
            jnp.broadcast_to(jnp.where(given, value, 0.0), wide).astype(bf16)
            for value in (jnp.ones_like(high), high, low)
        ]
        if half == 0:
            fresh = kv[...]
            if rows < LANES:
                fresh = jnp.concatenate([fresh, jnp.zeros((LANES - rows, cols), bf16)], 0)
            sources.append(fresh)
        source = jnp.concatenate(sources, 1)
        step = 128
        for at in range(0, shard, step):
            places = iota((step, LANES), 0) + at
            hit = (places == holes).astype(f32).astype(bf16)
            picked = jnp.dot(hit, source, preferred_element_type=f32)
            hole = picked[:, :LANES] > 0.5
            fresh_pos = picked[:, LANES : 2 * LANES] * 32 + picked[:, 2 * LANES : 3 * LANES]
            key_pos[half * shard + at : half * shard + at + step, :] = jnp.where(
                hole,
                fresh_pos + (index * shard).astype(f32),
                (places + block * shard).astype(f32),
            )
            if half == 0:
                for col in range(0, cols, LANES):
                    cache[at : at + step, col : col + LANES] = jnp.where(
                        hole,
                        picked[:, 3 * LANES + col : 4 * LANES + col],
                        stored[at : at + step, col : col + LANES].astype(f32),
                    ).astype(bf16)


def merge(order, slot, selected, stored, kv):
    shard, cols = stored.shape
    smem = pl.BlockSpec(memory_space=pltpu.SMEM)
    vmem = pl.BlockSpec(memory_space=pltpu.VMEM)
    return pl.pallas_call(
        merge_kernel,
        out_shape=(
            jax.ShapeDtypeStruct((shard, cols), bf16),
            jax.ShapeDtypeStruct((2 * shard, LANES), f32),
        ),
        in_specs=[smem, smem, vmem, vmem, vmem],
        out_specs=(vmem, vmem),
        compiler_params=pltpu.CompilerParams(vmem_limit_bytes=16 * MIB),
        cost_estimate=pl.CostEstimate(
            flops=4 * shard * cols * LANES, bytes_accessed=4 * shard * cols, transcendentals=0
        ),
        name="merge",
    )(order, slot, selected, stored, kv)


def attend_kernel(partners, *refs):
    count = len(partners)
    caches = refs[:2]
    key_pos, selected = refs[2:4]
    queries = refs[4 : 4 + count]
    outs = refs[4 + count : 4 + 2 * count]
    left, right, value, scores, weights, sem = refs[4 + 2 * count :]
    shard, cols = caches[0].shape
    rows = queries[0].shape[0]
    kv_heads = cols // (2 * HEAD_DIM)
    tall = GROUP * rows
    keys = 2 * shard
    scale = math.log2(math.e) / HEAD_DIM**0.5
    me = lax.axis_index("seq")
    copies = {}
    for half in range(2):
        for kind in range(2):
            for head in range(kv_heads):
                col = (kind * kv_heads + head) * HEAD_DIM
                target = (right, value)[kind]
                copy = pltpu.make_async_copy(
                    caches[half].at[:, col : col + HEAD_DIM],
                    target.at[head, half * shard : (half + 1) * shard, 0:HEAD_DIM],
                    sem.at[half, kind, head],
                )
                copy.start()
                copies[half, kind, head] = copy
    one_hot = (iota((rows, LANES), 0) == iota((rows, LANES), 1)).astype(f32).astype(bf16)
    for head in range(kv_heads):
        for member in range(GROUP):
            left[head, member * rows : (member + 1) * rows, HEAD_DIM : HEAD_DIM + LANES] = one_hot
        value[head, :, HEAD_DIM : HEAD_DIM + LANES] = jnp.ones((keys, LANES), bf16)

    def mask(at, head):
        row = selected[pl.ds(me ^ partners[at], 1), :].astype(f32)
        for place in range(0, keys, 256):
            right[head, place : place + 256, HEAD_DIM : HEAD_DIM + LANES] = jnp.where(
                key_pos[place : place + 256, :] <= row, 0.0, MASKED
            ).astype(bf16)

    def fill(at, head):
        for member in range(GROUP):
            col = (head * GROUP + member) * HEAD_DIM
            left[head, member * rows : (member + 1) * rows, 0:HEAD_DIM] = queries[at][:, col : col + HEAD_DIM]

    units = [(at, head) for at in range(count) for head in range(kv_heads)]
    step = 256
    best = {}
    for number in range(len(units) + 1):
        if number < len(units):
            at, head = units[number]
            if at == 0:
                for half in range(2):
                    copies[half, 0, head].wait()
            mask(at, head)
            fill(at, head)
        if number:
            old_at, old_head = units[number - 1]
            if old_at == 0:
                for half in range(2):
                    copies[half, 1, old_head].wait()
            top = jnp.max(best.pop(number - 1), 1, keepdims=True) * scale
        running = None
        for place in range(0, keys, step):
            if number < len(units):
                score = lax.dot_general(
                    left[head], right[head, place : place + step, :], NT, preferred_element_type=f32
                )
                scores[number % 2, :, place : place + step] = score
                for col in range(0, step, LANES):
                    part = score[:, col : col + LANES]
                    running = part if running is None else jnp.maximum(running, part)
            if number:
                slot = (number - 1) % 2
                weights[:, place : place + step] = jnp.exp2(
                    scores[slot, :, place : place + step] * scale - top
                ).astype(bf16)
        if number < len(units):
            best[number] = running
        if number:
            summed = jnp.dot(weights[...], value[old_head], preferred_element_type=f32)
            total = summed[:, HEAD_DIM : HEAD_DIM + LANES]
            context = (summed[:, :HEAD_DIM] / total).astype(bf16)
            level = top + jnp.log2(total)
            high = level.astype(bf16).astype(f32)
            middle = (level - high).astype(bf16).astype(f32)
            low = level - high - middle
            lane = iota((rows, LANES), 1)
            heads = kv_heads * GROUP
            out = outs[old_at]
            packed = jnp.zeros((rows, LANES), f32)
            for member in range(GROUP):
                which = old_head * GROUP + member
                span = slice(member * rows, (member + 1) * rows)
                out[:, which * HEAD_DIM : (which + 1) * HEAD_DIM] = context[span]
                for piece, source in enumerate((high, middle, low)):
                    packed = jnp.where(lane == piece * heads + which, source[span], packed)
            tail = slice(heads * HEAD_DIM, heads * HEAD_DIM + LANES)
            if old_head:
                packed = packed + out[:, tail].astype(f32)
            out[:, tail] = packed.astype(bf16)


def attend(partners, caches, key_pos, selected, queries):
    shard, cols = caches[0].shape
    rows, q_cols = queries[0].shape
    kv_heads = cols // (2 * HEAD_DIM)
    tall = GROUP * rows
    keys = 2 * shard
    count = len(queries)
    vmem = pl.BlockSpec(memory_space=pltpu.VMEM)
    hbm = pl.BlockSpec(memory_space=pl.ANY)
    out = pl.pallas_call(
        functools.partial(attend_kernel, partners),
        out_shape=[jax.ShapeDtypeStruct((rows, q_cols + LANES), bf16)] * count,
        in_specs=[hbm, hbm, vmem, vmem] + [vmem] * count,
        out_specs=[vmem] * count,
        scratch_shapes=[
            pltpu.VMEM((kv_heads, tall, HEAD_DIM + LANES), bf16),
            pltpu.VMEM((kv_heads, keys, HEAD_DIM + LANES), bf16),
            pltpu.VMEM((kv_heads, keys, HEAD_DIM + LANES), bf16),
            pltpu.VMEM((2, tall, keys), f32),
            pltpu.VMEM((tall, keys), bf16),
            pltpu.SemaphoreType.DMA((2, 2, kv_heads)),
        ],
        compiler_params=pltpu.CompilerParams(vmem_limit_bytes=32 * MIB),
        cost_estimate=pl.CostEstimate(
            flops=8 * count * kv_heads * tall * keys * HEAD_DIM,
            bytes_accessed=8 * shard * cols,
            transcendentals=count * kv_heads * tall * keys,
        ),
        name="attend",
    )(*caches, key_pos, selected, *queries)
    return list(out)


def finish_kernel(count, size, *refs):
    parts = refs[:count]
    w_any = refs[count]
    outs = refs[count + 1 : count + 1 + size]
    context, weights, sem = refs[count + 1 + size :]
    rows, feat = context.shape
    heads = feat // HEAD_DIM
    width = w_any.shape[1] // size
    me = lax.axis_index("head")
    copies = []
    for turn in range(size):
        target = lax.rem(me + turn, size) if size & (size - 1) else me ^ turn
        copy = pltpu.make_async_copy(
            w_any.at[:, pl.ds(pl.multiple_of(target * width, width), width)],
            weights.at[turn],
            sem.at[turn],
        )
        copies.append(copy)
    for copy in reversed(copies):
        copy.start()
    tails = [part[:, feat : feat + LANES].astype(f32) for part in parts]
    for head in range(heads):
        levels = []
        for tail in tails:
            pieces = [tail[:, piece * heads + head : piece * heads + head + 1] for piece in range(3)]
            levels.append(pieces[0] + pieces[1] + pieces[2])
        top = functools.reduce(jnp.maximum, levels)
        shares = [jnp.exp2(level - top) for level in levels]
        whole = functools.reduce(jnp.add, shares)
        span = slice(head * HEAD_DIM, (head + 1) * HEAD_DIM)
        mixed = functools.reduce(
            jnp.add, [(share / whole) * part[:, span].astype(f32) for share, part in zip(shares, parts)]
        )
        context[:, span] = mixed.astype(bf16)
    for turn in reversed(range(size)):
        copies[turn].wait()
        step = 256 if width % 256 == 0 else width
        for at in range(0, width, step):
            outs[turn][:, at : at + step] = jnp.dot(
                context[...], weights[turn, :, at : at + step], preferred_element_type=f32
            ).astype(outs[turn].dtype)


def finish(parts, w_out, size):
    rows = parts[0].shape[0]
    feat, cols = w_out.shape
    width = cols // size
    vmem = pl.BlockSpec(memory_space=pltpu.VMEM)
    hbm = pl.BlockSpec(memory_space=pl.ANY)
    return pl.pallas_call(
        functools.partial(finish_kernel, len(parts), size),
        out_shape=[jax.ShapeDtypeStruct((rows, width), f32 if turn == 0 else bf16) for turn in range(size)],
        in_specs=[vmem] * len(parts) + [hbm],
        out_specs=[vmem] * size,
        scratch_shapes=[
            pltpu.VMEM((rows, feat), bf16),
            pltpu.VMEM((size, feat, width), bf16),
            pltpu.SemaphoreType.DMA((size,)),
        ],
        compiler_params=pltpu.CompilerParams(vmem_limit_bytes=24 * MIB),
        cost_estimate=pl.CostEstimate(
            flops=2 * rows * feat * cols, bytes_accessed=2 * feat * cols, transcendentals=0
        ),
        name="finish",
    )(*parts, w_out)


def swap(value, axis, turn, size):
    return lax.ppermute(value, axis, [(at, at ^ turn) for at in range(size)])


def body(
    hidden, norm_gain, w_query, w_key, w_value, w_out, stored_kv, selected, prompt_order, store_slot
):
    seq_count = lax.axis_size("seq")
    head_count = lax.axis_size("head")
    rows = hidden.shape[0]
    shard, _, local_kv, _ = stored_kv.shape
    stored = stored_kv.reshape(shard, -1)
    table = jnp.pad(selected.reshape(seq_count, rows), ((0, 0), (0, LANES - rows)), constant_values=-1)
    query, kv = project(hidden, norm_gain, selected, w_query, w_key, w_value)
    turns = list(range(2, seq_count, 2))
    far_first = sorted(turns, key=lambda turn: (-bin(turn).count("1"), turn))
    queries = {turn: swap(query, "seq", turn, seq_count) for turn in far_first}
    queries[0] = query
    cache, key_pos = merge(prompt_order, store_slot, table, stored, kv)
    other = swap(cache, "seq", 1, seq_count)
    caches = (cache, other)
    parts = attend((0,), caches, key_pos, table, [query])
    near_first = far_first[::-1]
    for at in range(0, len(near_first), 2):
        some = near_first[at : at + 2]
        done = attend(tuple(some), caches, key_pos, table, [queries[turn] for turn in some])
        parts += [swap(part, "seq", turn, seq_count) for turn, part in zip(some, done)]
    blocks = finish(parts, w_out, head_count)
    total = blocks[0]
    arrived = [swap(blocks[turn], "head", turn, head_count) for turn in range(1, head_count)]
    for block in arrived:
        total = total + block.astype(f32)
    new_kv = kv.reshape(rows, 2, local_kv, HEAD_DIM)
    return (total.astype(bf16), new_kv)


def solution(mesh):
    in_specs = (
        P("seq", None),
        P(),
        P(None, "head"),
        P(None, "head"),
        P(None, "head"),
        P("head", None),
        P("seq", None, "head", None),
        P(),
        P(),
        P(),
    )
    out_specs = (P("seq", "head"), P("seq", None, "head", None))
    return jax.shard_map(body, mesh=mesh, in_specs=in_specs, out_specs=out_specs, check_vma=False)
```

time: 210 us -> 72.2 us (0.34); the launches traced: 206 us -> 71.4 us
  waiting for transfers between devices: 91.6 us -> 20.7 us
  blocking collectives: 33.9 us -> 0 us
  matrix products: 33.6 us -> 0 us
  Pallas kernels: 0 us -> 25.7 us
  other arithmetic: 16.7 us -> 0.77 us
  between operations: 14.2 us -> 0.78 us
  starting transfers between devices: 0.34 us -> 10.8 us
  local copies, waits for them, and re-layouts: 15.3 us -> 12.7 us
    reduce_scatter x2 -> x0, waiting for transfers between devices: 62.1 us -> none  [the longest x1 41.2 us: body(): lax.psum_scatter((sums * shrink[..., None]).astype(jnp.bfloat16), 'seq',...]
    dot_general x10 -> x0, matrix products: 33.6 us -> none  [the longest x3 12 us: attend(): jnp.einsum('qkgn,nkd->qkgd', weights.astype(jnp.bfloat16), values, prefer...]
    pallas_call x0 -> x6, Pallas kernels: none -> 25.7 us  [the longest x3 14 us: attend(): pl.pallas_call(functools.partial(attend_kernel, partners), out_shape=[jax...]
    pmax x1 -> x0, blocking collectives: 23.5 us -> none  [body(): highest = lax.pmax(tops.astype(jnp.bfloat16), 'seq').astype(tops.dtype)]
    ppermute x0 -> x10, waiting for transfers between devices: none -> 20.7 us  [swap(): return lax.ppermute(value, axis, [(at, at ^ turn) for at in range(size)])]
    all_gather x1 -> x0, waiting for transfers between devices: 16 us -> none  [body(): every_query = lax.all_gather(query, 'seq', axis=0, tiled=True)]
    unnamed x5 -> x0, waiting for transfers between devices: 13.6 us -> none
    reduce_sum x7 -> x0, other arithmetic: 10.9 us -> none  [the longest x3 9 us: attend(): total = jnp.sum(weights, -1)]
  transfers between devices with their start and end apart: 4 -> 10, of which waited for: 4 -> 6; matrix products, arithmetic and copies ran while one was open for 10% -> 1% of each run, Pallas kernels for 0% -> 20%
where the time goes in v1:
time: 72.2 us; the launch traced here: 71.4 us
  Pallas kernels  25.7 us (36%)
  waiting for transfers between devices  20.7 us (29%)
  local copies, waits for them, and re-layouts  12.7 us (18%)
  starting transfers between devices  10.8 us (15%)
  between operations  0.78 us (1%)
  other arithmetic  0.77 us (1%)
    ppermute x10, waiting for transfers between devices, swap(): return lax.ppermute(value, axis, [(at, at ^ turn) for at in range(size)])  20.7 us
    pallas_call x3, Pallas kernels, attend(): pl.pallas_call(functools.partial(attend_kernel, partners), out_shape=[jax...  14 us
    ppermute x10, starting transfers between devices, swap(): return lax.ppermute(value, axis, [(at, at ^ turn) for at in range(size)])  10.8 us
    unnamed x20, local copies, waits for them, and re-layouts  9.08 us
    pallas_call x1, Pallas kernels, project(): pl.pallas_call(functools.partial(project_kernel, width), out_shape=(jax.S...  6.62 us
    pallas_call x1, Pallas kernels, finish(): pl.pallas_call(functools.partial(finish_kernel, len(parts), size), out_sh...  3.67 us
    pallas_call x1, Pallas kernels, merge(): pl.pallas_call(merge_kernel, out_shape=(jax.ShapeDtypeStruct((shard, cols...  1.47 us
    reshape x1, local copies, waits for them, and re-layouts, body(): stored = stored_kv.reshape(shard, -1)  1.46 us
  transfers between devices with their start and end apart: 10, of which 6 were waited for; matrix products, arithmetic and copies ran while one was open for 1% of the time, Pallas kernels for 20%

profile of v1, /device:TPU:8, one launch (start us, length us, event | category | flops | bytes accessed | tf_op | source)
XLA Modules:
  0.0 71.4 jit_solution(18190496418237023280)
XLA Ops:
  0.6 0.8 %reshape.19 = s32[8,96]{1,0:T(8,128)S(1)} reshape(s32[768]{0:T(1024)} %param.18) | data formatting | bytes 6144 | tf_op jit(solution)/shard_map/reshape | solution.py:402
  1.4 0.7 reshape.22.selected
  2.1 1.5 %reshape.20.stored = bf16[1024,512]{1,0:T(8,128)(2,1)S(1)} reshape(bf16[1024,2,2,128]{3,2,1,0:T(2,128)(2,1)} %param.17) | data formatting | bytes 2097152 | tf_op jit(solution)/shard_map/reshape | solution.py:401
  3.6 3.4 %copy-done = bf16[4096,1024]{1,0:T(8,128)(2,1)S(1)} copy-done((bf16[4096,1024]{1,0:T(8,128)(2,1)S(1)}, bf16[4096,1024]{1,0:T(8,128)(2,1)}, u32[]{:S(2)}) %copy-start) | copy-done | bytes 8388632
  7.0 1.6 %copy-done.1 = bf16[4096,256]{1,0:T(8,128)(2,1)S(1)} copy-done((bf16[4096,256]{1,0:T(8,128)(2,1)S(1)}, bf16[4096,256]{1,0:T(8,128)(2,1)}, u32[]{:S(2)}) %copy-start.1) | copy-done | bytes 2097176
  8.6 1.6 %copy-done.2 = bf16[4096,256]{1,0:T(8,128)(2,1)S(1)} copy-done((bf16[4096,256]{1,0:T(8,128)(2,1)S(1)}, bf16[4096,256]{1,0:T(8,128)(2,1)}, u32[]{:S(2)}) %copy-start.2) | copy-done | bytes 2097176
  10.2 1.1 %copy-done.3 = bf16[96,4096]{1,0:T(8,128)(2,1)S(1)} copy-done((bf16[96,4096]{1,0:T(8,128)(2,1)S(1)}, bf16[96,4096]{1,0:T(8,128)(2,1)}, u32[]{:S(2)}) %copy-start.3) | copy-done | bytes 786456
  11.3 0.7 %copy-done.4 = f32[4096]{0:T(1024)S(1)} copy-done((f32[4096]{0:T(1024)S(1)}, f32[4096]{0:T(1024)}, u32[]{:S(2)}) %copy-start.4) | copy-done | bytes 16408
  12.0 0.7 copy-done.7
  12.7 6.6 %project.1 = (bf16[96,1024]{1,0:T(8,128)(2,1)S(1)}, bf16[96,512]{1,0:T(8,128)(2,1)S(1)}) custom-call(bf16[96,4096]{1,0:T(8,128)(2,1)S(1)} %copy-done.3, f32[1,4096]{1,0:T(1,128)S(1)} %bitcast.3, s32[1,768]{1,0:T(1,128)S(1)} %reshape.22.selected, f32[1,128]{1,0:T(1,128)S(1)} %copy-done.7, bf16[4096,1024]{1,0:T(8,128)(2,1)S(1)} %copy-done, ...), custom_call_target="tpu_custom_call" | custom-call | flops 1207959552 | bytes 13369344 | tf_op jit(solution)/shard_map/project/pallas_call | solution.py:92
  19.3 1.5 %merge.1 = (bf16[1024,512]{1,0:T(8,128)(2,1)S(1)}, f32[2048,128]{1,0:T(8,128)S(1)}) custom-call(s32[2]{0:T(128)S(1)} %copy-done.5, s32[2]{0:T(128)S(1)} %copy-done.6, s32[8,128]{1,0:T(8,128)S(1)} %pad.4.selected.refs_3_, bf16[1024,512]{1,0:T(8,128)(2,1)S(1)} %reshape.20.stored, bf16[96,512]{1,0:T(8,128)(2,1)S(1)} %get-tuple-element.12.kv), custom_call_target="tpu_custom_call" | custom-call | flops 268435456 | bytes 2097152 | tf_op jit(solution)/shard_map/merge/pallas_call | solution.py:171
  20.9 1.6 %collective-permute-start.1 = (bf16[96,1024]{1,0:T(8,128)(2,1)S(1)}, bf16[96,1024]{1,0:T(8,128)(2,1)S(1)}, u32[]{:S(2)}, u32[]{:S(2)}) collective-permute-start(bf16[96,1024]{1,0:T(8,128)(2,1)S(1)} %get-tuple-element.15.refs_4_), channel_id=1, source_target_pairs={{0,16},{4,20},{8,24},{12,28},{16,0},{20,4},{24,8},{28,12},{1,17},{... | collective-permute-start | bytes 589832 | tf_op jit(solution)/shard_map/ppermute | solution.py:391
  22.5 1.5 %collective-permute-start.2 = (bf16[96,1024]{1,0:T(8,128)(2,1)S(1)}, bf16[96,1024]{1,0:T(8,128)(2,1)S(1)}, u32[]{:S(2)}, u32[]{:S(2)}) collective-permute-start(bf16[96,1024]{1,0:T(8,128)(2,1)S(1)} %get-tuple-element.15.refs_4_), channel_id=1, source_target_pairs={{0,8},{4,12},{8,0},{12,4},{16,24},{20,28},{24,16},{28,20},{1,9},{5... | collective-permute-start | bytes 589832 | tf_op jit(solution)/shard_map/ppermute | solution.py:391
  23.9 0.5 collective-permute-start.5
  24.4 3.8 %collective-permute-done.1.refs_4_ = bf16[96,1024]{1,0:T(8,128)(2,1)S(1)} collective-permute-done((bf16[96,1024]{1,0:T(8,128)(2,1)S(1)}, bf16[96,1024]{1,0:T(8,128)(2,1)S(1)}, u32[]{:S(2)}, u32[]{:S(2)}) %collective-permute-start.1) | collective-permute-done | bytes 196640 | tf_op jit(solution)/shard_map/ppermute | solution.py:391
  28.2 2.0 %collective-permute-done.2.refs_5_ = bf16[96,1024]{1,0:T(8,128)(2,1)S(1)} collective-permute-done((bf16[96,1024]{1,0:T(8,128)(2,1)S(1)}, bf16[96,1024]{1,0:T(8,128)(2,1)S(1)}, u32[]{:S(2)}, u32[]{:S(2)}) %collective-permute-start.2) | collective-permute-done | bytes 196640 | tf_op jit(solution)/shard_map/ppermute | solution.py:391
  30.2 6.1 %attend.4 = (bf16[96,1152]{1,0:T(8,128)(2,1)S(1)}, bf16[96,1152]{1,0:T(8,128)(2,1)S(1)}) custom-call(bf16[1024,512]{1,0:T(8,128)(2,1)S(1)} %get-tuple-element.13.refs_0_, bf16[1024,512]{1,0:T(8,128)(2,1)S(1)} %collective-permute-done.refs_1_, f32[2048,128]{1,0:T(8,128)S(1)} %get-tuple-element.14.refs_2_, s32[8,128]{1,0:T(8,128)S(1)} %pad.4.selected.refs_3_, ...), custom_call_target="tpu_custom_call" | custom-call | flops 3221225472 | bytes 4194304 | tf_op jit(solution)/shard_map/attend/pallas_call | solution.py:299
  36.3 0.6 collective-permute-start.3
  36.9 1.5 %collective-permute-start.4 = (bf16[96,1152]{1,0:T(8,128)(2,1)S(1)}, bf16[96,1152]{1,0:T(8,128)(2,1)S(1)}, u32[]{:S(2)}, u32[]{:S(2)}) collective-permute-start(bf16[96,1152]{1,0:T(8,128)(2,1)S(1)} %get-tuple-element.17), channel_id=1, source_target_pairs={{0,8},{4,12},{8,0},{12,4},{16,24},{20,28},{24,16},{28,20},{1,9},{5... | collective-permute-start | bytes 663560 | tf_op jit(solution)/shard_map/ppermute | solution.py:391
  38.4 4.1 %attend.5 = bf16[96,1152]{1,0:T(8,128)(2,1)S(1)} custom-call(bf16[1024,512]{1,0:T(8,128)(2,1)S(1)} %get-tuple-element.13.refs_0_, bf16[1024,512]{1,0:T(8,128)(2,1)S(1)} %collective-permute-done.refs_1_, f32[2048,128]{1,0:T(8,128)S(1)} %get-tuple-element.14.refs_2_, s32[8,128]{1,0:T(8,128)S(1)} %pad.4.selected.refs_3_, ...), custom_call_target="tpu_custom_call" | custom-call | flops 1610612736 | bytes 4194304 | tf_op jit(solution)/shard_map/attend/pallas_call | solution.py:299
  42.4 1.6 %collective-permute-start.6 = (bf16[96,1152]{1,0:T(8,128)(2,1)S(1)}, bf16[96,1152]{1,0:T(8,128)(2,1)S(1)}, u32[]{:S(2)}, u32[]{:S(2)}) collective-permute-start(bf16[96,1152]{1,0:T(8,128)(2,1)S(1)} %attend.5), channel_id=1, source_target_pairs={{0,24},{4,28},{8,16},{12,20},{16,8},{20,12},{24,0},{28,4},{1,25},{... | collective-permute-start | bytes 663560 | tf_op jit(solution)/shard_map/ppermute | solution.py:391
  44.0 3.8 %attend.3.refs_0_ = bf16[96,1152]{1,0:T(8,128)(2,1)S(1)} custom-call(bf16[1024,512]{1,0:T(8,128)(2,1)S(1)} %get-tuple-element.13.refs_0_, bf16[1024,512]{1,0:T(8,128)(2,1)S(1)} %collective-permute-done.refs_1_, f32[2048,128]{1,0:T(8,128)S(1)} %get-tuple-element.14.refs_2_, s32[8,128]{1,0:T(8,128)S(1)} %pad.4.selected.refs_3_, ...), custom_call_target="tpu_custom_call" | custom-call | flops 1610612736 | bytes 4194304 | tf_op jit(solution)/shard_map/attend/pallas_call | solution.py:299
  47.8 1.5 %collective-permute-done.6.refs_3_ = bf16[96,1152]{1,0:T(8,128)(2,1)S(1)} collective-permute-done((bf16[96,1152]{1,0:T(8,128)(2,1)S(1)}, bf16[96,1152]{1,0:T(8,128)(2,1)S(1)}, u32[]{:S(2)}, u32[]{:S(2)}) %collective-permute-start.6) | collective-permute-done | bytes 221216 | tf_op jit(solution)/shard_map/ppermute | solution.py:391
  49.3 3.7 %finish.1 = (f32[96,1024]{1,0:T(8,128)S(1)}, bf16[96,1024]{1,0:T(8,128)(2,1)S(1)}, bf16[96,1024]{1,0:T(8,128)(2,1)S(1)}, bf16[96,1024]{1,0:T(8,128)(2,1)S(1)}) custom-call(bf16[96,1152]{1,0:T(8,128)(2,1)S(1)} %attend.3.refs_0_, bf16[96,1152]{1,0:T(8,128)(2,1)S(1)} %collective-permute-done.3.refs_1_, bf16[96,1152]{1,0:T(8,128)(2,1)S(1)} %collective-permute-done.4.refs_2_, ...), custom_call_target="tpu_custom_call" | custom-call | flops 805306368 | bytes 8388608 | tf_op jit(solution)/shard_map/finish/pallas_call | solution.py:372
  53.0 0.5 collective-permute-start.7
  53.5 2.6 %collective-permute-start.8 = (bf16[96,1024]{1,0:T(8,128)(2,1)S(1)}, bf16[96,1024]{1,0:T(8,128)(2,1)S(1)}, u32[]{:S(2)}, u32[]{:S(2)}) collective-permute-start(bf16[96,1024]{1,0:T(8,128)(2,1)S(1)} %get-tuple-element.20), channel_id=1, source_target_pairs={{0,2},{1,3},{2,0},{3,1},{4,6},{5,7},{6,4},{7,5},{8,10},{9,11},{10,... | collective-permute-start | bytes 589832 | tf_op jit(solution)/shard_map/ppermute | solution.py:391
  56.1 0.4 collective-permute-start.9
  56.5 0.7 reshape.23
  57.2 3.7 %collective-permute-done.7 = bf16[96,1024]{1,0:T(8,128)(2,1)S(1)} collective-permute-done((bf16[96,1024]{1,0:T(8,128)(2,1)S(1)}, bf16[96,1024]{1,0:T(8,128)(2,1)S(1)}, u32[]{:S(2)}, u32[]{:S(2)}) %collective-permute-start.7) | collective-permute-done | bytes 196640 | tf_op jit(solution)/shard_map/ppermute | solution.py:391
  60.9 6.6 %collective-permute-done.8 = bf16[96,1024]{1,0:T(8,128)(2,1)S(1)} collective-permute-done((bf16[96,1024]{1,0:T(8,128)(2,1)S(1)}, bf16[96,1024]{1,0:T(8,128)(2,1)S(1)}, u32[]{:S(2)}, u32[]{:S(2)}) %collective-permute-start.8) | collective-permute-done | bytes 196640 | tf_op jit(solution)/shard_map/ppermute | solution.py:391
  67.5 3.2 %collective-permute-done.9 = bf16[96,1024]{1,0:T(8,128)(2,1)S(1)} collective-permute-done((bf16[96,1024]{1,0:T(8,128)(2,1)S(1)}, bf16[96,1024]{1,0:T(8,128)(2,1)S(1)}, u32[]{:S(2)}, u32[]{:S(2)}) %collective-permute-start.9) | collective-permute-done | bytes 196640 | tf_op jit(solution)/shard_map/ppermute | solution.py:391
  70.7 0.8 %add_convert_fusion = bf16[96,1024]{1,0:T(8,128)(2,1)} fusion(bf16[96,1024]{1,0:T(8,128)(2,1)S(1)} %collective-permute-done.9, bf16[96,1024]{1,0:T(8,128)(2,1)S(1)} %collective-permute-done.8, f32[96,1024]{1,0:T(8,128)S(1)} %get-tuple-element.18, bf16[96,1024]{1,0:T(8,128)(2,1)S(1)} %collective-permute-done.7), kind=kLoop, calls=%fused_computation | loop fusion | flops 688128 | bytes 1179648 | tf_op jit(solution)/shard_map/convert_element_type | solution.py:423
  (21 shorter events, 0.1 us)
Async XLA Ops:
  0.6 18.7 %copy-start.5 = (s32[2]{0:T(128)S(1)}, s32[2]{0:T(128)}, u32[]{:S(2)}) copy-start(s32[2]{0:T(128)} %order.1) | copy-start | bytes 28
  0.6 18.7 %copy-start.6 = (s32[2]{0:T(128)S(1)}, s32[2]{0:T(128)}, u32[]{:S(2)}) copy-start(s32[2]{0:T(128)} %slot.1) | copy-start | bytes 28
  3.6 3.4 %copy-start = (bf16[4096,1024]{1,0:T(8,128)(2,1)S(1)}, bf16[4096,1024]{1,0:T(8,128)(2,1)}, u32[]{:S(2)}) copy-start(bf16[4096,1024]{1,0:T(8,128)(2,1)} %wq_any.1) | copy-start | bytes 25165828
  7.0 1.6 %copy-start.1 = (bf16[4096,256]{1,0:T(8,128)(2,1)S(1)}, bf16[4096,256]{1,0:T(8,128)(2,1)}, u32[]{:S(2)}) copy-start(bf16[4096,256]{1,0:T(8,128)(2,1)} %wk_any.1) | copy-start | bytes 6291460
  8.6 1.6 %copy-start.2 = (bf16[4096,256]{1,0:T(8,128)(2,1)S(1)}, bf16[4096,256]{1,0:T(8,128)(2,1)}, u32[]{:S(2)}) copy-start(bf16[4096,256]{1,0:T(8,128)(2,1)} %wv_any.1) | copy-start | bytes 6291460
  10.2 1.1 %copy-start.3 = (bf16[96,4096]{1,0:T(8,128)(2,1)S(1)}, bf16[96,4096]{1,0:T(8,128)(2,1)}, u32[]{:S(2)}) copy-start(bf16[96,4096]{1,0:T(8,128)(2,1)} %hidden_any.1) | copy-start | bytes 2359300
  11.3 0.7 %copy-start.4 = (f32[4096]{0:T(1024)S(1)}, f32[4096]{0:T(1024)}, u32[]{:S(2)}) copy-start(f32[4096]{0:T(1024)} %param.12) | copy-start | bytes 49156
  12.0 0.7 copy-start.7
  20.8 9.4 %collective-permute-start = (bf16[1024,512]{1,0:T(8,128)(2,1)S(1)}, bf16[1024,512]{1,0:T(8,128)(2,1)S(1)}, u32[]{:S(2)}, u32[]{:S(2)}) collective-permute-start(bf16[1024,512]{1,0:T(8,128)(2,1)S(1)} %get-tuple-element.13.refs_0_), channel_id=1, source_target_pairs={{0,4},{4,0},{8,12},{12,8},{16,20},{20,16},{24,28},{28,24},{1,5},{5... | collective-permute-start | bytes 3145736 | tf_op jit(solution)/shard_map/ppermute | solution.py:391
  20.9 7.3 %collective-permute-start.1 = (bf16[96,1024]{1,0:T(8,128)(2,1)S(1)}, bf16[96,1024]{1,0:T(8,128)(2,1)S(1)}, u32[]{:S(2)}, u32[]{:S(2)}) collective-permute-start(bf16[96,1024]{1,0:T(8,128)(2,1)S(1)} %get-tuple-element.15.refs_4_), channel_id=1, source_target_pairs={{0,16},{4,20},{8,24},{12,28},{16,0},{20,4},{24,8},{28,12},{1,17},{... | collective-permute-start | bytes 589832 | tf_op jit(solution)/shard_map/ppermute | solution.py:391
  22.5 7.7 %collective-permute-start.2 = (bf16[96,1024]{1,0:T(8,128)(2,1)S(1)}, bf16[96,1024]{1,0:T(8,128)(2,1)S(1)}, u32[]{:S(2)}, u32[]{:S(2)}) collective-permute-start(bf16[96,1024]{1,0:T(8,128)(2,1)S(1)} %get-tuple-element.15.refs_4_), channel_id=1, source_target_pairs={{0,8},{4,12},{8,0},{12,4},{16,24},{20,28},{24,16},{28,20},{1,9},{5... | collective-permute-start | bytes 589832 | tf_op jit(solution)/shard_map/ppermute | solution.py:391
  23.9 14.4 %collective-permute-start.5 = (bf16[96,1024]{1,0:T(8,128)(2,1)S(1)}, bf16[96,1024]{1,0:T(8,128)(2,1)S(1)}, u32[]{:S(2)}, u32[]{:S(2)}) collective-permute-start(bf16[96,1024]{1,0:T(8,128)(2,1)S(1)} %get-tuple-element.15.refs_4_), channel_id=1, source_target_pairs={{0,24},{4,28},{8,16},{12,20},{16,8},{20,12},{24,0},{28,4},{1,25},{... | collective-permute-start | bytes 589832 | tf_op jit(solution)/shard_map/ppermute | solution.py:391
  30.2 19.1 %slice-start = ((s8[8388608]{0:T(1024)(128)(4,1)}), s8[4194304]{0:T(1024)(128)(4,1)S(1)}, s32[]{:S(2)}) async-start(s8[8388608]{0:T(1024)(128)(4,1)} %bitcast.1), calls=%async_computation | async-start | bytes 8388608
  36.3 13.0 %slice-start.1 = ((s8[8388608]{0:T(1024)(128)(4,1)}), s8[4194304]{0:T(1024)(128)(4,1)S(1)}, s32[]{:S(2)}) async-start(s8[8388608]{0:T(1024)(128)(4,1)} %bitcast.1), calls=%async_computation.1 | async-start | bytes 8388608
  36.3 11.5 %collective-permute-start.3 = (bf16[96,1152]{1,0:T(8,128)(2,1)S(1)}, bf16[96,1152]{1,0:T(8,128)(2,1)S(1)}, u32[]{:S(2)}, u32[]{:S(2)}) collective-permute-start(bf16[96,1152]{1,0:T(8,128)(2,1)S(1)} %get-tuple-element.16), channel_id=1, source_target_pairs={{0,16},{4,20},{8,24},{12,28},{16,0},{20,4},{24,8},{28,12},{1,17},{... | collective-permute-start | bytes 663560 | tf_op jit(solution)/shard_map/ppermute | solution.py:391
  36.9 11.0 %collective-permute-start.4 = (bf16[96,1152]{1,0:T(8,128)(2,1)S(1)}, bf16[96,1152]{1,0:T(8,128)(2,1)S(1)}, u32[]{:S(2)}, u32[]{:S(2)}) collective-permute-start(bf16[96,1152]{1,0:T(8,128)(2,1)S(1)} %get-tuple-element.17), channel_id=1, source_target_pairs={{0,8},{4,12},{8,0},{12,4},{16,24},{20,28},{24,16},{28,20},{1,9},{5... | collective-permute-start | bytes 663560 | tf_op jit(solution)/shard_map/ppermute | solution.py:391
  42.4 6.9 %collective-permute-start.6 = (bf16[96,1152]{1,0:T(8,128)(2,1)S(1)}, bf16[96,1152]{1,0:T(8,128)(2,1)S(1)}, u32[]{:S(2)}, u32[]{:S(2)}) collective-permute-start(bf16[96,1152]{1,0:T(8,128)(2,1)S(1)} %attend.5), channel_id=1, source_target_pairs={{0,24},{4,28},{8,16},{12,20},{16,8},{20,12},{24,0},{28,4},{1,25},{... | collective-permute-start | bytes 663560 | tf_op jit(solution)/shard_map/ppermute | solution.py:391
  53.0 7.9 %collective-permute-start.7 = (bf16[96,1024]{1,0:T(8,128)(2,1)S(1)}, bf16[96,1024]{1,0:T(8,128)(2,1)S(1)}, u32[]{:S(2)}, u32[]{:S(2)}) collective-permute-start(bf16[96,1024]{1,0:T(8,128)(2,1)S(1)} %get-tuple-element.19), channel_id=1, source_target_pairs={{0,1},{1,0},{2,3},{3,2},{4,5},{5,4},{6,7},{7,6},{8,9},{9,8},{10,11... | collective-permute-start | bytes 589832 | tf_op jit(solution)/shard_map/ppermute | solution.py:391
  53.5 13.9 %collective-permute-start.8 = (bf16[96,1024]{1,0:T(8,128)(2,1)S(1)}, bf16[96,1024]{1,0:T(8,128)(2,1)S(1)}, u32[]{:S(2)}, u32[]{:S(2)}) collective-permute-start(bf16[96,1024]{1,0:T(8,128)(2,1)S(1)} %get-tuple-element.20), channel_id=1, source_target_pairs={{0,2},{1,3},{2,0},{3,1},{4,6},{5,7},{6,4},{7,5},{8,10},{9,11},{10,... | collective-permute-start | bytes 589832 | tf_op jit(solution)/shard_map/ppermute | solution.py:391
  56.1 14.6 %collective-permute-start.9 = (bf16[96,1024]{1,0:T(8,128)(2,1)S(1)}, bf16[96,1024]{1,0:T(8,128)(2,1)S(1)}, u32[]{:S(2)}, u32[]{:S(2)}) collective-permute-start(bf16[96,1024]{1,0:T(8,128)(2,1)S(1)} %get-tuple-element.21), channel_id=1, source_target_pairs={{0,3},{1,2},{2,1},{3,0},{4,7},{5,6},{6,5},{7,4},{8,11},{9,10},{10,... | collective-permute-start | bytes 589832 | tf_op jit(solution)/shard_map/ppermute | solution.py:391

commit v2 on v1

--- a/solution.py
+++ b/solution.py
@@ -34,7 +34,7 @@
 
 
 def project_kernel(
-    width, hidden_any, gain, selected, freq, wq_any, wk_any, wv_any, query, kv,
+    width, hidden_any, gain, selected, freq, wq_any, wk_any, wv_any, query, kv, table,
     hidden, normed, weights, sem,
 ):
     rows, feat = hidden.shape
@@ -52,10 +52,14 @@
         )
         copy.start()
         copies.append(copy)
-    total = selected.shape[1]
+    total = selected.shape[0]
     me = lax.axis_index("seq")
     mine = iota((rows, total), 1) == iota((rows, total), 0) + me * rows
-    positions = jnp.sum(jnp.where(mine, selected[...].astype(f32), 0.0), 1, keepdims=True)
+    listed = selected[...].reshape(1, total)
+    positions = jnp.sum(jnp.where(mine, listed.astype(f32), 0.0), 1, keepdims=True)
+    table[...] = jnp.full(table.shape, -1, jnp.int32)
+    for at in range(total // rows):
+        table[at : at + 1, 0:rows] = listed[:, at * rows : (at + 1) * rows]
     angle = positions * freq[...]
     cosine = jnp.cos(angle)
     sine = jnp.sin(angle)
@@ -94,21 +98,22 @@
         out_shape=(
             jax.ShapeDtypeStruct((rows, wq.shape[1]), bf16),
             jax.ShapeDtypeStruct((rows, wk.shape[1] + wv.shape[1]), bf16),
+            jax.ShapeDtypeStruct((selected.shape[0] // rows, LANES), jnp.int32),
         ),
         in_specs=[hbm, vmem, vmem, vmem, hbm, hbm, hbm],
-        out_specs=(vmem, vmem),
+        out_specs=(vmem, vmem, vmem),
         scratch_shapes=[
             pltpu.VMEM((rows, feat), bf16),
             pltpu.VMEM((rows, feat), bf16),
             pltpu.VMEM((feat, cols), bf16),
             pltpu.SemaphoreType.DMA((1 + cols // width,)),
         ],
-        compiler_params=pltpu.CompilerParams(vmem_limit_bytes=28 * MIB),
+        compiler_params=pltpu.CompilerParams(vmem_limit_bytes=56 * MIB),
         cost_estimate=pl.CostEstimate(
             flops=2 * rows * feat * cols, bytes_accessed=2 * feat * (cols + rows), transcendentals=0
         ),
         name="project",
-    )(hidden, gain.reshape(1, feat), selected.reshape(1, -1), freq, wq, wk, wv)
+    )(hidden, gain.reshape(1, feat), selected, freq, wq, wk, wv)
 
 
 def block_of(index, shard, order, slot):
@@ -121,9 +126,13 @@
 
 
 def merge_kernel(order, slot, selected, stored, kv, cache, key_pos):
-    shard, cols = stored.shape
+    shard, cols = cache.shape
+    kinds = cols // LANES
     rows = kv.shape[0]
+    step = 128
     me = lax.axis_index("seq")
+    spread = iota((step, kinds * step), 1) - kinds * iota((step, kinds * step), 0)
+    takes = [(spread == kind).astype(f32).astype(bf16) for kind in range(kinds)]
     for half in range(2):
         index = me if half == 0 else me ^ 1
         block = block_of(index, shard, order, slot)
@@ -143,7 +152,6 @@
                 fresh = jnp.concatenate([fresh, jnp.zeros((LANES - rows, cols), bf16)], 0)
             sources.append(fresh)
         source = jnp.concatenate(sources, 1)
-        step = 128
         for at in range(0, shard, step):
             places = iota((step, LANES), 0) + at
             hit = (places == holes).astype(f32).astype(bf16)
@@ -156,16 +164,19 @@
                 (places + block * shard).astype(f32),
             )
             if half == 0:
-                for col in range(0, cols, LANES):
+                mixed = stored[at * kinds : (at + step) * kinds, :]
+                for kind in range(kinds):
+                    col = kind * LANES
                     cache[at : at + step, col : col + LANES] = jnp.where(
                         hole,
                         picked[:, 3 * LANES + col : 4 * LANES + col],
-                        stored[at : at + step, col : col + LANES].astype(f32),
+                        jnp.dot(takes[kind], mixed, preferred_element_type=f32),
                     ).astype(bf16)
 
 
 def merge(order, slot, selected, stored, kv):
-    shard, cols = stored.shape
+    cols = kv.shape[1]
+    shard = stored.shape[0] * LANES // cols
     smem = pl.BlockSpec(memory_space=pltpu.SMEM)
     vmem = pl.BlockSpec(memory_space=pltpu.VMEM)
     return pl.pallas_call(
@@ -177,9 +188,7 @@
         in_specs=[smem, smem, vmem, vmem, vmem],
         out_specs=(vmem, vmem),
         compiler_params=pltpu.CompilerParams(vmem_limit_bytes=16 * MIB),
-        cost_estimate=pl.CostEstimate(
-            flops=4 * shard * cols * LANES, bytes_accessed=4 * shard * cols, transcendentals=0
-        ),
+        cost_estimate=pl.CostEstimate(flops=1000, bytes_accessed=1000, transcendentals=0),
         name="merge",
     )(order, slot, selected, stored, kv)
 
@@ -322,24 +331,13 @@
 
 def finish_kernel(count, size, *refs):
     parts = refs[:count]
-    w_any = refs[count]
+    weights = refs[count]
     outs = refs[count + 1 : count + 1 + size]
-    context, weights, sem = refs[count + 1 + size :]
+    (context,) = refs[count + 1 + size :]
     rows, feat = context.shape
     heads = feat // HEAD_DIM
-    width = w_any.shape[1] // size
+    width = weights.shape[1] // size
     me = lax.axis_index("head")
-    copies = []
-    for turn in range(size):
-        target = lax.rem(me + turn, size) if size & (size - 1) else me ^ turn
-        copy = pltpu.make_async_copy(
-            w_any.at[:, pl.ds(pl.multiple_of(target * width, width), width)],
-            weights.at[turn],
-            sem.at[turn],
-        )
-        copies.append(copy)
-    for copy in reversed(copies):
-        copy.start()
     tails = [part[:, feat : feat + LANES].astype(f32) for part in parts]
     for head in range(heads):
         levels = []
@@ -354,12 +352,13 @@
             jnp.add, [(share / whole) * part[:, span].astype(f32) for share, part in zip(shares, parts)]
         )
         context[:, span] = mixed.astype(bf16)
-    for turn in reversed(range(size)):
-        copies[turn].wait()
+    for turn in range(size):
+        start = (me ^ turn) * width
         step = 256 if width % 256 == 0 else width
         for at in range(0, width, step):
+            part = weights[:, pl.ds(pl.multiple_of(start + at, step), step)]
             outs[turn][:, at : at + step] = jnp.dot(
-                context[...], weights[turn, :, at : at + step], preferred_element_type=f32
+                context[...], part, preferred_element_type=f32
             ).astype(outs[turn].dtype)
 
 
@@ -368,16 +367,13 @@
     feat, cols = w_out.shape
     width = cols // size
     vmem = pl.BlockSpec(memory_space=pltpu.VMEM)
-    hbm = pl.BlockSpec(memory_space=pl.ANY)
     return pl.pallas_call(
         functools.partial(finish_kernel, len(parts), size),
         out_shape=[jax.ShapeDtypeStruct((rows, width), f32 if turn == 0 else bf16) for turn in range(size)],
-        in_specs=[vmem] * len(parts) + [hbm],
+        in_specs=[vmem] * (len(parts) + 1),
         out_specs=[vmem] * size,
         scratch_shapes=[
             pltpu.VMEM((rows, feat), bf16),
-            pltpu.VMEM((size, feat, width), bf16),
-            pltpu.SemaphoreType.DMA((size,)),
         ],
         compiler_params=pltpu.CompilerParams(vmem_limit_bytes=24 * MIB),
         cost_estimate=pl.CostEstimate(
@@ -398,13 +394,11 @@
     head_count = lax.axis_size("head")
     rows = hidden.shape[0]
     shard, _, local_kv, _ = stored_kv.shape
-    stored = stored_kv.reshape(shard, -1)
-    table = jnp.pad(selected.reshape(seq_count, rows), ((0, 0), (0, LANES - rows)), constant_values=-1)
-    query, kv = project(hidden, norm_gain, selected, w_query, w_key, w_value)
+    stored = stored_kv.reshape(-1, HEAD_DIM)
+    query, kv, table = project(hidden, norm_gain, selected, w_query, w_key, w_value)
     turns = list(range(2, seq_count, 2))
     far_first = sorted(turns, key=lambda turn: (-bin(turn).count("1"), turn))
     queries = {turn: swap(query, "seq", turn, seq_count) for turn in far_first}
-    queries[0] = query
     cache, key_pos = merge(prompt_order, store_slot, table, stored, kv)
     other = swap(cache, "seq", 1, seq_count)
     caches = (cache, other)

time: 72.2 us -> 63.3 us (0.88)
  local copies, waits for them, and re-layouts: 12.7 us -> 2.96 us
  Pallas kernels: 25.7 us -> 26.5 us
    unnamed x20 -> x22, local copies, waits for them, and re-layouts: 9.08 us -> 2.29 us
    reshape x3 -> x0, local copies, waits for them, and re-layouts: 2.92 us -> none  [the longest x1 1.46 us: body(): stored = stored_kv.reshape(shard, -1)]
    pallas_call x1, Pallas kernels: 3.67 us -> 2.2 us  [finish(): pl.pallas_call(functools.partial(finish_kernel, len(parts), size), out_sh...]
    pallas_call x1, Pallas kernels: 6.62 us -> 7.82 us  [project(): pl.pallas_call(functools.partial(project_kernel, width), out_shape=(jax.S...]
    pallas_call x1, Pallas kernels: 1.47 us -> 2.56 us  [merge(): pl.pallas_call(merge_kernel, out_shape=(jax.ShapeDtypeStruct((shard, cols...]
  transfers between devices with their start and end apart: 10 -> 10, of which waited for: 6 -> 6; matrix products, arithmetic and copies ran while one was open for 1% -> 1% of each run, Pallas kernels for 20% -> 22%
where the time goes in v2:
time: 63.3 us; the launch traced here: 62.7 us
  Pallas kernels  26.5 us (42%)
  waiting for transfers between devices  20.9 us (33%)
  starting transfers between devices  10.8 us (17%)
  local copies, waits for them, and re-layouts  2.96 us (5%)
  between operations  0.79 us (1%)
  other arithmetic  0.77 us (1%)
    ppermute x10, waiting for transfers between devices, swap(): return lax.ppermute(value, axis, [(at, at ^ turn) for at in range(size)])  20.9 us
    pallas_call x3, Pallas kernels, attend(): pl.pallas_call(functools.partial(attend_kernel, partners), out_shape=[jax...  13.9 us
    ppermute x10, starting transfers between devices, swap(): return lax.ppermute(value, axis, [(at, at ^ turn) for at in range(size)])  10.8 us
    pallas_call x1, Pallas kernels, project(): pl.pallas_call(functools.partial(project_kernel, width), out_shape=(jax.S...  7.82 us
    pallas_call x1, Pallas kernels, merge(): pl.pallas_call(merge_kernel, out_shape=(jax.ShapeDtypeStruct((shard, cols...  2.56 us
    unnamed x22, local copies, waits for them, and re-layouts  2.29 us
    pallas_call x1, Pallas kernels, finish(): pl.pallas_call(functools.partial(finish_kernel, len(parts), size), out_sh...  2.2 us
  transfers between devices with their start and end apart: 10, of which 6 were waited for; matrix products, arithmetic and copies ran while one was open for 1% of the time, Pallas kernels for 22%

profile of v2, /device:TPU:8, one launch (start us, length us, event | category | flops | bytes accessed | tf_op | source)
XLA Modules:
  0.0 62.7 jit_solution(6929274889845015788)
XLA Ops:
  0.7 7.8 %project.1 = (bf16[96,1024]{1,0:T(8,128)(2,1)}, bf16[96,512]{1,0:T(8,128)(2,1)}, s32[8,128]{1,0:T(8,128)}) custom-call(bf16[96,4096]{1,0:T(8,128)(2,1)} %hidden_any.1, f32[1,4096]{1,0:T(1,128)} %bitcast.5, s32[768]{0:T(1024)} %selected.1, f32[1,128]{1,0:T(1,128)} %constant.2.clone.freq, bf16[4096,1024]{1,0:T(8,128)(2,1)} %wq_any.1, ...), custom_call_target="tpu_custom_call" | custom-call | flops 1207959552 | bytes 13369344 | tf_op jit(solution)/shard_map/project/pallas_call | solution.py:96
  8.5 0.0 copy-start.1
  8.5 0.9 %copy-done.1 = bf16[96,512]{1,0:T(8,128)(2,1)S(1)} copy-done((bf16[96,512]{1,0:T(8,128)(2,1)S(1)}, bf16[96,512]{1,0:T(8,128)(2,1)}, u32[]{:S(2)}) %copy-start.1) | copy-done | bytes 98328
  9.4 0.7 %copy-done.3 = s32[8,128]{1,0:T(8,128)S(1)} copy-done((s32[8,128]{1,0:T(8,128)S(1)}, s32[8,128]{1,0:T(8,128)}, u32[]{:S(2)}) %copy-start.3) | copy-done | bytes 4120
  10.1 2.6 %merge.1 = (bf16[1024,512]{1,0:T(8,128)(2,1)S(1)}, f32[2048,128]{1,0:T(8,128)S(1)}) custom-call(s32[2]{0:T(128)S(1)} %copy-done.6, s32[2]{0:T(128)S(1)} %copy-done.7, s32[8,128]{1,0:T(8,128)S(1)} %copy-done.3, bf16[4096,128]{1,0:T(8,128)(2,1)S(1)} %bitcast.4, bf16[96,512]{1,0:T(8,128)(2,1)S(1)} %copy-done.1), custom_call_target="tpu_custom_call" | custom-call | flops 1000 | bytes 1000 | tf_op jit(solution)/shard_map/merge/pallas_call | solution.py:182
  12.7 0.1 collective-permute-start
  12.7 1.6 %collective-permute-start.1 = (bf16[96,1024]{1,0:T(8,128)(2,1)}, bf16[96,1024]{1,0:T(8,128)(2,1)S(1)}, u32[]{:S(2)}, u32[]{:S(2)}) collective-permute-start(bf16[96,1024]{1,0:T(8,128)(2,1)} %get-tuple-element.17.refs_4_), channel_id=1, source_target_pairs={{0,16},{4,20},{8,24},{12,28},{16,0},{20,4},{24,8},{28,12},{1,17},{... | collective-permute-start | bytes 589832 | tf_op jit(solution)/shard_map/ppermute | solution.py:387
  14.3 1.5 %collective-permute-start.2 = (bf16[96,1024]{1,0:T(8,128)(2,1)}, bf16[96,1024]{1,0:T(8,128)(2,1)S(1)}, u32[]{:S(2)}, u32[]{:S(2)}) collective-permute-start(bf16[96,1024]{1,0:T(8,128)(2,1)} %get-tuple-element.17.refs_4_), channel_id=1, source_target_pairs={{0,8},{4,12},{8,0},{12,4},{16,24},{20,28},{24,16},{28,20},{1,9},{5... | collective-permute-start | bytes 589832 | tf_op jit(solution)/shard_map/ppermute | solution.py:387
  15.8 0.5 collective-permute-start.5
  16.3 4.0 %collective-permute-done.1.refs_4_ = bf16[96,1024]{1,0:T(8,128)(2,1)S(1)} collective-permute-done((bf16[96,1024]{1,0:T(8,128)(2,1)}, bf16[96,1024]{1,0:T(8,128)(2,1)S(1)}, u32[]{:S(2)}, u32[]{:S(2)}) %collective-permute-start.1) | collective-permute-done | bytes 196640 | tf_op jit(solution)/shard_map/ppermute | solution.py:387
  20.3 2.0 %collective-permute-done.2.refs_5_ = bf16[96,1024]{1,0:T(8,128)(2,1)S(1)} collective-permute-done((bf16[96,1024]{1,0:T(8,128)(2,1)}, bf16[96,1024]{1,0:T(8,128)(2,1)S(1)}, u32[]{:S(2)}, u32[]{:S(2)}) %collective-permute-start.2) | collective-permute-done | bytes 196640 | tf_op jit(solution)/shard_map/ppermute | solution.py:387
  22.3 0.0 collective-permute-done.refs_1_
  22.3 0.7 %copy-done.4 = s32[8,128]{1,0:T(8,128)S(1)} copy-done((s32[8,128]{1,0:T(8,128)S(1)}, s32[8,128]{1,0:T(8,128)}, u32[]{:S(2)}) %copy-start.4) | copy-done | bytes 4120
  23.0 6.1 %attend.4 = (bf16[96,1152]{1,0:T(8,128)(2,1)S(1)}, bf16[96,1152]{1,0:T(8,128)(2,1)S(1)}) custom-call(bf16[1024,512]{1,0:T(8,128)(2,1)S(1)} %get-tuple-element.15.refs_0_, bf16[1024,512]{1,0:T(8,128)(2,1)S(1)} %collective-permute-done.refs_1_, f32[2048,128]{1,0:T(8,128)S(1)} %get-tuple-element.16.refs_2_, s32[8,128]{1,0:T(8,128)S(1)} %copy-done.4, ...), custom_call_target="tpu_custom_call" | custom-call | flops 3221225472 | bytes 4194304 | tf_op jit(solution)/shard_map/attend/pallas_call | solution.py:308
  29.1 0.0 slice-start.1
  29.1 0.6 collective-permute-start.3
  29.6 1.5 %collective-permute-start.4 = (bf16[96,1152]{1,0:T(8,128)(2,1)S(1)}, bf16[96,1152]{1,0:T(8,128)(2,1)S(1)}, u32[]{:S(2)}, u32[]{:S(2)}) collective-permute-start(bf16[96,1152]{1,0:T(8,128)(2,1)S(1)} %get-tuple-element.19), channel_id=1, source_target_pairs={{0,8},{4,12},{8,0},{12,4},{16,24},{20,28},{24,16},{28,20},{1,9},{5... | collective-permute-start | bytes 663560 | tf_op jit(solution)/shard_map/ppermute | solution.py:387
  31.1 4.0 %attend.5 = bf16[96,1152]{1,0:T(8,128)(2,1)S(1)} custom-call(bf16[1024,512]{1,0:T(8,128)(2,1)S(1)} %get-tuple-element.15.refs_0_, bf16[1024,512]{1,0:T(8,128)(2,1)S(1)} %collective-permute-done.refs_1_, f32[2048,128]{1,0:T(8,128)S(1)} %get-tuple-element.16.refs_2_, s32[8,128]{1,0:T(8,128)S(1)} %copy-done.4, bf16[96,1024]{1,0:T(8,128)(2,1)S(1)} %collective-permute-done.5.refs_4_), custom_call_target="tpu_custom_call" | custom-call | flops 1610612736 | bytes 4194304 | tf_op jit(solution)/shard_map/attend/pallas_call | solution.py:308
  35.2 0.0 copy-start.2
  35.2 1.6 %collective-permute-start.6 = (bf16[96,1152]{1,0:T(8,128)(2,1)S(1)}, bf16[96,1152]{1,0:T(8,128)(2,1)S(1)}, u32[]{:S(2)}, u32[]{:S(2)}) collective-permute-start(bf16[96,1152]{1,0:T(8,128)(2,1)S(1)} %attend.5), channel_id=1, source_target_pairs={{0,24},{4,28},{8,16},{12,20},{16,8},{20,12},{24,0},{28,4},{1,25},{... | collective-permute-start | bytes 663560 | tf_op jit(solution)/shard_map/ppermute | solution.py:387
  36.7 3.9 %attend.3.refs_0_ = bf16[96,1152]{1,0:T(8,128)(2,1)S(1)} custom-call(bf16[1024,512]{1,0:T(8,128)(2,1)S(1)} %get-tuple-element.15.refs_0_, bf16[1024,512]{1,0:T(8,128)(2,1)S(1)} %collective-permute-done.refs_1_, f32[2048,128]{1,0:T(8,128)S(1)} %get-tuple-element.16.refs_2_, s32[8,128]{1,0:T(8,128)S(1)} %copy-done.5, bf16[96,1024]{1,0:T(8,128)(2,1)S(1)} %copy-done.8), custom_call_target="tpu_custom_call" | custom-call | flops 1610612736 | bytes 4194304 | tf_op jit(solution)/shard_map/attend/pallas_call | solution.py:308
  40.6 0.0 collective-permute-done.3.refs_1_
  40.6 1.5 %collective-permute-done.6.refs_3_ = bf16[96,1152]{1,0:T(8,128)(2,1)S(1)} collective-permute-done((bf16[96,1152]{1,0:T(8,128)(2,1)S(1)}, bf16[96,1152]{1,0:T(8,128)(2,1)S(1)}, u32[]{:S(2)}, u32[]{:S(2)}) %collective-permute-start.6) | collective-permute-done | bytes 221216 | tf_op jit(solution)/shard_map/ppermute | solution.py:387
  42.1 2.2 %finish.1 = (f32[96,1024]{1,0:T(8,128)S(1)}, bf16[96,1024]{1,0:T(8,128)(2,1)S(1)}, bf16[96,1024]{1,0:T(8,128)(2,1)S(1)}, bf16[96,1024]{1,0:T(8,128)(2,1)S(1)}) custom-call(bf16[96,1152]{1,0:T(8,128)(2,1)S(1)} %attend.3.refs_0_, bf16[96,1152]{1,0:T(8,128)(2,1)S(1)} %collective-permute-done.3.refs_1_, bf16[96,1152]{1,0:T(8,128)(2,1)S(1)} %collective-permute-done.4.refs_2_, ...), custom_call_target="tpu_custom_call" | custom-call | flops 805306368 | bytes 8388608 | tf_op jit(solution)/shard_map/finish/pallas_call | solution.py:370
  44.3 0.5 collective-permute-start.7
  44.8 2.6 %collective-permute-start.8 = (bf16[96,1024]{1,0:T(8,128)(2,1)S(1)}, bf16[96,1024]{1,0:T(8,128)(2,1)S(1)}, u32[]{:S(2)}, u32[]{:S(2)}) collective-permute-start(bf16[96,1024]{1,0:T(8,128)(2,1)S(1)} %get-tuple-element.22), channel_id=1, source_target_pairs={{0,2},{1,3},{2,0},{3,1},{4,6},{5,7},{6,4},{7,5},{8,10},{9,11},{10,... | collective-permute-start | bytes 589832 | tf_op jit(solution)/shard_map/ppermute | solution.py:387
  47.4 0.4 collective-permute-start.9
  47.8 0.7 %reshape.15 = bf16[96,2,2,128]{3,2,1,0:T(2,128)(2,1)} reshape(bf16[96,512]{1,0:T(8,128)(2,1)S(1)} %copy-done.2) | data formatting | bytes 196608 | tf_op jit(solution)/shard_map/reshape | solution.py:416
  48.5 3.7 %collective-permute-done.7 = bf16[96,1024]{1,0:T(8,128)(2,1)S(1)} collective-permute-done((bf16[96,1024]{1,0:T(8,128)(2,1)S(1)}, bf16[96,1024]{1,0:T(8,128)(2,1)S(1)}, u32[]{:S(2)}, u32[]{:S(2)}) %collective-permute-start.7) | collective-permute-done | bytes 196640 | tf_op jit(solution)/shard_map/ppermute | solution.py:387
  52.2 6.5 %collective-permute-done.8 = bf16[96,1024]{1,0:T(8,128)(2,1)S(1)} collective-permute-done((bf16[96,1024]{1,0:T(8,128)(2,1)S(1)}, bf16[96,1024]{1,0:T(8,128)(2,1)S(1)}, u32[]{:S(2)}, u32[]{:S(2)}) %collective-permute-start.8) | collective-permute-done | bytes 196640 | tf_op jit(solution)/shard_map/ppermute | solution.py:387
  58.7 3.2 %collective-permute-done.9 = bf16[96,1024]{1,0:T(8,128)(2,1)S(1)} collective-permute-done((bf16[96,1024]{1,0:T(8,128)(2,1)S(1)}, bf16[96,1024]{1,0:T(8,128)(2,1)S(1)}, u32[]{:S(2)}, u32[]{:S(2)}) %collective-permute-start.9) | collective-permute-done | bytes 196640 | tf_op jit(solution)/shard_map/ppermute | solution.py:387
  61.9 0.8 %add_convert_fusion = bf16[96,1024]{1,0:T(8,128)(2,1)} fusion(bf16[96,1024]{1,0:T(8,128)(2,1)S(1)} %collective-permute-done.9, bf16[96,1024]{1,0:T(8,128)(2,1)S(1)} %collective-permute-done.8, f32[96,1024]{1,0:T(8,128)S(1)} %get-tuple-element.20, bf16[96,1024]{1,0:T(8,128)(2,1)S(1)} %collective-permute-done.7), kind=kLoop, calls=%fused_computation | loop fusion | flops 688128 | bytes 1179648 | tf_op jit(solution)/shard_map/convert_element_type | solution.py:417
  (19 shorter events, 0.0 us)
Async XLA Ops:
  0.6 7.9 %copy-start = (bf16[1024,2,2,128]{3,2,1,0:T(2,128)(2,1)S(1)}, bf16[1024,2,2,128]{3,2,1,0:T(2,128)(2,1)}, u32[]{:S(2)}) copy-start(bf16[1024,2,2,128]{3,2,1,0:T(2,128)(2,1)} %param.17) | copy-start | bytes 3145732
  0.6 7.9 %copy-start.6 = (s32[2]{0:T(128)S(1)}, s32[2]{0:T(128)}, u32[]{:S(2)}) copy-start(s32[2]{0:T(128)} %order.1) | copy-start | bytes 28
  0.7 7.9 %copy-start.7 = (s32[2]{0:T(128)S(1)}, s32[2]{0:T(128)}, u32[]{:S(2)}) copy-start(s32[2]{0:T(128)} %slot.1) | copy-start | bytes 28
  8.5 0.9 %copy-start.1 = (bf16[96,512]{1,0:T(8,128)(2,1)S(1)}, bf16[96,512]{1,0:T(8,128)(2,1)}, u32[]{:S(2)}) copy-start(bf16[96,512]{1,0:T(8,128)(2,1)} %get-tuple-element.14.kv) | copy-start | bytes 294916
  9.4 0.7 %copy-start.3 = (s32[8,128]{1,0:T(8,128)S(1)}, s32[8,128]{1,0:T(8,128)}, u32[]{:S(2)}) copy-start(s32[8,128]{1,0:T(8,128)} %get-tuple-element.13.selected.refs_3_) | copy-start | bytes 12292
  12.7 9.6 %collective-permute-start = (bf16[1024,512]{1,0:T(8,128)(2,1)S(1)}, bf16[1024,512]{1,0:T(8,128)(2,1)S(1)}, u32[]{:S(2)}, u32[]{:S(2)}) collective-permute-start(bf16[1024,512]{1,0:T(8,128)(2,1)S(1)} %get-tuple-element.15.refs_0_), channel_id=1, source_target_pairs={{0,4},{4,0},{8,12},{12,8},{16,20},{20,16},{24,28},{28,24},{1,5},{5... | collective-permute-start | bytes 3145736 | tf_op jit(solution)/shard_map/ppermute | solution.py:387
  12.7 7.5 %collective-permute-start.1 = (bf16[96,1024]{1,0:T(8,128)(2,1)}, bf16[96,1024]{1,0:T(8,128)(2,1)S(1)}, u32[]{:S(2)}, u32[]{:S(2)}) collective-permute-start(bf16[96,1024]{1,0:T(8,128)(2,1)} %get-tuple-element.17.refs_4_), channel_id=1, source_target_pairs={{0,16},{4,20},{8,24},{12,28},{16,0},{20,4},{24,8},{28,12},{1,17},{... | collective-permute-start | bytes 589832 | tf_op jit(solution)/shard_map/ppermute | solution.py:387
  14.3 8.0 %collective-permute-start.2 = (bf16[96,1024]{1,0:T(8,128)(2,1)}, bf16[96,1024]{1,0:T(8,128)(2,1)S(1)}, u32[]{:S(2)}, u32[]{:S(2)}) collective-permute-start(bf16[96,1024]{1,0:T(8,128)(2,1)} %get-tuple-element.17.refs_4_), channel_id=1, source_target_pairs={{0,8},{4,12},{8,0},{12,4},{16,24},{20,28},{24,16},{28,20},{1,9},{5... | collective-permute-start | bytes 589832 | tf_op jit(solution)/shard_map/ppermute | solution.py:387
  15.8 15.3 %collective-permute-start.5 = (bf16[96,1024]{1,0:T(8,128)(2,1)}, bf16[96,1024]{1,0:T(8,128)(2,1)S(1)}, u32[]{:S(2)}, u32[]{:S(2)}) collective-permute-start(bf16[96,1024]{1,0:T(8,128)(2,1)} %get-tuple-element.17.refs_4_), channel_id=1, source_target_pairs={{0,24},{4,28},{8,16},{12,20},{16,8},{20,12},{24,0},{28,4},{1,25},{... | collective-permute-start | bytes 589832 | tf_op jit(solution)/shard_map/ppermute | solution.py:387
  22.3 0.7 %copy-start.4 = (s32[8,128]{1,0:T(8,128)S(1)}, s32[8,128]{1,0:T(8,128)}, u32[]{:S(2)}) copy-start(s32[8,128]{1,0:T(8,128)} %get-tuple-element.13.selected.refs_3_) | copy-start | bytes 12292
  23.0 13.8 %copy-start.5 = (s32[8,128]{1,0:T(8,128)S(1)}, s32[8,128]{1,0:T(8,128)}, u32[]{:S(2)}) copy-start(s32[8,128]{1,0:T(8,128)} %get-tuple-element.13.selected.refs_3_) | copy-start | bytes 12292
  23.0 13.8 %copy-start.8 = (bf16[96,1024]{1,0:T(8,128)(2,1)S(1)}, bf16[96,1024]{1,0:T(8,128)(2,1)}, u32[]{:S(2)}) copy-start(bf16[96,1024]{1,0:T(8,128)(2,1)} %get-tuple-element.17.refs_4_) | copy-start | bytes 589828
  23.0 19.1 %slice-start = ((s8[8388608]{0:T(1024)(128)(4,1)}), s8[4194304]{0:T(1024)(128)(4,1)S(1)}, s32[]{:S(2)}) async-start(s8[8388608]{0:T(1024)(128)(4,1)} %bitcast.2), calls=%async_computation | async-start | bytes 8388608
  29.1 13.0 %slice-start.1 = ((s8[8388608]{0:T(1024)(128)(4,1)}), s8[4194304]{0:T(1024)(128)(4,1)S(1)}, s32[]{:S(2)}) async-start(s8[8388608]{0:T(1024)(128)(4,1)} %bitcast.2), calls=%async_computation.1 | async-start | bytes 8388608
  29.1 11.5 %collective-permute-start.3 = (bf16[96,1152]{1,0:T(8,128)(2,1)S(1)}, bf16[96,1152]{1,0:T(8,128)(2,1)S(1)}, u32[]{:S(2)}, u32[]{:S(2)}) collective-permute-start(bf16[96,1152]{1,0:T(8,128)(2,1)S(1)} %get-tuple-element.18), channel_id=1, source_target_pairs={{0,16},{4,20},{8,24},{12,28},{16,0},{20,4},{24,8},{28,12},{1,17},{... | collective-permute-start | bytes 663560 | tf_op jit(solution)/shard_map/ppermute | solution.py:387
  29.6 11.0 %collective-permute-start.4 = (bf16[96,1152]{1,0:T(8,128)(2,1)S(1)}, bf16[96,1152]{1,0:T(8,128)(2,1)S(1)}, u32[]{:S(2)}, u32[]{:S(2)}) collective-permute-start(bf16[96,1152]{1,0:T(8,128)(2,1)S(1)} %get-tuple-element.19), channel_id=1, source_target_pairs={{0,8},{4,12},{8,0},{12,4},{16,24},{20,28},{24,16},{28,20},{1,9},{5... | collective-permute-start | bytes 663560 | tf_op jit(solution)/shard_map/ppermute | solution.py:387
  35.2 12.7 %copy-start.2 = (bf16[96,512]{1,0:T(8,128)(2,1)S(1)}, bf16[96,512]{1,0:T(8,128)(2,1)}, u32[]{:S(2)}) copy-start(bf16[96,512]{1,0:T(8,128)(2,1)} %get-tuple-element.14.kv) | copy-start | bytes 294916
  35.2 6.9 %collective-permute-start.6 = (bf16[96,1152]{1,0:T(8,128)(2,1)S(1)}, bf16[96,1152]{1,0:T(8,128)(2,1)S(1)}, u32[]{:S(2)}, u32[]{:S(2)}) collective-permute-start(bf16[96,1152]{1,0:T(8,128)(2,1)S(1)} %attend.5), channel_id=1, source_target_pairs={{0,24},{4,28},{8,16},{12,20},{16,8},{20,12},{24,0},{28,4},{1,25},{... | collective-permute-start | bytes 663560 | tf_op jit(solution)/shard_map/ppermute | solution.py:387
  44.3 7.9 %collective-permute-start.7 = (bf16[96,1024]{1,0:T(8,128)(2,1)S(1)}, bf16[96,1024]{1,0:T(8,128)(2,1)S(1)}, u32[]{:S(2)}, u32[]{:S(2)}) collective-permute-start(bf16[96,1024]{1,0:T(8,128)(2,1)S(1)} %get-tuple-element.21), channel_id=1, source_target_pairs={{0,1},{1,0},{2,3},{3,2},{4,5},{5,4},{6,7},{7,6},{8,9},{9,8},{10,11... | collective-permute-start | bytes 589832 | tf_op jit(solution)/shard_map/ppermute | solution.py:387
  44.8 13.9 %collective-permute-start.8 = (bf16[96,1024]{1,0:T(8,128)(2,1)S(1)}, bf16[96,1024]{1,0:T(8,128)(2,1)S(1)}, u32[]{:S(2)}, u32[]{:S(2)}) collective-permute-start(bf16[96,1024]{1,0:T(8,128)(2,1)S(1)} %get-tuple-element.22), channel_id=1, source_target_pairs={{0,2},{1,3},{2,0},{3,1},{4,6},{5,7},{6,4},{7,5},{8,10},{9,11},{10,... | collective-permute-start | bytes 589832 | tf_op jit(solution)/shard_map/ppermute | solution.py:387
  47.4 14.5 %collective-permute-start.9 = (bf16[96,1024]{1,0:T(8,128)(2,1)S(1)}, bf16[96,1024]{1,0:T(8,128)(2,1)S(1)}, u32[]{:S(2)}, u32[]{:S(2)}) collective-permute-start(bf16[96,1024]{1,0:T(8,128)(2,1)S(1)} %get-tuple-element.23), channel_id=1, source_target_pairs={{0,3},{1,2},{2,1},{3,0},{4,7},{5,6},{6,5},{7,4},{8,11},{9,10},{10,... | collective-permute-start | bytes 589832 | tf_op jit(solution)/shard_map/ppermute | solution.py:387

commit v3 on v2

--- a/solution.py
+++ b/solution.py
@@ -108,7 +108,7 @@
             pltpu.VMEM((feat, cols), bf16),
             pltpu.SemaphoreType.DMA((1 + cols // width,)),
         ],
-        compiler_params=pltpu.CompilerParams(vmem_limit_bytes=56 * MIB),
+        compiler_params=pltpu.CompilerParams(vmem_limit_bytes=52 * MIB),
         cost_estimate=pl.CostEstimate(
             flops=2 * rows * feat * cols, bytes_accessed=2 * feat * (cols + rows), transcendentals=0
         ),
@@ -125,56 +125,51 @@
     return place * per + lax.rem(index, per)
 
 
-def merge_kernel(order, slot, selected, stored, kv, cache, key_pos):
-    shard, cols = cache.shape
+def merge_kernel(order, slot, selected, stored, stored_other, kv, kv_other, cache, key_pos, wide):
+    _, shard, cols = cache.shape
     kinds = cols // LANES
     rows = kv.shape[0]
     step = 128
     me = lax.axis_index("seq")
-    spread = iota((step, kinds * step), 1) - kinds * iota((step, kinds * step), 0)
-    takes = [(spread == kind).astype(f32).astype(bf16) for kind in range(kinds)]
     for half in range(2):
-        index = me if half == 0 else me ^ 1
+        index = me ^ half
         block = block_of(index, shard, order, slot)
         holes = selected[pl.ds(block, 1), :] - block * shard
         offsets = column_of(selected[pl.ds(index, 1), :] - index * shard)
         high = jnp.floor(offsets * (1.0 / 32))
         low = offsets - 32 * high
-        wide = (LANES, LANES)
         given = iota((LANES, 1), 0) < rows
         sources = [
-            jnp.broadcast_to(jnp.where(given, value, 0.0), wide).astype(bf16)
-            for value in (jnp.ones_like(high), high, low)
+            jnp.broadcast_to(jnp.where(given, value, 0.0), (LANES, LANES)).astype(bf16)
+            for value in (high, low + 1)
         ]
-        if half == 0:
-            fresh = kv[...]
-            if rows < LANES:
-                fresh = jnp.concatenate([fresh, jnp.zeros((LANES - rows, cols), bf16)], 0)
-            sources.append(fresh)
-        source = jnp.concatenate(sources, 1)
+        fresh = (kv, kv_other)[half][...]
+        if rows < LANES:
+            fresh = jnp.concatenate([fresh, jnp.zeros((LANES - rows, cols), bf16)], 0)
+        source = jnp.concatenate(sources + [fresh], 1)
         for at in range(0, shard, step):
             places = iota((step, LANES), 0) + at
             hit = (places == holes).astype(f32).astype(bf16)
             picked = jnp.dot(hit, source, preferred_element_type=f32)
-            hole = picked[:, :LANES] > 0.5
-            fresh_pos = picked[:, LANES : 2 * LANES] * 32 + picked[:, 2 * LANES : 3 * LANES]
+            mark = picked[:, LANES : 2 * LANES]
+            hole = mark > 0.5
             key_pos[half * shard + at : half * shard + at + step, :] = jnp.where(
                 hole,
-                fresh_pos + (index * shard).astype(f32),
+                picked[:, :LANES] * 32 + (mark - 1) + (index * shard).astype(f32),
                 (places + block * shard).astype(f32),
             )
-            if half == 0:
-                mixed = stored[at * kinds : (at + step) * kinds, :]
-                for kind in range(kinds):
-                    col = kind * LANES
-                    cache[at : at + step, col : col + LANES] = jnp.where(
-                        hole,
-                        picked[:, 3 * LANES + col : 4 * LANES + col],
-                        jnp.dot(takes[kind], mixed, preferred_element_type=f32),
-                    ).astype(bf16)
-
-
-def merge(order, slot, selected, stored, kv):
+            slot_at = (at // step) % 2
+            wide[slot_at] = (stored, stored_other)[half][at * kinds : (at + step) * kinds, :].astype(f32)
+            for kind in range(kinds):
+                col = kind * LANES
+                cache[half, at : at + step, col : col + LANES] = jnp.where(
+                    hole,
+                    picked[:, 2 * LANES + col : 3 * LANES + col],
+                    wide[slot_at, pl.ds(kind, step, stride=kinds), :],
+                ).astype(bf16)
+
+
+def merge(order, slot, selected, stored, stored_other, kv, kv_other):
     cols = kv.shape[1]
     shard = stored.shape[0] * LANES // cols
     smem = pl.BlockSpec(memory_space=pltpu.SMEM)
@@ -182,85 +177,71 @@
     return pl.pallas_call(
         merge_kernel,
         out_shape=(
-            jax.ShapeDtypeStruct((shard, cols), bf16),
+            jax.ShapeDtypeStruct((2, shard, cols), bf16),
             jax.ShapeDtypeStruct((2 * shard, LANES), f32),
         ),
-        in_specs=[smem, smem, vmem, vmem, vmem],
+        in_specs=[smem, smem] + [vmem] * 5,
         out_specs=(vmem, vmem),
+        scratch_shapes=[pltpu.VMEM((2, 128 * cols // LANES, LANES), f32)],
         compiler_params=pltpu.CompilerParams(vmem_limit_bytes=16 * MIB),
         cost_estimate=pl.CostEstimate(flops=1000, bytes_accessed=1000, transcendentals=0),
         name="merge",
-    )(order, slot, selected, stored, kv)
+    )(order, slot, selected, stored, stored_other, kv, kv_other)
 
 
 def attend_kernel(partners, *refs):
     count = len(partners)
-    caches = refs[:2]
-    key_pos, selected = refs[2:4]
-    queries = refs[4 : 4 + count]
-    outs = refs[4 + count : 4 + 2 * count]
-    left, right, value, scores, weights, sem = refs[4 + 2 * count :]
-    shard, cols = caches[0].shape
+    cache, key_pos, selected = refs[:3]
+    queries = refs[3 : 3 + count]
+    outs = refs[3 + count : 3 + 2 * count]
+    scores, weights, masks = refs[3 + 2 * count :]
+    _, shard, cols = cache.shape
     rows = queries[0].shape[0]
     kv_heads = cols // (2 * HEAD_DIM)
-    tall = GROUP * rows
+    heads = kv_heads * GROUP
     keys = 2 * shard
+    step = 256
     scale = math.log2(math.e) / HEAD_DIM**0.5
     me = lax.axis_index("seq")
-    copies = {}
-    for half in range(2):
-        for kind in range(2):
-            for head in range(kv_heads):
-                col = (kind * kv_heads + head) * HEAD_DIM
-                target = (right, value)[kind]
-                copy = pltpu.make_async_copy(
-                    caches[half].at[:, col : col + HEAD_DIM],
-                    target.at[head, half * shard : (half + 1) * shard, 0:HEAD_DIM],
-                    sem.at[half, kind, head],
-                )
-                copy.start()
-                copies[half, kind, head] = copy
     one_hot = (iota((rows, LANES), 0) == iota((rows, LANES), 1)).astype(f32).astype(bf16)
-    for head in range(kv_heads):
-        for member in range(GROUP):
-            left[head, member * rows : (member + 1) * rows, HEAD_DIM : HEAD_DIM + LANES] = one_hot
-        value[head, :, HEAD_DIM : HEAD_DIM + LANES] = jnp.ones((keys, LANES), bf16)
-
-    def mask(at, head):
+    ones = jnp.ones((keys, LANES), bf16)
+
+    def mask(at):
         row = selected[pl.ds(me ^ partners[at], 1), :].astype(f32)
-        for place in range(0, keys, 256):
-            right[head, place : place + 256, HEAD_DIM : HEAD_DIM + LANES] = jnp.where(
-                key_pos[place : place + 256, :] <= row, 0.0, MASKED
+        for place in range(0, keys, step):
+            masks[at % 2, place : place + step, :] = jnp.where(
+                key_pos[place : place + step, :] <= row, 0.0, MASKED
             ).astype(bf16)
 
-    def fill(at, head):
+    def left(at, head):
+        parts = []
         for member in range(GROUP):
             col = (head * GROUP + member) * HEAD_DIM
-            left[head, member * rows : (member + 1) * rows, 0:HEAD_DIM] = queries[at][:, col : col + HEAD_DIM]
+            parts.append(jnp.concatenate([queries[at][:, col : col + HEAD_DIM], one_hot], 1))
+        return jnp.concatenate(parts, 0)
+
+    def cached(place, size, kind, head):
+        col = (kind * kv_heads + head) * HEAD_DIM
+        return cache[place // shard, place % shard : place % shard + size, col : col + HEAD_DIM]
 
     units = [(at, head) for at in range(count) for head in range(kv_heads)]
-    step = 256
     best = {}
     for number in range(len(units) + 1):
         if number < len(units):
             at, head = units[number]
-            if at == 0:
-                for half in range(2):
-                    copies[half, 0, head].wait()
-            mask(at, head)
-            fill(at, head)
+            if head == 0:
+                mask(at)
+            stream = left(at, head)
         if number:
             old_at, old_head = units[number - 1]
-            if old_at == 0:
-                for half in range(2):
-                    copies[half, 1, old_head].wait()
             top = jnp.max(best.pop(number - 1), 1, keepdims=True) * scale
         running = None
         for place in range(0, keys, step):
             if number < len(units):
-                score = lax.dot_general(
-                    left[head], right[head, place : place + step, :], NT, preferred_element_type=f32
+                right = jnp.concatenate(
+                    [cached(place, step, 0, head), masks[at % 2, place : place + step, :]], 1
                 )
+                score = lax.dot_general(stream, right, NT, preferred_element_type=f32)
                 scores[number % 2, :, place : place + step] = score
                 for col in range(0, step, LANES):
                     part = score[:, col : col + LANES]
@@ -273,7 +254,10 @@
         if number < len(units):
             best[number] = running
         if number:
-            summed = jnp.dot(weights[...], value[old_head], preferred_element_type=f32)
+            value = jnp.concatenate([cached(half * shard, shard, 1, old_head) for half in range(2)], 0)
+            summed = jnp.dot(
+                weights[...], jnp.concatenate([value, ones], 1), preferred_element_type=f32
+            )
             total = summed[:, HEAD_DIM : HEAD_DIM + LANES]
             context = (summed[:, :HEAD_DIM] / total).astype(bf16)
             level = top + jnp.log2(total)
@@ -281,7 +265,6 @@
             middle = (level - high).astype(bf16).astype(f32)
             low = level - high - middle
             lane = iota((rows, LANES), 1)
-            heads = kv_heads * GROUP
             out = outs[old_at]
             packed = jnp.zeros((rows, LANES), f32)
             for member in range(GROUP):
@@ -296,36 +279,32 @@
             out[:, tail] = packed.astype(bf16)
 
 
-def attend(partners, caches, key_pos, selected, queries):
-    shard, cols = caches[0].shape
+def attend(partners, cache, key_pos, selected, queries):
+    _, shard, cols = cache.shape
     rows, q_cols = queries[0].shape
     kv_heads = cols // (2 * HEAD_DIM)
     tall = GROUP * rows
     keys = 2 * shard
     count = len(queries)
     vmem = pl.BlockSpec(memory_space=pltpu.VMEM)
-    hbm = pl.BlockSpec(memory_space=pl.ANY)
     out = pl.pallas_call(
         functools.partial(attend_kernel, partners),
         out_shape=[jax.ShapeDtypeStruct((rows, q_cols + LANES), bf16)] * count,
-        in_specs=[hbm, hbm, vmem, vmem] + [vmem] * count,
+        in_specs=[vmem] * (3 + count),
         out_specs=[vmem] * count,
         scratch_shapes=[
-            pltpu.VMEM((kv_heads, tall, HEAD_DIM + LANES), bf16),
-            pltpu.VMEM((kv_heads, keys, HEAD_DIM + LANES), bf16),
-            pltpu.VMEM((kv_heads, keys, HEAD_DIM + LANES), bf16),
             pltpu.VMEM((2, tall, keys), f32),
             pltpu.VMEM((tall, keys), bf16),
-            pltpu.SemaphoreType.DMA((2, 2, kv_heads)),
+            pltpu.VMEM((2, keys, LANES), bf16),
         ],
-        compiler_params=pltpu.CompilerParams(vmem_limit_bytes=32 * MIB),
+        compiler_params=pltpu.CompilerParams(vmem_limit_bytes=24 * MIB),
         cost_estimate=pl.CostEstimate(
             flops=8 * count * kv_heads * tall * keys * HEAD_DIM,
             bytes_accessed=8 * shard * cols,
             transcendentals=count * kv_heads * tall * keys,
         ),
         name="attend",
-    )(*caches, key_pos, selected, *queries)
+    )(cache, key_pos, selected, *queries)
     return list(out)
 
 
@@ -395,19 +374,17 @@
     rows = hidden.shape[0]
     shard, _, local_kv, _ = stored_kv.shape
     stored = stored_kv.reshape(-1, HEAD_DIM)
+    stored_other = swap(stored, "seq", 1, seq_count)
     query, kv, table = project(hidden, norm_gain, selected, w_query, w_key, w_value)
     turns = list(range(2, seq_count, 2))
-    far_first = sorted(turns, key=lambda turn: (-bin(turn).count("1"), turn))
-    queries = {turn: swap(query, "seq", turn, seq_count) for turn in far_first}
-    cache, key_pos = merge(prompt_order, store_slot, table, stored, kv)
-    other = swap(cache, "seq", 1, seq_count)
-    caches = (cache, other)
-    parts = attend((0,), caches, key_pos, table, [query])
-    near_first = far_first[::-1]
-    for at in range(0, len(near_first), 2):
-        some = near_first[at : at + 2]
-        done = attend(tuple(some), caches, key_pos, table, [queries[turn] for turn in some])
-        parts += [swap(part, "seq", turn, seq_count) for turn, part in zip(some, done)]
+    near_first = sorted(turns, key=lambda turn: (bin(turn).count("1"), turn))
+    queries = {turn: swap(query, "seq", turn, seq_count) for turn in near_first}
+    kv_other = swap(kv, "seq", 1, seq_count)
+    cache, key_pos = merge(prompt_order, store_slot, table, stored, stored_other, kv, kv_other)
+    parts = attend((0,), cache, key_pos, table, [query])
+    for turn in near_first:
+        (part,) = attend((turn,), cache, key_pos, table, [queries[turn]])
+        parts.append(swap(part, "seq", turn, seq_count))
     blocks = finish(parts, w_out, head_count)
     total = blocks[0]
     arrived = [swap(blocks[turn], "head", turn, head_count) for turn in range(1, head_count)]

time: 63.3 us -> 60.1 us (0.949)
  the two profiles are of different devices: /device:TPU:8 before, /device:TPU:0 now
where the time goes in v3:
time: 60.1 us; the launch traced here: 59.8 us
  waiting for transfers between devices  20.7 us (34%)
  Pallas kernels  19.7 us (33%)
  starting transfers between devices  14 us (23%)
  local copies, waits for them, and re-layouts  3.88 us (6%)
  other arithmetic  0.77 us (1%)
  between operations  0.71 us (1%)
    ppermute x11, waiting for transfers between devices, swap(): return lax.ppermute(value, axis, [(at, at ^ turn) for at in range(size)])  20.7 us
    ppermute x11, starting transfers between devices, swap(): return lax.ppermute(value, axis, [(at, at ^ turn) for at in range(size)])  14 us
    pallas_call x4, Pallas kernels, attend(): pl.pallas_call(functools.partial(attend_kernel, partners), out_shape=[jax...  9.42 us
    pallas_call x1, Pallas kernels, project(): pl.pallas_call(functools.partial(project_kernel, width), out_shape=(jax.S...  6.24 us
    unnamed x18, local copies, waits for them, and re-layouts  3.21 us
    pallas_call x1, Pallas kernels, finish(): pl.pallas_call(functools.partial(finish_kernel, len(parts), size), out_sh...  2.18 us
    pallas_call x1, Pallas kernels, merge(): pl.pallas_call(merge_kernel, out_shape=(jax.ShapeDtypeStruct((2, shard, c...  1.87 us
  transfers between devices with their start and end apart: 11, of which 7 were waited for; matrix products, arithmetic and copies ran while one was open for 1% of the time, Pallas kernels for 29%

profile of v3, /device:TPU:0, one launch (start us, length us, event | category | flops | bytes accessed | tf_op | source)
XLA Modules:
  0.0 59.8 jit_solution(1395305893625271653)
XLA Ops:
  0.6 0.5 collective-permute-start
  1.2 1.1 %copy-done.1 = bf16[96,4096]{1,0:T(8,128)(2,1)S(1)} copy-done((bf16[96,4096]{1,0:T(8,128)(2,1)S(1)}, bf16[96,4096]{1,0:T(8,128)(2,1)}, u32[]{:S(2)}) %copy-start.1) | copy-done | bytes 786456
  2.3 0.7 %copy-done.2 = f32[4096]{0:T(1024)S(1)} copy-done((f32[4096]{0:T(1024)S(1)}, f32[4096]{0:T(1024)}, u32[]{:S(2)}) %copy-start.2) | copy-done | bytes 16408
  3.0 0.7 %copy-done.3 = s32[768]{0:T(1024)S(1)} copy-done((s32[768]{0:T(1024)S(1)}, s32[768]{0:T(1024)}, u32[]{:S(2)}) %copy-start.3) | copy-done | bytes 3096
  3.7 0.7 %copy-done.4 = f32[1,128]{1,0:T(1,128)S(1)} copy-done((f32[1,128]{1,0:T(1,128)S(1)}, f32[1,128]{1,0:T(1,128)}, u32[]{:S(2)}) %copy-start.4) | copy-done | bytes 536
  4.4 6.2 %project.1 = (bf16[96,1024]{1,0:T(8,128)(2,1)S(1)}, bf16[96,512]{1,0:T(8,128)(2,1)S(1)}, s32[8,128]{1,0:T(8,128)S(1)}) custom-call(bf16[96,4096]{1,0:T(8,128)(2,1)S(1)} %copy-done.1, f32[1,4096]{1,0:T(1,128)S(1)} %bitcast.6, s32[768]{0:T(1024)S(1)} %copy-done.3, f32[1,128]{1,0:T(1,128)S(1)} %copy-done.4, bf16[4096,1024]{1,0:T(8,128)(2,1)} %wq_any.1, ...), custom_call_target="tpu_custom_call" | custom-call | flops 1207959552 | bytes 13369344 | tf_op jit(solution)/shard_map/project/pallas_call | solution.py:96
  10.6 3.5 %collective-permute-start.6 = (bf16[96,1024]{1,0:T(8,128)(2,1)S(1)}, bf16[96,1024]{1,0:T(8,128)(2,1)S(1)}, u32[]{:S(2)}, u32[]{:S(2)}) collective-permute-start(bf16[96,1024]{1,0:T(8,128)(2,1)S(1)} %get-tuple-element.15.refs_3_), channel_id=1, source_target_pairs={{0,24},{4,28},{8,16},{12,20},{16,8},{20,12},{24,0},{28,4},{1,25},{... | collective-permute-start | bytes 589832 | tf_op jit(solution)/shard_map/ppermute | solution.py:366
  14.1 0.2 collective-permute-start.1
  14.3 0.5 collective-permute-start.4
  14.8 0.4 collective-permute-start.2
  15.3 0.2 collective-permute-done.1.kv_other
  15.4 0.0 collective-permute-done.stored_other
  15.4 1.9 %merge.1 = (bf16[2,1024,512]{2,1,0:T(8,128)(2,1)S(1)}, f32[2048,128]{1,0:T(8,128)S(1)}) custom-call(s32[2]{0:T(128)S(1)} %copy-done.5, s32[2]{0:T(128)S(1)} %copy-done.6, s32[8,128]{1,0:T(8,128)S(1)} %get-tuple-element.11.selected.refs_2_, bf16[4096,128]{1,0:T(8,128)(2,1)S(1)} %bitcast.5, bf16[4096,128]{1,0:T(8,128)(2,1)S(1)} %collective-permute-done.stored_other, ...), custom_call_target="tpu_custom_call" | custom-call | flops 1000 | bytes 1000 | tf_op jit(solution)/shard_map/merge/pallas_call | solution.py:177
  17.3 2.6 %collective-permute-done.6.refs_3_ = bf16[96,1024]{1,0:T(8,128)(2,1)S(1)} collective-permute-done((bf16[96,1024]{1,0:T(8,128)(2,1)S(1)}, bf16[96,1024]{1,0:T(8,128)(2,1)S(1)}, u32[]{:S(2)}, u32[]{:S(2)}) %collective-permute-start.6) | collective-permute-done | bytes 196640 | tf_op jit(solution)/shard_map/ppermute | solution.py:366
  19.9 2.3 %attend.7 = bf16[96,1152]{1,0:T(8,128)(2,1)S(1)} custom-call(bf16[2,1024,512]{2,1,0:T(8,128)(2,1)S(1)} %get-tuple-element.13.refs_0_, f32[2048,128]{1,0:T(8,128)S(1)} %get-tuple-element.14.refs_1_, s32[8,128]{1,0:T(8,128)S(1)} %get-tuple-element.11.selected.refs_2_, bf16[96,1024]{1,0:T(8,128)(2,1)S(1)} %collective-permute-done.6.refs_3_), custom_call_target="tpu_custom_call" | custom-call | flops 1610612736 | bytes 4194304 | tf_op jit(solution)/shard_map/attend/pallas_call | solution.py:290
  22.2 2.9 %collective-permute-start.7 = (bf16[96,1152]{1,0:T(8,128)(2,1)S(1)}, bf16[96,1152]{1,0:T(8,128)(2,1)S(1)}, u32[]{:S(2)}, u32[]{:S(2)}) collective-permute-start(bf16[96,1152]{1,0:T(8,128)(2,1)S(1)} %attend.7), channel_id=1, source_target_pairs={{0,24},{4,28},{8,16},{12,20},{16,8},{20,12},{24,0},{28,4},{1,25},{... | collective-permute-start | bytes 663560 | tf_op jit(solution)/shard_map/ppermute | solution.py:366
  25.1 2.3 %attend.6 = bf16[96,1152]{1,0:T(8,128)(2,1)S(1)} custom-call(bf16[2,1024,512]{2,1,0:T(8,128)(2,1)S(1)} %get-tuple-element.13.refs_0_, f32[2048,128]{1,0:T(8,128)S(1)} %get-tuple-element.14.refs_1_, s32[8,128]{1,0:T(8,128)S(1)} %get-tuple-element.11.selected.refs_2_, bf16[96,1024]{1,0:T(8,128)(2,1)S(1)} %collective-permute-done.4.refs_3_), custom_call_target="tpu_custom_call" | custom-call | flops 1610612736 | bytes 4194304 | tf_op jit(solution)/shard_map/attend/pallas_call | solution.py:290
  27.5 0.0 slice-start.1
  27.5 0.6 collective-permute-start.5
  28.0 2.3 %attend.5 = bf16[96,1152]{1,0:T(8,128)(2,1)S(1)} custom-call(bf16[2,1024,512]{2,1,0:T(8,128)(2,1)S(1)} %get-tuple-element.13.refs_0_, f32[2048,128]{1,0:T(8,128)S(1)} %get-tuple-element.14.refs_1_, s32[8,128]{1,0:T(8,128)S(1)} %get-tuple-element.11.selected.refs_2_, bf16[96,1024]{1,0:T(8,128)(2,1)S(1)} %collective-permute-done.2.refs_3_), custom_call_target="tpu_custom_call" | custom-call | flops 1610612736 | bytes 4194304 | tf_op jit(solution)/shard_map/attend/pallas_call | solution.py:290
  30.4 0.9 %collective-permute-start.3 = (bf16[96,1152]{1,0:T(8,128)(2,1)S(1)}, bf16[96,1152]{1,0:T(8,128)(2,1)S(1)}, u32[]{:S(2)}, u32[]{:S(2)}) collective-permute-start(bf16[96,1152]{1,0:T(8,128)(2,1)S(1)} %attend.5), channel_id=1, source_target_pairs={{0,8},{4,12},{8,0},{12,4},{16,24},{20,28},{24,16},{28,20},{1,9},{5... | collective-permute-start | bytes 663560 | tf_op jit(solution)/shard_map/ppermute | solution.py:366
  31.2 2.5 %attend.4.refs_0_ = bf16[96,1152]{1,0:T(8,128)(2,1)S(1)} custom-call(bf16[2,1024,512]{2,1,0:T(8,128)(2,1)S(1)} %get-tuple-element.13.refs_0_, f32[2048,128]{1,0:T(8,128)S(1)} %get-tuple-element.14.refs_1_, s32[8,128]{1,0:T(8,128)S(1)} %get-tuple-element.11.selected.refs_2_, bf16[96,1024]{1,0:T(8,128)(2,1)S(1)} %get-tuple-element.15.refs_3_), custom_call_target="tpu_custom_call" | custom-call | flops 1610612736 | bytes 4194304 | tf_op jit(solution)/shard_map/attend/pallas_call | solution.py:290
  33.8 1.2 %collective-permute-done.5.refs_2_ = bf16[96,1152]{1,0:T(8,128)(2,1)S(1)} collective-permute-done((bf16[96,1152]{1,0:T(8,128)(2,1)S(1)}, bf16[96,1152]{1,0:T(8,128)(2,1)S(1)}, u32[]{:S(2)}, u32[]{:S(2)}) %collective-permute-start.5) | collective-permute-done | bytes 221216 | tf_op jit(solution)/shard_map/ppermute | solution.py:366
  35.0 2.5 %collective-permute-done.3.refs_1_ = bf16[96,1152]{1,0:T(8,128)(2,1)S(1)} collective-permute-done((bf16[96,1152]{1,0:T(8,128)(2,1)S(1)}, bf16[96,1152]{1,0:T(8,128)(2,1)S(1)}, u32[]{:S(2)}, u32[]{:S(2)}) %collective-permute-start.3) | collective-permute-done | bytes 221216 | tf_op jit(solution)/shard_map/ppermute | solution.py:366
  37.5 2.2 %finish.1 = (f32[96,1024]{1,0:T(8,128)S(1)}, bf16[96,1024]{1,0:T(8,128)(2,1)S(1)}, bf16[96,1024]{1,0:T(8,128)(2,1)S(1)}, bf16[96,1024]{1,0:T(8,128)(2,1)S(1)}) custom-call(bf16[96,1152]{1,0:T(8,128)(2,1)S(1)} %attend.4.refs_0_, bf16[96,1152]{1,0:T(8,128)(2,1)S(1)} %collective-permute-done.3.refs_1_, bf16[96,1152]{1,0:T(8,128)(2,1)S(1)} %collective-permute-done.5.refs_2_, ...), custom_call_target="tpu_custom_call" | custom-call | flops 805306368 | bytes 8388608 | tf_op jit(solution)/shard_map/finish/pallas_call | solution.py:349
  39.7 3.7 %collective-permute-start.10 = (bf16[96,1024]{1,0:T(8,128)(2,1)S(1)}, bf16[96,1024]{1,0:T(8,128)(2,1)S(1)}, u32[]{:S(2)}, u32[]{:S(2)}) collective-permute-start(bf16[96,1024]{1,0:T(8,128)(2,1)S(1)} %get-tuple-element.19), channel_id=1, source_target_pairs={{0,3},{1,2},{2,1},{3,0},{4,7},{5,6},{6,5},{7,4},{8,11},{9,10},{10,... | collective-permute-start | bytes 589832 | tf_op jit(solution)/shard_map/ppermute | solution.py:366
  43.3 0.8 %collective-permute-start.9 = (bf16[96,1024]{1,0:T(8,128)(2,1)S(1)}, bf16[96,1024]{1,0:T(8,128)(2,1)S(1)}, u32[]{:S(2)}, u32[]{:S(2)}) collective-permute-start(bf16[96,1024]{1,0:T(8,128)(2,1)S(1)} %get-tuple-element.18), channel_id=1, source_target_pairs={{0,2},{1,3},{2,0},{3,1},{4,6},{5,7},{6,4},{7,5},{8,10},{9,11},{10,... | collective-permute-start | bytes 589832 | tf_op jit(solution)/shard_map/ppermute | solution.py:366
  44.1 0.7 %reshape.15 = bf16[96,2,2,128]{3,2,1,0:T(2,128)(2,1)} reshape(bf16[96,512]{1,0:T(8,128)(2,1)S(1)} %get-tuple-element.12.kv) | data formatting | bytes 196608 | tf_op jit(solution)/shard_map/reshape | solution.py:393
  44.8 4.6 %collective-permute-done.10 = bf16[96,1024]{1,0:T(8,128)(2,1)S(1)} collective-permute-done((bf16[96,1024]{1,0:T(8,128)(2,1)S(1)}, bf16[96,1024]{1,0:T(8,128)(2,1)S(1)}, u32[]{:S(2)}, u32[]{:S(2)}) %collective-permute-start.10) | collective-permute-done | bytes 196640 | tf_op jit(solution)/shard_map/ppermute | solution.py:366
  49.4 3.5 %collective-permute-done.8 = bf16[96,1024]{1,0:T(8,128)(2,1)S(1)} collective-permute-done((bf16[96,1024]{1,0:T(8,128)(2,1)S(1)}, bf16[96,1024]{1,0:T(8,128)(2,1)S(1)}, u32[]{:S(2)}, u32[]{:S(2)}) %collective-permute-start.8) | collective-permute-done | bytes 196640 | tf_op jit(solution)/shard_map/ppermute | solution.py:366
  52.9 6.1 %collective-permute-done.9 = bf16[96,1024]{1,0:T(8,128)(2,1)S(1)} collective-permute-done((bf16[96,1024]{1,0:T(8,128)(2,1)S(1)}, bf16[96,1024]{1,0:T(8,128)(2,1)S(1)}, u32[]{:S(2)}, u32[]{:S(2)}) %collective-permute-start.9) | collective-permute-done | bytes 196640 | tf_op jit(solution)/shard_map/ppermute | solution.py:366
  59.0 0.8 %add_convert_fusion = bf16[96,1024]{1,0:T(8,128)(2,1)} fusion(bf16[96,1024]{1,0:T(8,128)(2,1)S(1)} %collective-permute-done.10, bf16[96,1024]{1,0:T(8,128)(2,1)S(1)} %collective-permute-done.9, f32[96,1024]{1,0:T(8,128)S(1)} %get-tuple-element.16, bf16[96,1024]{1,0:T(8,128)(2,1)S(1)} %collective-permute-done.8), kind=kLoop, calls=%fused_computation | loop fusion | flops 688128 | bytes 1179648 | tf_op jit(solution)/shard_map/convert_element_type | solution.py:394
  (18 shorter events, 0.0 us)
Async XLA Ops:
  0.6 14.8 %collective-permute-start = (bf16[4096,128]{1,0:T(8,128)(2,1)}, bf16[4096,128]{1,0:T(8,128)(2,1)S(1)}, u32[]{:S(2)}, u32[]{:S(2)}) collective-permute-start(bf16[4096,128]{1,0:T(8,128)(2,1)} %bitcast.4), channel_id=1, source_target_pairs={{0,4},{4,0},{8,12},{12,8},{16,20},{20,16},{24,28},{28,24},{1,5},{5... | collective-permute-start | bytes 3145736 | tf_op jit(solution)/shard_map/ppermute | solution.py:366
  1.2 1.1 %copy-start.1 = (bf16[96,4096]{1,0:T(8,128)(2,1)S(1)}, bf16[96,4096]{1,0:T(8,128)(2,1)}, u32[]{:S(2)}) copy-start(bf16[96,4096]{1,0:T(8,128)(2,1)} %hidden_any.1) | copy-start | bytes 2359300
  2.3 0.7 %copy-start.2 = (f32[4096]{0:T(1024)S(1)}, f32[4096]{0:T(1024)}, u32[]{:S(2)}) copy-start(f32[4096]{0:T(1024)} %param.12) | copy-start | bytes 49156
  3.0 0.7 %copy-start.3 = (s32[768]{0:T(1024)S(1)}, s32[768]{0:T(1024)}, u32[]{:S(2)}) copy-start(s32[768]{0:T(1024)} %selected.1) | copy-start | bytes 9220
  3.7 0.7 %copy-start.4 = (f32[1,128]{1,0:T(1,128)S(1)}, f32[1,128]{1,0:T(1,128)}, u32[]{:S(2)}) copy-start(f32[1,128]{1,0:T(1,128)} %constant.2.clone.freq) | copy-start | bytes 1540
  4.3 11.1 %copy-start = (bf16[1024,2,2,128]{3,2,1,0:T(2,128)(2,1)S(1)}, bf16[1024,2,2,128]{3,2,1,0:T(2,128)(2,1)}, u32[]{:S(2)}) copy-start(bf16[1024,2,2,128]{3,2,1,0:T(2,128)(2,1)} %param.17) | copy-start | bytes 3145732
  4.3 11.1 %copy-start.5 = (s32[2]{0:T(128)S(1)}, s32[2]{0:T(128)}, u32[]{:S(2)}) copy-start(s32[2]{0:T(128)} %order.1) | copy-start | bytes 28
  4.3 11.1 %copy-start.6 = (s32[2]{0:T(128)S(1)}, s32[2]{0:T(128)}, u32[]{:S(2)}) copy-start(s32[2]{0:T(128)} %slot.1) | copy-start | bytes 28
  10.6 9.3 %collective-permute-start.6 = (bf16[96,1024]{1,0:T(8,128)(2,1)S(1)}, bf16[96,1024]{1,0:T(8,128)(2,1)S(1)}, u32[]{:S(2)}, u32[]{:S(2)}) collective-permute-start(bf16[96,1024]{1,0:T(8,128)(2,1)S(1)} %get-tuple-element.15.refs_3_), channel_id=1, source_target_pairs={{0,24},{4,28},{8,16},{12,20},{16,8},{20,12},{24,0},{28,4},{1,25},{... | collective-permute-start | bytes 589832 | tf_op jit(solution)/shard_map/ppermute | solution.py:366
  14.1 1.3 %collective-permute-start.1 = (bf16[96,512]{1,0:T(8,128)(2,1)S(1)}, bf16[96,512]{1,0:T(8,128)(2,1)S(1)}, u32[]{:S(2)}, u32[]{:S(2)}) collective-permute-start(bf16[96,512]{1,0:T(8,128)(2,1)S(1)} %get-tuple-element.12.kv), channel_id=1, source_target_pairs={{0,4},{4,0},{8,12},{12,8},{16,20},{20,16},{24,28},{28,24},{1,5},{5... | collective-permute-start | bytes 294920 | tf_op jit(solution)/shard_map/ppermute | solution.py:366
  14.3 10.8 %collective-permute-start.4 = (bf16[96,1024]{1,0:T(8,128)(2,1)S(1)}, bf16[96,1024]{1,0:T(8,128)(2,1)S(1)}, u32[]{:S(2)}, u32[]{:S(2)}) collective-permute-start(bf16[96,1024]{1,0:T(8,128)(2,1)S(1)} %get-tuple-element.15.refs_3_), channel_id=1, source_target_pairs={{0,16},{4,20},{8,24},{12,28},{16,0},{20,4},{24,8},{28,12},{1,17},{... | collective-permute-start | bytes 589832 | tf_op jit(solution)/shard_map/ppermute | solution.py:366
  14.8 13.2 %collective-permute-start.2 = (bf16[96,1024]{1,0:T(8,128)(2,1)S(1)}, bf16[96,1024]{1,0:T(8,128)(2,1)S(1)}, u32[]{:S(2)}, u32[]{:S(2)}) collective-permute-start(bf16[96,1024]{1,0:T(8,128)(2,1)S(1)} %get-tuple-element.15.refs_3_), channel_id=1, source_target_pairs={{0,8},{4,12},{8,0},{12,4},{16,24},{20,28},{24,16},{28,20},{1,9},{5... | collective-permute-start | bytes 589832 | tf_op jit(solution)/shard_map/ppermute | solution.py:366
  22.2 11.5 %collective-permute-start.7 = (bf16[96,1152]{1,0:T(8,128)(2,1)S(1)}, bf16[96,1152]{1,0:T(8,128)(2,1)S(1)}, u32[]{:S(2)}, u32[]{:S(2)}) collective-permute-start(bf16[96,1152]{1,0:T(8,128)(2,1)S(1)} %attend.7), channel_id=1, source_target_pairs={{0,24},{4,28},{8,16},{12,20},{16,8},{20,12},{24,0},{28,4},{1,25},{... | collective-permute-start | bytes 663560 | tf_op jit(solution)/shard_map/ppermute | solution.py:366
  25.1 12.3 %slice-start = ((s8[8388608]{0:T(1024)(128)(4,1)}), s8[4194304]{0:T(1024)(128)(4,1)S(1)}, s32[]{:S(2)}) async-start(s8[8388608]{0:T(1024)(128)(4,1)} %bitcast.2), calls=%async_computation | async-start | bytes 8388608
  27.5 10.0 %slice-start.1 = ((s8[8388608]{0:T(1024)(128)(4,1)}), s8[4194304]{0:T(1024)(128)(4,1)S(1)}, s32[]{:S(2)}) async-start(s8[8388608]{0:T(1024)(128)(4,1)} %bitcast.2), calls=%async_computation.1 | async-start | bytes 8388608
  27.5 7.5 %collective-permute-start.5 = (bf16[96,1152]{1,0:T(8,128)(2,1)S(1)}, bf16[96,1152]{1,0:T(8,128)(2,1)S(1)}, u32[]{:S(2)}, u32[]{:S(2)}) collective-permute-start(bf16[96,1152]{1,0:T(8,128)(2,1)S(1)} %attend.6), channel_id=1, source_target_pairs={{0,16},{4,20},{8,24},{12,28},{16,0},{20,4},{24,8},{28,12},{1,17},{... | collective-permute-start | bytes 663560 | tf_op jit(solution)/shard_map/ppermute | solution.py:366
  30.4 7.1 %collective-permute-start.3 = (bf16[96,1152]{1,0:T(8,128)(2,1)S(1)}, bf16[96,1152]{1,0:T(8,128)(2,1)S(1)}, u32[]{:S(2)}, u32[]{:S(2)}) collective-permute-start(bf16[96,1152]{1,0:T(8,128)(2,1)S(1)} %attend.5), channel_id=1, source_target_pairs={{0,8},{4,12},{8,0},{12,4},{16,24},{20,28},{24,16},{28,20},{1,9},{5... | collective-permute-start | bytes 663560 | tf_op jit(solution)/shard_map/ppermute | solution.py:366
  39.7 9.7 %collective-permute-start.10 = (bf16[96,1024]{1,0:T(8,128)(2,1)S(1)}, bf16[96,1024]{1,0:T(8,128)(2,1)S(1)}, u32[]{:S(2)}, u32[]{:S(2)}) collective-permute-start(bf16[96,1024]{1,0:T(8,128)(2,1)S(1)} %get-tuple-element.19), channel_id=1, source_target_pairs={{0,3},{1,2},{2,1},{3,0},{4,7},{5,6},{6,5},{7,4},{8,11},{9,10},{10,... | collective-permute-start | bytes 589832 | tf_op jit(solution)/shard_map/ppermute | solution.py:366
  43.3 9.6 %collective-permute-start.8 = (bf16[96,1024]{1,0:T(8,128)(2,1)S(1)}, bf16[96,1024]{1,0:T(8,128)(2,1)S(1)}, u32[]{:S(2)}, u32[]{:S(2)}) collective-permute-start(bf16[96,1024]{1,0:T(8,128)(2,1)S(1)} %get-tuple-element.17), channel_id=1, source_target_pairs={{0,1},{1,0},{2,3},{3,2},{4,5},{5,4},{6,7},{7,6},{8,9},{9,8},{10,11... | collective-permute-start | bytes 589832 | tf_op jit(solution)/shard_map/ppermute | solution.py:366
  43.3 15.7 %collective-permute-start.9 = (bf16[96,1024]{1,0:T(8,128)(2,1)S(1)}, bf16[96,1024]{1,0:T(8,128)(2,1)S(1)}, u32[]{:S(2)}, u32[]{:S(2)}) collective-permute-start(bf16[96,1024]{1,0:T(8,128)(2,1)S(1)} %get-tuple-element.18), channel_id=1, source_target_pairs={{0,2},{1,3},{2,0},{3,1},{4,6},{5,7},{6,4},{7,5},{8,10},{9,11},{10,... | collective-permute-start | bytes 589832 | tf_op jit(solution)/shard_map/ppermute | solution.py:366

commit v4 on v3

--- a/solution.py
+++ b/solution.py
@@ -34,13 +34,18 @@
 
 
 def project_kernel(
-    width, hidden_any, gain, selected, freq, wq_any, wk_any, wv_any, query, kv, table,
-    hidden, normed, weights, sem,
+    width, hidden_any, gain_any, selected_any, freq_any, wq_any, wk_any, wv_any, query, kv, table,
+    hidden, gain, selected, freq, normed, weights, first_sem, sem,
 ):
     rows, feat = hidden.shape
     q_cols, k_cols, v_cols = wq_any.shape[1], wk_any.shape[1], wv_any.shape[1]
-    first = pltpu.make_async_copy(hidden_any, hidden, sem.at[0])
-    first.start()
+    pairs = ((hidden_any, hidden), (gain_any, gain), (selected_any, selected), (freq_any, freq))
+    firsts = [
+        pltpu.make_async_copy(source, target, first_sem.at[number])
+        for number, (source, target) in enumerate(pairs)
+    ]
+    for copy in firsts:
+        copy.start()
     chunks = []
     for source, count, base in ((wk_any, k_cols, 0), (wq_any, q_cols, k_cols), (wv_any, v_cols, k_cols + q_cols)):
         for at in range(0, count, width):
@@ -48,10 +53,12 @@
     copies = []
     for number, (source, at, place) in enumerate(chunks):
         copy = pltpu.make_async_copy(
-            source.at[:, at : at + width], weights.at[:, place : place + width], sem.at[number + 1]
+            source.at[:, at : at + width], weights.at[:, place : place + width], sem.at[number]
         )
         copy.start()
         copies.append(copy)
+    for copy in firsts[1:]:
+        copy.wait()
     total = selected.shape[0]
     me = lax.axis_index("seq")
     mine = iota((rows, total), 1) == iota((rows, total), 0) + me * rows
@@ -64,7 +71,7 @@
     cosine = jnp.cos(angle)
     sine = jnp.sin(angle)
     sine = jnp.where(iota(sine.shape, 1) < HEAD_DIM // 2, -sine, sine)
-    first.wait()
+    firsts[0].wait()
     step = 16
     for at in range(0, rows, step):
         wide = hidden[at : at + step, :].astype(f32)
@@ -92,7 +99,7 @@
     freq = 500000.0 ** (-(np.arange(HEAD_DIM // 2, dtype=np.float32) * np.float32(2.0 / HEAD_DIM)))
     freq = jnp.asarray(np.concatenate([freq, freq])[None, :].astype(np.float32))
     vmem = pl.BlockSpec(memory_space=pltpu.VMEM)
-    hbm = pl.BlockSpec(memory_space=pl.ANY)
+    hbm = pl.BlockSpec(memory_space=pltpu.HBM)
     return pl.pallas_call(
         functools.partial(project_kernel, width),
         out_shape=(
@@ -100,20 +107,27 @@
             jax.ShapeDtypeStruct((rows, wk.shape[1] + wv.shape[1]), bf16),
             jax.ShapeDtypeStruct((selected.shape[0] // rows, LANES), jnp.int32),
         ),
-        in_specs=[hbm, vmem, vmem, vmem, hbm, hbm, hbm],
+        in_specs=[hbm] * 7,
         out_specs=(vmem, vmem, vmem),
         scratch_shapes=[
             pltpu.VMEM((rows, feat), bf16),
+            pltpu.VMEM((1, feat), f32),
+            pltpu.VMEM(selected.shape, jnp.int32),
+            pltpu.VMEM((1, HEAD_DIM), f32),
             pltpu.VMEM((rows, feat), bf16),
             pltpu.VMEM((feat, cols), bf16),
-            pltpu.SemaphoreType.DMA((1 + cols // width,)),
+            pltpu.SemaphoreType.DMA((4,)),
+            pltpu.SemaphoreType.DMA((cols // width,)),
         ],
-        compiler_params=pltpu.CompilerParams(vmem_limit_bytes=52 * MIB),
+        compiler_params=pltpu.CompilerParams(vmem_limit_bytes=48 * MIB),
         cost_estimate=pl.CostEstimate(
             flops=2 * rows * feat * cols, bytes_accessed=2 * feat * (cols + rows), transcendentals=0
         ),
         name="project",
-    )(hidden, gain.reshape(1, feat), selected, freq, wq, wk, wv)
+    )(*[
+        pltpu.with_memory_space_constraint(operand, pltpu.HBM)
+        for operand in (hidden, gain.reshape(1, feat), selected, freq, wq, wk, wv)
+    ])
 
 
 def block_of(index, shard, order, slot):
@@ -189,16 +203,16 @@
     )(order, slot, selected, stored, stored_other, kv, kv_other)
 
 
-def attend_kernel(partners, *refs):
+def attend_kernel(partners, served, *refs):
     count = len(partners)
     cache, key_pos, selected = refs[:3]
     queries = refs[3 : 3 + count]
-    outs = refs[3 + count : 3 + 2 * count]
-    scores, weights, masks = refs[3 + 2 * count :]
+    outs = refs[-3 - count : -3]
+    scores, weights, masks = refs[-3:]
     _, shard, cols = cache.shape
     rows = queries[0].shape[0]
     kv_heads = cols // (2 * HEAD_DIM)
-    heads = kv_heads * GROUP
+    heads = len(served) * GROUP
     keys = 2 * shard
     step = 256
     scale = math.log2(math.e) / HEAD_DIM**0.5
@@ -224,12 +238,12 @@
         col = (kind * kv_heads + head) * HEAD_DIM
         return cache[place // shard, place % shard : place % shard + size, col : col + HEAD_DIM]
 
-    units = [(at, head) for at in range(count) for head in range(kv_heads)]
+    units = [(at, head) for at in range(count) for head in served]
     best = {}
     for number in range(len(units) + 1):
         if number < len(units):
             at, head = units[number]
-            if head == 0:
+            if head == served[0]:
                 mask(at)
             stream = left(at, head)
         if number:
@@ -268,29 +282,29 @@
             out = outs[old_at]
             packed = jnp.zeros((rows, LANES), f32)
             for member in range(GROUP):
-                which = old_head * GROUP + member
+                which = served.index(old_head) * GROUP + member
                 span = slice(member * rows, (member + 1) * rows)
                 out[:, which * HEAD_DIM : (which + 1) * HEAD_DIM] = context[span]
                 for piece, source in enumerate((high, middle, low)):
                     packed = jnp.where(lane == piece * heads + which, source[span], packed)
             tail = slice(heads * HEAD_DIM, heads * HEAD_DIM + LANES)
-            if old_head:
+            if old_head != served[0]:
                 packed = packed + out[:, tail].astype(f32)
             out[:, tail] = packed.astype(bf16)
 
 
-def attend(partners, cache, key_pos, selected, queries):
+def attend(partners, served, cache, key_pos, selected, queries, earlier):
     _, shard, cols = cache.shape
-    rows, q_cols = queries[0].shape
-    kv_heads = cols // (2 * HEAD_DIM)
+    rows = queries[0].shape[0]
+    out_cols = len(served) * GROUP * HEAD_DIM + LANES
     tall = GROUP * rows
     keys = 2 * shard
     count = len(queries)
     vmem = pl.BlockSpec(memory_space=pltpu.VMEM)
     out = pl.pallas_call(
-        functools.partial(attend_kernel, partners),
-        out_shape=[jax.ShapeDtypeStruct((rows, q_cols + LANES), bf16)] * count,
-        in_specs=[vmem] * (3 + count),
+        functools.partial(attend_kernel, partners, served),
+        out_shape=[jax.ShapeDtypeStruct((rows, out_cols), bf16)] * count,
+        in_specs=[vmem] * (3 + count) + [pl.BlockSpec(memory_space=pl.ANY)] * len(earlier),
         out_specs=[vmem] * count,
         scratch_shapes=[
             pltpu.VMEM((2, tall, keys), f32),
@@ -299,38 +313,45 @@
         ],
         compiler_params=pltpu.CompilerParams(vmem_limit_bytes=24 * MIB),
         cost_estimate=pl.CostEstimate(
-            flops=8 * count * kv_heads * tall * keys * HEAD_DIM,
+            flops=8 * count * len(served) * tall * keys * HEAD_DIM,
             bytes_accessed=8 * shard * cols,
-            transcendentals=count * kv_heads * tall * keys,
+            transcendentals=count * len(served) * tall * keys,
         ),
         name="attend",
-    )(cache, key_pos, selected, *queries)
+    )(cache, key_pos, selected, *queries, *earlier)
     return list(out)
 
 
-def finish_kernel(count, size, *refs):
+def finish_kernel(groups, size, *refs):
+    count = sum(len(group) for group in groups)
     parts = refs[:count]
     weights = refs[count]
     outs = refs[count + 1 : count + 1 + size]
     (context,) = refs[count + 1 + size :]
-    rows, feat = context.shape
-    heads = feat // HEAD_DIM
     width = weights.shape[1] // size
     me = lax.axis_index("head")
-    tails = [part[:, feat : feat + LANES].astype(f32) for part in parts]
-    for head in range(heads):
-        levels = []
-        for tail in tails:
-            pieces = [tail[:, piece * heads + head : piece * heads + head + 1] for piece in range(3)]
-            levels.append(pieces[0] + pieces[1] + pieces[2])
-        top = functools.reduce(jnp.maximum, levels)
-        shares = [jnp.exp2(level - top) for level in levels]
+    found = {}
+    at = 0
+    for group in groups:
+        for served in group:
+            part = parts[at]
+            at += 1
+            heads = len(served) * GROUP
+            tail = part[:, heads * HEAD_DIM : heads * HEAD_DIM + LANES].astype(f32)
+            for number in range(heads):
+                head = served[number // GROUP] * GROUP + number % GROUP
+                pieces = [tail[:, piece * heads + number : piece * heads + number + 1] for piece in range(3)]
+                level = pieces[0] + pieces[1] + pieces[2]
+                found.setdefault(head, []).append((level, part, slice(number * HEAD_DIM, (number + 1) * HEAD_DIM)))
+    for head, entries in found.items():
+        top = functools.reduce(jnp.maximum, [level for level, _, _ in entries])
+        shares = [jnp.exp2(level - top) for level, _, _ in entries]
         whole = functools.reduce(jnp.add, shares)
-        span = slice(head * HEAD_DIM, (head + 1) * HEAD_DIM)
         mixed = functools.reduce(
-            jnp.add, [(share / whole) * part[:, span].astype(f32) for share, part in zip(shares, parts)]
+            jnp.add,
+            [(share / whole) * part[:, span].astype(f32) for share, (_, part, span) in zip(shares, entries)],
         )
-        context[:, span] = mixed.astype(bf16)
+        context[:, head * HEAD_DIM : (head + 1) * HEAD_DIM] = mixed.astype(bf16)
     for turn in range(size):
         start = (me ^ turn) * width
         step = 256 if width % 256 == 0 else width
@@ -341,13 +362,15 @@
             ).astype(outs[turn].dtype)
 
 
-def finish(parts, w_out, size):
+def finish(groups, w_out, size):
+    parts = [part for group in groups for _, part in group]
+    served = [[which for which, _ in group] for group in groups]
     rows = parts[0].shape[0]
     feat, cols = w_out.shape
     width = cols // size
     vmem = pl.BlockSpec(memory_space=pltpu.VMEM)
     return pl.pallas_call(
-        functools.partial(finish_kernel, len(parts), size),
+        functools.partial(finish_kernel, served, size),
         out_shape=[jax.ShapeDtypeStruct((rows, width), f32 if turn == 0 else bf16) for turn in range(size)],
         in_specs=[vmem] * (len(parts) + 1),
         out_specs=[vmem] * size,
@@ -376,16 +399,25 @@
     stored = stored_kv.reshape(-1, HEAD_DIM)
     stored_other = swap(stored, "seq", 1, seq_count)
     query, kv, table = project(hidden, norm_gain, selected, w_query, w_key, w_value)
-    turns = list(range(2, seq_count, 2))
-    near_first = sorted(turns, key=lambda turn: (bin(turn).count("1"), turn))
-    queries = {turn: swap(query, "seq", turn, seq_count) for turn in near_first}
+    turns = sorted(range(2, seq_count, 2), key=lambda turn: (-bin(turn).count("1"), turn))
+    queries = {turn: swap(query, "seq", turn, seq_count) for turn in turns}
     kv_other = swap(kv, "seq", 1, seq_count)
     cache, key_pos = merge(prompt_order, store_slot, table, stored, stored_other, kv, kv_other)
-    parts = attend((0,), cache, key_pos, table, [query])
-    for turn in near_first:
-        (part,) = attend((turn,), cache, key_pos, table, [queries[turn]])
-        parts.append(swap(part, "seq", turn, seq_count))
-    blocks = finish(parts, w_out, head_count)
+    every = tuple(range(local_kv))
+    groups = []
+    done = []
+    far, near = turns[:-2], turns[-2:]
+    for turn in far:
+        done = attend((turn,), every, cache, key_pos, table, [queries[turn]], done)
+        groups.append([(every, swap(done[0], "seq", turn, seq_count))])
+    split = {turn: [] for turn in near}
+    for head in every:
+        done = attend(tuple(near), (head,), cache, key_pos, table, [queries[turn] for turn in near], done)
+        for turn, part in zip(near, done):
+            split[turn].append(((head,), swap(part, "seq", turn, seq_count)))
+    groups += list(split.values())
+    groups.append([(every, attend((0,), every, cache, key_pos, table, [query], done)[0])])
+    blocks = finish(groups, w_out, head_count)
     total = blocks[0]
     arrived = [swap(blocks[turn], "head", turn, head_count) for turn in range(1, head_count)]
     for block in arrived:

time: 60.1 us -> 58.4 us (0.972)
  the two profiles are of different devices: /device:TPU:0 before, /device:TPU:8 now
where the time goes in v4:
time: 58.4 us; the launch traced here: 57.9 us
  Pallas kernels  22.9 us (39%)
  waiting for transfers between devices  18.7 us (32%)
  starting transfers between devices  14.1 us (24%)
  other arithmetic  0.77 us (1%)
  between operations  0.76 us (1%)
  local copies, waits for them, and re-layouts  0.69 us (1%)
    ppermute x13, waiting for transfers between devices, swap(): return lax.ppermute(value, axis, [(at, at ^ turn) for at in range(size)])  18.7 us
    ppermute x13, starting transfers between devices, swap(): return lax.ppermute(value, axis, [(at, at ^ turn) for at in range(size)])  14.1 us
    pallas_call x4, Pallas kernels, attend(): pl.pallas_call(functools.partial(attend_kernel, partners, served), out_sh...  9.37 us
    pallas_call x1, Pallas kernels, project(): pl.pallas_call(functools.partial(project_kernel, width), out_shape=(jax.S...  9.3 us
    pallas_call x1, Pallas kernels, finish(): pl.pallas_call(functools.partial(finish_kernel, served, size), out_shape=...  2.38 us
    pallas_call x1, Pallas kernels, merge(): pl.pallas_call(merge_kernel, out_shape=(jax.ShapeDtypeStruct((2, shard, c...  1.86 us
  transfers between devices with their start and end apart: 13, of which 7 were waited for; matrix products, arithmetic and copies ran while one was open for 1% of the time, Pallas kernels for 35%

profile of v4, /device:TPU:8, one launch (start us, length us, event | category | flops | bytes accessed | tf_op | source)
XLA Modules:
  0.0 57.9 jit_solution(7398845262696099866)
XLA Ops:
  0.6 0.1 collective-permute-start
  0.7 9.3 %project.1 = (bf16[96,1024]{1,0:T(8,128)(2,1)S(1)}, bf16[96,512]{1,0:T(8,128)(2,1)S(1)}, s32[8,128]{1,0:T(8,128)S(1)}) custom-call(bf16[96,4096]{1,0:T(8,128)(2,1)} %hidden_any.1, f32[1,4096]{1,0:T(1,128)} %bitcast.6, s32[768]{0:T(1024)} %selected_any.1, f32[1,128]{1,0:T(1,128)} %constant.2.clone.freq_any, bf16[4096,1024]{1,0:T(8,128)(2,1)} %wq_any.1, ...), custom_call_target="tpu_custom_call" | custom-call | flops 1207959552 | bytes 13369344 | tf_op jit(solution)/shard_map/project/pallas_call | solution.py:103
  10.0 2.5 %collective-permute-start.2 = (bf16[96,1024]{1,0:T(8,128)(2,1)S(1)}, bf16[96,1024]{1,0:T(8,128)(2,1)S(1)}, u32[]{:S(2)}, u32[]{:S(2)}) collective-permute-start(bf16[96,1024]{1,0:T(8,128)(2,1)S(1)} %get-tuple-element.19.refs_3_), channel_id=1, source_target_pairs={{0,24},{4,28},{8,16},{12,20},{16,8},{20,12},{24,0},{28,4},{1,25},{... | collective-permute-start | bytes 589832 | tf_op jit(solution)/shard_map/ppermute | solution.py:389
  12.6 0.2 collective-permute-start.1
  12.8 0.5 collective-permute-start.4
  13.3 0.5 collective-permute-start.5
  13.8 0.1 collective-permute-done.1.kv_other
  13.9 0.0 collective-permute-done.stored_other
  13.9 1.9 %merge.1 = (bf16[2,1024,512]{2,1,0:T(8,128)(2,1)S(1)}, f32[2048,128]{1,0:T(8,128)S(1)}) custom-call(s32[2]{0:T(128)S(1)} %copy-done.1, s32[2]{0:T(128)S(1)} %copy-done.2, s32[8,128]{1,0:T(8,128)S(1)} %get-tuple-element.15.selected.refs_2_, bf16[4096,128]{1,0:T(8,128)(2,1)S(1)} %bitcast.5, bf16[4096,128]{1,0:T(8,128)(2,1)S(1)} %collective-permute-done.stored_other, ...), custom_call_target="tpu_custom_call" | custom-call | flops 1000 | bytes 1000 | tf_op jit(solution)/shard_map/merge/pallas_call | solution.py:191
  15.7 3.0 %collective-permute-done.2.refs_3_ = bf16[96,1024]{1,0:T(8,128)(2,1)S(1)} collective-permute-done((bf16[96,1024]{1,0:T(8,128)(2,1)S(1)}, bf16[96,1024]{1,0:T(8,128)(2,1)S(1)}, u32[]{:S(2)}, u32[]{:S(2)}) %collective-permute-start.2) | collective-permute-done | bytes 196640 | tf_op jit(solution)/shard_map/ppermute | solution.py:389
  18.8 2.3 %attend.4.refs_5_ = bf16[96,1152]{1,0:T(8,128)(2,1)S(1)} custom-call(bf16[2,1024,512]{2,1,0:T(8,128)(2,1)S(1)} %get-tuple-element.17.refs_0_, f32[2048,128]{1,0:T(8,128)S(1)} %get-tuple-element.18.refs_1_, s32[8,128]{1,0:T(8,128)S(1)} %get-tuple-element.15.selected.refs_2_, bf16[96,1024]{1,0:T(8,128)(2,1)S(1)} %collective-permute-done.2.refs_3_), custom_call_target="tpu_custom_call" | custom-call | flops 1610612736 | bytes 4194304 | tf_op jit(solution)/shard_map/attend/pallas_call | solution.py:304
  21.1 2.5 %collective-permute-start.3 = (bf16[96,1152]{1,0:T(8,128)(2,1)S(1)}, bf16[96,1152]{1,0:T(8,128)(2,1)S(1)}, u32[]{:S(2)}, u32[]{:S(2)}) collective-permute-start(bf16[96,1152]{1,0:T(8,128)(2,1)S(1)} %attend.4.refs_5_), channel_id=1, source_target_pairs={{0,24},{4,28},{8,16},{12,20},{16,8},{20,12},{24,0},{28,4},{1,25},{... | collective-permute-start | bytes 663560 | tf_op jit(solution)/shard_map/ppermute | solution.py:389
  23.6 0.0 collective-permute-done.4.refs_3_
  23.6 2.3 %attend.5 = (bf16[96,640]{1,0:T(8,128)(2,1)S(1)}, bf16[96,640]{1,0:T(8,128)(2,1)S(1)}) custom-call(bf16[2,1024,512]{2,1,0:T(8,128)(2,1)S(1)} %get-tuple-element.17.refs_0_, f32[2048,128]{1,0:T(8,128)S(1)} %get-tuple-element.18.refs_1_, s32[8,128]{1,0:T(8,128)S(1)} %get-tuple-element.15.selected.refs_2_, bf16[96,1024]{1,0:T(8,128)(2,1)S(1)} %collective-permute-done.4.refs_3_, ...), custom_call_target="tpu_custom_call" | custom-call | flops 1610612736 | bytes 4194304 | tf_op jit(solution)/shard_map/attend/pallas_call | solution.py:304
  25.9 0.6 %collective-permute-start.6 = (bf16[96,640]{1,0:T(8,128)(2,1)S(1)}, bf16[96,640]{1,0:T(8,128)(2,1)S(1)}, u32[]{:S(2)}, u32[]{:S(2)}) collective-permute-start(bf16[96,640]{1,0:T(8,128)(2,1)S(1)} %get-tuple-element.20.refs_5_), channel_id=1, source_target_pairs={{0,8},{4,12},{8,0},{12,4},{16,24},{20,28},{24,16},{28,20},{1,9},{5... | collective-permute-start | bytes 368648 | tf_op jit(solution)/shard_map/ppermute | solution.py:389
  26.5 1.4 %collective-permute-start.8 = (bf16[96,640]{1,0:T(8,128)(2,1)S(1)}, bf16[96,640]{1,0:T(8,128)(2,1)S(1)}, u32[]{:S(2)}, u32[]{:S(2)}) collective-permute-start(bf16[96,640]{1,0:T(8,128)(2,1)S(1)} %get-tuple-element.21.refs_6_), channel_id=1, source_target_pairs={{0,16},{4,20},{8,24},{12,28},{16,0},{20,4},{24,8},{28,12},{1,17},{... | collective-permute-start | bytes 368648 | tf_op jit(solution)/shard_map/ppermute | solution.py:389
  27.9 2.3 %attend.6 = (bf16[96,640]{1,0:T(8,128)(2,1)S(1)}, bf16[96,640]{1,0:T(8,128)(2,1)S(1)}) custom-call(bf16[2,1024,512]{2,1,0:T(8,128)(2,1)S(1)} %get-tuple-element.17.refs_0_, f32[2048,128]{1,0:T(8,128)S(1)} %get-tuple-element.18.refs_1_, s32[8,128]{1,0:T(8,128)S(1)} %get-tuple-element.15.selected.refs_2_, bf16[96,1024]{1,0:T(8,128)(2,1)S(1)} %collective-permute-done.4.refs_3_, ...), custom_call_target="tpu_custom_call" | custom-call | flops 1610612736 | bytes 4194304 | tf_op jit(solution)/shard_map/attend/pallas_call | solution.py:304
  30.2 0.7 %collective-permute-start.7 = (bf16[96,640]{1,0:T(8,128)(2,1)S(1)}, bf16[96,640]{1,0:T(8,128)(2,1)S(1)}, u32[]{:S(2)}, u32[]{:S(2)}) collective-permute-start(bf16[96,640]{1,0:T(8,128)(2,1)S(1)} %get-tuple-element.22.refs_4_), channel_id=1, source_target_pairs={{0,8},{4,12},{8,0},{12,4},{16,24},{20,28},{24,16},{28,20},{1,9},{5... | collective-permute-start | bytes 368648 | tf_op jit(solution)/shard_map/ppermute | solution.py:389
  30.9 1.5 %collective-permute-start.9 = (bf16[96,640]{1,0:T(8,128)(2,1)S(1)}, bf16[96,640]{1,0:T(8,128)(2,1)S(1)}, u32[]{:S(2)}, u32[]{:S(2)}) collective-permute-start(bf16[96,640]{1,0:T(8,128)(2,1)S(1)} %get-tuple-element.23.refs_5_), channel_id=1, source_target_pairs={{0,16},{4,20},{8,24},{12,28},{16,0},{20,4},{24,8},{28,12},{1,17},{... | collective-permute-start | bytes 368648 | tf_op jit(solution)/shard_map/ppermute | solution.py:389
  32.4 2.5 %attend.7.refs_5_ = bf16[96,1152]{1,0:T(8,128)(2,1)S(1)} custom-call(bf16[2,1024,512]{2,1,0:T(8,128)(2,1)S(1)} %get-tuple-element.17.refs_0_, f32[2048,128]{1,0:T(8,128)S(1)} %get-tuple-element.18.refs_1_, s32[8,128]{1,0:T(8,128)S(1)} %get-tuple-element.15.selected.refs_2_, bf16[96,1024]{1,0:T(8,128)(2,1)S(1)} %get-tuple-element.19.refs_3_, ...), custom_call_target="tpu_custom_call" | custom-call | flops 1610612736 | bytes 4194304 | tf_op jit(solution)/shard_map/attend/pallas_call | solution.py:304
  34.9 0.3 collective-permute-done.7.refs_2_
  35.1 0.6 %collective-permute-done.9.refs_4_ = bf16[96,640]{1,0:T(8,128)(2,1)S(1)} collective-permute-done((bf16[96,640]{1,0:T(8,128)(2,1)S(1)}, bf16[96,640]{1,0:T(8,128)(2,1)S(1)}, u32[]{:S(2)}, u32[]{:S(2)}) %collective-permute-start.9) | collective-permute-done | bytes 122912 | tf_op jit(solution)/shard_map/ppermute | solution.py:389
  35.7 0.0 collective-permute-done.3.refs_0_
  35.8 2.4 %finish.1 = (f32[96,1024]{1,0:T(8,128)S(1)}, bf16[96,1024]{1,0:T(8,128)(2,1)S(1)}, bf16[96,1024]{1,0:T(8,128)(2,1)S(1)}, bf16[96,1024]{1,0:T(8,128)(2,1)S(1)}) custom-call(bf16[96,1152]{1,0:T(8,128)(2,1)S(1)} %collective-permute-done.3.refs_0_, bf16[96,640]{1,0:T(8,128)(2,1)S(1)} %collective-permute-done.6.refs_1_, ...), custom_call_target="tpu_custom_call" | custom-call | flops 805306368 | bytes 8388608 | tf_op jit(solution)/shard_map/finish/pallas_call | solution.py:372
  38.2 0.5 collective-permute-start.10
  38.7 2.6 %collective-permute-start.11 = (bf16[96,1024]{1,0:T(8,128)(2,1)S(1)}, bf16[96,1024]{1,0:T(8,128)(2,1)S(1)}, u32[]{:S(2)}, u32[]{:S(2)}) collective-permute-start(bf16[96,1024]{1,0:T(8,128)(2,1)S(1)} %get-tuple-element.26), channel_id=1, source_target_pairs={{0,2},{1,3},{2,0},{3,1},{4,6},{5,7},{6,4},{7,5},{8,10},{9,11},{10,... | collective-permute-start | bytes 589832 | tf_op jit(solution)/shard_map/ppermute | solution.py:389
  41.3 0.4 collective-permute-start.12
  41.7 0.7 %reshape.15 = bf16[96,2,2,128]{3,2,1,0:T(2,128)(2,1)} reshape(bf16[96,512]{1,0:T(8,128)(2,1)S(1)} %get-tuple-element.16.kv) | data formatting | bytes 196608 | tf_op jit(solution)/shard_map/reshape | solution.py:425
  42.4 3.5 %collective-permute-done.10 = bf16[96,1024]{1,0:T(8,128)(2,1)S(1)} collective-permute-done((bf16[96,1024]{1,0:T(8,128)(2,1)S(1)}, bf16[96,1024]{1,0:T(8,128)(2,1)S(1)}, u32[]{:S(2)}, u32[]{:S(2)}) %collective-permute-start.10) | collective-permute-done | bytes 196640 | tf_op jit(solution)/shard_map/ppermute | solution.py:389
  45.9 8.0 %collective-permute-done.11 = bf16[96,1024]{1,0:T(8,128)(2,1)S(1)} collective-permute-done((bf16[96,1024]{1,0:T(8,128)(2,1)S(1)}, bf16[96,1024]{1,0:T(8,128)(2,1)S(1)}, u32[]{:S(2)}, u32[]{:S(2)}) %collective-permute-start.11) | collective-permute-done | bytes 196640 | tf_op jit(solution)/shard_map/ppermute | solution.py:389
  53.9 3.2 %collective-permute-done.12 = bf16[96,1024]{1,0:T(8,128)(2,1)S(1)} collective-permute-done((bf16[96,1024]{1,0:T(8,128)(2,1)S(1)}, bf16[96,1024]{1,0:T(8,128)(2,1)S(1)}, u32[]{:S(2)}, u32[]{:S(2)}) %collective-permute-start.12) | collective-permute-done | bytes 196640 | tf_op jit(solution)/shard_map/ppermute | solution.py:389
  57.1 0.8 %add_convert_fusion = bf16[96,1024]{1,0:T(8,128)(2,1)} fusion(bf16[96,1024]{1,0:T(8,128)(2,1)S(1)} %collective-permute-done.12, bf16[96,1024]{1,0:T(8,128)(2,1)S(1)} %collective-permute-done.11, f32[96,1024]{1,0:T(8,128)S(1)} %get-tuple-element.24, bf16[96,1024]{1,0:T(8,128)(2,1)S(1)} %collective-permute-done.10), kind=kLoop, calls=%fused_computation | loop fusion | flops 688128 | bytes 1179648 | tf_op jit(solution)/shard_map/convert_element_type | solution.py:426
  (14 shorter events, 0.0 us)
Async XLA Ops:
  0.6 13.2 %collective-permute-start = (bf16[4096,128]{1,0:T(8,128)(2,1)}, bf16[4096,128]{1,0:T(8,128)(2,1)S(1)}, u32[]{:S(2)}, u32[]{:S(2)}) collective-permute-start(bf16[4096,128]{1,0:T(8,128)(2,1)} %bitcast.4), channel_id=1, source_target_pairs={{0,4},{4,0},{8,12},{12,8},{16,20},{20,16},{24,28},{28,24},{1,5},{5... | collective-permute-start | bytes 3145736 | tf_op jit(solution)/shard_map/ppermute | solution.py:389
  0.7 13.2 %copy-start = (bf16[1024,2,2,128]{3,2,1,0:T(2,128)(2,1)S(1)}, bf16[1024,2,2,128]{3,2,1,0:T(2,128)(2,1)}, u32[]{:S(2)}) copy-start(bf16[1024,2,2,128]{3,2,1,0:T(2,128)(2,1)} %param.17) | copy-start | bytes 3145732
  0.7 13.1 %copy-start.1 = (s32[2]{0:T(128)S(1)}, s32[2]{0:T(128)}, u32[]{:S(2)}) copy-start(s32[2]{0:T(128)} %order.1) | copy-start | bytes 28
  0.7 13.1 %copy-start.2 = (s32[2]{0:T(128)S(1)}, s32[2]{0:T(128)}, u32[]{:S(2)}) copy-start(s32[2]{0:T(128)} %slot.1) | copy-start | bytes 28
  10.0 8.7 %collective-permute-start.2 = (bf16[96,1024]{1,0:T(8,128)(2,1)S(1)}, bf16[96,1024]{1,0:T(8,128)(2,1)S(1)}, u32[]{:S(2)}, u32[]{:S(2)}) collective-permute-start(bf16[96,1024]{1,0:T(8,128)(2,1)S(1)} %get-tuple-element.19.refs_3_), channel_id=1, source_target_pairs={{0,24},{4,28},{8,16},{12,20},{16,8},{20,12},{24,0},{28,4},{1,25},{... | collective-permute-start | bytes 589832 | tf_op jit(solution)/shard_map/ppermute | solution.py:389
  12.6 1.3 %collective-permute-start.1 = (bf16[96,512]{1,0:T(8,128)(2,1)S(1)}, bf16[96,512]{1,0:T(8,128)(2,1)S(1)}, u32[]{:S(2)}, u32[]{:S(2)}) collective-permute-start(bf16[96,512]{1,0:T(8,128)(2,1)S(1)} %get-tuple-element.16.kv), channel_id=1, source_target_pairs={{0,4},{4,0},{8,12},{12,8},{16,20},{20,16},{24,28},{28,24},{1,5},{5... | collective-permute-start | bytes 294920 | tf_op jit(solution)/shard_map/ppermute | solution.py:389
  12.8 10.8 %collective-permute-start.4 = (bf16[96,1024]{1,0:T(8,128)(2,1)S(1)}, bf16[96,1024]{1,0:T(8,128)(2,1)S(1)}, u32[]{:S(2)}, u32[]{:S(2)}) collective-permute-start(bf16[96,1024]{1,0:T(8,128)(2,1)S(1)} %get-tuple-element.19.refs_3_), channel_id=1, source_target_pairs={{0,8},{4,12},{8,0},{12,4},{16,24},{20,28},{24,16},{28,20},{1,9},{5... | collective-permute-start | bytes 589832 | tf_op jit(solution)/shard_map/ppermute | solution.py:389
  13.3 10.3 %collective-permute-start.5 = (bf16[96,1024]{1,0:T(8,128)(2,1)S(1)}, bf16[96,1024]{1,0:T(8,128)(2,1)S(1)}, u32[]{:S(2)}, u32[]{:S(2)}) collective-permute-start(bf16[96,1024]{1,0:T(8,128)(2,1)S(1)} %get-tuple-element.19.refs_3_), channel_id=1, source_target_pairs={{0,16},{4,20},{8,24},{12,28},{16,0},{20,4},{24,8},{28,12},{1,17},{... | collective-permute-start | bytes 589832 | tf_op jit(solution)/shard_map/ppermute | solution.py:389
  21.1 14.7 %collective-permute-start.3 = (bf16[96,1152]{1,0:T(8,128)(2,1)S(1)}, bf16[96,1152]{1,0:T(8,128)(2,1)S(1)}, u32[]{:S(2)}, u32[]{:S(2)}) collective-permute-start(bf16[96,1152]{1,0:T(8,128)(2,1)S(1)} %attend.4.refs_5_), channel_id=1, source_target_pairs={{0,24},{4,28},{8,16},{12,20},{16,8},{20,12},{24,0},{28,4},{1,25},{... | collective-permute-start | bytes 663560 | tf_op jit(solution)/shard_map/ppermute | solution.py:389
  23.6 12.2 %slice-start = ((s8[8388608]{0:T(1024)(128)(4,1)}), s8[4194304]{0:T(1024)(128)(4,1)S(1)}, s32[]{:S(2)}) async-start(s8[8388608]{0:T(1024)(128)(4,1)} %bitcast.2), calls=%async_computation | async-start | bytes 8388608
  25.9 9.9 %collective-permute-start.6 = (bf16[96,640]{1,0:T(8,128)(2,1)S(1)}, bf16[96,640]{1,0:T(8,128)(2,1)S(1)}, u32[]{:S(2)}, u32[]{:S(2)}) collective-permute-start(bf16[96,640]{1,0:T(8,128)(2,1)S(1)} %get-tuple-element.20.refs_5_), channel_id=1, source_target_pairs={{0,8},{4,12},{8,0},{12,4},{16,24},{20,28},{24,16},{28,20},{1,9},{5... | collective-permute-start | bytes 368648 | tf_op jit(solution)/shard_map/ppermute | solution.py:389
  26.5 9.3 %slice-start.1 = ((s8[8388608]{0:T(1024)(128)(4,1)}), s8[4194304]{0:T(1024)(128)(4,1)S(1)}, s32[]{:S(2)}) async-start(s8[8388608]{0:T(1024)(128)(4,1)} %bitcast.2), calls=%async_computation.1 | async-start | bytes 8388608
  26.5 9.2 %collective-permute-start.8 = (bf16[96,640]{1,0:T(8,128)(2,1)S(1)}, bf16[96,640]{1,0:T(8,128)(2,1)S(1)}, u32[]{:S(2)}, u32[]{:S(2)}) collective-permute-start(bf16[96,640]{1,0:T(8,128)(2,1)S(1)} %get-tuple-element.21.refs_6_), channel_id=1, source_target_pairs={{0,16},{4,20},{8,24},{12,28},{16,0},{20,4},{24,8},{28,12},{1,17},{... | collective-permute-start | bytes 368648 | tf_op jit(solution)/shard_map/ppermute | solution.py:389
  30.2 4.9 %collective-permute-start.7 = (bf16[96,640]{1,0:T(8,128)(2,1)S(1)}, bf16[96,640]{1,0:T(8,128)(2,1)S(1)}, u32[]{:S(2)}, u32[]{:S(2)}) collective-permute-start(bf16[96,640]{1,0:T(8,128)(2,1)S(1)} %get-tuple-element.22.refs_4_), channel_id=1, source_target_pairs={{0,8},{4,12},{8,0},{12,4},{16,24},{20,28},{24,16},{28,20},{1,9},{5... | collective-permute-start | bytes 368648 | tf_op jit(solution)/shard_map/ppermute | solution.py:389
  30.9 4.9 %collective-permute-start.9 = (bf16[96,640]{1,0:T(8,128)(2,1)S(1)}, bf16[96,640]{1,0:T(8,128)(2,1)S(1)}, u32[]{:S(2)}, u32[]{:S(2)}) collective-permute-start(bf16[96,640]{1,0:T(8,128)(2,1)S(1)} %get-tuple-element.23.refs_5_), channel_id=1, source_target_pairs={{0,16},{4,20},{8,24},{12,28},{16,0},{20,4},{24,8},{28,12},{1,17},{... | collective-permute-start | bytes 368648 | tf_op jit(solution)/shard_map/ppermute | solution.py:389
  38.2 7.8 %collective-permute-start.10 = (bf16[96,1024]{1,0:T(8,128)(2,1)S(1)}, bf16[96,1024]{1,0:T(8,128)(2,1)S(1)}, u32[]{:S(2)}, u32[]{:S(2)}) collective-permute-start(bf16[96,1024]{1,0:T(8,128)(2,1)S(1)} %get-tuple-element.25), channel_id=1, source_target_pairs={{0,1},{1,0},{2,3},{3,2},{4,5},{5,4},{6,7},{7,6},{8,9},{9,8},{10,11... | collective-permute-start | bytes 589832 | tf_op jit(solution)/shard_map/ppermute | solution.py:389
  38.7 15.2 %collective-permute-start.11 = (bf16[96,1024]{1,0:T(8,128)(2,1)S(1)}, bf16[96,1024]{1,0:T(8,128)(2,1)S(1)}, u32[]{:S(2)}, u32[]{:S(2)}) collective-permute-start(bf16[96,1024]{1,0:T(8,128)(2,1)S(1)} %get-tuple-element.26), channel_id=1, source_target_pairs={{0,2},{1,3},{2,0},{3,1},{4,6},{5,7},{6,4},{7,5},{8,10},{9,11},{10,... | collective-permute-start | bytes 589832 | tf_op jit(solution)/shard_map/ppermute | solution.py:389
  41.3 15.8 %collective-permute-start.12 = (bf16[96,1024]{1,0:T(8,128)(2,1)S(1)}, bf16[96,1024]{1,0:T(8,128)(2,1)S(1)}, u32[]{:S(2)}, u32[]{:S(2)}) collective-permute-start(bf16[96,1024]{1,0:T(8,128)(2,1)S(1)} %get-tuple-element.27), channel_id=1, source_target_pairs={{0,3},{1,2},{2,1},{3,0},{4,7},{5,6},{6,5},{7,4},{8,11},{9,10},{10,... | collective-permute-start | bytes 589832 | tf_op jit(solution)/shard_map/ppermute | solution.py:389

commit v5 on v3

--- a/solution.py
+++ b/solution.py
@@ -34,13 +34,18 @@
 
 
 def project_kernel(
-    width, hidden_any, gain, selected, freq, wq_any, wk_any, wv_any, query, kv, table,
-    hidden, normed, weights, sem,
+    width, hidden_any, gain_any, selected_any, freq_any, wq_any, wk_any, wv_any, query, kv, table,
+    hidden, gain, selected, freq, normed, weights, first_sem, sem,
 ):
     rows, feat = hidden.shape
     q_cols, k_cols, v_cols = wq_any.shape[1], wk_any.shape[1], wv_any.shape[1]
-    first = pltpu.make_async_copy(hidden_any, hidden, sem.at[0])
-    first.start()
+    pairs = ((hidden_any, hidden), (gain_any, gain), (selected_any, selected), (freq_any, freq))
+    firsts = [
+        pltpu.make_async_copy(source, target, first_sem.at[number])
+        for number, (source, target) in enumerate(pairs)
+    ]
+    for copy in firsts:
+        copy.start()
     chunks = []
     for source, count, base in ((wk_any, k_cols, 0), (wq_any, q_cols, k_cols), (wv_any, v_cols, k_cols + q_cols)):
         for at in range(0, count, width):
@@ -48,10 +53,12 @@
     copies = []
     for number, (source, at, place) in enumerate(chunks):
         copy = pltpu.make_async_copy(
-            source.at[:, at : at + width], weights.at[:, place : place + width], sem.at[number + 1]
+            source.at[:, at : at + width], weights.at[:, place : place + width], sem.at[number]
         )
-        copy.start()
+        copy.start(priority=1)
         copies.append(copy)
+    for copy in firsts[1:]:
+        copy.wait()
     total = selected.shape[0]
     me = lax.axis_index("seq")
     mine = iota((rows, total), 1) == iota((rows, total), 0) + me * rows
@@ -64,7 +71,7 @@
     cosine = jnp.cos(angle)
     sine = jnp.sin(angle)
     sine = jnp.where(iota(sine.shape, 1) < HEAD_DIM // 2, -sine, sine)
-    first.wait()
+    firsts[0].wait()
     step = 16
     for at in range(0, rows, step):
         wide = hidden[at : at + step, :].astype(f32)
@@ -92,7 +99,7 @@
     freq = 500000.0 ** (-(np.arange(HEAD_DIM // 2, dtype=np.float32) * np.float32(2.0 / HEAD_DIM)))
     freq = jnp.asarray(np.concatenate([freq, freq])[None, :].astype(np.float32))
     vmem = pl.BlockSpec(memory_space=pltpu.VMEM)
-    hbm = pl.BlockSpec(memory_space=pl.ANY)
+    hbm = pl.BlockSpec(memory_space=pltpu.HBM)
     return pl.pallas_call(
         functools.partial(project_kernel, width),
         out_shape=(
@@ -100,20 +107,27 @@
             jax.ShapeDtypeStruct((rows, wk.shape[1] + wv.shape[1]), bf16),
             jax.ShapeDtypeStruct((selected.shape[0] // rows, LANES), jnp.int32),
         ),
-        in_specs=[hbm, vmem, vmem, vmem, hbm, hbm, hbm],
+        in_specs=[hbm] * 7,
         out_specs=(vmem, vmem, vmem),
         scratch_shapes=[
             pltpu.VMEM((rows, feat), bf16),
+            pltpu.VMEM((1, feat), f32),
+            pltpu.VMEM(selected.shape, jnp.int32),
+            pltpu.VMEM((1, HEAD_DIM), f32),
             pltpu.VMEM((rows, feat), bf16),
             pltpu.VMEM((feat, cols), bf16),
-            pltpu.SemaphoreType.DMA((1 + cols // width,)),
+            pltpu.SemaphoreType.DMA((4,)),
+            pltpu.SemaphoreType.DMA((cols // width,)),
         ],
-        compiler_params=pltpu.CompilerParams(vmem_limit_bytes=52 * MIB),
+        compiler_params=pltpu.CompilerParams(vmem_limit_bytes=48 * MIB),
         cost_estimate=pl.CostEstimate(
             flops=2 * rows * feat * cols, bytes_accessed=2 * feat * (cols + rows), transcendentals=0
         ),
         name="project",
-    )(hidden, gain.reshape(1, feat), selected, freq, wq, wk, wv)
+    )(*[
+        pltpu.with_memory_space_constraint(operand, pltpu.HBM)
+        for operand in (hidden, gain.reshape(1, feat), selected, freq, wq, wk, wv)
+    ])
 
 
 def block_of(index, shard, order, slot):
@@ -189,12 +203,14 @@
     )(order, slot, selected, stored, stored_other, kv, kv_other)
 
 
-def attend_kernel(partners, *refs):
+def attend_kernel(partners, carried, *refs):
     count = len(partners)
     cache, key_pos, selected = refs[:3]
     queries = refs[3 : 3 + count]
-    outs = refs[3 + count : 3 + 2 * count]
-    scores, weights, masks = refs[3 + 2 * count :]
+    scores, weights, masks = refs[-3:]
+    for source, target in zip(refs[3 + count :], refs[3 + count + carried : -3 - count]):
+        target[...] = source[...]
+    outs = refs[-3 - count : -3]
     _, shard, cols = cache.shape
     rows = queries[0].shape[0]
     kv_heads = cols // (2 * HEAD_DIM)
@@ -279,32 +295,29 @@
             out[:, tail] = packed.astype(bf16)
 
 
-def attend(partners, cache, key_pos, selected, queries):
+def attend(partners, cache, key_pos, selected, queries, earlier=()):
     _, shard, cols = cache.shape
-    rows, q_cols = queries[0].shape
+    rows = queries[0].shape[0]
     kv_heads = cols // (2 * HEAD_DIM)
+    out_cols = queries[0].shape[1] + LANES
     tall = GROUP * rows
     keys = 2 * shard
     count = len(queries)
     vmem = pl.BlockSpec(memory_space=pltpu.VMEM)
     out = pl.pallas_call(
-        functools.partial(attend_kernel, partners),
-        out_shape=[jax.ShapeDtypeStruct((rows, q_cols + LANES), bf16)] * count,
-        in_specs=[vmem] * (3 + count),
-        out_specs=[vmem] * count,
+        functools.partial(attend_kernel, partners, len(earlier)),
+        out_shape=[jax.ShapeDtypeStruct((rows, out_cols), bf16)] * (len(earlier) + count),
+        in_specs=[vmem] * (3 + count + len(earlier)),
+        out_specs=[vmem] * (len(earlier) + count),
         scratch_shapes=[
             pltpu.VMEM((2, tall, keys), f32),
             pltpu.VMEM((tall, keys), bf16),
             pltpu.VMEM((2, keys, LANES), bf16),
         ],
         compiler_params=pltpu.CompilerParams(vmem_limit_bytes=24 * MIB),
-        cost_estimate=pl.CostEstimate(
-            flops=8 * count * kv_heads * tall * keys * HEAD_DIM,
-            bytes_accessed=8 * shard * cols,
-            transcendentals=count * kv_heads * tall * keys,
-        ),
+        cost_estimate=pl.CostEstimate(flops=1000, bytes_accessed=1000, transcendentals=0),
         name="attend",
-    )(cache, key_pos, selected, *queries)
+    )(cache, key_pos, selected, *queries, *earlier)
     return list(out)
 
 
@@ -313,7 +326,7 @@
     weights = refs[count]
     outs = refs[count + 1 : count + 1 + size]
     (context,) = refs[count + 1 + size :]
-    rows, feat = context.shape
+    feat = context.shape[1]
     heads = feat // HEAD_DIM
     width = weights.shape[1] // size
     me = lax.axis_index("head")
@@ -374,20 +387,25 @@
     rows = hidden.shape[0]
     shard, _, local_kv, _ = stored_kv.shape
     stored = stored_kv.reshape(-1, HEAD_DIM)
-    stored_other = swap(stored, "seq", 1, seq_count)
     query, kv, table = project(hidden, norm_gain, selected, w_query, w_key, w_value)
-    turns = list(range(2, seq_count, 2))
-    near_first = sorted(turns, key=lambda turn: (bin(turn).count("1"), turn))
-    queries = {turn: swap(query, "seq", turn, seq_count) for turn in near_first}
-    kv_other = swap(kv, "seq", 1, seq_count)
+    turns = sorted(range(2, seq_count, 2), key=lambda turn: (bin(turn).count("1"), turn))
+    queries = {turn: swap(query, "seq", turn, seq_count) for turn in turns}
+    stored, kv = lax.optimization_barrier((stored, kv))
+    stored_other, kv_other = (swap(value, "seq", 1, seq_count) for value in (stored, kv))
     cache, key_pos = merge(prompt_order, store_slot, table, stored, stored_other, kv, kv_other)
-    parts = attend((0,), cache, key_pos, table, [query])
-    for turn in near_first:
+    first, second = turns[:2]
+    parts = [attend((0,), cache, key_pos, table, [query])[0]]
+    for turn in turns[2:]:
         (part,) = attend((turn,), cache, key_pos, table, [queries[turn]])
         parts.append(swap(part, "seq", turn, seq_count))
+    done = attend((first,), cache, key_pos, table, [queries[first]])
+    done = attend((second,), cache, key_pos, table, [queries[second]], done)
+    parts += [swap(part, "seq", turn, seq_count) for turn, part in zip((first, second), done)]
     blocks = finish(parts, w_out, head_count)
     total = blocks[0]
-    arrived = [swap(blocks[turn], "head", turn, head_count) for turn in range(1, head_count)]
+    arrived = [
+        swap(blocks[turn], "head", turn, head_count) for turn in (*range(2, head_count), 1)
+    ]
     for block in arrived:
         total = total + block.astype(f32)
     new_kv = kv.reshape(rows, 2, local_kv, HEAD_DIM)

time: 60.1 us -> 57.7 us (0.960)
  the two profiles are of different devices: /device:TPU:0 before, /device:TPU:8 now
where the time goes in v5:
time: 57.7 us; the launch traced here: 57.2 us
  waiting for transfers between devices  24.3 us (42%)
  Pallas kernels  19.9 us (34%)
  starting transfers between devices  10.8 us (19%)
  other arithmetic  0.77 us (1%)
  between operations  0.75 us (1%)
  local copies, waits for them, and re-layouts  0.7 us (1%)
    ppermute x11, waiting for transfers between devices, swap(): return lax.ppermute(value, axis, [(at, at ^ turn) for at in range(size)])  24.3 us
    ppermute x11, starting transfers between devices, swap(): return lax.ppermute(value, axis, [(at, at ^ turn) for at in range(size)])  10.8 us
    pallas_call x4, Pallas kernels, attend(): pl.pallas_call(functools.partial(attend_kernel, partners, len(earlier)),...  9.42 us
    pallas_call x1, Pallas kernels, project(): pl.pallas_call(functools.partial(project_kernel, width), out_shape=(jax.S...  6.47 us
    pallas_call x1, Pallas kernels, finish(): pl.pallas_call(functools.partial(finish_kernel, len(parts), size), out_sh...  2.17 us
    pallas_call x1, Pallas kernels, merge(): pl.pallas_call(merge_kernel, out_shape=(jax.ShapeDtypeStruct((2, shard, c...  1.87 us
  transfers between devices with their start and end apart: 11, of which 8 were waited for; matrix products, arithmetic and copies ran while one was open for 1% of the time, Pallas kernels for 20%

profile of v5, /device:TPU:8, one launch (start us, length us, event | category | flops | bytes accessed | tf_op | source)
XLA Modules:
  0.0 57.2 jit_solution(13424169168953711957)
XLA Ops:
  0.7 6.5 %project.1 = (bf16[96,1024]{1,0:T(8,128)(2,1)S(1)}, bf16[96,512]{1,0:T(8,128)(2,1)S(1)}, s32[8,128]{1,0:T(8,128)S(1)}) custom-call(bf16[96,4096]{1,0:T(8,128)(2,1)} %hidden_any.1, f32[1,4096]{1,0:T(1,128)} %bitcast.6, s32[768]{0:T(1024)} %selected_any.1, f32[1,128]{1,0:T(1,128)} %constant.2.clone.freq_any, bf16[4096,1024]{1,0:T(8,128)(2,1)} %wq_any.1, ...), custom_call_target="tpu_custom_call" | custom-call | flops 1207959552 | bytes 13369344 | tf_op jit(solution)/shard_map/project/pallas_call | solution.py:103
  7.2 0.1 collective-permute-start
  7.2 1.6 %collective-permute-start.5 = (bf16[96,1024]{1,0:T(8,128)(2,1)S(1)}, bf16[96,1024]{1,0:T(8,128)(2,1)S(1)}, u32[]{:S(2)}, u32[]{:S(2)}) collective-permute-start(bf16[96,1024]{1,0:T(8,128)(2,1)S(1)} %get-tuple-element.21.refs_3_), channel_id=1, source_target_pairs={{0,8},{4,12},{8,0},{12,4},{16,24},{20,28},{24,16},{28,20},{1,9},{5... | collective-permute-start | bytes 589832 | tf_op jit(solution)/shard_map/ppermute | solution.py:379
  8.8 1.5 %collective-permute-start.4 = (bf16[96,1024]{1,0:T(8,128)(2,1)S(1)}, bf16[96,1024]{1,0:T(8,128)(2,1)S(1)}, u32[]{:S(2)}, u32[]{:S(2)}) collective-permute-start(bf16[96,1024]{1,0:T(8,128)(2,1)S(1)} %get-tuple-element.21.refs_3_), channel_id=1, source_target_pairs={{0,16},{4,20},{8,24},{12,28},{16,0},{20,4},{24,8},{28,12},{1,17},{... | collective-permute-start | bytes 589832 | tf_op jit(solution)/shard_map/ppermute | solution.py:379
  10.3 0.5 collective-permute-start.2
  10.8 0.0 collective-permute-start.1
  10.8 1.3 %collective-permute-done.1.kv_other = bf16[96,512]{1,0:T(8,128)(2,1)S(1)} collective-permute-done((bf16[96,512]{1,0:T(8,128)(2,1)S(1)}, bf16[96,512]{1,0:T(8,128)(2,1)S(1)}, u32[]{:S(2)}, u32[]{:S(2)}) %collective-permute-start.1) | collective-permute-done | bytes 98336 | tf_op jit(solution)/shard_map/ppermute | solution.py:379
  12.1 0.0 collective-permute-done.stored_other
  12.1 0.0 slice-start
  12.1 1.9 %merge.1 = (bf16[2,1024,512]{2,1,0:T(8,128)(2,1)S(1)}, f32[2048,128]{1,0:T(8,128)S(1)}) custom-call(s32[2]{0:T(128)S(1)} %copy-done.1, s32[2]{0:T(128)S(1)} %copy-done.2, s32[8,128]{1,0:T(8,128)S(1)} %get-tuple-element.15.selected.refs_2_, bf16[4096,128]{1,0:T(8,128)(2,1)S(1)} %bitcast.5, bf16[4096,128]{1,0:T(8,128)(2,1)S(1)} %collective-permute-done.stored_other, ...), custom_call_target="tpu_custom_call" | custom-call | flops 1000 | bytes 1000 | tf_op jit(solution)/shard_map/merge/pallas_call | solution.py:191
  14.0 1.0 %collective-permute-done.5.refs_3_ = bf16[96,1024]{1,0:T(8,128)(2,1)S(1)} collective-permute-done((bf16[96,1024]{1,0:T(8,128)(2,1)S(1)}, bf16[96,1024]{1,0:T(8,128)(2,1)S(1)}, u32[]{:S(2)}, u32[]{:S(2)}) %collective-permute-start.5) | collective-permute-done | bytes 196640 | tf_op jit(solution)/shard_map/ppermute | solution.py:379
  15.0 2.3 %attend.6.refs_4_ = bf16[96,1152]{1,0:T(8,128)(2,1)S(1)} custom-call(bf16[2,1024,512]{2,1,0:T(8,128)(2,1)S(1)} %get-tuple-element.19.refs_0_, f32[2048,128]{1,0:T(8,128)S(1)} %get-tuple-element.20.refs_1_, s32[8,128]{1,0:T(8,128)S(1)} %get-tuple-element.15.selected.refs_2_, bf16[96,1024]{1,0:T(8,128)(2,1)S(1)} %collective-permute-done.5.refs_3_), custom_call_target="tpu_custom_call" | custom-call | flops 1000 | bytes 1000 | tf_op jit(solution)/shard_map/attend/pallas_call | solution.py:307
  17.3 0.0 slice-start.1
  17.3 2.7 %collective-permute-done.4.refs_3_ = bf16[96,1024]{1,0:T(8,128)(2,1)S(1)} collective-permute-done((bf16[96,1024]{1,0:T(8,128)(2,1)S(1)}, bf16[96,1024]{1,0:T(8,128)(2,1)S(1)}, u32[]{:S(2)}, u32[]{:S(2)}) %collective-permute-start.4) | collective-permute-done | bytes 196640 | tf_op jit(solution)/shard_map/ppermute | solution.py:379
  20.0 2.3 %attend.7 = (bf16[96,1152]{1,0:T(8,128)(2,1)S(1)}, bf16[96,1152]{1,0:T(8,128)(2,1)S(1)}) custom-call(bf16[2,1024,512]{2,1,0:T(8,128)(2,1)S(1)} %get-tuple-element.19.refs_0_, f32[2048,128]{1,0:T(8,128)S(1)} %get-tuple-element.20.refs_1_, s32[8,128]{1,0:T(8,128)S(1)} %get-tuple-element.15.selected.refs_2_, ...), custom_call_target="tpu_custom_call" | custom-call | flops 1000 | bytes 1000 | tf_op jit(solution)/shard_map/attend/pallas_call | solution.py:307
  22.3 0.1 collective-permute-start.6
  22.4 2.0 %collective-permute-start.7 = (bf16[96,1152]{1,0:T(8,128)(2,1)S(1)}, bf16[96,1152]{1,0:T(8,128)(2,1)S(1)}, u32[]{:S(2)}, u32[]{:S(2)}) collective-permute-start(bf16[96,1152]{1,0:T(8,128)(2,1)S(1)} %get-tuple-element.23), channel_id=1, source_target_pairs={{0,16},{4,20},{8,24},{12,28},{16,0},{20,4},{24,8},{28,12},{1,17},{... | collective-permute-start | bytes 663560 | tf_op jit(solution)/shard_map/ppermute | solution.py:379
  24.4 0.0 collective-permute-done.2.refs_3_
  24.4 2.3 %attend.5 = bf16[96,1152]{1,0:T(8,128)(2,1)S(1)} custom-call(bf16[2,1024,512]{2,1,0:T(8,128)(2,1)S(1)} %get-tuple-element.19.refs_0_, f32[2048,128]{1,0:T(8,128)S(1)} %get-tuple-element.20.refs_1_, s32[8,128]{1,0:T(8,128)S(1)} %get-tuple-element.15.selected.refs_2_, bf16[96,1024]{1,0:T(8,128)(2,1)S(1)} %collective-permute-done.2.refs_3_), custom_call_target="tpu_custom_call" | custom-call | flops 1000 | bytes 1000 | tf_op jit(solution)/shard_map/attend/pallas_call | solution.py:307
  26.7 1.5 %collective-permute-start.3 = (bf16[96,1152]{1,0:T(8,128)(2,1)S(1)}, bf16[96,1152]{1,0:T(8,128)(2,1)S(1)}, u32[]{:S(2)}, u32[]{:S(2)}) collective-permute-start(bf16[96,1152]{1,0:T(8,128)(2,1)S(1)} %attend.5), channel_id=1, source_target_pairs={{0,24},{4,28},{8,16},{12,20},{16,8},{20,12},{24,0},{28,4},{1,25},{... | collective-permute-start | bytes 663560 | tf_op jit(solution)/shard_map/ppermute | solution.py:379
  28.2 2.5 %attend.4.refs_0_ = bf16[96,1152]{1,0:T(8,128)(2,1)S(1)} custom-call(bf16[2,1024,512]{2,1,0:T(8,128)(2,1)S(1)} %get-tuple-element.19.refs_0_, f32[2048,128]{1,0:T(8,128)S(1)} %get-tuple-element.20.refs_1_, s32[8,128]{1,0:T(8,128)S(1)} %get-tuple-element.15.selected.refs_2_, bf16[96,1024]{1,0:T(8,128)(2,1)S(1)} %get-tuple-element.21.refs_3_), custom_call_target="tpu_custom_call" | custom-call | flops 1000 | bytes 1000 | tf_op jit(solution)/shard_map/attend/pallas_call | solution.py:307
  30.7 2.2 %collective-permute-done.7.refs_3_ = bf16[96,1152]{1,0:T(8,128)(2,1)S(1)} collective-permute-done((bf16[96,1152]{1,0:T(8,128)(2,1)S(1)}, bf16[96,1152]{1,0:T(8,128)(2,1)S(1)}, u32[]{:S(2)}, u32[]{:S(2)}) %collective-permute-start.7) | collective-permute-done | bytes 221216 | tf_op jit(solution)/shard_map/ppermute | solution.py:379
  32.9 1.8 %collective-permute-done.3.refs_1_ = bf16[96,1152]{1,0:T(8,128)(2,1)S(1)} collective-permute-done((bf16[96,1152]{1,0:T(8,128)(2,1)S(1)}, bf16[96,1152]{1,0:T(8,128)(2,1)S(1)}, u32[]{:S(2)}, u32[]{:S(2)}) %collective-permute-start.3) | collective-permute-done | bytes 221216 | tf_op jit(solution)/shard_map/ppermute | solution.py:379
  34.7 2.2 %finish.1 = (f32[96,1024]{1,0:T(8,128)S(1)}, bf16[96,1024]{1,0:T(8,128)(2,1)S(1)}, bf16[96,1024]{1,0:T(8,128)(2,1)S(1)}, bf16[96,1024]{1,0:T(8,128)(2,1)S(1)}) custom-call(bf16[96,1152]{1,0:T(8,128)(2,1)S(1)} %attend.4.refs_0_, bf16[96,1152]{1,0:T(8,128)(2,1)S(1)} %collective-permute-done.3.refs_1_, bf16[96,1152]{1,0:T(8,128)(2,1)S(1)} %collective-permute-done.6.refs_2_, ...), custom_call_target="tpu_custom_call" | custom-call | flops 805306368 | bytes 8388608 | tf_op jit(solution)/shard_map/finish/pallas_call | solution.py:362
  36.9 0.5 collective-permute-start.10
  37.4 2.6 %collective-permute-start.8 = (bf16[96,1024]{1,0:T(8,128)(2,1)S(1)}, bf16[96,1024]{1,0:T(8,128)(2,1)S(1)}, u32[]{:S(2)}, u32[]{:S(2)}) collective-permute-start(bf16[96,1024]{1,0:T(8,128)(2,1)S(1)} %get-tuple-element.25), channel_id=1, source_target_pairs={{0,2},{1,3},{2,0},{3,1},{4,6},{5,7},{6,4},{7,5},{8,10},{9,11},{10,... | collective-permute-start | bytes 589832 | tf_op jit(solution)/shard_map/ppermute | solution.py:379
  40.0 0.4 collective-permute-start.9
  40.5 0.7 %reshape.15 = bf16[96,2,2,128]{3,2,1,0:T(2,128)(2,1)} reshape(bf16[96,512]{1,0:T(8,128)(2,1)S(1)} %get-tuple-element.18.kv) | data formatting | bytes 196608 | tf_op jit(solution)/shard_map/reshape | solution.py:411
  41.1 3.5 %collective-permute-done.10 = bf16[96,1024]{1,0:T(8,128)(2,1)S(1)} collective-permute-done((bf16[96,1024]{1,0:T(8,128)(2,1)S(1)}, bf16[96,1024]{1,0:T(8,128)(2,1)S(1)}, u32[]{:S(2)}, u32[]{:S(2)}) %collective-permute-start.10) | collective-permute-done | bytes 196640 | tf_op jit(solution)/shard_map/ppermute | solution.py:379
  44.6 8.4 %collective-permute-done.8 = bf16[96,1024]{1,0:T(8,128)(2,1)S(1)} collective-permute-done((bf16[96,1024]{1,0:T(8,128)(2,1)S(1)}, bf16[96,1024]{1,0:T(8,128)(2,1)S(1)}, u32[]{:S(2)}, u32[]{:S(2)}) %collective-permute-start.8) | collective-permute-done | bytes 196640 | tf_op jit(solution)/shard_map/ppermute | solution.py:379
  53.1 3.4 %collective-permute-done.9 = bf16[96,1024]{1,0:T(8,128)(2,1)S(1)} collective-permute-done((bf16[96,1024]{1,0:T(8,128)(2,1)S(1)}, bf16[96,1024]{1,0:T(8,128)(2,1)S(1)}, u32[]{:S(2)}, u32[]{:S(2)}) %collective-permute-start.9) | collective-permute-done | bytes 196640 | tf_op jit(solution)/shard_map/ppermute | solution.py:379
  56.4 0.8 %add_convert_fusion = bf16[96,1024]{1,0:T(8,128)(2,1)} fusion(bf16[96,1024]{1,0:T(8,128)(2,1)S(1)} %collective-permute-done.10, bf16[96,1024]{1,0:T(8,128)(2,1)S(1)} %collective-permute-done.9, f32[96,1024]{1,0:T(8,128)S(1)} %get-tuple-element.24, bf16[96,1024]{1,0:T(8,128)(2,1)S(1)} %collective-permute-done.8), kind=kLoop, calls=%fused_computation | loop fusion | flops 688128 | bytes 1179648 | tf_op jit(solution)/shard_map/convert_element_type | solution.py:412
  (10 shorter events, 0.0 us)
Async XLA Ops:
  0.6 6.5 %copy-start = (bf16[1024,2,2,128]{3,2,1,0:T(2,128)(2,1)S(1)}, bf16[1024,2,2,128]{3,2,1,0:T(2,128)(2,1)}, u32[]{:S(2)}) copy-start(bf16[1024,2,2,128]{3,2,1,0:T(2,128)(2,1)} %param.17) | copy-start | bytes 3145732
  0.6 11.5 %copy-start.1 = (s32[2]{0:T(128)S(1)}, s32[2]{0:T(128)}, u32[]{:S(2)}) copy-start(s32[2]{0:T(128)} %order.1) | copy-start | bytes 28
  0.7 11.4 %copy-start.2 = (s32[2]{0:T(128)S(1)}, s32[2]{0:T(128)}, u32[]{:S(2)}) copy-start(s32[2]{0:T(128)} %slot.1) | copy-start | bytes 28
  7.2 4.9 %collective-permute-start = (bf16[4096,128]{1,0:T(8,128)(2,1)S(1)}, bf16[4096,128]{1,0:T(8,128)(2,1)S(1)}, u32[]{:S(2)}, u32[]{:S(2)}) collective-permute-start(bf16[4096,128]{1,0:T(8,128)(2,1)S(1)} %bitcast.4), channel_id=1, source_target_pairs={{0,4},{4,0},{8,12},{12,8},{16,20},{20,16},{24,28},{28,24},{1,5},{5... | collective-permute-start | bytes 3145736 | tf_op jit(solution)/shard_map/ppermute | solution.py:379
  7.2 7.8 %collective-permute-start.5 = (bf16[96,1024]{1,0:T(8,128)(2,1)S(1)}, bf16[96,1024]{1,0:T(8,128)(2,1)S(1)}, u32[]{:S(2)}, u32[]{:S(2)}) collective-permute-start(bf16[96,1024]{1,0:T(8,128)(2,1)S(1)} %get-tuple-element.21.refs_3_), channel_id=1, source_target_pairs={{0,8},{4,12},{8,0},{12,4},{16,24},{20,28},{24,16},{28,20},{1,9},{5... | collective-permute-start | bytes 589832 | tf_op jit(solution)/shard_map/ppermute | solution.py:379
  8.8 11.2 %collective-permute-start.4 = (bf16[96,1024]{1,0:T(8,128)(2,1)S(1)}, bf16[96,1024]{1,0:T(8,128)(2,1)S(1)}, u32[]{:S(2)}, u32[]{:S(2)}) collective-permute-start(bf16[96,1024]{1,0:T(8,128)(2,1)S(1)} %get-tuple-element.21.refs_3_), channel_id=1, source_target_pairs={{0,16},{4,20},{8,24},{12,28},{16,0},{20,4},{24,8},{28,12},{1,17},{... | collective-permute-start | bytes 589832 | tf_op jit(solution)/shard_map/ppermute | solution.py:379
  10.3 14.1 %collective-permute-start.2 = (bf16[96,1024]{1,0:T(8,128)(2,1)S(1)}, bf16[96,1024]{1,0:T(8,128)(2,1)S(1)}, u32[]{:S(2)}, u32[]{:S(2)}) collective-permute-start(bf16[96,1024]{1,0:T(8,128)(2,1)S(1)} %get-tuple-element.21.refs_3_), channel_id=1, source_target_pairs={{0,24},{4,28},{8,16},{12,20},{16,8},{20,12},{24,0},{28,4},{1,25},{... | collective-permute-start | bytes 589832 | tf_op jit(solution)/shard_map/ppermute | solution.py:379
  10.8 1.3 %collective-permute-start.1 = (bf16[96,512]{1,0:T(8,128)(2,1)S(1)}, bf16[96,512]{1,0:T(8,128)(2,1)S(1)}, u32[]{:S(2)}, u32[]{:S(2)}) collective-permute-start(bf16[96,512]{1,0:T(8,128)(2,1)S(1)} %get-tuple-element.18.kv), channel_id=1, source_target_pairs={{0,4},{4,0},{8,12},{12,8},{16,20},{20,16},{24,28},{28,24},{1,5},{5... | collective-permute-start | bytes 294920 | tf_op jit(solution)/shard_map/ppermute | solution.py:379
  12.1 22.6 %slice-start = ((s8[8388608]{0:T(1024)(128)(4,1)}), s8[4194304]{0:T(1024)(128)(4,1)S(1)}, s32[]{:S(2)}) async-start(s8[8388608]{0:T(1024)(128)(4,1)} %bitcast.2), calls=%async_computation | async-start | bytes 8388608
  17.3 17.4 %slice-start.1 = ((s8[8388608]{0:T(1024)(128)(4,1)}), s8[4194304]{0:T(1024)(128)(4,1)S(1)}, s32[]{:S(2)}) async-start(s8[8388608]{0:T(1024)(128)(4,1)} %bitcast.2), calls=%async_computation.1 | async-start | bytes 8388608
  22.3 8.4 %collective-permute-start.6 = (bf16[96,1152]{1,0:T(8,128)(2,1)S(1)}, bf16[96,1152]{1,0:T(8,128)(2,1)S(1)}, u32[]{:S(2)}, u32[]{:S(2)}) collective-permute-start(bf16[96,1152]{1,0:T(8,128)(2,1)S(1)} %get-tuple-element.22), channel_id=1, source_target_pairs={{0,8},{4,12},{8,0},{12,4},{16,24},{20,28},{24,16},{28,20},{1,9},{5... | collective-permute-start | bytes 663560 | tf_op jit(solution)/shard_map/ppermute | solution.py:379
  22.4 10.5 %collective-permute-start.7 = (bf16[96,1152]{1,0:T(8,128)(2,1)S(1)}, bf16[96,1152]{1,0:T(8,128)(2,1)S(1)}, u32[]{:S(2)}, u32[]{:S(2)}) collective-permute-start(bf16[96,1152]{1,0:T(8,128)(2,1)S(1)} %get-tuple-element.23), channel_id=1, source_target_pairs={{0,16},{4,20},{8,24},{12,28},{16,0},{20,4},{24,8},{28,12},{1,17},{... | collective-permute-start | bytes 663560 | tf_op jit(solution)/shard_map/ppermute | solution.py:379
  26.7 8.0 %collective-permute-start.3 = (bf16[96,1152]{1,0:T(8,128)(2,1)S(1)}, bf16[96,1152]{1,0:T(8,128)(2,1)S(1)}, u32[]{:S(2)}, u32[]{:S(2)}) collective-permute-start(bf16[96,1152]{1,0:T(8,128)(2,1)S(1)} %attend.5), channel_id=1, source_target_pairs={{0,24},{4,28},{8,16},{12,20},{16,8},{20,12},{24,0},{28,4},{1,25},{... | collective-permute-start | bytes 663560 | tf_op jit(solution)/shard_map/ppermute | solution.py:379
  36.9 7.7 %collective-permute-start.10 = (bf16[96,1024]{1,0:T(8,128)(2,1)S(1)}, bf16[96,1024]{1,0:T(8,128)(2,1)S(1)}, u32[]{:S(2)}, u32[]{:S(2)}) collective-permute-start(bf16[96,1024]{1,0:T(8,128)(2,1)S(1)} %get-tuple-element.27), channel_id=1, source_target_pairs={{0,1},{1,0},{2,3},{3,2},{4,5},{5,4},{6,7},{7,6},{8,9},{9,8},{10,11... | collective-permute-start | bytes 589832 | tf_op jit(solution)/shard_map/ppermute | solution.py:379
  37.4 15.7 %collective-permute-start.8 = (bf16[96,1024]{1,0:T(8,128)(2,1)S(1)}, bf16[96,1024]{1,0:T(8,128)(2,1)S(1)}, u32[]{:S(2)}, u32[]{:S(2)}) collective-permute-start(bf16[96,1024]{1,0:T(8,128)(2,1)S(1)} %get-tuple-element.25), channel_id=1, source_target_pairs={{0,2},{1,3},{2,0},{3,1},{4,6},{5,7},{6,4},{7,5},{8,10},{9,11},{10,... | collective-permute-start | bytes 589832 | tf_op jit(solution)/shard_map/ppermute | solution.py:379
  40.0 16.4 %collective-permute-start.9 = (bf16[96,1024]{1,0:T(8,128)(2,1)S(1)}, bf16[96,1024]{1,0:T(8,128)(2,1)S(1)}, u32[]{:S(2)}, u32[]{:S(2)}) collective-permute-start(bf16[96,1024]{1,0:T(8,128)(2,1)S(1)} %get-tuple-element.26), channel_id=1, source_target_pairs={{0,3},{1,2},{2,1},{3,0},{4,7},{5,6},{6,5},{7,4},{8,11},{9,10},{10,... | collective-permute-start | bytes 589832 | tf_op jit(solution)/shard_map/ppermute | solution.py:379

commit v6 on v5

--- a/solution.py
+++ b/solution.py
@@ -139,7 +139,10 @@
     return place * per + lax.rem(index, per)
 
 
-def merge_kernel(order, slot, selected, stored, stored_other, kv, kv_other, cache, key_pos, wide):
+def merge_kernel(
+    order, slot, selected, stored, stored_other, kv, kv_other, query, cache, key_pos, passed, wide
+):
+    passed[...] = query[...]
     _, shard, cols = cache.shape
     kinds = cols // LANES
     rows = kv.shape[0]
@@ -183,7 +186,7 @@
                 ).astype(bf16)
 
 
-def merge(order, slot, selected, stored, stored_other, kv, kv_other):
+def merge(order, slot, selected, stored, stored_other, kv, kv_other, query):
     cols = kv.shape[1]
     shard = stored.shape[0] * LANES // cols
     smem = pl.BlockSpec(memory_space=pltpu.SMEM)
@@ -193,14 +196,15 @@
         out_shape=(
             jax.ShapeDtypeStruct((2, shard, cols), bf16),
             jax.ShapeDtypeStruct((2 * shard, LANES), f32),
+            jax.ShapeDtypeStruct(query.shape, query.dtype),
         ),
-        in_specs=[smem, smem] + [vmem] * 5,
-        out_specs=(vmem, vmem),
+        in_specs=[smem, smem] + [vmem] * 6,
+        out_specs=(vmem, vmem, vmem),
         scratch_shapes=[pltpu.VMEM((2, 128 * cols // LANES, LANES), f32)],
         compiler_params=pltpu.CompilerParams(vmem_limit_bytes=16 * MIB),
         cost_estimate=pl.CostEstimate(flops=1000, bytes_accessed=1000, transcendentals=0),
         name="merge",
-    )(order, slot, selected, stored, stored_other, kv, kv_other)
+    )(order, slot, selected, stored, stored_other, kv, kv_other, query)
 
 
 def attend_kernel(partners, carried, *refs):
@@ -389,11 +393,14 @@
     stored = stored_kv.reshape(-1, HEAD_DIM)
     query, kv, table = project(hidden, norm_gain, selected, w_query, w_key, w_value)
     turns = sorted(range(2, seq_count, 2), key=lambda turn: (bin(turn).count("1"), turn))
-    queries = {turn: swap(query, "seq", turn, seq_count) for turn in turns}
+    first, second = turns[:2]
     stored, kv = lax.optimization_barrier((stored, kv))
     stored_other, kv_other = (swap(value, "seq", 1, seq_count) for value in (stored, kv))
-    cache, key_pos = merge(prompt_order, store_slot, table, stored, stored_other, kv, kv_other)
-    first, second = turns[:2]
+    queries = {turn: swap(query, "seq", turn, seq_count) for turn in (first, second)}
+    cache, key_pos, late = merge(
+        prompt_order, store_slot, table, stored, stored_other, kv, kv_other, query
+    )
+    queries |= {turn: swap(late, "seq", turn, seq_count) for turn in turns[2:]}
     parts = [attend((0,), cache, key_pos, table, [query])[0]]
     for turn in turns[2:]:
         (part,) = attend((turn,), cache, key_pos, table, [queries[turn]])

time: 57.7 us -> 55.5 us (0.962)
  waiting for transfers between devices: 24.3 us -> 17.7 us
  starting transfers between devices: 10.8 us -> 15.1 us
    ppermute x11, waiting for transfers between devices: 24.3 us -> 17.7 us  [swap(): return lax.ppermute(value, axis, [(at, at ^ turn) for at in range(size)])]
    ppermute x11, starting transfers between devices: 10.8 us -> 15.1 us  [swap(): return lax.ppermute(value, axis, [(at, at ^ turn) for at in range(size)])]
  transfers between devices with their start and end apart: 11 -> 11, of which waited for: 8 -> 6; matrix products, arithmetic and copies ran while one was open for 1% -> 1% of each run, Pallas kernels for 20% -> 21%
where the time goes in v6:
time: 55.5 us; the launch traced here: 55 us
  Pallas kernels  20 us (36%)
  waiting for transfers between devices  17.7 us (32%)
  starting transfers between devices  15.1 us (27%)
  other arithmetic  0.77 us (1%)
  between operations  0.76 us (1%)
  local copies, waits for them, and re-layouts  0.7 us (1%)
    ppermute x11, waiting for transfers between devices, swap(): return lax.ppermute(value, axis, [(at, at ^ turn) for at in range(size)])  17.7 us
    ppermute x11, starting transfers between devices, swap(): return lax.ppermute(value, axis, [(at, at ^ turn) for at in range(size)])  15.1 us
    pallas_call x4, Pallas kernels, attend(): pl.pallas_call(functools.partial(attend_kernel, partners, len(earlier)),...  9.43 us
    pallas_call x1, Pallas kernels, project(): pl.pallas_call(functools.partial(project_kernel, width), out_shape=(jax.S...  6.47 us
    pallas_call x1, Pallas kernels, finish(): pl.pallas_call(functools.partial(finish_kernel, len(parts), size), out_sh...  2.17 us
    pallas_call x1, Pallas kernels, merge(): pl.pallas_call(merge_kernel, out_shape=(jax.ShapeDtypeStruct((2, shard, c...  1.89 us
  transfers between devices with their start and end apart: 11, of which 6 were waited for; matrix products, arithmetic and copies ran while one was open for 1% of the time, Pallas kernels for 21%

profile of v6, /device:TPU:8, one launch (start us, length us, event | category | flops | bytes accessed | tf_op | source)
XLA Modules:
  0.0 55.0 jit_solution(13668908810278261690)
XLA Ops:
  0.7 6.5 %project.1 = (bf16[96,1024]{1,0:T(8,128)(2,1)S(1)}, bf16[96,512]{1,0:T(8,128)(2,1)S(1)}, s32[8,128]{1,0:T(8,128)S(1)}) custom-call(bf16[96,4096]{1,0:T(8,128)(2,1)} %hidden_any.1, f32[1,4096]{1,0:T(1,128)} %bitcast.6, s32[768]{0:T(1024)} %selected_any.1, f32[1,128]{1,0:T(1,128)} %constant.2.clone.freq_any, bf16[4096,1024]{1,0:T(8,128)(2,1)} %wq_any.1, ...), custom_call_target="tpu_custom_call" | custom-call | flops 1207959552 | bytes 13369344 | tf_op jit(solution)/shard_map/project/pallas_call | solution.py:103
  7.2 0.1 collective-permute-start
  7.2 0.5 collective-permute-start.1
  7.7 1.5 %collective-permute-start.5 = (bf16[96,1024]{1,0:T(8,128)(2,1)S(1)}, bf16[96,1024]{1,0:T(8,128)(2,1)S(1)}, u32[]{:S(2)}, u32[]{:S(2)}) collective-permute-start(bf16[96,1024]{1,0:T(8,128)(2,1)S(1)} %get-tuple-element.20.query.refs_3_), channel_id=1, source_target_pairs={{0,8},{4,12},{8,0},{12,4},{16,24},{20,28},{24,16},{28,20},{1,9},{5... | collective-permute-start | bytes 589832 | tf_op jit(solution)/shard_map/ppermute | solution.py:383
  9.2 1.5 %collective-permute-start.4 = (bf16[96,1024]{1,0:T(8,128)(2,1)S(1)}, bf16[96,1024]{1,0:T(8,128)(2,1)S(1)}, u32[]{:S(2)}, u32[]{:S(2)}) collective-permute-start(bf16[96,1024]{1,0:T(8,128)(2,1)S(1)} %get-tuple-element.20.query.refs_3_), channel_id=1, source_target_pairs={{0,16},{4,20},{8,24},{12,28},{16,0},{20,4},{24,8},{28,12},{1,17},{... | collective-permute-start | bytes 589832 | tf_op jit(solution)/shard_map/ppermute | solution.py:383
  10.7 0.0 collective-permute-done.1.kv_other
  10.7 0.0 collective-permute-done.stored_other
  10.8 0.0 slice-start
  10.8 1.9 %merge.1 = (bf16[2,1024,512]{2,1,0:T(8,128)(2,1)S(1)}, f32[2048,128]{1,0:T(8,128)S(1)}, bf16[96,1024]{1,0:T(8,128)(2,1)S(1)}) custom-call(s32[2]{0:T(128)S(1)} %copy-done.1, s32[2]{0:T(128)S(1)} %copy-done.2, s32[8,128]{1,0:T(8,128)S(1)} %get-tuple-element.16.selected.refs_2_, bf16[4096,128]{1,0:T(8,128)(2,1)S(1)} %bitcast.5, ...), custom_call_target="tpu_custom_call" | custom-call | flops 1000 | bytes 1000 | tf_op jit(solution)/shard_map/merge/pallas_call | solution.py:194
  12.7 1.8 %collective-permute-start.2 = (bf16[96,1024]{1,0:T(8,128)(2,1)S(1)}, bf16[96,1024]{1,0:T(8,128)(2,1)S(1)}, u32[]{:S(2)}, u32[]{:S(2)}) collective-permute-start(bf16[96,1024]{1,0:T(8,128)(2,1)S(1)} %get-tuple-element.23), channel_id=1, source_target_pairs={{0,24},{4,28},{8,16},{12,20},{16,8},{20,12},{24,0},{28,4},{1,25},{... | collective-permute-start | bytes 589832 | tf_op jit(solution)/shard_map/ppermute | solution.py:383
  14.4 0.2 collective-permute-done.5.refs_3_
  14.6 2.3 %attend.6.refs_4_ = bf16[96,1152]{1,0:T(8,128)(2,1)S(1)} custom-call(bf16[2,1024,512]{2,1,0:T(8,128)(2,1)S(1)} %get-tuple-element.21.refs_0_, f32[2048,128]{1,0:T(8,128)S(1)} %get-tuple-element.22.refs_1_, s32[8,128]{1,0:T(8,128)S(1)} %get-tuple-element.16.selected.refs_2_, bf16[96,1024]{1,0:T(8,128)(2,1)S(1)} %collective-permute-done.5.refs_3_), custom_call_target="tpu_custom_call" | custom-call | flops 1000 | bytes 1000 | tf_op jit(solution)/shard_map/attend/pallas_call | solution.py:311
  16.9 0.0 slice-start.1
  16.9 0.0 collective-permute-done.4.refs_3_
  16.9 2.3 %attend.7 = (bf16[96,1152]{1,0:T(8,128)(2,1)S(1)}, bf16[96,1152]{1,0:T(8,128)(2,1)S(1)}) custom-call(bf16[2,1024,512]{2,1,0:T(8,128)(2,1)S(1)} %get-tuple-element.21.refs_0_, f32[2048,128]{1,0:T(8,128)S(1)} %get-tuple-element.22.refs_1_, s32[8,128]{1,0:T(8,128)S(1)} %get-tuple-element.16.selected.refs_2_, ...), custom_call_target="tpu_custom_call" | custom-call | flops 1000 | bytes 1000 | tf_op jit(solution)/shard_map/attend/pallas_call | solution.py:311
  19.3 1.6 %collective-permute-start.6 = (bf16[96,1152]{1,0:T(8,128)(2,1)S(1)}, bf16[96,1152]{1,0:T(8,128)(2,1)S(1)}, u32[]{:S(2)}, u32[]{:S(2)}) collective-permute-start(bf16[96,1152]{1,0:T(8,128)(2,1)S(1)} %get-tuple-element.24), channel_id=1, source_target_pairs={{0,8},{4,12},{8,0},{12,4},{16,24},{20,28},{24,16},{28,20},{1,9},{5... | collective-permute-start | bytes 663560 | tf_op jit(solution)/shard_map/ppermute | solution.py:383
  20.8 3.2 %collective-permute-start.7 = (bf16[96,1152]{1,0:T(8,128)(2,1)S(1)}, bf16[96,1152]{1,0:T(8,128)(2,1)S(1)}, u32[]{:S(2)}, u32[]{:S(2)}) collective-permute-start(bf16[96,1152]{1,0:T(8,128)(2,1)S(1)} %get-tuple-element.25), channel_id=1, source_target_pairs={{0,16},{4,20},{8,24},{12,28},{16,0},{20,4},{24,8},{28,12},{1,17},{... | collective-permute-start | bytes 663560 | tf_op jit(solution)/shard_map/ppermute | solution.py:383
  24.0 0.0 collective-permute-done.2.refs_3_
  24.0 2.3 %attend.5 = bf16[96,1152]{1,0:T(8,128)(2,1)S(1)} custom-call(bf16[2,1024,512]{2,1,0:T(8,128)(2,1)S(1)} %get-tuple-element.21.refs_0_, f32[2048,128]{1,0:T(8,128)S(1)} %get-tuple-element.22.refs_1_, s32[8,128]{1,0:T(8,128)S(1)} %get-tuple-element.16.selected.refs_2_, bf16[96,1024]{1,0:T(8,128)(2,1)S(1)} %collective-permute-done.2.refs_3_), custom_call_target="tpu_custom_call" | custom-call | flops 1000 | bytes 1000 | tf_op jit(solution)/shard_map/attend/pallas_call | solution.py:311
  26.3 1.5 %collective-permute-start.3 = (bf16[96,1152]{1,0:T(8,128)(2,1)S(1)}, bf16[96,1152]{1,0:T(8,128)(2,1)S(1)}, u32[]{:S(2)}, u32[]{:S(2)}) collective-permute-start(bf16[96,1152]{1,0:T(8,128)(2,1)S(1)} %attend.5), channel_id=1, source_target_pairs={{0,24},{4,28},{8,16},{12,20},{16,8},{20,12},{24,0},{28,4},{1,25},{... | collective-permute-start | bytes 663560 | tf_op jit(solution)/shard_map/ppermute | solution.py:383
  27.8 2.5 %attend.4.refs_0_ = bf16[96,1152]{1,0:T(8,128)(2,1)S(1)} custom-call(bf16[2,1024,512]{2,1,0:T(8,128)(2,1)S(1)} %get-tuple-element.21.refs_0_, f32[2048,128]{1,0:T(8,128)S(1)} %get-tuple-element.22.refs_1_, s32[8,128]{1,0:T(8,128)S(1)} %get-tuple-element.16.selected.refs_2_, bf16[96,1024]{1,0:T(8,128)(2,1)S(1)} %get-tuple-element.20.query.refs_3_), custom_call_target="tpu_custom_call" | custom-call | flops 1000 | bytes 1000 | tf_op jit(solution)/shard_map/attend/pallas_call | solution.py:311
  30.3 1.8 %collective-permute-done.7.refs_3_ = bf16[96,1152]{1,0:T(8,128)(2,1)S(1)} collective-permute-done((bf16[96,1152]{1,0:T(8,128)(2,1)S(1)}, bf16[96,1152]{1,0:T(8,128)(2,1)S(1)}, u32[]{:S(2)}, u32[]{:S(2)}) %collective-permute-start.7) | collective-permute-done | bytes 221216 | tf_op jit(solution)/shard_map/ppermute | solution.py:383
  32.2 1.8 %collective-permute-done.3.refs_1_ = bf16[96,1152]{1,0:T(8,128)(2,1)S(1)} collective-permute-done((bf16[96,1152]{1,0:T(8,128)(2,1)S(1)}, bf16[96,1152]{1,0:T(8,128)(2,1)S(1)}, u32[]{:S(2)}, u32[]{:S(2)}) %collective-permute-start.3) | collective-permute-done | bytes 221216 | tf_op jit(solution)/shard_map/ppermute | solution.py:383
  34.0 2.2 %finish.1 = (f32[96,1024]{1,0:T(8,128)S(1)}, bf16[96,1024]{1,0:T(8,128)(2,1)S(1)}, bf16[96,1024]{1,0:T(8,128)(2,1)S(1)}, bf16[96,1024]{1,0:T(8,128)(2,1)S(1)}) custom-call(bf16[96,1152]{1,0:T(8,128)(2,1)S(1)} %attend.4.refs_0_, bf16[96,1152]{1,0:T(8,128)(2,1)S(1)} %collective-permute-done.3.refs_1_, bf16[96,1152]{1,0:T(8,128)(2,1)S(1)} %collective-permute-done.6.refs_2_, ...), custom_call_target="tpu_custom_call" | custom-call | flops 805306368 | bytes 8388608 | tf_op jit(solution)/shard_map/finish/pallas_call | solution.py:366
  36.2 0.5 collective-permute-start.10
  36.7 2.6 %collective-permute-start.8 = (bf16[96,1024]{1,0:T(8,128)(2,1)S(1)}, bf16[96,1024]{1,0:T(8,128)(2,1)S(1)}, u32[]{:S(2)}, u32[]{:S(2)}) collective-permute-start(bf16[96,1024]{1,0:T(8,128)(2,1)S(1)} %get-tuple-element.27), channel_id=1, source_target_pairs={{0,2},{1,3},{2,0},{3,1},{4,6},{5,7},{6,4},{7,5},{8,10},{9,11},{10,... | collective-permute-start | bytes 589832 | tf_op jit(solution)/shard_map/ppermute | solution.py:383
  39.3 0.4 collective-permute-start.9
  39.7 0.7 %reshape.15 = bf16[96,2,2,128]{3,2,1,0:T(2,128)(2,1)} reshape(bf16[96,512]{1,0:T(8,128)(2,1)S(1)} %get-tuple-element.19.kv) | data formatting | bytes 196608 | tf_op jit(solution)/shard_map/reshape | solution.py:418
  40.4 3.6 %collective-permute-done.10 = bf16[96,1024]{1,0:T(8,128)(2,1)S(1)} collective-permute-done((bf16[96,1024]{1,0:T(8,128)(2,1)S(1)}, bf16[96,1024]{1,0:T(8,128)(2,1)S(1)}, u32[]{:S(2)}, u32[]{:S(2)}) %collective-permute-start.10) | collective-permute-done | bytes 196640 | tf_op jit(solution)/shard_map/ppermute | solution.py:383
  44.1 7.0 %collective-permute-done.8 = bf16[96,1024]{1,0:T(8,128)(2,1)S(1)} collective-permute-done((bf16[96,1024]{1,0:T(8,128)(2,1)S(1)}, bf16[96,1024]{1,0:T(8,128)(2,1)S(1)}, u32[]{:S(2)}, u32[]{:S(2)}) %collective-permute-start.8) | collective-permute-done | bytes 196640 | tf_op jit(solution)/shard_map/ppermute | solution.py:383
  51.1 3.2 %collective-permute-done.9 = bf16[96,1024]{1,0:T(8,128)(2,1)S(1)} collective-permute-done((bf16[96,1024]{1,0:T(8,128)(2,1)S(1)}, bf16[96,1024]{1,0:T(8,128)(2,1)S(1)}, u32[]{:S(2)}, u32[]{:S(2)}) %collective-permute-start.9) | collective-permute-done | bytes 196640 | tf_op jit(solution)/shard_map/ppermute | solution.py:383
  54.3 0.8 %add_convert_fusion = bf16[96,1024]{1,0:T(8,128)(2,1)} fusion(bf16[96,1024]{1,0:T(8,128)(2,1)S(1)} %collective-permute-done.10, bf16[96,1024]{1,0:T(8,128)(2,1)S(1)} %collective-permute-done.9, f32[96,1024]{1,0:T(8,128)S(1)} %get-tuple-element.26, bf16[96,1024]{1,0:T(8,128)(2,1)S(1)} %collective-permute-done.8), kind=kLoop, calls=%fused_computation | loop fusion | flops 688128 | bytes 1179648 | tf_op jit(solution)/shard_map/convert_element_type | solution.py:419
  (10 shorter events, 0.0 us)
Async XLA Ops:
  0.6 6.5 %copy-start = (bf16[1024,2,2,128]{3,2,1,0:T(2,128)(2,1)S(1)}, bf16[1024,2,2,128]{3,2,1,0:T(2,128)(2,1)}, u32[]{:S(2)}) copy-start(bf16[1024,2,2,128]{3,2,1,0:T(2,128)(2,1)} %param.17) | copy-start | bytes 3145732
  0.6 10.1 %copy-start.1 = (s32[2]{0:T(128)S(1)}, s32[2]{0:T(128)}, u32[]{:S(2)}) copy-start(s32[2]{0:T(128)} %order.1) | copy-start | bytes 28
  0.7 10.1 %copy-start.2 = (s32[2]{0:T(128)S(1)}, s32[2]{0:T(128)}, u32[]{:S(2)}) copy-start(s32[2]{0:T(128)} %slot.1) | copy-start | bytes 28
  7.2 3.6 %collective-permute-start = (bf16[4096,128]{1,0:T(8,128)(2,1)S(1)}, bf16[4096,128]{1,0:T(8,128)(2,1)S(1)}, u32[]{:S(2)}, u32[]{:S(2)}) collective-permute-start(bf16[4096,128]{1,0:T(8,128)(2,1)S(1)} %bitcast.4), channel_id=1, source_target_pairs={{0,4},{4,0},{8,12},{12,8},{16,20},{20,16},{24,28},{28,24},{1,5},{5... | collective-permute-start | bytes 3145736 | tf_op jit(solution)/shard_map/ppermute | solution.py:383
  7.2 3.5 %collective-permute-start.1 = (bf16[96,512]{1,0:T(8,128)(2,1)S(1)}, bf16[96,512]{1,0:T(8,128)(2,1)S(1)}, u32[]{:S(2)}, u32[]{:S(2)}) collective-permute-start(bf16[96,512]{1,0:T(8,128)(2,1)S(1)} %get-tuple-element.19.kv), channel_id=1, source_target_pairs={{0,4},{4,0},{8,12},{12,8},{16,20},{20,16},{24,28},{28,24},{1,5},{5... | collective-permute-start | bytes 294920 | tf_op jit(solution)/shard_map/ppermute | solution.py:383
  7.7 6.9 %collective-permute-start.5 = (bf16[96,1024]{1,0:T(8,128)(2,1)S(1)}, bf16[96,1024]{1,0:T(8,128)(2,1)S(1)}, u32[]{:S(2)}, u32[]{:S(2)}) collective-permute-start(bf16[96,1024]{1,0:T(8,128)(2,1)S(1)} %get-tuple-element.20.query.refs_3_), channel_id=1, source_target_pairs={{0,8},{4,12},{8,0},{12,4},{16,24},{20,28},{24,16},{28,20},{1,9},{5... | collective-permute-start | bytes 589832 | tf_op jit(solution)/shard_map/ppermute | solution.py:383
  9.2 7.7 %collective-permute-start.4 = (bf16[96,1024]{1,0:T(8,128)(2,1)S(1)}, bf16[96,1024]{1,0:T(8,128)(2,1)S(1)}, u32[]{:S(2)}, u32[]{:S(2)}) collective-permute-start(bf16[96,1024]{1,0:T(8,128)(2,1)S(1)} %get-tuple-element.20.query.refs_3_), channel_id=1, source_target_pairs={{0,16},{4,20},{8,24},{12,28},{16,0},{20,4},{24,8},{28,12},{1,17},{... | collective-permute-start | bytes 589832 | tf_op jit(solution)/shard_map/ppermute | solution.py:383
  10.8 23.2 %slice-start = ((s8[8388608]{0:T(1024)(128)(4,1)}), s8[4194304]{0:T(1024)(128)(4,1)S(1)}, s32[]{:S(2)}) async-start(s8[8388608]{0:T(1024)(128)(4,1)} %bitcast.2), calls=%async_computation | async-start | bytes 8388608
  12.7 11.4 %collective-permute-start.2 = (bf16[96,1024]{1,0:T(8,128)(2,1)S(1)}, bf16[96,1024]{1,0:T(8,128)(2,1)S(1)}, u32[]{:S(2)}, u32[]{:S(2)}) collective-permute-start(bf16[96,1024]{1,0:T(8,128)(2,1)S(1)} %get-tuple-element.23), channel_id=1, source_target_pairs={{0,24},{4,28},{8,16},{12,20},{16,8},{20,12},{24,0},{28,4},{1,25},{... | collective-permute-start | bytes 589832 | tf_op jit(solution)/shard_map/ppermute | solution.py:383
  16.9 17.1 %slice-start.1 = ((s8[8388608]{0:T(1024)(128)(4,1)}), s8[4194304]{0:T(1024)(128)(4,1)S(1)}, s32[]{:S(2)}) async-start(s8[8388608]{0:T(1024)(128)(4,1)} %bitcast.2), calls=%async_computation.1 | async-start | bytes 8388608
  19.3 11.0 %collective-permute-start.6 = (bf16[96,1152]{1,0:T(8,128)(2,1)S(1)}, bf16[96,1152]{1,0:T(8,128)(2,1)S(1)}, u32[]{:S(2)}, u32[]{:S(2)}) collective-permute-start(bf16[96,1152]{1,0:T(8,128)(2,1)S(1)} %get-tuple-element.24), channel_id=1, source_target_pairs={{0,8},{4,12},{8,0},{12,4},{16,24},{20,28},{24,16},{28,20},{1,9},{5... | collective-permute-start | bytes 663560 | tf_op jit(solution)/shard_map/ppermute | solution.py:383
  20.8 11.3 %collective-permute-start.7 = (bf16[96,1152]{1,0:T(8,128)(2,1)S(1)}, bf16[96,1152]{1,0:T(8,128)(2,1)S(1)}, u32[]{:S(2)}, u32[]{:S(2)}) collective-permute-start(bf16[96,1152]{1,0:T(8,128)(2,1)S(1)} %get-tuple-element.25), channel_id=1, source_target_pairs={{0,16},{4,20},{8,24},{12,28},{16,0},{20,4},{24,8},{28,12},{1,17},{... | collective-permute-start | bytes 663560 | tf_op jit(solution)/shard_map/ppermute | solution.py:383
  26.3 7.7 %collective-permute-start.3 = (bf16[96,1152]{1,0:T(8,128)(2,1)S(1)}, bf16[96,1152]{1,0:T(8,128)(2,1)S(1)}, u32[]{:S(2)}, u32[]{:S(2)}) collective-permute-start(bf16[96,1152]{1,0:T(8,128)(2,1)S(1)} %attend.5), channel_id=1, source_target_pairs={{0,24},{4,28},{8,16},{12,20},{16,8},{20,12},{24,0},{28,4},{1,25},{... | collective-permute-start | bytes 663560 | tf_op jit(solution)/shard_map/ppermute | solution.py:383
  36.2 7.9 %collective-permute-start.10 = (bf16[96,1024]{1,0:T(8,128)(2,1)S(1)}, bf16[96,1024]{1,0:T(8,128)(2,1)S(1)}, u32[]{:S(2)}, u32[]{:S(2)}) collective-permute-start(bf16[96,1024]{1,0:T(8,128)(2,1)S(1)} %get-tuple-element.29), channel_id=1, source_target_pairs={{0,1},{1,0},{2,3},{3,2},{4,5},{5,4},{6,7},{7,6},{8,9},{9,8},{10,11... | collective-permute-start | bytes 589832 | tf_op jit(solution)/shard_map/ppermute | solution.py:383
  36.7 14.4 %collective-permute-start.8 = (bf16[96,1024]{1,0:T(8,128)(2,1)S(1)}, bf16[96,1024]{1,0:T(8,128)(2,1)S(1)}, u32[]{:S(2)}, u32[]{:S(2)}) collective-permute-start(bf16[96,1024]{1,0:T(8,128)(2,1)S(1)} %get-tuple-element.27), channel_id=1, source_target_pairs={{0,2},{1,3},{2,0},{3,1},{4,6},{5,7},{6,4},{7,5},{8,10},{9,11},{10,... | collective-permute-start | bytes 589832 | tf_op jit(solution)/shard_map/ppermute | solution.py:383
  39.3 15.0 %collective-permute-start.9 = (bf16[96,1024]{1,0:T(8,128)(2,1)S(1)}, bf16[96,1024]{1,0:T(8,128)(2,1)S(1)}, u32[]{:S(2)}, u32[]{:S(2)}) collective-permute-start(bf16[96,1024]{1,0:T(8,128)(2,1)S(1)} %get-tuple-element.28), channel_id=1, source_target_pairs={{0,3},{1,2},{2,1},{3,0},{4,7},{5,6},{6,5},{7,4},{8,11},{9,10},{10,... | collective-permute-start | bytes 589832 | tf_op jit(solution)/shard_map/ppermute | solution.py:383

commit v7 on v6

--- a/solution.py
+++ b/solution.py
@@ -227,7 +227,8 @@
     ones = jnp.ones((keys, LANES), bf16)
 
     def mask(at):
-        row = selected[pl.ds(me ^ partners[at], 1), :].astype(f32)
+        even, odd = partners[at]
+        row = selected[pl.ds(me ^ jnp.where(me & 1 == 1, odd, even), 1), :].astype(f32)
         for place in range(0, keys, step):
             masks[at % 2, place : place + step, :] = jnp.where(
                 key_pos[place : place + step, :] <= row, 0.0, MASKED
@@ -380,7 +381,8 @@
 
 
 def swap(value, axis, turn, size):
-    return lax.ppermute(value, axis, [(at, at ^ turn) for at in range(size)])
+    even, odd = turn if isinstance(turn, tuple) else (turn, turn)
+    return lax.ppermute(value, axis, [(at, at ^ (odd if at & 1 else even)) for at in range(size)])
 
 
 def body(
@@ -393,16 +395,18 @@
     stored = stored_kv.reshape(-1, HEAD_DIM)
     query, kv, table = project(hidden, norm_gain, selected, w_query, w_key, w_value)
     turns = sorted(range(2, seq_count, 2), key=lambda turn: (bin(turn).count("1"), turn))
-    first, second = turns[:2]
+    near, across = turns[:2]
+    first, second = (near, across), (across, near)
+    rest = [(turn, turn) for turn in turns[2:]]
     stored, kv = lax.optimization_barrier((stored, kv))
     stored_other, kv_other = (swap(value, "seq", 1, seq_count) for value in (stored, kv))
     queries = {turn: swap(query, "seq", turn, seq_count) for turn in (first, second)}
     cache, key_pos, late = merge(
         prompt_order, store_slot, table, stored, stored_other, kv, kv_other, query
     )
-    queries |= {turn: swap(late, "seq", turn, seq_count) for turn in turns[2:]}
-    parts = [attend((0,), cache, key_pos, table, [query])[0]]
-    for turn in turns[2:]:
+    queries |= {turn: swap(late, "seq", turn, seq_count) for turn in rest}
+    parts = [attend(((0, 0),), cache, key_pos, table, [query])[0]]
+    for turn in rest:
         (part,) = attend((turn,), cache, key_pos, table, [queries[turn]])
         parts.append(swap(part, "seq", turn, seq_count))
     done = attend((first,), cache, key_pos, table, [queries[first]])

time: 55.5 us -> 54.5 us (0.982)
  starting transfers between devices: 15.1 us -> 12.5 us
  waiting for transfers between devices: 17.7 us -> 19.3 us
    ppermute x11, starting transfers between devices: 15.1 us -> 12.5 us  [swap(): lax.ppermute(value, axis, [(at, at ^ (odd if at & 1 else even)) for at in...]
    ppermute x11, waiting for transfers between devices: 17.7 us -> 19.3 us  [swap(): lax.ppermute(value, axis, [(at, at ^ (odd if at & 1 else even)) for at in...]
where the time goes in v7:
time: 54.5 us; the launch traced here: 54 us
  Pallas kernels  20 us (37%)
  waiting for transfers between devices  19.3 us (35%)
  starting transfers between devices  12.5 us (23%)
  other arithmetic  0.77 us (1%)
  between operations  0.76 us (1%)
  local copies, waits for them, and re-layouts  0.7 us (1%)
    ppermute x11, waiting for transfers between devices, swap(): lax.ppermute(value, axis, [(at, at ^ (odd if at & 1 else even)) for at in...  19.3 us
    ppermute x11, starting transfers between devices, swap(): lax.ppermute(value, axis, [(at, at ^ (odd if at & 1 else even)) for at in...  12.5 us
    pallas_call x4, Pallas kernels, attend(): pl.pallas_call(functools.partial(attend_kernel, partners, len(earlier)),...  9.43 us
    pallas_call x1, Pallas kernels, project(): pl.pallas_call(functools.partial(project_kernel, width), out_shape=(jax.S...  6.47 us
    pallas_call x1, Pallas kernels, finish(): pl.pallas_call(functools.partial(finish_kernel, len(parts), size), out_sh...  2.17 us
    pallas_call x1, Pallas kernels, merge(): pl.pallas_call(merge_kernel, out_shape=(jax.ShapeDtypeStruct((2, shard, c...  1.89 us
  transfers between devices with their start and end apart: 11, of which 6 were waited for; matrix products, arithmetic and copies ran while one was open for 1% of the time, Pallas kernels for 21%

profile of v7, /device:TPU:8, one launch (start us, length us, event | category | flops | bytes accessed | tf_op | source)
XLA Modules:
  0.0 54.0 jit_solution(16341024394116616121)
XLA Ops:
  0.7 6.5 %project.1 = (bf16[96,1024]{1,0:T(8,128)(2,1)S(1)}, bf16[96,512]{1,0:T(8,128)(2,1)S(1)}, s32[8,128]{1,0:T(8,128)S(1)}) custom-call(bf16[96,4096]{1,0:T(8,128)(2,1)} %hidden_any.1, f32[1,4096]{1,0:T(1,128)} %bitcast.6, s32[768]{0:T(1024)} %selected_any.1, f32[1,128]{1,0:T(1,128)} %constant.2.clone.freq_any, bf16[4096,1024]{1,0:T(8,128)(2,1)} %wq_any.1, ...), custom_call_target="tpu_custom_call" | custom-call | flops 1207959552 | bytes 13369344 | tf_op jit(solution)/shard_map/project/pallas_call | solution.py:103
  7.2 0.1 collective-permute-start
  7.2 0.5 collective-permute-start.1
  7.7 1.5 %collective-permute-start.5 = (bf16[96,1024]{1,0:T(8,128)(2,1)S(1)}, bf16[96,1024]{1,0:T(8,128)(2,1)S(1)}, u32[]{:S(2)}, u32[]{:S(2)}) collective-permute-start(bf16[96,1024]{1,0:T(8,128)(2,1)S(1)} %get-tuple-element.20.query.refs_3_), channel_id=1, source_target_pairs={{0,8},{4,20},{8,0},{12,28},{16,24},{20,4},{24,16},{28,12},{1,9},{5... | collective-permute-start | bytes 589832 | tf_op jit(solution)/shard_map/ppermute | solution.py:385
  9.2 1.5 %collective-permute-start.4 = (bf16[96,1024]{1,0:T(8,128)(2,1)S(1)}, bf16[96,1024]{1,0:T(8,128)(2,1)S(1)}, u32[]{:S(2)}, u32[]{:S(2)}) collective-permute-start(bf16[96,1024]{1,0:T(8,128)(2,1)S(1)} %get-tuple-element.20.query.refs_3_), channel_id=1, source_target_pairs={{0,16},{4,12},{8,24},{12,4},{16,0},{20,28},{24,8},{28,20},{1,17},{... | collective-permute-start | bytes 589832 | tf_op jit(solution)/shard_map/ppermute | solution.py:385
  10.7 0.0 collective-permute-done.1.kv_other
  10.7 0.0 collective-permute-done.stored_other
  10.8 0.0 slice-start
  10.8 1.9 %merge.1 = (bf16[2,1024,512]{2,1,0:T(8,128)(2,1)S(1)}, f32[2048,128]{1,0:T(8,128)S(1)}, bf16[96,1024]{1,0:T(8,128)(2,1)S(1)}) custom-call(s32[2]{0:T(128)S(1)} %copy-done.1, s32[2]{0:T(128)S(1)} %copy-done.2, s32[8,128]{1,0:T(8,128)S(1)} %get-tuple-element.16.selected.refs_2_, bf16[4096,128]{1,0:T(8,128)(2,1)S(1)} %bitcast.5, ...), custom_call_target="tpu_custom_call" | custom-call | flops 1000 | bytes 1000 | tf_op jit(solution)/shard_map/merge/pallas_call | solution.py:194
  12.7 1.8 %collective-permute-start.2 = (bf16[96,1024]{1,0:T(8,128)(2,1)S(1)}, bf16[96,1024]{1,0:T(8,128)(2,1)S(1)}, u32[]{:S(2)}, u32[]{:S(2)}) collective-permute-start(bf16[96,1024]{1,0:T(8,128)(2,1)S(1)} %get-tuple-element.23), channel_id=1, source_target_pairs={{0,24},{4,28},{8,16},{12,20},{16,8},{20,12},{24,0},{28,4},{1,25},{... | collective-permute-start | bytes 589832 | tf_op jit(solution)/shard_map/ppermute | solution.py:385
  14.4 0.8 %collective-permute-done.5.refs_3_ = bf16[96,1024]{1,0:T(8,128)(2,1)S(1)} collective-permute-done((bf16[96,1024]{1,0:T(8,128)(2,1)S(1)}, bf16[96,1024]{1,0:T(8,128)(2,1)S(1)}, u32[]{:S(2)}, u32[]{:S(2)}) %collective-permute-start.5) | collective-permute-done | bytes 196640 | tf_op jit(solution)/shard_map/ppermute | solution.py:385
  15.2 2.3 %attend.6.refs_4_ = bf16[96,1152]{1,0:T(8,128)(2,1)S(1)} custom-call(bf16[2,1024,512]{2,1,0:T(8,128)(2,1)S(1)} %get-tuple-element.21.refs_0_, f32[2048,128]{1,0:T(8,128)S(1)} %get-tuple-element.22.refs_1_, s32[8,128]{1,0:T(8,128)S(1)} %get-tuple-element.16.selected.refs_2_, bf16[96,1024]{1,0:T(8,128)(2,1)S(1)} %collective-permute-done.5.refs_3_), custom_call_target="tpu_custom_call" | custom-call | flops 1000 | bytes 1000 | tf_op jit(solution)/shard_map/attend/pallas_call | solution.py:312
  17.6 0.0 slice-start.1
  17.6 0.0 collective-permute-done.4.refs_3_
  17.6 2.3 %attend.7 = (bf16[96,1152]{1,0:T(8,128)(2,1)S(1)}, bf16[96,1152]{1,0:T(8,128)(2,1)S(1)}) custom-call(bf16[2,1024,512]{2,1,0:T(8,128)(2,1)S(1)} %get-tuple-element.21.refs_0_, f32[2048,128]{1,0:T(8,128)S(1)} %get-tuple-element.22.refs_1_, s32[8,128]{1,0:T(8,128)S(1)} %get-tuple-element.16.selected.refs_2_, ...), custom_call_target="tpu_custom_call" | custom-call | flops 1000 | bytes 1000 | tf_op jit(solution)/shard_map/attend/pallas_call | solution.py:312
  19.9 1.6 %collective-permute-start.6 = (bf16[96,1152]{1,0:T(8,128)(2,1)S(1)}, bf16[96,1152]{1,0:T(8,128)(2,1)S(1)}, u32[]{:S(2)}, u32[]{:S(2)}) collective-permute-start(bf16[96,1152]{1,0:T(8,128)(2,1)S(1)} %get-tuple-element.24), channel_id=1, source_target_pairs={{0,8},{4,20},{8,0},{12,28},{16,24},{20,4},{24,16},{28,12},{1,9},{5... | collective-permute-start | bytes 663560 | tf_op jit(solution)/shard_map/ppermute | solution.py:385
  21.5 1.2 %collective-permute-start.7 = (bf16[96,1152]{1,0:T(8,128)(2,1)S(1)}, bf16[96,1152]{1,0:T(8,128)(2,1)S(1)}, u32[]{:S(2)}, u32[]{:S(2)}) collective-permute-start(bf16[96,1152]{1,0:T(8,128)(2,1)S(1)} %get-tuple-element.25), channel_id=1, source_target_pairs={{0,16},{4,12},{8,24},{12,4},{16,0},{20,28},{24,8},{28,20},{1,17},{... | collective-permute-start | bytes 663560 | tf_op jit(solution)/shard_map/ppermute | solution.py:385
  22.7 0.0 collective-permute-done.2.refs_3_
  22.7 2.3 %attend.5 = bf16[96,1152]{1,0:T(8,128)(2,1)S(1)} custom-call(bf16[2,1024,512]{2,1,0:T(8,128)(2,1)S(1)} %get-tuple-element.21.refs_0_, f32[2048,128]{1,0:T(8,128)S(1)} %get-tuple-element.22.refs_1_, s32[8,128]{1,0:T(8,128)S(1)} %get-tuple-element.16.selected.refs_2_, bf16[96,1024]{1,0:T(8,128)(2,1)S(1)} %collective-permute-done.2.refs_3_), custom_call_target="tpu_custom_call" | custom-call | flops 1000 | bytes 1000 | tf_op jit(solution)/shard_map/attend/pallas_call | solution.py:312
  25.0 0.9 %collective-permute-start.3 = (bf16[96,1152]{1,0:T(8,128)(2,1)S(1)}, bf16[96,1152]{1,0:T(8,128)(2,1)S(1)}, u32[]{:S(2)}, u32[]{:S(2)}) collective-permute-start(bf16[96,1152]{1,0:T(8,128)(2,1)S(1)} %attend.5), channel_id=1, source_target_pairs={{0,24},{4,28},{8,16},{12,20},{16,8},{20,12},{24,0},{28,4},{1,25},{... | collective-permute-start | bytes 663560 | tf_op jit(solution)/shard_map/ppermute | solution.py:385
  25.8 2.5 %attend.4.refs_0_ = bf16[96,1152]{1,0:T(8,128)(2,1)S(1)} custom-call(bf16[2,1024,512]{2,1,0:T(8,128)(2,1)S(1)} %get-tuple-element.21.refs_0_, f32[2048,128]{1,0:T(8,128)S(1)} %get-tuple-element.22.refs_1_, s32[8,128]{1,0:T(8,128)S(1)} %get-tuple-element.16.selected.refs_2_, bf16[96,1024]{1,0:T(8,128)(2,1)S(1)} %get-tuple-element.20.query.refs_3_), custom_call_target="tpu_custom_call" | custom-call | flops 1000 | bytes 1000 | tf_op jit(solution)/shard_map/attend/pallas_call | solution.py:312
  28.4 2.5 %collective-permute-done.7.refs_3_ = bf16[96,1152]{1,0:T(8,128)(2,1)S(1)} collective-permute-done((bf16[96,1152]{1,0:T(8,128)(2,1)S(1)}, bf16[96,1152]{1,0:T(8,128)(2,1)S(1)}, u32[]{:S(2)}, u32[]{:S(2)}) %collective-permute-start.7) | collective-permute-done | bytes 221216 | tf_op jit(solution)/shard_map/ppermute | solution.py:385
  30.9 1.4 %collective-permute-done.3.refs_1_ = bf16[96,1152]{1,0:T(8,128)(2,1)S(1)} collective-permute-done((bf16[96,1152]{1,0:T(8,128)(2,1)S(1)}, bf16[96,1152]{1,0:T(8,128)(2,1)S(1)}, u32[]{:S(2)}, u32[]{:S(2)}) %collective-permute-start.3) | collective-permute-done | bytes 221216 | tf_op jit(solution)/shard_map/ppermute | solution.py:385
  32.3 2.2 %finish.1 = (f32[96,1024]{1,0:T(8,128)S(1)}, bf16[96,1024]{1,0:T(8,128)(2,1)S(1)}, bf16[96,1024]{1,0:T(8,128)(2,1)S(1)}, bf16[96,1024]{1,0:T(8,128)(2,1)S(1)}) custom-call(bf16[96,1152]{1,0:T(8,128)(2,1)S(1)} %attend.4.refs_0_, bf16[96,1152]{1,0:T(8,128)(2,1)S(1)} %collective-permute-done.3.refs_1_, bf16[96,1152]{1,0:T(8,128)(2,1)S(1)} %collective-permute-done.6.refs_2_, ...), custom_call_target="tpu_custom_call" | custom-call | flops 805306368 | bytes 8388608 | tf_op jit(solution)/shard_map/finish/pallas_call | solution.py:367
  34.5 0.5 collective-permute-start.10
  35.0 2.6 %collective-permute-start.8 = (bf16[96,1024]{1,0:T(8,128)(2,1)S(1)}, bf16[96,1024]{1,0:T(8,128)(2,1)S(1)}, u32[]{:S(2)}, u32[]{:S(2)}) collective-permute-start(bf16[96,1024]{1,0:T(8,128)(2,1)S(1)} %get-tuple-element.27), channel_id=1, source_target_pairs={{0,2},{1,3},{2,0},{3,1},{4,6},{5,7},{6,4},{7,5},{8,10},{9,11},{10,... | collective-permute-start | bytes 589832 | tf_op jit(solution)/shard_map/ppermute | solution.py:385
  37.6 0.4 collective-permute-start.9
  38.0 0.7 %reshape.15 = bf16[96,2,2,128]{3,2,1,0:T(2,128)(2,1)} reshape(bf16[96,512]{1,0:T(8,128)(2,1)S(1)} %get-tuple-element.19.kv) | data formatting | bytes 196608 | tf_op jit(solution)/shard_map/reshape | solution.py:422
  38.7 3.6 %collective-permute-done.10 = bf16[96,1024]{1,0:T(8,128)(2,1)S(1)} collective-permute-done((bf16[96,1024]{1,0:T(8,128)(2,1)S(1)}, bf16[96,1024]{1,0:T(8,128)(2,1)S(1)}, u32[]{:S(2)}, u32[]{:S(2)}) %collective-permute-start.10) | collective-permute-done | bytes 196640 | tf_op jit(solution)/shard_map/ppermute | solution.py:385
  42.3 7.7 %collective-permute-done.8 = bf16[96,1024]{1,0:T(8,128)(2,1)S(1)} collective-permute-done((bf16[96,1024]{1,0:T(8,128)(2,1)S(1)}, bf16[96,1024]{1,0:T(8,128)(2,1)S(1)}, u32[]{:S(2)}, u32[]{:S(2)}) %collective-permute-start.8) | collective-permute-done | bytes 196640 | tf_op jit(solution)/shard_map/ppermute | solution.py:385
  50.0 3.3 %collective-permute-done.9 = bf16[96,1024]{1,0:T(8,128)(2,1)S(1)} collective-permute-done((bf16[96,1024]{1,0:T(8,128)(2,1)S(1)}, bf16[96,1024]{1,0:T(8,128)(2,1)S(1)}, u32[]{:S(2)}, u32[]{:S(2)}) %collective-permute-start.9) | collective-permute-done | bytes 196640 | tf_op jit(solution)/shard_map/ppermute | solution.py:385
  53.3 0.8 %add_convert_fusion = bf16[96,1024]{1,0:T(8,128)(2,1)} fusion(bf16[96,1024]{1,0:T(8,128)(2,1)S(1)} %collective-permute-done.10, bf16[96,1024]{1,0:T(8,128)(2,1)S(1)} %collective-permute-done.9, f32[96,1024]{1,0:T(8,128)S(1)} %get-tuple-element.26, bf16[96,1024]{1,0:T(8,128)(2,1)S(1)} %collective-permute-done.8), kind=kLoop, calls=%fused_computation | loop fusion | flops 688128 | bytes 1179648 | tf_op jit(solution)/shard_map/convert_element_type | solution.py:423
  (10 shorter events, 0.0 us)
Async XLA Ops:
  0.6 6.5 %copy-start = (bf16[1024,2,2,128]{3,2,1,0:T(2,128)(2,1)S(1)}, bf16[1024,2,2,128]{3,2,1,0:T(2,128)(2,1)}, u32[]{:S(2)}) copy-start(bf16[1024,2,2,128]{3,2,1,0:T(2,128)(2,1)} %param.17) | copy-start | bytes 3145732
  0.6 10.1 %copy-start.1 = (s32[2]{0:T(128)S(1)}, s32[2]{0:T(128)}, u32[]{:S(2)}) copy-start(s32[2]{0:T(128)} %order.1) | copy-start | bytes 28
  0.7 10.1 %copy-start.2 = (s32[2]{0:T(128)S(1)}, s32[2]{0:T(128)}, u32[]{:S(2)}) copy-start(s32[2]{0:T(128)} %slot.1) | copy-start | bytes 28
  7.2 3.6 %collective-permute-start = (bf16[4096,128]{1,0:T(8,128)(2,1)S(1)}, bf16[4096,128]{1,0:T(8,128)(2,1)S(1)}, u32[]{:S(2)}, u32[]{:S(2)}) collective-permute-start(bf16[4096,128]{1,0:T(8,128)(2,1)S(1)} %bitcast.4), channel_id=1, source_target_pairs={{0,4},{4,0},{8,12},{12,8},{16,20},{20,16},{24,28},{28,24},{1,5},{5... | collective-permute-start | bytes 3145736 | tf_op jit(solution)/shard_map/ppermute | solution.py:385
  7.2 3.5 %collective-permute-start.1 = (bf16[96,512]{1,0:T(8,128)(2,1)S(1)}, bf16[96,512]{1,0:T(8,128)(2,1)S(1)}, u32[]{:S(2)}, u32[]{:S(2)}) collective-permute-start(bf16[96,512]{1,0:T(8,128)(2,1)S(1)} %get-tuple-element.19.kv), channel_id=1, source_target_pairs={{0,4},{4,0},{8,12},{12,8},{16,20},{20,16},{24,28},{28,24},{1,5},{5... | collective-permute-start | bytes 294920 | tf_op jit(solution)/shard_map/ppermute | solution.py:385
  7.7 7.5 %collective-permute-start.5 = (bf16[96,1024]{1,0:T(8,128)(2,1)S(1)}, bf16[96,1024]{1,0:T(8,128)(2,1)S(1)}, u32[]{:S(2)}, u32[]{:S(2)}) collective-permute-start(bf16[96,1024]{1,0:T(8,128)(2,1)S(1)} %get-tuple-element.20.query.refs_3_), channel_id=1, source_target_pairs={{0,8},{4,20},{8,0},{12,28},{16,24},{20,4},{24,16},{28,12},{1,9},{5... | collective-permute-start | bytes 589832 | tf_op jit(solution)/shard_map/ppermute | solution.py:385
  9.2 8.3 %collective-permute-start.4 = (bf16[96,1024]{1,0:T(8,128)(2,1)S(1)}, bf16[96,1024]{1,0:T(8,128)(2,1)S(1)}, u32[]{:S(2)}, u32[]{:S(2)}) collective-permute-start(bf16[96,1024]{1,0:T(8,128)(2,1)S(1)} %get-tuple-element.20.query.refs_3_), channel_id=1, source_target_pairs={{0,16},{4,12},{8,24},{12,4},{16,0},{20,28},{24,8},{28,20},{1,17},{... | collective-permute-start | bytes 589832 | tf_op jit(solution)/shard_map/ppermute | solution.py:385
  10.8 21.5 %slice-start = ((s8[8388608]{0:T(1024)(128)(4,1)}), s8[4194304]{0:T(1024)(128)(4,1)S(1)}, s32[]{:S(2)}) async-start(s8[8388608]{0:T(1024)(128)(4,1)} %bitcast.2), calls=%async_computation | async-start | bytes 8388608
  12.7 10.0 %collective-permute-start.2 = (bf16[96,1024]{1,0:T(8,128)(2,1)S(1)}, bf16[96,1024]{1,0:T(8,128)(2,1)S(1)}, u32[]{:S(2)}, u32[]{:S(2)}) collective-permute-start(bf16[96,1024]{1,0:T(8,128)(2,1)S(1)} %get-tuple-element.23), channel_id=1, source_target_pairs={{0,24},{4,28},{8,16},{12,20},{16,8},{20,12},{24,0},{28,4},{1,25},{... | collective-permute-start | bytes 589832 | tf_op jit(solution)/shard_map/ppermute | solution.py:385
  17.6 14.7 %slice-start.1 = ((s8[8388608]{0:T(1024)(128)(4,1)}), s8[4194304]{0:T(1024)(128)(4,1)S(1)}, s32[]{:S(2)}) async-start(s8[8388608]{0:T(1024)(128)(4,1)} %bitcast.2), calls=%async_computation.1 | async-start | bytes 8388608
  19.9 8.4 %collective-permute-start.6 = (bf16[96,1152]{1,0:T(8,128)(2,1)S(1)}, bf16[96,1152]{1,0:T(8,128)(2,1)S(1)}, u32[]{:S(2)}, u32[]{:S(2)}) collective-permute-start(bf16[96,1152]{1,0:T(8,128)(2,1)S(1)} %get-tuple-element.24), channel_id=1, source_target_pairs={{0,8},{4,20},{8,0},{12,28},{16,24},{20,4},{24,16},{28,12},{1,9},{5... | collective-permute-start | bytes 663560 | tf_op jit(solution)/shard_map/ppermute | solution.py:385
  21.5 9.4 %collective-permute-start.7 = (bf16[96,1152]{1,0:T(8,128)(2,1)S(1)}, bf16[96,1152]{1,0:T(8,128)(2,1)S(1)}, u32[]{:S(2)}, u32[]{:S(2)}) collective-permute-start(bf16[96,1152]{1,0:T(8,128)(2,1)S(1)} %get-tuple-element.25), channel_id=1, source_target_pairs={{0,16},{4,12},{8,24},{12,4},{16,0},{20,28},{24,8},{28,20},{1,17},{... | collective-permute-start | bytes 663560 | tf_op jit(solution)/shard_map/ppermute | solution.py:385
  25.0 7.3 %collective-permute-start.3 = (bf16[96,1152]{1,0:T(8,128)(2,1)S(1)}, bf16[96,1152]{1,0:T(8,128)(2,1)S(1)}, u32[]{:S(2)}, u32[]{:S(2)}) collective-permute-start(bf16[96,1152]{1,0:T(8,128)(2,1)S(1)} %attend.5), channel_id=1, source_target_pairs={{0,24},{4,28},{8,16},{12,20},{16,8},{20,12},{24,0},{28,4},{1,25},{... | collective-permute-start | bytes 663560 | tf_op jit(solution)/shard_map/ppermute | solution.py:385
  34.5 7.8 %collective-permute-start.10 = (bf16[96,1024]{1,0:T(8,128)(2,1)S(1)}, bf16[96,1024]{1,0:T(8,128)(2,1)S(1)}, u32[]{:S(2)}, u32[]{:S(2)}) collective-permute-start(bf16[96,1024]{1,0:T(8,128)(2,1)S(1)} %get-tuple-element.29), channel_id=1, source_target_pairs={{0,1},{1,0},{2,3},{3,2},{4,5},{5,4},{6,7},{7,6},{8,9},{9,8},{10,11... | collective-permute-start | bytes 589832 | tf_op jit(solution)/shard_map/ppermute | solution.py:385
  35.0 15.0 %collective-permute-start.8 = (bf16[96,1024]{1,0:T(8,128)(2,1)S(1)}, bf16[96,1024]{1,0:T(8,128)(2,1)S(1)}, u32[]{:S(2)}, u32[]{:S(2)}) collective-permute-start(bf16[96,1024]{1,0:T(8,128)(2,1)S(1)} %get-tuple-element.27), channel_id=1, source_target_pairs={{0,2},{1,3},{2,0},{3,1},{4,6},{5,7},{6,4},{7,5},{8,10},{9,11},{10,... | collective-permute-start | bytes 589832 | tf_op jit(solution)/shard_map/ppermute | solution.py:385
  37.6 15.7 %collective-permute-start.9 = (bf16[96,1024]{1,0:T(8,128)(2,1)S(1)}, bf16[96,1024]{1,0:T(8,128)(2,1)S(1)}, u32[]{:S(2)}, u32[]{:S(2)}) collective-permute-start(bf16[96,1024]{1,0:T(8,128)(2,1)S(1)} %get-tuple-element.28), channel_id=1, source_target_pairs={{0,3},{1,2},{2,1},{3,0},{4,7},{5,6},{6,5},{7,4},{8,11},{9,10},{10,... | collective-permute-start | bytes 589832 | tf_op jit(solution)/shard_map/ppermute | solution.py:385

commit v8 on v7

--- a/solution.py
+++ b/solution.py
@@ -385,6 +385,24 @@
     return lax.ppermute(value, axis, [(at, at ^ (odd if at & 1 else even)) for at in range(size)])
 
 
+def sum_heads(blocks, size):
+    if size != 4:
+        arrived = [swap(blocks[turn], "head", turn, size) for turn in range(1, size)]
+    else:
+        me = lax.axis_index("head")
+        ends = (me == 0) | (me == 3)
+        far = lax.ppermute(blocks[3], "head", [(0, 3), (3, 0)])
+        beside = swap(blocks[1], "head", 1, size)
+        step = lax.ppermute(blocks[2], "head", [(0, 1), (1, 3), (3, 2), (2, 0)])
+        both = (blocks[3].astype(f32) + step.astype(f32)).astype(bf16)
+        middle = lax.ppermute(both, "head", [(1, 2), (2, 1)])
+        arrived = [far, beside, jnp.where(ends, step, middle)]
+    total = blocks[0]
+    for block in arrived:
+        total = total + block.astype(f32)
+    return total.astype(bf16)
+
+
 def body(
     hidden, norm_gain, w_query, w_key, w_value, w_out, stored_kv, selected, prompt_order, store_slot
 ):
@@ -413,14 +431,9 @@
     done = attend((second,), cache, key_pos, table, [queries[second]], done)
     parts += [swap(part, "seq", turn, seq_count) for turn, part in zip((first, second), done)]
     blocks = finish(parts, w_out, head_count)
-    total = blocks[0]
-    arrived = [
-        swap(blocks[turn], "head", turn, head_count) for turn in (*range(2, head_count), 1)
-    ]
-    for block in arrived:
-        total = total + block.astype(f32)
+    total = sum_heads(blocks, head_count)
     new_kv = kv.reshape(rows, 2, local_kv, HEAD_DIM)
-    return (total.astype(bf16), new_kv)
+    return (total, new_kv)
 
 
 def solution(mesh):

time: 54.5 us -> 53.7 us (0.985)
  waiting for transfers between devices: 19.3 us -> 13.8 us
  starting transfers between devices: 12.5 us -> 17.4 us
    ppermute x11 -> x9, waiting for transfers between devices: 19.3 us -> 5.62 us  [swap(): lax.ppermute(value, axis, [(at, at ^ (odd if at & 1 else even)) for at in...]
    ppermute x0 -> x3, waiting for transfers between devices: none -> 8.2 us  [the longest x1 4.1 us: sum_heads(): step = lax.ppermute(blocks[2], 'head', [(0, 1), (1, 3), (3, 2), (2, 0)])]
    ppermute x0 -> x3, starting transfers between devices: none -> 5.22 us  [the longest x1 2.64 us: sum_heads(): step = lax.ppermute(blocks[2], 'head', [(0, 1), (1, 3), (3, 2), (2, 0)])]
    ppermute x11 -> x9, starting transfers between devices: 12.5 us -> 12.2 us  [swap(): lax.ppermute(value, axis, [(at, at ^ (odd if at & 1 else even)) for at in...]
  transfers between devices with their start and end apart: 11 -> 12, of which waited for: 6 -> 6; matrix products, arithmetic and copies ran while one was open for 1% -> 1% of each run, Pallas kernels for 21% -> 21%
where the time goes in v8:
time: 53.7 us; the launch traced here: 53.5 us
  Pallas kernels  20 us (37%)
  starting transfers between devices  17.4 us (32%)
  waiting for transfers between devices  13.8 us (26%)
  other arithmetic  0.86 us (2%)
  between operations  0.79 us (1%)
  local copies, waits for them, and re-layouts  0.7 us (1%)
    ppermute x9, starting transfers between devices, swap(): lax.ppermute(value, axis, [(at, at ^ (odd if at & 1 else even)) for at in...  12.2 us
    pallas_call x4, Pallas kernels, attend(): pl.pallas_call(functools.partial(attend_kernel, partners, len(earlier)),...  9.43 us
    pallas_call x1, Pallas kernels, project(): pl.pallas_call(functools.partial(project_kernel, width), out_shape=(jax.S...  6.47 us
    ppermute x9, waiting for transfers between devices, swap(): lax.ppermute(value, axis, [(at, at ^ (odd if at & 1 else even)) for at in...  5.62 us
    ppermute x1, waiting for transfers between devices, sum_heads(): step = lax.ppermute(blocks[2], 'head', [(0, 1), (1, 3), (3, 2), (2, 0)])  4.1 us
    ppermute x1, waiting for transfers between devices, sum_heads(): middle = lax.ppermute(both, 'head', [(1, 2), (2, 1)])  4.1 us
    ppermute x1, starting transfers between devices, sum_heads(): step = lax.ppermute(blocks[2], 'head', [(0, 1), (1, 3), (3, 2), (2, 0)])  2.64 us
    pallas_call x1, Pallas kernels, finish(): pl.pallas_call(functools.partial(finish_kernel, len(parts), size), out_sh...  2.17 us
  transfers between devices with their start and end apart: 12, of which 6 were waited for; matrix products, arithmetic and copies ran while one was open for 1% of the time, Pallas kernels for 21%

profile of v8, /device:TPU:8, one launch (start us, length us, event | category | flops | bytes accessed | tf_op | source)
XLA Modules:
  0.0 53.5 jit_solution(15043256404001940161)
XLA Ops:
  0.7 6.5 %project.1 = (bf16[96,1024]{1,0:T(8,128)(2,1)S(1)}, bf16[96,512]{1,0:T(8,128)(2,1)S(1)}, s32[8,128]{1,0:T(8,128)S(1)}) custom-call(bf16[96,4096]{1,0:T(8,128)(2,1)} %hidden_any.1, f32[1,4096]{1,0:T(1,128)} %bitcast.6, s32[768]{0:T(1024)} %selected_any.1, f32[1,128]{1,0:T(1,128)} %constant.10.clone.freq_any, bf16[4096,1024]{1,0:T(8,128)(2,1)} %wq_any.1, ...), custom_call_target="tpu_custom_call" | custom-call | flops 1207959552 | bytes 13369344 | tf_op jit(solution)/shard_map/project/pallas_call | solution.py:103
  7.2 0.1 collective-permute-start
  7.2 0.5 collective-permute-start.1
  7.7 1.5 %collective-permute-start.5 = (bf16[96,1024]{1,0:T(8,128)(2,1)S(1)}, bf16[96,1024]{1,0:T(8,128)(2,1)S(1)}, u32[]{:S(2)}, u32[]{:S(2)}) collective-permute-start(bf16[96,1024]{1,0:T(8,128)(2,1)S(1)} %get-tuple-element.20.query.refs_3_), channel_id=1, source_target_pairs={{0,8},{4,20},{8,0},{12,28},{16,24},{20,4},{24,16},{28,12},{1,9},{5... | collective-permute-start | bytes 589832 | tf_op jit(solution)/shard_map/ppermute | solution.py:385
  9.2 1.5 %collective-permute-start.4 = (bf16[96,1024]{1,0:T(8,128)(2,1)S(1)}, bf16[96,1024]{1,0:T(8,128)(2,1)S(1)}, u32[]{:S(2)}, u32[]{:S(2)}) collective-permute-start(bf16[96,1024]{1,0:T(8,128)(2,1)S(1)} %get-tuple-element.20.query.refs_3_), channel_id=1, source_target_pairs={{0,16},{4,12},{8,24},{12,4},{16,0},{20,28},{24,8},{28,20},{1,17},{... | collective-permute-start | bytes 589832 | tf_op jit(solution)/shard_map/ppermute | solution.py:385
  10.7 0.0 collective-permute-done.1.kv_other
  10.7 0.0 collective-permute-done.stored_other
  10.8 0.0 slice-start
  10.8 1.9 %merge.1 = (bf16[2,1024,512]{2,1,0:T(8,128)(2,1)S(1)}, f32[2048,128]{1,0:T(8,128)S(1)}, bf16[96,1024]{1,0:T(8,128)(2,1)S(1)}) custom-call(s32[2]{0:T(128)S(1)} %copy-done.1, s32[2]{0:T(128)S(1)} %copy-done.2, s32[8,128]{1,0:T(8,128)S(1)} %get-tuple-element.16.selected.refs_2_, bf16[4096,128]{1,0:T(8,128)(2,1)S(1)} %bitcast.5, ...), custom_call_target="tpu_custom_call" | custom-call | flops 1000 | bytes 1000 | tf_op jit(solution)/shard_map/merge/pallas_call | solution.py:194
  12.7 1.8 %collective-permute-start.2 = (bf16[96,1024]{1,0:T(8,128)(2,1)S(1)}, bf16[96,1024]{1,0:T(8,128)(2,1)S(1)}, u32[]{:S(2)}, u32[]{:S(2)}) collective-permute-start(bf16[96,1024]{1,0:T(8,128)(2,1)S(1)} %get-tuple-element.23), channel_id=1, source_target_pairs={{0,24},{4,28},{8,16},{12,20},{16,8},{20,12},{24,0},{28,4},{1,25},{... | collective-permute-start | bytes 589832 | tf_op jit(solution)/shard_map/ppermute | solution.py:385
  14.4 0.8 %collective-permute-done.5.refs_3_ = bf16[96,1024]{1,0:T(8,128)(2,1)S(1)} collective-permute-done((bf16[96,1024]{1,0:T(8,128)(2,1)S(1)}, bf16[96,1024]{1,0:T(8,128)(2,1)S(1)}, u32[]{:S(2)}, u32[]{:S(2)}) %collective-permute-start.5) | collective-permute-done | bytes 196640 | tf_op jit(solution)/shard_map/ppermute | solution.py:385
  15.2 2.3 %attend.6.refs_4_ = bf16[96,1152]{1,0:T(8,128)(2,1)S(1)} custom-call(bf16[2,1024,512]{2,1,0:T(8,128)(2,1)S(1)} %get-tuple-element.21.refs_0_, f32[2048,128]{1,0:T(8,128)S(1)} %get-tuple-element.22.refs_1_, s32[8,128]{1,0:T(8,128)S(1)} %get-tuple-element.16.selected.refs_2_, bf16[96,1024]{1,0:T(8,128)(2,1)S(1)} %collective-permute-done.5.refs_3_), custom_call_target="tpu_custom_call" | custom-call | flops 1000 | bytes 1000 | tf_op jit(solution)/shard_map/attend/pallas_call | solution.py:312
  17.6 0.0 slice-start.1
  17.6 2.3 %attend.7 = (bf16[96,1152]{1,0:T(8,128)(2,1)S(1)}, bf16[96,1152]{1,0:T(8,128)(2,1)S(1)}) custom-call(bf16[2,1024,512]{2,1,0:T(8,128)(2,1)S(1)} %get-tuple-element.21.refs_0_, f32[2048,128]{1,0:T(8,128)S(1)} %get-tuple-element.22.refs_1_, s32[8,128]{1,0:T(8,128)S(1)} %get-tuple-element.16.selected.refs_2_, ...), custom_call_target="tpu_custom_call" | custom-call | flops 1000 | bytes 1000 | tf_op jit(solution)/shard_map/attend/pallas_call | solution.py:312
  19.9 1.6 %collective-permute-start.6 = (bf16[96,1152]{1,0:T(8,128)(2,1)S(1)}, bf16[96,1152]{1,0:T(8,128)(2,1)S(1)}, u32[]{:S(2)}, u32[]{:S(2)}) collective-permute-start(bf16[96,1152]{1,0:T(8,128)(2,1)S(1)} %get-tuple-element.24), channel_id=1, source_target_pairs={{0,8},{4,20},{8,0},{12,28},{16,24},{20,4},{24,16},{28,12},{1,9},{5... | collective-permute-start | bytes 663560 | tf_op jit(solution)/shard_map/ppermute | solution.py:385
  21.5 1.2 %collective-permute-start.7 = (bf16[96,1152]{1,0:T(8,128)(2,1)S(1)}, bf16[96,1152]{1,0:T(8,128)(2,1)S(1)}, u32[]{:S(2)}, u32[]{:S(2)}) collective-permute-start(bf16[96,1152]{1,0:T(8,128)(2,1)S(1)} %get-tuple-element.25), channel_id=1, source_target_pairs={{0,16},{4,12},{8,24},{12,4},{16,0},{20,28},{24,8},{28,20},{1,17},{... | collective-permute-start | bytes 663560 | tf_op jit(solution)/shard_map/ppermute | solution.py:385
  22.7 0.0 collective-permute-done.2.refs_3_
  22.7 2.3 %attend.5 = bf16[96,1152]{1,0:T(8,128)(2,1)S(1)} custom-call(bf16[2,1024,512]{2,1,0:T(8,128)(2,1)S(1)} %get-tuple-element.21.refs_0_, f32[2048,128]{1,0:T(8,128)S(1)} %get-tuple-element.22.refs_1_, s32[8,128]{1,0:T(8,128)S(1)} %get-tuple-element.16.selected.refs_2_, bf16[96,1024]{1,0:T(8,128)(2,1)S(1)} %collective-permute-done.2.refs_3_), custom_call_target="tpu_custom_call" | custom-call | flops 1000 | bytes 1000 | tf_op jit(solution)/shard_map/attend/pallas_call | solution.py:312
  25.0 0.9 %collective-permute-start.3 = (bf16[96,1152]{1,0:T(8,128)(2,1)S(1)}, bf16[96,1152]{1,0:T(8,128)(2,1)S(1)}, u32[]{:S(2)}, u32[]{:S(2)}) collective-permute-start(bf16[96,1152]{1,0:T(8,128)(2,1)S(1)} %attend.5), channel_id=1, source_target_pairs={{0,24},{4,28},{8,16},{12,20},{16,8},{20,12},{24,0},{28,4},{1,25},{... | collective-permute-start | bytes 663560 | tf_op jit(solution)/shard_map/ppermute | solution.py:385
  25.8 2.5 %attend.4.refs_0_ = bf16[96,1152]{1,0:T(8,128)(2,1)S(1)} custom-call(bf16[2,1024,512]{2,1,0:T(8,128)(2,1)S(1)} %get-tuple-element.21.refs_0_, f32[2048,128]{1,0:T(8,128)S(1)} %get-tuple-element.22.refs_1_, s32[8,128]{1,0:T(8,128)S(1)} %get-tuple-element.16.selected.refs_2_, bf16[96,1024]{1,0:T(8,128)(2,1)S(1)} %get-tuple-element.20.query.refs_3_), custom_call_target="tpu_custom_call" | custom-call | flops 1000 | bytes 1000 | tf_op jit(solution)/shard_map/attend/pallas_call | solution.py:312
  28.4 2.5 %collective-permute-done.7.refs_3_ = bf16[96,1152]{1,0:T(8,128)(2,1)S(1)} collective-permute-done((bf16[96,1152]{1,0:T(8,128)(2,1)S(1)}, bf16[96,1152]{1,0:T(8,128)(2,1)S(1)}, u32[]{:S(2)}, u32[]{:S(2)}) %collective-permute-start.7) | collective-permute-done | bytes 221216 | tf_op jit(solution)/shard_map/ppermute | solution.py:385
  30.9 1.4 %collective-permute-done.3.refs_1_ = bf16[96,1152]{1,0:T(8,128)(2,1)S(1)} collective-permute-done((bf16[96,1152]{1,0:T(8,128)(2,1)S(1)}, bf16[96,1152]{1,0:T(8,128)(2,1)S(1)}, u32[]{:S(2)}, u32[]{:S(2)}) %collective-permute-start.3) | collective-permute-done | bytes 221216 | tf_op jit(solution)/shard_map/ppermute | solution.py:385
  32.3 2.2 %finish.1 = (f32[96,1024]{1,0:T(8,128)S(1)}, bf16[96,1024]{1,0:T(8,128)(2,1)S(1)}, bf16[96,1024]{1,0:T(8,128)(2,1)S(1)}, bf16[96,1024]{1,0:T(8,128)(2,1)S(1)}) custom-call(bf16[96,1152]{1,0:T(8,128)(2,1)S(1)} %attend.4.refs_0_, bf16[96,1152]{1,0:T(8,128)(2,1)S(1)} %collective-permute-done.3.refs_1_, bf16[96,1152]{1,0:T(8,128)(2,1)S(1)} %collective-permute-done.6.refs_2_, ...), custom_call_target="tpu_custom_call" | custom-call | flops 805306368 | bytes 8388608 | tf_op jit(solution)/shard_map/finish/pallas_call | solution.py:367
  34.5 2.6 %collective-permute-start.10 = (bf16[96,1024]{1,0:T(8,128)(2,1)S(1)}, bf16[96,1024]{1,0:T(8,128)(2,1)S(1)}, u32[]{:S(2)}, u32[]{:S(2)}) collective-permute-start(bf16[96,1024]{1,0:T(8,128)(2,1)S(1)} %get-tuple-element.29), channel_id=1, source_target_pairs={{0,1},{1,3},{3,2},{2,0},{4,5},{5,7},{7,6},{6,4},{8,9},{9,11},{11,1... | collective-permute-start | bytes 589832 | tf_op jit(solution)/shard_map/ppermute | solution.py:396
  37.1 0.7 %collective-permute-start.8 = (bf16[96,1024]{1,0:T(8,128)(2,1)S(1)}, bf16[96,1024]{1,0:T(8,128)(2,1)S(1)}, u32[]{:S(2)}, u32[]{:S(2)}) collective-permute-start(bf16[96,1024]{1,0:T(8,128)(2,1)S(1)} %get-tuple-element.27), channel_id=1, source_target_pairs={{0,3},{3,0},{4,7},{7,4},{8,11},{11,8},{12,15},{15,12},{16,19},{19,... | collective-permute-start | bytes 589832 | tf_op jit(solution)/shard_map/ppermute | solution.py:394
  37.8 3.2 %collective-permute-start.9 = (bf16[96,1024]{1,0:T(8,128)(2,1)S(1)}, bf16[96,1024]{1,0:T(8,128)(2,1)S(1)}, u32[]{:S(2)}, u32[]{:S(2)}) collective-permute-start(bf16[96,1024]{1,0:T(8,128)(2,1)S(1)} %get-tuple-element.28), channel_id=1, source_target_pairs={{0,1},{1,0},{2,3},{3,2},{4,5},{5,4},{6,7},{7,6},{8,9},{9,8},{10,11... | collective-permute-start | bytes 589832 | tf_op jit(solution)/shard_map/ppermute | solution.py:385
  41.0 4.1 %collective-permute-done.10 = bf16[96,1024]{1,0:T(8,128)(2,1)S(1)} collective-permute-done((bf16[96,1024]{1,0:T(8,128)(2,1)S(1)}, bf16[96,1024]{1,0:T(8,128)(2,1)S(1)}, u32[]{:S(2)}, u32[]{:S(2)}) %collective-permute-start.10) | collective-permute-done | bytes 196640 | tf_op jit(solution)/shard_map/ppermute | solution.py:396
  45.2 1.9 %collective-permute-start.11 = (bf16[96,1024]{1,0:T(8,128)(2,1)S(1)}, bf16[96,1024]{1,0:T(8,128)(2,1)S(1)}, u32[]{:S(2)}, u32[]{:S(2)}) collective-permute-start(bf16[96,1024]{1,0:T(8,128)(2,1)S(1)} %add_convert_fusion.1), channel_id=1, source_target_pairs={{1,2},{2,1},{5,6},{6,5},{9,10},{10,9},{13,14},{14,13},{17,18},{18,... | collective-permute-start | bytes 589832 | tf_op jit(solution)/shard_map/ppermute | solution.py:398
  47.1 0.7 %reshape.15 = bf16[96,2,2,128]{3,2,1,0:T(2,128)(2,1)} reshape(bf16[96,512]{1,0:T(8,128)(2,1)S(1)} %get-tuple-element.19.kv) | data formatting | bytes 196608 | tf_op jit(solution)/shard_map/reshape | solution.py:435
  47.8 0.9 %collective-permute-done.9 = bf16[96,1024]{1,0:T(8,128)(2,1)S(1)} collective-permute-done((bf16[96,1024]{1,0:T(8,128)(2,1)S(1)}, bf16[96,1024]{1,0:T(8,128)(2,1)S(1)}, u32[]{:S(2)}, u32[]{:S(2)}) %collective-permute-start.9) | collective-permute-done | bytes 196640 | tf_op jit(solution)/shard_map/ppermute | solution.py:385
  48.6 4.1 %collective-permute-done.11 = bf16[96,1024]{1,0:T(8,128)(2,1)S(1)} collective-permute-done((bf16[96,1024]{1,0:T(8,128)(2,1)S(1)}, bf16[96,1024]{1,0:T(8,128)(2,1)S(1)}, u32[]{:S(2)}, u32[]{:S(2)}) %collective-permute-start.11) | collective-permute-done | bytes 196640 | tf_op jit(solution)/shard_map/ppermute | solution.py:398
  52.7 0.8 %add_convert_fusion = bf16[96,1024]{1,0:T(8,128)(2,1)} fusion(bf16[96,1024]{1,0:T(8,128)(2,1)S(1)} %collective-permute-done.9, f32[96,1024]{1,0:T(8,128)S(1)} %get-tuple-element.26, bf16[96,1024]{1,0:T(8,128)(2,1)S(1)} %collective-permute-done.8, bf16[96,1024]{1,0:T(8,128)(2,1)S(1)} %collective-permute-done.10, ...), kind=kLoop, calls=%fused_computation | loop fusion | flops 786432 | bytes 1376257 | tf_op jit(solution)/shard_map/convert_element_type | solution.py:403
  (13 shorter events, 0.1 us)
Async XLA Ops:
  0.6 6.5 %copy-start = (bf16[1024,2,2,128]{3,2,1,0:T(2,128)(2,1)S(1)}, bf16[1024,2,2,128]{3,2,1,0:T(2,128)(2,1)}, u32[]{:S(2)}) copy-start(bf16[1024,2,2,128]{3,2,1,0:T(2,128)(2,1)} %param.17) | copy-start | bytes 3145732
  0.6 10.1 %copy-start.1 = (s32[2]{0:T(128)S(1)}, s32[2]{0:T(128)}, u32[]{:S(2)}) copy-start(s32[2]{0:T(128)} %order.1) | copy-start | bytes 28
  0.7 10.1 %copy-start.2 = (s32[2]{0:T(128)S(1)}, s32[2]{0:T(128)}, u32[]{:S(2)}) copy-start(s32[2]{0:T(128)} %slot.1) | copy-start | bytes 28
  7.2 3.6 %collective-permute-start = (bf16[4096,128]{1,0:T(8,128)(2,1)S(1)}, bf16[4096,128]{1,0:T(8,128)(2,1)S(1)}, u32[]{:S(2)}, u32[]{:S(2)}) collective-permute-start(bf16[4096,128]{1,0:T(8,128)(2,1)S(1)} %bitcast.4), channel_id=1, source_target_pairs={{0,4},{4,0},{8,12},{12,8},{16,20},{20,16},{24,28},{28,24},{1,5},{5... | collective-permute-start | bytes 3145736 | tf_op jit(solution)/shard_map/ppermute | solution.py:385
  7.2 3.5 %collective-permute-start.1 = (bf16[96,512]{1,0:T(8,128)(2,1)S(1)}, bf16[96,512]{1,0:T(8,128)(2,1)S(1)}, u32[]{:S(2)}, u32[]{:S(2)}) collective-permute-start(bf16[96,512]{1,0:T(8,128)(2,1)S(1)} %get-tuple-element.19.kv), channel_id=1, source_target_pairs={{0,4},{4,0},{8,12},{12,8},{16,20},{20,16},{24,28},{28,24},{1,5},{5... | collective-permute-start | bytes 294920 | tf_op jit(solution)/shard_map/ppermute | solution.py:385
  7.7 7.5 %collective-permute-start.5 = (bf16[96,1024]{1,0:T(8,128)(2,1)S(1)}, bf16[96,1024]{1,0:T(8,128)(2,1)S(1)}, u32[]{:S(2)}, u32[]{:S(2)}) collective-permute-start(bf16[96,1024]{1,0:T(8,128)(2,1)S(1)} %get-tuple-element.20.query.refs_3_), channel_id=1, source_target_pairs={{0,8},{4,20},{8,0},{12,28},{16,24},{20,4},{24,16},{28,12},{1,9},{5... | collective-permute-start | bytes 589832 | tf_op jit(solution)/shard_map/ppermute | solution.py:385
  9.2 8.3 %collective-permute-start.4 = (bf16[96,1024]{1,0:T(8,128)(2,1)S(1)}, bf16[96,1024]{1,0:T(8,128)(2,1)S(1)}, u32[]{:S(2)}, u32[]{:S(2)}) collective-permute-start(bf16[96,1024]{1,0:T(8,128)(2,1)S(1)} %get-tuple-element.20.query.refs_3_), channel_id=1, source_target_pairs={{0,16},{4,12},{8,24},{12,4},{16,0},{20,28},{24,8},{28,20},{1,17},{... | collective-permute-start | bytes 589832 | tf_op jit(solution)/shard_map/ppermute | solution.py:385
  10.8 21.5 %slice-start = ((s8[8388608]{0:T(1024)(128)(4,1)}), s8[4194304]{0:T(1024)(128)(4,1)S(1)}, s32[]{:S(2)}) async-start(s8[8388608]{0:T(1024)(128)(4,1)} %bitcast.2), calls=%async_computation | async-start | bytes 8388608
  12.7 10.0 %collective-permute-start.2 = (bf16[96,1024]{1,0:T(8,128)(2,1)S(1)}, bf16[96,1024]{1,0:T(8,128)(2,1)S(1)}, u32[]{:S(2)}, u32[]{:S(2)}) collective-permute-start(bf16[96,1024]{1,0:T(8,128)(2,1)S(1)} %get-tuple-element.23), channel_id=1, source_target_pairs={{0,24},{4,28},{8,16},{12,20},{16,8},{20,12},{24,0},{28,4},{1,25},{... | collective-permute-start | bytes 589832 | tf_op jit(solution)/shard_map/ppermute | solution.py:385
  17.6 14.7 %slice-start.1 = ((s8[8388608]{0:T(1024)(128)(4,1)}), s8[4194304]{0:T(1024)(128)(4,1)S(1)}, s32[]{:S(2)}) async-start(s8[8388608]{0:T(1024)(128)(4,1)} %bitcast.2), calls=%async_computation.1 | async-start | bytes 8388608
  19.9 8.4 %collective-permute-start.6 = (bf16[96,1152]{1,0:T(8,128)(2,1)S(1)}, bf16[96,1152]{1,0:T(8,128)(2,1)S(1)}, u32[]{:S(2)}, u32[]{:S(2)}) collective-permute-start(bf16[96,1152]{1,0:T(8,128)(2,1)S(1)} %get-tuple-element.24), channel_id=1, source_target_pairs={{0,8},{4,20},{8,0},{12,28},{16,24},{20,4},{24,16},{28,12},{1,9},{5... | collective-permute-start | bytes 663560 | tf_op jit(solution)/shard_map/ppermute | solution.py:385
  21.5 9.4 %collective-permute-start.7 = (bf16[96,1152]{1,0:T(8,128)(2,1)S(1)}, bf16[96,1152]{1,0:T(8,128)(2,1)S(1)}, u32[]{:S(2)}, u32[]{:S(2)}) collective-permute-start(bf16[96,1152]{1,0:T(8,128)(2,1)S(1)} %get-tuple-element.25), channel_id=1, source_target_pairs={{0,16},{4,12},{8,24},{12,4},{16,0},{20,28},{24,8},{28,20},{1,17},{... | collective-permute-start | bytes 663560 | tf_op jit(solution)/shard_map/ppermute | solution.py:385
  25.0 7.3 %collective-permute-start.3 = (bf16[96,1152]{1,0:T(8,128)(2,1)S(1)}, bf16[96,1152]{1,0:T(8,128)(2,1)S(1)}, u32[]{:S(2)}, u32[]{:S(2)}) collective-permute-start(bf16[96,1152]{1,0:T(8,128)(2,1)S(1)} %attend.5), channel_id=1, source_target_pairs={{0,24},{4,28},{8,16},{12,20},{16,8},{20,12},{24,0},{28,4},{1,25},{... | collective-permute-start | bytes 663560 | tf_op jit(solution)/shard_map/ppermute | solution.py:385
  34.5 10.6 %collective-permute-start.10 = (bf16[96,1024]{1,0:T(8,128)(2,1)S(1)}, bf16[96,1024]{1,0:T(8,128)(2,1)S(1)}, u32[]{:S(2)}, u32[]{:S(2)}) collective-permute-start(bf16[96,1024]{1,0:T(8,128)(2,1)S(1)} %get-tuple-element.29), channel_id=1, source_target_pairs={{0,1},{1,3},{3,2},{2,0},{4,5},{5,7},{7,6},{6,4},{8,9},{9,11},{11,1... | collective-permute-start | bytes 589832 | tf_op jit(solution)/shard_map/ppermute | solution.py:396
  37.1 10.7 %collective-permute-start.8 = (bf16[96,1024]{1,0:T(8,128)(2,1)S(1)}, bf16[96,1024]{1,0:T(8,128)(2,1)S(1)}, u32[]{:S(2)}, u32[]{:S(2)}) collective-permute-start(bf16[96,1024]{1,0:T(8,128)(2,1)S(1)} %get-tuple-element.27), channel_id=1, source_target_pairs={{0,3},{3,0},{4,7},{7,4},{8,11},{11,8},{12,15},{15,12},{16,19},{19,... | collective-permute-start | bytes 589832 | tf_op jit(solution)/shard_map/ppermute | solution.py:394
  37.8 10.8 %collective-permute-start.9 = (bf16[96,1024]{1,0:T(8,128)(2,1)S(1)}, bf16[96,1024]{1,0:T(8,128)(2,1)S(1)}, u32[]{:S(2)}, u32[]{:S(2)}) collective-permute-start(bf16[96,1024]{1,0:T(8,128)(2,1)S(1)} %get-tuple-element.28), channel_id=1, source_target_pairs={{0,1},{1,0},{2,3},{3,2},{4,5},{5,4},{6,7},{7,6},{8,9},{9,8},{10,11... | collective-permute-start | bytes 589832 | tf_op jit(solution)/shard_map/ppermute | solution.py:385
  45.2 7.6 %collective-permute-start.11 = (bf16[96,1024]{1,0:T(8,128)(2,1)S(1)}, bf16[96,1024]{1,0:T(8,128)(2,1)S(1)}, u32[]{:S(2)}, u32[]{:S(2)}) collective-permute-start(bf16[96,1024]{1,0:T(8,128)(2,1)S(1)} %add_convert_fusion.1), channel_id=1, source_target_pairs={{1,2},{2,1},{5,6},{6,5},{9,10},{10,9},{13,14},{14,13},{17,18},{18,... | collective-permute-start | bytes 589832 | tf_op jit(solution)/shard_map/ppermute | solution.py:398

commit v9 on v8

--- a/solution.py
+++ b/solution.py
@@ -392,10 +392,11 @@
         me = lax.axis_index("head")
         ends = (me == 0) | (me == 3)
         far = lax.ppermute(blocks[3], "head", [(0, 3), (3, 0)])
-        beside = swap(blocks[1], "head", 1, size)
         step = lax.ppermute(blocks[2], "head", [(0, 1), (1, 3), (3, 2), (2, 0)])
         both = (blocks[3].astype(f32) + step.astype(f32)).astype(bf16)
+        late, both = lax.optimization_barrier((blocks[1], both))
         middle = lax.ppermute(both, "head", [(1, 2), (2, 1)])
+        beside = swap(late, "head", 1, size)
         arrived = [far, beside, jnp.where(ends, step, middle)]
     total = blocks[0]
     for block in arrived:

time: 53.7 us -> 54.7 us (1.019)
  starting transfers between devices: 17.4 us -> 18.6 us
  waiting for transfers between devices: 13.8 us -> 13.2 us
    ppermute x1, starting transfers between devices: 1.92 us -> 6.25 us  [sum_heads(): middle = lax.ppermute(both, 'head', [(1, 2), (2, 1)])]
    ppermute x9, starting transfers between devices: 12.2 us -> 9.03 us  [swap(): lax.ppermute(value, axis, [(at, at ^ (odd if at & 1 else even)) for at in...]
    ppermute x1, waiting for transfers between devices: 4.1 us -> 5.48 us  [sum_heads(): step = lax.ppermute(blocks[2], 'head', [(0, 1), (1, 3), (3, 2), (2, 0)])]
    ppermute x1, waiting for transfers between devices: 4.1 us -> 2.95 us  [sum_heads(): middle = lax.ppermute(both, 'head', [(1, 2), (2, 1)])]
    ppermute x9, waiting for transfers between devices: 5.62 us -> 4.76 us  [swap(): lax.ppermute(value, axis, [(at, at ^ (odd if at & 1 else even)) for at in...]
  transfers between devices with their start and end apart: 12 -> 12, of which waited for: 6 -> 5; matrix products, arithmetic and copies ran while one was open for 1% -> 1% of each run, Pallas kernels for 21% -> 21%
where the time goes in v9:
time: 54.7 us; the launch traced here: 54.1 us
  Pallas kernels  20 us (37%)
  starting transfers between devices  18.6 us (34%)
  waiting for transfers between devices  13.2 us (24%)
  other arithmetic  0.86 us (2%)
  between operations  0.79 us (1%)
  local copies, waits for them, and re-layouts  0.7 us (1%)
    pallas_call x4, Pallas kernels, attend(): pl.pallas_call(functools.partial(attend_kernel, partners, len(earlier)),...  9.43 us
    ppermute x9, starting transfers between devices, swap(): lax.ppermute(value, axis, [(at, at ^ (odd if at & 1 else even)) for at in...  9.03 us
    pallas_call x1, Pallas kernels, project(): pl.pallas_call(functools.partial(project_kernel, width), out_shape=(jax.S...  6.47 us
    ppermute x1, starting transfers between devices, sum_heads(): middle = lax.ppermute(both, 'head', [(1, 2), (2, 1)])  6.25 us
    ppermute x1, waiting for transfers between devices, sum_heads(): step = lax.ppermute(blocks[2], 'head', [(0, 1), (1, 3), (3, 2), (2, 0)])  5.48 us
    ppermute x9, waiting for transfers between devices, swap(): lax.ppermute(value, axis, [(at, at ^ (odd if at & 1 else even)) for at in...  4.76 us
    ppermute x1, waiting for transfers between devices, sum_heads(): middle = lax.ppermute(both, 'head', [(1, 2), (2, 1)])  2.95 us
    ppermute x1, starting transfers between devices, sum_heads(): step = lax.ppermute(blocks[2], 'head', [(0, 1), (1, 3), (3, 2), (2, 0)])  2.64 us
  transfers between devices with their start and end apart: 12, of which 5 were waited for; matrix products, arithmetic and copies ran while one was open for 1% of the time, Pallas kernels for 21%

profile of v9, /device:TPU:8, one launch (start us, length us, event | category | flops | bytes accessed | tf_op | source)
XLA Modules:
  0.0 54.1 jit_solution(13037757096858107127)
XLA Ops:
  0.7 6.5 %project.1 = (bf16[96,1024]{1,0:T(8,128)(2,1)S(1)}, bf16[96,512]{1,0:T(8,128)(2,1)S(1)}, s32[8,128]{1,0:T(8,128)S(1)}) custom-call(bf16[96,4096]{1,0:T(8,128)(2,1)} %hidden_any.1, f32[1,4096]{1,0:T(1,128)} %bitcast.6, s32[768]{0:T(1024)} %selected_any.1, f32[1,128]{1,0:T(1,128)} %constant.10.clone.freq_any, bf16[4096,1024]{1,0:T(8,128)(2,1)} %wq_any.1, ...), custom_call_target="tpu_custom_call" | custom-call | flops 1207959552 | bytes 13369344 | tf_op jit(solution)/shard_map/project/pallas_call | solution.py:103
  7.2 0.1 collective-permute-start
  7.2 0.5 collective-permute-start.1
  7.7 1.5 %collective-permute-start.5 = (bf16[96,1024]{1,0:T(8,128)(2,1)S(1)}, bf16[96,1024]{1,0:T(8,128)(2,1)S(1)}, u32[]{:S(2)}, u32[]{:S(2)}) collective-permute-start(bf16[96,1024]{1,0:T(8,128)(2,1)S(1)} %get-tuple-element.22.query.refs_3_), channel_id=1, source_target_pairs={{0,8},{4,20},{8,0},{12,28},{16,24},{20,4},{24,16},{28,12},{1,9},{5... | collective-permute-start | bytes 589832 | tf_op jit(solution)/shard_map/ppermute | solution.py:385
  9.2 1.5 %collective-permute-start.4 = (bf16[96,1024]{1,0:T(8,128)(2,1)S(1)}, bf16[96,1024]{1,0:T(8,128)(2,1)S(1)}, u32[]{:S(2)}, u32[]{:S(2)}) collective-permute-start(bf16[96,1024]{1,0:T(8,128)(2,1)S(1)} %get-tuple-element.22.query.refs_3_), channel_id=1, source_target_pairs={{0,16},{4,12},{8,24},{12,4},{16,0},{20,28},{24,8},{28,20},{1,17},{... | collective-permute-start | bytes 589832 | tf_op jit(solution)/shard_map/ppermute | solution.py:385
  10.7 0.0 collective-permute-done.1.kv_other
  10.7 0.0 collective-permute-done.stored_other
  10.8 0.0 slice-start
  10.8 1.9 %merge.1 = (bf16[2,1024,512]{2,1,0:T(8,128)(2,1)S(1)}, f32[2048,128]{1,0:T(8,128)S(1)}, bf16[96,1024]{1,0:T(8,128)(2,1)S(1)}) custom-call(s32[2]{0:T(128)S(1)} %copy-done.1, s32[2]{0:T(128)S(1)} %copy-done.2, s32[8,128]{1,0:T(8,128)S(1)} %get-tuple-element.18.selected.refs_2_, bf16[4096,128]{1,0:T(8,128)(2,1)S(1)} %bitcast.5, ...), custom_call_target="tpu_custom_call" | custom-call | flops 1000 | bytes 1000 | tf_op jit(solution)/shard_map/merge/pallas_call | solution.py:194
  12.7 1.8 %collective-permute-start.2 = (bf16[96,1024]{1,0:T(8,128)(2,1)S(1)}, bf16[96,1024]{1,0:T(8,128)(2,1)S(1)}, u32[]{:S(2)}, u32[]{:S(2)}) collective-permute-start(bf16[96,1024]{1,0:T(8,128)(2,1)S(1)} %get-tuple-element.25), channel_id=1, source_target_pairs={{0,24},{4,28},{8,16},{12,20},{16,8},{20,12},{24,0},{28,4},{1,25},{... | collective-permute-start | bytes 589832 | tf_op jit(solution)/shard_map/ppermute | solution.py:385
  14.4 0.8 %collective-permute-done.5.refs_3_ = bf16[96,1024]{1,0:T(8,128)(2,1)S(1)} collective-permute-done((bf16[96,1024]{1,0:T(8,128)(2,1)S(1)}, bf16[96,1024]{1,0:T(8,128)(2,1)S(1)}, u32[]{:S(2)}, u32[]{:S(2)}) %collective-permute-start.5) | collective-permute-done | bytes 196640 | tf_op jit(solution)/shard_map/ppermute | solution.py:385
  15.2 2.3 %attend.6.refs_4_ = bf16[96,1152]{1,0:T(8,128)(2,1)S(1)} custom-call(bf16[2,1024,512]{2,1,0:T(8,128)(2,1)S(1)} %get-tuple-element.23.refs_0_, f32[2048,128]{1,0:T(8,128)S(1)} %get-tuple-element.24.refs_1_, s32[8,128]{1,0:T(8,128)S(1)} %get-tuple-element.18.selected.refs_2_, bf16[96,1024]{1,0:T(8,128)(2,1)S(1)} %collective-permute-done.5.refs_3_), custom_call_target="tpu_custom_call" | custom-call | flops 1000 | bytes 1000 | tf_op jit(solution)/shard_map/attend/pallas_call | solution.py:312
  17.6 0.0 slice-start.1
  17.6 0.0 collective-permute-done.4.refs_3_
  17.6 2.3 %attend.7 = (bf16[96,1152]{1,0:T(8,128)(2,1)S(1)}, bf16[96,1152]{1,0:T(8,128)(2,1)S(1)}) custom-call(bf16[2,1024,512]{2,1,0:T(8,128)(2,1)S(1)} %get-tuple-element.23.refs_0_, f32[2048,128]{1,0:T(8,128)S(1)} %get-tuple-element.24.refs_1_, s32[8,128]{1,0:T(8,128)S(1)} %get-tuple-element.18.selected.refs_2_, ...), custom_call_target="tpu_custom_call" | custom-call | flops 1000 | bytes 1000 | tf_op jit(solution)/shard_map/attend/pallas_call | solution.py:312
  19.9 1.6 %collective-permute-start.6 = (bf16[96,1152]{1,0:T(8,128)(2,1)S(1)}, bf16[96,1152]{1,0:T(8,128)(2,1)S(1)}, u32[]{:S(2)}, u32[]{:S(2)}) collective-permute-start(bf16[96,1152]{1,0:T(8,128)(2,1)S(1)} %get-tuple-element.26), channel_id=1, source_target_pairs={{0,8},{4,20},{8,0},{12,28},{16,24},{20,4},{24,16},{28,12},{1,9},{5... | collective-permute-start | bytes 663560 | tf_op jit(solution)/shard_map/ppermute | solution.py:385
  21.5 1.2 %collective-permute-start.7 = (bf16[96,1152]{1,0:T(8,128)(2,1)S(1)}, bf16[96,1152]{1,0:T(8,128)(2,1)S(1)}, u32[]{:S(2)}, u32[]{:S(2)}) collective-permute-start(bf16[96,1152]{1,0:T(8,128)(2,1)S(1)} %get-tuple-element.27), channel_id=1, source_target_pairs={{0,16},{4,12},{8,24},{12,4},{16,0},{20,28},{24,8},{28,20},{1,17},{... | collective-permute-start | bytes 663560 | tf_op jit(solution)/shard_map/ppermute | solution.py:385
  22.7 2.3 %attend.5 = bf16[96,1152]{1,0:T(8,128)(2,1)S(1)} custom-call(bf16[2,1024,512]{2,1,0:T(8,128)(2,1)S(1)} %get-tuple-element.23.refs_0_, f32[2048,128]{1,0:T(8,128)S(1)} %get-tuple-element.24.refs_1_, s32[8,128]{1,0:T(8,128)S(1)} %get-tuple-element.18.selected.refs_2_, bf16[96,1024]{1,0:T(8,128)(2,1)S(1)} %collective-permute-done.2.refs_3_), custom_call_target="tpu_custom_call" | custom-call | flops 1000 | bytes 1000 | tf_op jit(solution)/shard_map/attend/pallas_call | solution.py:312
  25.0 0.9 %collective-permute-start.3 = (bf16[96,1152]{1,0:T(8,128)(2,1)S(1)}, bf16[96,1152]{1,0:T(8,128)(2,1)S(1)}, u32[]{:S(2)}, u32[]{:S(2)}) collective-permute-start(bf16[96,1152]{1,0:T(8,128)(2,1)S(1)} %attend.5), channel_id=1, source_target_pairs={{0,24},{4,28},{8,16},{12,20},{16,8},{20,12},{24,0},{28,4},{1,25},{... | collective-permute-start | bytes 663560 | tf_op jit(solution)/shard_map/ppermute | solution.py:385
  25.8 2.5 %attend.4.refs_0_ = bf16[96,1152]{1,0:T(8,128)(2,1)S(1)} custom-call(bf16[2,1024,512]{2,1,0:T(8,128)(2,1)S(1)} %get-tuple-element.23.refs_0_, f32[2048,128]{1,0:T(8,128)S(1)} %get-tuple-element.24.refs_1_, s32[8,128]{1,0:T(8,128)S(1)} %get-tuple-element.18.selected.refs_2_, bf16[96,1024]{1,0:T(8,128)(2,1)S(1)} %get-tuple-element.22.query.refs_3_), custom_call_target="tpu_custom_call" | custom-call | flops 1000 | bytes 1000 | tf_op jit(solution)/shard_map/attend/pallas_call | solution.py:312
  28.4 2.5 %collective-permute-done.7.refs_3_ = bf16[96,1152]{1,0:T(8,128)(2,1)S(1)} collective-permute-done((bf16[96,1152]{1,0:T(8,128)(2,1)S(1)}, bf16[96,1152]{1,0:T(8,128)(2,1)S(1)}, u32[]{:S(2)}, u32[]{:S(2)}) %collective-permute-start.7) | collective-permute-done | bytes 221216 | tf_op jit(solution)/shard_map/ppermute | solution.py:385
  30.9 1.4 %collective-permute-done.3.refs_1_ = bf16[96,1152]{1,0:T(8,128)(2,1)S(1)} collective-permute-done((bf16[96,1152]{1,0:T(8,128)(2,1)S(1)}, bf16[96,1152]{1,0:T(8,128)(2,1)S(1)}, u32[]{:S(2)}, u32[]{:S(2)}) %collective-permute-start.3) | collective-permute-done | bytes 221216 | tf_op jit(solution)/shard_map/ppermute | solution.py:385
  32.3 2.2 %finish.1 = (f32[96,1024]{1,0:T(8,128)S(1)}, bf16[96,1024]{1,0:T(8,128)(2,1)S(1)}, bf16[96,1024]{1,0:T(8,128)(2,1)S(1)}, bf16[96,1024]{1,0:T(8,128)(2,1)S(1)}) custom-call(bf16[96,1152]{1,0:T(8,128)(2,1)S(1)} %attend.4.refs_0_, bf16[96,1152]{1,0:T(8,128)(2,1)S(1)} %collective-permute-done.3.refs_1_, bf16[96,1152]{1,0:T(8,128)(2,1)S(1)} %collective-permute-done.6.refs_2_, ...), custom_call_target="tpu_custom_call" | custom-call | flops 805306368 | bytes 8388608 | tf_op jit(solution)/shard_map/finish/pallas_call | solution.py:367
  34.5 2.6 %collective-permute-start.9 = (bf16[96,1024]{1,0:T(8,128)(2,1)S(1)}, bf16[96,1024]{1,0:T(8,128)(2,1)S(1)}, u32[]{:S(2)}, u32[]{:S(2)}) collective-permute-start(bf16[96,1024]{1,0:T(8,128)(2,1)S(1)} %get-tuple-element.31), channel_id=1, source_target_pairs={{0,1},{1,3},{3,2},{2,0},{4,5},{5,7},{7,6},{6,4},{8,9},{9,11},{11,1... | collective-permute-start | bytes 589832 | tf_op jit(solution)/shard_map/ppermute | solution.py:395
  37.1 0.7 %collective-permute-start.8 = (bf16[96,1024]{1,0:T(8,128)(2,1)S(1)}, bf16[96,1024]{1,0:T(8,128)(2,1)S(1)}, u32[]{:S(2)}, u32[]{:S(2)}) collective-permute-start(bf16[96,1024]{1,0:T(8,128)(2,1)S(1)} %get-tuple-element.29), channel_id=1, source_target_pairs={{0,3},{3,0},{4,7},{7,4},{8,11},{11,8},{12,15},{15,12},{16,19},{19,... | collective-permute-start | bytes 589832 | tf_op jit(solution)/shard_map/ppermute | solution.py:394
  37.8 5.5 %collective-permute-done.9 = bf16[96,1024]{1,0:T(8,128)(2,1)S(1)} collective-permute-done((bf16[96,1024]{1,0:T(8,128)(2,1)S(1)}, bf16[96,1024]{1,0:T(8,128)(2,1)S(1)}, u32[]{:S(2)}, u32[]{:S(2)}) %collective-permute-start.9) | collective-permute-done | bytes 196640 | tf_op jit(solution)/shard_map/ppermute | solution.py:395
  43.3 0.1 collective-permute-start.10
  43.4 6.2 %collective-permute-start.11 = (bf16[96,1024]{1,0:T(8,128)(2,1)S(1)}, bf16[96,1024]{1,0:T(8,128)(2,1)S(1)}, u32[]{:S(2)}, u32[]{:S(2)}) collective-permute-start(bf16[96,1024]{1,0:T(8,128)(2,1)S(1)} %add_convert_fusion.1), channel_id=1, source_target_pairs={{1,2},{2,1},{5,6},{6,5},{9,10},{10,9},{13,14},{14,13},{17,18},{18,... | collective-permute-start | bytes 589832 | tf_op jit(solution)/shard_map/ppermute | solution.py:398
  49.6 0.7 %reshape.15 = bf16[96,2,2,128]{3,2,1,0:T(2,128)(2,1)} reshape(bf16[96,512]{1,0:T(8,128)(2,1)S(1)} %get-tuple-element.21.kv) | data formatting | bytes 196608 | tf_op jit(solution)/shard_map/reshape | solution.py:436
  50.3 0.0 collective-permute-done.8
  50.3 3.0 %collective-permute-done.11 = bf16[96,1024]{1,0:T(8,128)(2,1)S(1)} collective-permute-done((bf16[96,1024]{1,0:T(8,128)(2,1)S(1)}, bf16[96,1024]{1,0:T(8,128)(2,1)S(1)}, u32[]{:S(2)}, u32[]{:S(2)}) %collective-permute-start.11) | collective-permute-done | bytes 196640 | tf_op jit(solution)/shard_map/ppermute | solution.py:398
  53.3 0.8 %add_convert_fusion = bf16[96,1024]{1,0:T(8,128)(2,1)} fusion(bf16[96,1024]{1,0:T(8,128)(2,1)S(1)} %collective-permute-done.10, f32[96,1024]{1,0:T(8,128)S(1)} %get-tuple-element.28, bf16[96,1024]{1,0:T(8,128)(2,1)S(1)} %collective-permute-done.8, bf16[96,1024]{1,0:T(8,128)(2,1)S(1)} %collective-permute-done.9, ...), kind=kLoop, calls=%fused_computation | loop fusion | flops 786432 | bytes 1376257 | tf_op jit(solution)/shard_map/convert_element_type | solution.py:404
  (13 shorter events, 0.1 us)
Async XLA Ops:
  0.6 6.5 %copy-start = (bf16[1024,2,2,128]{3,2,1,0:T(2,128)(2,1)S(1)}, bf16[1024,2,2,128]{3,2,1,0:T(2,128)(2,1)}, u32[]{:S(2)}) copy-start(bf16[1024,2,2,128]{3,2,1,0:T(2,128)(2,1)} %param.17) | copy-start | bytes 3145732
  0.6 10.1 %copy-start.1 = (s32[2]{0:T(128)S(1)}, s32[2]{0:T(128)}, u32[]{:S(2)}) copy-start(s32[2]{0:T(128)} %order.1) | copy-start | bytes 28
  0.7 10.1 %copy-start.2 = (s32[2]{0:T(128)S(1)}, s32[2]{0:T(128)}, u32[]{:S(2)}) copy-start(s32[2]{0:T(128)} %slot.1) | copy-start | bytes 28
  7.2 3.6 %collective-permute-start = (bf16[4096,128]{1,0:T(8,128)(2,1)S(1)}, bf16[4096,128]{1,0:T(8,128)(2,1)S(1)}, u32[]{:S(2)}, u32[]{:S(2)}) collective-permute-start(bf16[4096,128]{1,0:T(8,128)(2,1)S(1)} %bitcast.4), channel_id=1, source_target_pairs={{0,4},{4,0},{8,12},{12,8},{16,20},{20,16},{24,28},{28,24},{1,5},{5... | collective-permute-start | bytes 3145736 | tf_op jit(solution)/shard_map/ppermute | solution.py:385
  7.2 3.5 %collective-permute-start.1 = (bf16[96,512]{1,0:T(8,128)(2,1)S(1)}, bf16[96,512]{1,0:T(8,128)(2,1)S(1)}, u32[]{:S(2)}, u32[]{:S(2)}) collective-permute-start(bf16[96,512]{1,0:T(8,128)(2,1)S(1)} %get-tuple-element.21.kv), channel_id=1, source_target_pairs={{0,4},{4,0},{8,12},{12,8},{16,20},{20,16},{24,28},{28,24},{1,5},{5... | collective-permute-start | bytes 294920 | tf_op jit(solution)/shard_map/ppermute | solution.py:385
  7.7 7.5 %collective-permute-start.5 = (bf16[96,1024]{1,0:T(8,128)(2,1)S(1)}, bf16[96,1024]{1,0:T(8,128)(2,1)S(1)}, u32[]{:S(2)}, u32[]{:S(2)}) collective-permute-start(bf16[96,1024]{1,0:T(8,128)(2,1)S(1)} %get-tuple-element.22.query.refs_3_), channel_id=1, source_target_pairs={{0,8},{4,20},{8,0},{12,28},{16,24},{20,4},{24,16},{28,12},{1,9},{5... | collective-permute-start | bytes 589832 | tf_op jit(solution)/shard_map/ppermute | solution.py:385
  9.2 8.3 %collective-permute-start.4 = (bf16[96,1024]{1,0:T(8,128)(2,1)S(1)}, bf16[96,1024]{1,0:T(8,128)(2,1)S(1)}, u32[]{:S(2)}, u32[]{:S(2)}) collective-permute-start(bf16[96,1024]{1,0:T(8,128)(2,1)S(1)} %get-tuple-element.22.query.refs_3_), channel_id=1, source_target_pairs={{0,16},{4,12},{8,24},{12,4},{16,0},{20,28},{24,8},{28,20},{1,17},{... | collective-permute-start | bytes 589832 | tf_op jit(solution)/shard_map/ppermute | solution.py:385
  10.8 21.5 %slice-start = ((s8[8388608]{0:T(1024)(128)(4,1)}), s8[4194304]{0:T(1024)(128)(4,1)S(1)}, s32[]{:S(2)}) async-start(s8[8388608]{0:T(1024)(128)(4,1)} %bitcast.2), calls=%async_computation | async-start | bytes 8388608
  12.7 10.0 %collective-permute-start.2 = (bf16[96,1024]{1,0:T(8,128)(2,1)S(1)}, bf16[96,1024]{1,0:T(8,128)(2,1)S(1)}, u32[]{:S(2)}, u32[]{:S(2)}) collective-permute-start(bf16[96,1024]{1,0:T(8,128)(2,1)S(1)} %get-tuple-element.25), channel_id=1, source_target_pairs={{0,24},{4,28},{8,16},{12,20},{16,8},{20,12},{24,0},{28,4},{1,25},{... | collective-permute-start | bytes 589832 | tf_op jit(solution)/shard_map/ppermute | solution.py:385
  17.6 14.7 %slice-start.1 = ((s8[8388608]{0:T(1024)(128)(4,1)}), s8[4194304]{0:T(1024)(128)(4,1)S(1)}, s32[]{:S(2)}) async-start(s8[8388608]{0:T(1024)(128)(4,1)} %bitcast.2), calls=%async_computation.1 | async-start | bytes 8388608
  19.9 8.4 %collective-permute-start.6 = (bf16[96,1152]{1,0:T(8,128)(2,1)S(1)}, bf16[96,1152]{1,0:T(8,128)(2,1)S(1)}, u32[]{:S(2)}, u32[]{:S(2)}) collective-permute-start(bf16[96,1152]{1,0:T(8,128)(2,1)S(1)} %get-tuple-element.26), channel_id=1, source_target_pairs={{0,8},{4,20},{8,0},{12,28},{16,24},{20,4},{24,16},{28,12},{1,9},{5... | collective-permute-start | bytes 663560 | tf_op jit(solution)/shard_map/ppermute | solution.py:385
  21.5 9.4 %collective-permute-start.7 = (bf16[96,1152]{1,0:T(8,128)(2,1)S(1)}, bf16[96,1152]{1,0:T(8,128)(2,1)S(1)}, u32[]{:S(2)}, u32[]{:S(2)}) collective-permute-start(bf16[96,1152]{1,0:T(8,128)(2,1)S(1)} %get-tuple-element.27), channel_id=1, source_target_pairs={{0,16},{4,12},{8,24},{12,4},{16,0},{20,28},{24,8},{28,20},{1,17},{... | collective-permute-start | bytes 663560 | tf_op jit(solution)/shard_map/ppermute | solution.py:385
  25.0 7.3 %collective-permute-start.3 = (bf16[96,1152]{1,0:T(8,128)(2,1)S(1)}, bf16[96,1152]{1,0:T(8,128)(2,1)S(1)}, u32[]{:S(2)}, u32[]{:S(2)}) collective-permute-start(bf16[96,1152]{1,0:T(8,128)(2,1)S(1)} %attend.5), channel_id=1, source_target_pairs={{0,24},{4,28},{8,16},{12,20},{16,8},{20,12},{24,0},{28,4},{1,25},{... | collective-permute-start | bytes 663560 | tf_op jit(solution)/shard_map/ppermute | solution.py:385
  34.5 8.8 %collective-permute-start.9 = (bf16[96,1024]{1,0:T(8,128)(2,1)S(1)}, bf16[96,1024]{1,0:T(8,128)(2,1)S(1)}, u32[]{:S(2)}, u32[]{:S(2)}) collective-permute-start(bf16[96,1024]{1,0:T(8,128)(2,1)S(1)} %get-tuple-element.31), channel_id=1, source_target_pairs={{0,1},{1,3},{3,2},{2,0},{4,5},{5,7},{7,6},{6,4},{8,9},{9,11},{11,1... | collective-permute-start | bytes 589832 | tf_op jit(solution)/shard_map/ppermute | solution.py:395
  37.1 13.2 %collective-permute-start.8 = (bf16[96,1024]{1,0:T(8,128)(2,1)S(1)}, bf16[96,1024]{1,0:T(8,128)(2,1)S(1)}, u32[]{:S(2)}, u32[]{:S(2)}) collective-permute-start(bf16[96,1024]{1,0:T(8,128)(2,1)S(1)} %get-tuple-element.29), channel_id=1, source_target_pairs={{0,3},{3,0},{4,7},{7,4},{8,11},{11,8},{12,15},{15,12},{16,19},{19,... | collective-permute-start | bytes 589832 | tf_op jit(solution)/shard_map/ppermute | solution.py:394
  43.3 7.0 %collective-permute-start.10 = (bf16[96,1024]{1,0:T(8,128)(2,1)S(1)}, bf16[96,1024]{1,0:T(8,128)(2,1)S(1)}, u32[]{:S(2)}, u32[]{:S(2)}) collective-permute-start(bf16[96,1024]{1,0:T(8,128)(2,1)S(1)} %get-tuple-element.32), channel_id=1, source_target_pairs={{0,1},{1,0},{2,3},{3,2},{4,5},{5,4},{6,7},{7,6},{8,9},{9,8},{10,11... | collective-permute-start | bytes 589832 | tf_op jit(solution)/shard_map/ppermute | solution.py:385
  43.4 9.9 %collective-permute-start.11 = (bf16[96,1024]{1,0:T(8,128)(2,1)S(1)}, bf16[96,1024]{1,0:T(8,128)(2,1)S(1)}, u32[]{:S(2)}, u32[]{:S(2)}) collective-permute-start(bf16[96,1024]{1,0:T(8,128)(2,1)S(1)} %add_convert_fusion.1), channel_id=1, source_target_pairs={{1,2},{2,1},{5,6},{6,5},{9,10},{10,9},{13,14},{14,13},{17,18},{18,... | collective-permute-start | bytes 589832 | tf_op jit(solution)/shard_map/ppermute | solution.py:398

commit v10 on v8

--- a/solution.py
+++ b/solution.py
@@ -207,14 +207,13 @@
     )(order, slot, selected, stored, stored_other, kv, kv_other, query)
 
 
-def attend_kernel(partners, carried, *refs):
+def attend_kernel(partners, *refs):
     count = len(partners)
     cache, key_pos, selected = refs[:3]
     queries = refs[3 : 3 + count]
-    scores, weights, masks = refs[-3:]
-    for source, target in zip(refs[3 + count :], refs[3 + count + carried : -3 - count]):
-        target[...] = source[...]
-    outs = refs[-3 - count : -3]
+    outs = refs[3 + count : 3 + 2 * count]
+    levels = refs[3 + 2 * count : 3 + 3 * count]
+    scores, weights, masks = refs[3 + 3 * count :]
     _, shard, cols = cache.shape
     rows = queries[0].shape[0]
     kv_heads = cols // (2 * HEAD_DIM)
@@ -223,7 +222,8 @@
     step = 256
     scale = math.log2(math.e) / HEAD_DIM**0.5
     me = lax.axis_index("seq")
-    one_hot = (iota((rows, LANES), 0) == iota((rows, LANES), 1)).astype(f32).astype(bf16)
+    diagonal = iota((rows, LANES), 0) == iota((rows, LANES), 1)
+    one_hot = diagonal.astype(f32).astype(bf16)
     ones = jnp.ones((keys, LANES), bf16)
 
     def mask(at):
@@ -282,38 +282,28 @@
             total = summed[:, HEAD_DIM : HEAD_DIM + LANES]
             context = (summed[:, :HEAD_DIM] / total).astype(bf16)
             level = top + jnp.log2(total)
-            high = level.astype(bf16).astype(f32)
-            middle = (level - high).astype(bf16).astype(f32)
-            low = level - high - middle
-            lane = iota((rows, LANES), 1)
-            out = outs[old_at]
-            packed = jnp.zeros((rows, LANES), f32)
             for member in range(GROUP):
                 which = old_head * GROUP + member
                 span = slice(member * rows, (member + 1) * rows)
-                out[:, which * HEAD_DIM : (which + 1) * HEAD_DIM] = context[span]
-                for piece, source in enumerate((high, middle, low)):
-                    packed = jnp.where(lane == piece * heads + which, source[span], packed)
-            tail = slice(heads * HEAD_DIM, heads * HEAD_DIM + LANES)
-            if old_head:
-                packed = packed + out[:, tail].astype(f32)
-            out[:, tail] = packed.astype(bf16)
-
-
-def attend(partners, cache, key_pos, selected, queries, earlier=()):
+                outs[old_at][:, which * HEAD_DIM : (which + 1) * HEAD_DIM] = context[span]
+                levels[old_at][which : which + 1, :] = jnp.sum(
+                    jnp.where(diagonal, level[span], 0.0), 0, keepdims=True
+                )
+
+
+def attend(partners, cache, key_pos, selected, queries):
     _, shard, cols = cache.shape
-    rows = queries[0].shape[0]
-    kv_heads = cols // (2 * HEAD_DIM)
-    out_cols = queries[0].shape[1] + LANES
+    rows, q_cols = queries[0].shape
     tall = GROUP * rows
     keys = 2 * shard
     count = len(queries)
     vmem = pl.BlockSpec(memory_space=pltpu.VMEM)
     out = pl.pallas_call(
-        functools.partial(attend_kernel, partners, len(earlier)),
-        out_shape=[jax.ShapeDtypeStruct((rows, out_cols), bf16)] * (len(earlier) + count),
-        in_specs=[vmem] * (3 + count + len(earlier)),
-        out_specs=[vmem] * (len(earlier) + count),
+        functools.partial(attend_kernel, partners),
+        out_shape=[jax.ShapeDtypeStruct((rows, q_cols), bf16)] * count
+        + [jax.ShapeDtypeStruct((q_cols // HEAD_DIM, LANES), f32)] * count,
+        in_specs=[vmem] * (3 + count),
+        out_specs=[vmem] * (2 * count),
         scratch_shapes=[
             pltpu.VMEM((2, tall, keys), f32),
             pltpu.VMEM((tall, keys), bf16),
@@ -322,31 +312,28 @@
         compiler_params=pltpu.CompilerParams(vmem_limit_bytes=24 * MIB),
         cost_estimate=pl.CostEstimate(flops=1000, bytes_accessed=1000, transcendentals=0),
         name="attend",
-    )(cache, key_pos, selected, *queries, *earlier)
-    return list(out)
+    )(cache, key_pos, selected, *queries)
+    return list(zip(out[:count], out[count:]))
 
 
 def finish_kernel(count, size, *refs):
     parts = refs[:count]
-    weights = refs[count]
-    outs = refs[count + 1 : count + 1 + size]
-    (context,) = refs[count + 1 + size :]
-    feat = context.shape[1]
-    heads = feat // HEAD_DIM
+    levels = [ref[...] for ref in refs[count : 2 * count]]
+    weights = refs[2 * count]
+    outs = refs[2 * count + 1 : 2 * count + 1 + size]
+    (context,) = refs[2 * count + 1 + size :]
+    rows, feat = context.shape
     width = weights.shape[1] // size
     me = lax.axis_index("head")
-    tails = [part[:, feat : feat + LANES].astype(f32) for part in parts]
-    for head in range(heads):
-        levels = []
-        for tail in tails:
-            pieces = [tail[:, piece * heads + head : piece * heads + head + 1] for piece in range(3)]
-            levels.append(pieces[0] + pieces[1] + pieces[2])
-        top = functools.reduce(jnp.maximum, levels)
-        shares = [jnp.exp2(level - top) for level in levels]
-        whole = functools.reduce(jnp.add, shares)
+    top = functools.reduce(jnp.maximum, levels)
+    shares = [jnp.exp2(level - top) for level in levels]
+    whole = functools.reduce(jnp.add, shares)
+    shares = [jnp.transpose(share / whole) for share in shares]
+    for head in range(feat // HEAD_DIM):
         span = slice(head * HEAD_DIM, (head + 1) * HEAD_DIM)
         mixed = functools.reduce(
-            jnp.add, [(share / whole) * part[:, span].astype(f32) for share, part in zip(shares, parts)]
+            jnp.add,
+            [share[:rows, head : head + 1] * part[:, span].astype(f32) for share, part in zip(shares, parts)],
         )
         context[:, span] = mixed.astype(bf16)
     for turn in range(size):
@@ -359,7 +346,8 @@
             ).astype(outs[turn].dtype)
 
 
-def finish(parts, w_out, size):
+def finish(pairs, w_out, size):
+    parts, levels = zip(*pairs)
     rows = parts[0].shape[0]
     feat, cols = w_out.shape
     width = cols // size
@@ -367,7 +355,7 @@
     return pl.pallas_call(
         functools.partial(finish_kernel, len(parts), size),
         out_shape=[jax.ShapeDtypeStruct((rows, width), f32 if turn == 0 else bf16) for turn in range(size)],
-        in_specs=[vmem] * (len(parts) + 1),
+        in_specs=[vmem] * (2 * len(parts) + 1),
         out_specs=[vmem] * size,
         scratch_shapes=[
             pltpu.VMEM((rows, feat), bf16),
@@ -377,7 +365,7 @@
             flops=2 * rows * feat * cols, bytes_accessed=2 * feat * cols, transcendentals=0
         ),
         name="finish",
-    )(*parts, w_out)
+    )(*parts, *levels, w_out)
 
 
 def swap(value, axis, turn, size):
@@ -391,9 +379,9 @@
     else:
         me = lax.axis_index("head")
         ends = (me == 0) | (me == 3)
+        step = lax.ppermute(blocks[2], "head", [(0, 1), (1, 3), (3, 2), (2, 0)])
         far = lax.ppermute(blocks[3], "head", [(0, 3), (3, 0)])
         beside = swap(blocks[1], "head", 1, size)
-        step = lax.ppermute(blocks[2], "head", [(0, 1), (1, 3), (3, 2), (2, 0)])
         both = (blocks[3].astype(f32) + step.astype(f32)).astype(bf16)
         middle = lax.ppermute(both, "head", [(1, 2), (2, 1)])
         arrived = [far, beside, jnp.where(ends, step, middle)]
@@ -423,14 +411,16 @@
         prompt_order, store_slot, table, stored, stored_other, kv, kv_other, query
     )
     queries |= {turn: swap(late, "seq", turn, seq_count) for turn in rest}
-    parts = [attend(((0, 0),), cache, key_pos, table, [query])[0]]
+    pairs = attend(((0, 0),), cache, key_pos, table, [query])
+
+    def give_back(turns):
+        for turn, pair in zip(turns, attend(turns, cache, key_pos, table, [queries[turn] for turn in turns])):
+            pairs.append(tuple(swap(value, "seq", turn, seq_count) for value in pair))
+
     for turn in rest:
-        (part,) = attend((turn,), cache, key_pos, table, [queries[turn]])
-        parts.append(swap(part, "seq", turn, seq_count))
-    done = attend((first,), cache, key_pos, table, [queries[first]])
-    done = attend((second,), cache, key_pos, table, [queries[second]], done)
-    parts += [swap(part, "seq", turn, seq_count) for turn, part in zip((first, second), done)]
-    blocks = finish(parts, w_out, head_count)
+        give_back((turn,))
+    give_back((first, second))
+    blocks = finish(pairs, w_out, head_count)
     total = sum_heads(blocks, head_count)
     new_kv = kv.reshape(rows, 2, local_kv, HEAD_DIM)
     return (total, new_kv)

time: 53.7 us -> 58.5 us (1.089)
  starting transfers between devices: 17.4 us -> 22.4 us
    ppermute x9 -> x12, starting transfers between devices: 12.2 us -> 17.2 us  [swap(): lax.ppermute(value, axis, [(at, at ^ (odd if at & 1 else even)) for at in...]
    ppermute x9 -> x12, waiting for transfers between devices: 5.62 us -> 4.05 us  [swap(): lax.ppermute(value, axis, [(at, at ^ (odd if at & 1 else even)) for at in...]
    ppermute x1, waiting for transfers between devices: 4.1 us -> 5.25 us  [sum_heads(): step = lax.ppermute(blocks[2], 'head', [(0, 1), (1, 3), (3, 2), (2, 0)])]
    pallas_call x4 -> x3, Pallas kernels: 9.43 us -> 9.1 us  [attend(): pl.pallas_call(functools.partial(attend_kernel, partners), out_shape=[jax...]
  transfers between devices with their start and end apart: 12 -> 15, of which waited for: 6 -> 5; matrix products, arithmetic and copies ran while one was open for 1% -> 1% of each run, Pallas kernels for 21% -> 19%
where the time goes in v10:
time: 58.5 us; the launch traced here: 58.3 us
  starting transfers between devices  22.4 us (38%)
  Pallas kernels  19.6 us (34%)
  waiting for transfers between devices  14 us (24%)
  other arithmetic  0.86 us (1%)
  between operations  0.8 us (1%)
  local copies, waits for them, and re-layouts  0.68 us (1%)
    ppermute x12, starting transfers between devices, swap(): lax.ppermute(value, axis, [(at, at ^ (odd if at & 1 else even)) for at in...  17.2 us
    pallas_call x3, Pallas kernels, attend(): pl.pallas_call(functools.partial(attend_kernel, partners), out_shape=[jax...  9.1 us
    pallas_call x1, Pallas kernels, project(): pl.pallas_call(functools.partial(project_kernel, width), out_shape=(jax.S...  6.47 us
    ppermute x1, waiting for transfers between devices, sum_heads(): step = lax.ppermute(blocks[2], 'head', [(0, 1), (1, 3), (3, 2), (2, 0)])  5.25 us
    ppermute x1, waiting for transfers between devices, sum_heads(): middle = lax.ppermute(both, 'head', [(1, 2), (2, 1)])  4.66 us
    ppermute x12, waiting for transfers between devices, swap(): lax.ppermute(value, axis, [(at, at ^ (odd if at & 1 else even)) for at in...  4.05 us
    ppermute x1, starting transfers between devices, sum_heads(): step = lax.ppermute(blocks[2], 'head', [(0, 1), (1, 3), (3, 2), (2, 0)])  2.64 us
    pallas_call x1, Pallas kernels, finish(): pl.pallas_call(functools.partial(finish_kernel, len(parts), size), out_sh...  2.19 us
  transfers between devices with their start and end apart: 15, of which 5 were waited for; matrix products, arithmetic and copies ran while one was open for 1% of the time, Pallas kernels for 19%

profile of v10, /device:TPU:8, one launch (start us, length us, event | category | flops | bytes accessed | tf_op | source)
XLA Modules:
  0.0 58.3 jit_solution(18087834537871638471)
XLA Ops:
  0.7 6.5 %project.1 = (bf16[96,1024]{1,0:T(8,128)(2,1)S(1)}, bf16[96,512]{1,0:T(8,128)(2,1)S(1)}, s32[8,128]{1,0:T(8,128)S(1)}) custom-call(bf16[96,4096]{1,0:T(8,128)(2,1)} %hidden_any.1, f32[1,4096]{1,0:T(1,128)} %bitcast.4, s32[768]{0:T(1024)} %selected_any.1, f32[1,128]{1,0:T(1,128)} %constant.10.clone.freq_any, bf16[4096,1024]{1,0:T(8,128)(2,1)} %wq_any.1, ...), custom_call_target="tpu_custom_call" | custom-call | flops 1207959552 | bytes 13369344 | tf_op jit(solution)/shard_map/project/pallas_call | solution.py:103
  7.2 0.1 collective-permute-start
  7.2 0.5 collective-permute-start.1
  7.7 1.5 %collective-permute-start.4 = (bf16[96,1024]{1,0:T(8,128)(2,1)S(1)}, bf16[96,1024]{1,0:T(8,128)(2,1)S(1)}, u32[]{:S(2)}, u32[]{:S(2)}) collective-permute-start(bf16[96,1024]{1,0:T(8,128)(2,1)S(1)} %get-tuple-element.26.query.refs_3_), channel_id=1, source_target_pairs={{0,8},{4,20},{8,0},{12,28},{16,24},{20,4},{24,16},{28,12},{1,9},{5... | collective-permute-start | bytes 589832 | tf_op jit(solution)/shard_map/ppermute | solution.py:373
  9.2 1.5 %collective-permute-start.5 = (bf16[96,1024]{1,0:T(8,128)(2,1)S(1)}, bf16[96,1024]{1,0:T(8,128)(2,1)S(1)}, u32[]{:S(2)}, u32[]{:S(2)}) collective-permute-start(bf16[96,1024]{1,0:T(8,128)(2,1)S(1)} %get-tuple-element.26.query.refs_3_), channel_id=1, source_target_pairs={{0,16},{4,12},{8,24},{12,4},{16,0},{20,28},{24,8},{28,20},{1,17},{... | collective-permute-start | bytes 589832 | tf_op jit(solution)/shard_map/ppermute | solution.py:373
  10.7 0.0 collective-permute-done.1.kv_other
  10.7 0.0 collective-permute-done.stored_other
  10.8 1.9 %merge.1 = (bf16[2,1024,512]{2,1,0:T(8,128)(2,1)S(1)}, f32[2048,128]{1,0:T(8,128)S(1)}, bf16[96,1024]{1,0:T(8,128)(2,1)S(1)}) custom-call(s32[2]{0:T(128)S(1)} %copy-done.2, s32[2]{0:T(128)S(1)} %copy-done.3, s32[8,128]{1,0:T(8,128)S(1)} %get-tuple-element.22.selected.refs_2_, bf16[4096,128]{1,0:T(8,128)(2,1)S(1)} %bitcast.3, ...), custom_call_target="tpu_custom_call" | custom-call | flops 1000 | bytes 1000 | tf_op jit(solution)/shard_map/merge/pallas_call | solution.py:194
  12.6 1.8 %collective-permute-start.2 = (bf16[96,1024]{1,0:T(8,128)(2,1)S(1)}, bf16[96,1024]{1,0:T(8,128)(2,1)S(1)}, u32[]{:S(2)}, u32[]{:S(2)}) collective-permute-start(bf16[96,1024]{1,0:T(8,128)(2,1)S(1)} %get-tuple-element.30), channel_id=1, source_target_pairs={{0,24},{4,28},{8,16},{12,20},{16,8},{20,12},{24,0},{28,4},{1,25},{... | collective-permute-start | bytes 589832 | tf_op jit(solution)/shard_map/ppermute | solution.py:373
  14.4 0.8 %collective-permute-done.4.refs_3_ = bf16[96,1024]{1,0:T(8,128)(2,1)S(1)} collective-permute-done((bf16[96,1024]{1,0:T(8,128)(2,1)S(1)}, bf16[96,1024]{1,0:T(8,128)(2,1)S(1)}, u32[]{:S(2)}, u32[]{:S(2)}) %collective-permute-start.4) | collective-permute-done | bytes 196640 | tf_op jit(solution)/shard_map/ppermute | solution.py:373
  15.2 0.0 collective-permute-done.5.refs_4_
  15.3 4.5 %attend.5 = (bf16[96,1024]{1,0:T(8,128)(2,1)S(1)}, bf16[96,1024]{1,0:T(8,128)(2,1)S(1)}, f32[8,128]{1,0:T(8,128)S(1)}, f32[8,128]{1,0:T(8,128)S(1)}) custom-call(bf16[2,1024,512]{2,1,0:T(8,128)(2,1)S(1)} %get-tuple-element.27.refs_0_, f32[2048,128]{1,0:T(8,128)S(1)} %get-tuple-element.28.refs_1_, s32[8,128]{1,0:T(8,128)S(1)} %get-tuple-element.22.selected.refs_2_, ...), custom_call_target="tpu_custom_call" | custom-call | flops 1000 | bytes 1000 | tf_op jit(solution)/shard_map/attend/pallas_call | solution.py:301
  19.7 1.6 %collective-permute-start.6 = (bf16[96,1024]{1,0:T(8,128)(2,1)S(1)}, bf16[96,1024]{1,0:T(8,128)(2,1)S(1)}, u32[]{:S(2)}, u32[]{:S(2)}) collective-permute-start(bf16[96,1024]{1,0:T(8,128)(2,1)S(1)} %get-tuple-element.32), channel_id=1, source_target_pairs={{0,8},{4,20},{8,0},{12,28},{16,24},{20,4},{24,16},{28,12},{1,9},{5... | collective-permute-start | bytes 589832 | tf_op jit(solution)/shard_map/ppermute | solution.py:373
  21.3 1.3 %collective-permute-start.7 = (bf16[96,1024]{1,0:T(8,128)(2,1)S(1)}, bf16[96,1024]{1,0:T(8,128)(2,1)S(1)}, u32[]{:S(2)}, u32[]{:S(2)}) collective-permute-start(bf16[96,1024]{1,0:T(8,128)(2,1)S(1)} %get-tuple-element.33), channel_id=1, source_target_pairs={{0,16},{4,12},{8,24},{12,4},{16,0},{20,28},{24,8},{28,20},{1,17},{... | collective-permute-start | bytes 589832 | tf_op jit(solution)/shard_map/ppermute | solution.py:373
  22.5 0.0 collective-permute-done.2.refs_3_
  22.5 2.2 %attend.4 = (bf16[96,1024]{1,0:T(8,128)(2,1)S(1)}, f32[8,128]{1,0:T(8,128)S(1)}) custom-call(bf16[2,1024,512]{2,1,0:T(8,128)(2,1)S(1)} %get-tuple-element.27.refs_0_, f32[2048,128]{1,0:T(8,128)S(1)} %get-tuple-element.28.refs_1_, s32[8,128]{1,0:T(8,128)S(1)} %get-tuple-element.22.selected.refs_2_, bf16[96,1024]{1,0:T(8,128)(2,1)S(1)} %collective-permute-done.2.refs_3_), custom_call_target="tpu_custom_call" | custom-call | flops 1000 | bytes 1000 | tf_op jit(solution)/shard_map/attend/pallas_call | solution.py:301
  24.8 0.8 %collective-permute-start.3 = (bf16[96,1024]{1,0:T(8,128)(2,1)S(1)}, bf16[96,1024]{1,0:T(8,128)(2,1)S(1)}, u32[]{:S(2)}, u32[]{:S(2)}) collective-permute-start(bf16[96,1024]{1,0:T(8,128)(2,1)S(1)} %get-tuple-element.31), channel_id=1, source_target_pairs={{0,24},{4,28},{8,16},{12,20},{16,8},{20,12},{24,0},{28,4},{1,25},{... | collective-permute-start | bytes 589832 | tf_op jit(solution)/shard_map/ppermute | solution.py:373
  25.6 1.2 %collective-permute-start.10 = (f32[8,128]{1,0:T(8,128)S(1)}, f32[8,128]{1,0:T(8,128)S(1)}, u32[]{:S(2)}, u32[]{:S(2)}) collective-permute-start(f32[8,128]{1,0:T(8,128)S(1)} %get-tuple-element.37), channel_id=1, source_target_pairs={{0,16},{4,12},{8,24},{12,4},{16,0},{20,28},{24,8},{28,20},{1,17},{... | collective-permute-start | bytes 12296 | tf_op jit(solution)/shard_map/ppermute | solution.py:373
  26.7 1.6 %collective-permute-start.9 = (f32[8,128]{1,0:T(8,128)S(1)}, f32[8,128]{1,0:T(8,128)S(1)}, u32[]{:S(2)}, u32[]{:S(2)}) collective-permute-start(f32[8,128]{1,0:T(8,128)S(1)} %get-tuple-element.36), channel_id=1, source_target_pairs={{0,8},{4,20},{8,0},{12,28},{16,24},{20,4},{24,16},{28,12},{1,9},{5... | collective-permute-start | bytes 12296 | tf_op jit(solution)/shard_map/ppermute | solution.py:373
  28.3 1.2 %collective-permute-done.10.refs_7_ = f32[8,128]{1,0:T(8,128)S(1)} collective-permute-done((f32[8,128]{1,0:T(8,128)S(1)}, f32[8,128]{1,0:T(8,128)S(1)}, u32[]{:S(2)}, u32[]{:S(2)}) %collective-permute-start.10) | collective-permute-done | bytes 4128 | tf_op jit(solution)/shard_map/ppermute | solution.py:373
  29.5 2.2 %collective-permute-start.8 = (f32[8,128]{1,0:T(8,128)S(1)}, f32[8,128]{1,0:T(8,128)S(1)}, u32[]{:S(2)}, u32[]{:S(2)}) collective-permute-start(f32[8,128]{1,0:T(8,128)S(1)} %get-tuple-element.35), channel_id=1, source_target_pairs={{0,24},{4,28},{8,16},{12,20},{16,8},{20,12},{24,0},{28,4},{1,25},{... | collective-permute-start | bytes 12296 | tf_op jit(solution)/shard_map/ppermute | solution.py:373
  31.8 2.4 %attend.3 = (bf16[96,1024]{1,0:T(8,128)(2,1)S(1)}, f32[8,128]{1,0:T(8,128)S(1)}) custom-call(bf16[2,1024,512]{2,1,0:T(8,128)(2,1)S(1)} %get-tuple-element.27.refs_0_, f32[2048,128]{1,0:T(8,128)S(1)} %get-tuple-element.28.refs_1_, s32[8,128]{1,0:T(8,128)S(1)} %get-tuple-element.22.selected.refs_2_, bf16[96,1024]{1,0:T(8,128)(2,1)S(1)} %get-tuple-element.26.query.refs_3_), custom_call_target="tpu_custom_call" | custom-call | flops 1000 | bytes 1000 | tf_op jit(solution)/shard_map/attend/pallas_call | solution.py:301
  34.2 2.2 %finish.1 = (f32[96,1024]{1,0:T(8,128)S(1)}, bf16[96,1024]{1,0:T(8,128)(2,1)S(1)}, bf16[96,1024]{1,0:T(8,128)(2,1)S(1)}, bf16[96,1024]{1,0:T(8,128)(2,1)S(1)}) custom-call(bf16[96,1024]{1,0:T(8,128)(2,1)S(1)} %get-tuple-element.29.refs_0_, bf16[96,1024]{1,0:T(8,128)(2,1)S(1)} %collective-permute-done.3.refs_1_, ...), custom_call_target="tpu_custom_call" | custom-call | flops 805306368 | bytes 8388608 | tf_op jit(solution)/shard_map/finish/pallas_call | solution.py:355
  36.4 2.6 %collective-permute-start.13 = (bf16[96,1024]{1,0:T(8,128)(2,1)S(1)}, bf16[96,1024]{1,0:T(8,128)(2,1)S(1)}, u32[]{:S(2)}, u32[]{:S(2)}) collective-permute-start(bf16[96,1024]{1,0:T(8,128)(2,1)S(1)} %get-tuple-element.41), channel_id=1, source_target_pairs={{0,1},{1,3},{3,2},{2,0},{4,5},{5,7},{7,6},{6,4},{8,9},{9,11},{11,1... | collective-permute-start | bytes 589832 | tf_op jit(solution)/shard_map/ppermute | solution.py:382
  39.1 0.7 %collective-permute-start.11 = (bf16[96,1024]{1,0:T(8,128)(2,1)S(1)}, bf16[96,1024]{1,0:T(8,128)(2,1)S(1)}, u32[]{:S(2)}, u32[]{:S(2)}) collective-permute-start(bf16[96,1024]{1,0:T(8,128)(2,1)S(1)} %get-tuple-element.39), channel_id=1, source_target_pairs={{0,3},{3,0},{4,7},{7,4},{8,11},{11,8},{12,15},{15,12},{16,19},{19,... | collective-permute-start | bytes 589832 | tf_op jit(solution)/shard_map/ppermute | solution.py:383
  39.7 3.2 %collective-permute-start.12 = (bf16[96,1024]{1,0:T(8,128)(2,1)S(1)}, bf16[96,1024]{1,0:T(8,128)(2,1)S(1)}, u32[]{:S(2)}, u32[]{:S(2)}) collective-permute-start(bf16[96,1024]{1,0:T(8,128)(2,1)S(1)} %get-tuple-element.40), channel_id=1, source_target_pairs={{0,1},{1,0},{2,3},{3,2},{4,5},{5,4},{6,7},{7,6},{8,9},{9,8},{10,11... | collective-permute-start | bytes 589832 | tf_op jit(solution)/shard_map/ppermute | solution.py:373
  43.0 5.2 %collective-permute-done.13 = bf16[96,1024]{1,0:T(8,128)(2,1)S(1)} collective-permute-done((bf16[96,1024]{1,0:T(8,128)(2,1)S(1)}, bf16[96,1024]{1,0:T(8,128)(2,1)S(1)}, u32[]{:S(2)}, u32[]{:S(2)}) %collective-permute-start.13) | collective-permute-done | bytes 196640 | tf_op jit(solution)/shard_map/ppermute | solution.py:382
  48.3 1.9 %collective-permute-start.14 = (bf16[96,1024]{1,0:T(8,128)(2,1)S(1)}, bf16[96,1024]{1,0:T(8,128)(2,1)S(1)}, u32[]{:S(2)}, u32[]{:S(2)}) collective-permute-start(bf16[96,1024]{1,0:T(8,128)(2,1)S(1)} %add_convert_fusion.1), channel_id=1, source_target_pairs={{1,2},{2,1},{5,6},{6,5},{9,10},{10,9},{13,14},{14,13},{17,18},{18,... | collective-permute-start | bytes 589832 | tf_op jit(solution)/shard_map/ppermute | solution.py:386
  50.2 0.7 %reshape.15 = bf16[96,2,2,128]{3,2,1,0:T(2,128)(2,1)} reshape(bf16[96,512]{1,0:T(8,128)(2,1)S(1)} %get-tuple-element.25.kv) | data formatting | bytes 196608 | tf_op jit(solution)/shard_map/reshape | solution.py:425
  50.9 2.0 %collective-permute-done.12 = bf16[96,1024]{1,0:T(8,128)(2,1)S(1)} collective-permute-done((bf16[96,1024]{1,0:T(8,128)(2,1)S(1)}, bf16[96,1024]{1,0:T(8,128)(2,1)S(1)}, u32[]{:S(2)}, u32[]{:S(2)}) %collective-permute-start.12) | collective-permute-done | bytes 196640 | tf_op jit(solution)/shard_map/ppermute | solution.py:373
  52.8 4.7 %collective-permute-done.14 = bf16[96,1024]{1,0:T(8,128)(2,1)S(1)} collective-permute-done((bf16[96,1024]{1,0:T(8,128)(2,1)S(1)}, bf16[96,1024]{1,0:T(8,128)(2,1)S(1)}, u32[]{:S(2)}, u32[]{:S(2)}) %collective-permute-start.14) | collective-permute-done | bytes 196640 | tf_op jit(solution)/shard_map/ppermute | solution.py:386
  57.5 0.8 %add_convert_fusion = bf16[96,1024]{1,0:T(8,128)(2,1)} fusion(bf16[96,1024]{1,0:T(8,128)(2,1)S(1)} %collective-permute-done.12, f32[96,1024]{1,0:T(8,128)S(1)} %get-tuple-element.38, bf16[96,1024]{1,0:T(8,128)(2,1)S(1)} %collective-permute-done.11, bf16[96,1024]{1,0:T(8,128)(2,1)S(1)} %collective-permute-done.13, ...), kind=kLoop, calls=%fused_computation | loop fusion | flops 786432 | bytes 1376257 | tf_op jit(solution)/shard_map/convert_element_type | solution.py:391
  (15 shorter events, 0.1 us)
Async XLA Ops:
  0.6 6.5 %copy-start.1 = (bf16[1024,2,2,128]{3,2,1,0:T(2,128)(2,1)S(1)}, bf16[1024,2,2,128]{3,2,1,0:T(2,128)(2,1)}, u32[]{:S(2)}) copy-start(bf16[1024,2,2,128]{3,2,1,0:T(2,128)(2,1)} %param.17) | copy-start | bytes 3145732
  0.6 10.1 %copy-start.2 = (s32[2]{0:T(128)S(1)}, s32[2]{0:T(128)}, u32[]{:S(2)}) copy-start(s32[2]{0:T(128)} %order.1) | copy-start | bytes 28
  0.7 10.1 %copy-start.3 = (s32[2]{0:T(128)S(1)}, s32[2]{0:T(128)}, u32[]{:S(2)}) copy-start(s32[2]{0:T(128)} %slot.1) | copy-start | bytes 28
  7.2 3.6 %collective-permute-start = (bf16[4096,128]{1,0:T(8,128)(2,1)S(1)}, bf16[4096,128]{1,0:T(8,128)(2,1)S(1)}, u32[]{:S(2)}, u32[]{:S(2)}) collective-permute-start(bf16[4096,128]{1,0:T(8,128)(2,1)S(1)} %bitcast.2), channel_id=1, source_target_pairs={{0,4},{4,0},{8,12},{12,8},{16,20},{20,16},{24,28},{28,24},{1,5},{5... | collective-permute-start | bytes 3145736 | tf_op jit(solution)/shard_map/ppermute | solution.py:373
  7.2 3.5 %collective-permute-start.1 = (bf16[96,512]{1,0:T(8,128)(2,1)S(1)}, bf16[96,512]{1,0:T(8,128)(2,1)S(1)}, u32[]{:S(2)}, u32[]{:S(2)}) collective-permute-start(bf16[96,512]{1,0:T(8,128)(2,1)S(1)} %get-tuple-element.25.kv), channel_id=1, source_target_pairs={{0,4},{4,0},{8,12},{12,8},{16,20},{20,16},{24,28},{28,24},{1,5},{5... | collective-permute-start | bytes 294920 | tf_op jit(solution)/shard_map/ppermute | solution.py:373
  7.7 7.5 %collective-permute-start.4 = (bf16[96,1024]{1,0:T(8,128)(2,1)S(1)}, bf16[96,1024]{1,0:T(8,128)(2,1)S(1)}, u32[]{:S(2)}, u32[]{:S(2)}) collective-permute-start(bf16[96,1024]{1,0:T(8,128)(2,1)S(1)} %get-tuple-element.26.query.refs_3_), channel_id=1, source_target_pairs={{0,8},{4,20},{8,0},{12,28},{16,24},{20,4},{24,16},{28,12},{1,9},{5... | collective-permute-start | bytes 589832 | tf_op jit(solution)/shard_map/ppermute | solution.py:373
  9.2 6.0 %collective-permute-start.5 = (bf16[96,1024]{1,0:T(8,128)(2,1)S(1)}, bf16[96,1024]{1,0:T(8,128)(2,1)S(1)}, u32[]{:S(2)}, u32[]{:S(2)}) collective-permute-start(bf16[96,1024]{1,0:T(8,128)(2,1)S(1)} %get-tuple-element.26.query.refs_3_), channel_id=1, source_target_pairs={{0,16},{4,12},{8,24},{12,4},{16,0},{20,28},{24,8},{28,20},{1,17},{... | collective-permute-start | bytes 589832 | tf_op jit(solution)/shard_map/ppermute | solution.py:373
  12.6 9.9 %collective-permute-start.2 = (bf16[96,1024]{1,0:T(8,128)(2,1)S(1)}, bf16[96,1024]{1,0:T(8,128)(2,1)S(1)}, u32[]{:S(2)}, u32[]{:S(2)}) collective-permute-start(bf16[96,1024]{1,0:T(8,128)(2,1)S(1)} %get-tuple-element.30), channel_id=1, source_target_pairs={{0,24},{4,28},{8,16},{12,20},{16,8},{20,12},{24,0},{28,4},{1,25},{... | collective-permute-start | bytes 589832 | tf_op jit(solution)/shard_map/ppermute | solution.py:373
  15.3 19.0 %copy-start = (bf16[1024,4096]{1,0:T(8,128)(2,1)S(1)}, bf16[1024,4096]{1,0:T(8,128)(2,1)}, u32[]{:S(2)}) copy-start(bf16[1024,4096]{1,0:T(8,128)(2,1)} %refs_8_.1) | copy-start | bytes 25165828
  19.7 14.5 %collective-permute-start.6 = (bf16[96,1024]{1,0:T(8,128)(2,1)S(1)}, bf16[96,1024]{1,0:T(8,128)(2,1)S(1)}, u32[]{:S(2)}, u32[]{:S(2)}) collective-permute-start(bf16[96,1024]{1,0:T(8,128)(2,1)S(1)} %get-tuple-element.32), channel_id=1, source_target_pairs={{0,8},{4,20},{8,0},{12,28},{16,24},{20,4},{24,16},{28,12},{1,9},{5... | collective-permute-start | bytes 589832 | tf_op jit(solution)/shard_map/ppermute | solution.py:373
  21.3 12.9 %collective-permute-start.7 = (bf16[96,1024]{1,0:T(8,128)(2,1)S(1)}, bf16[96,1024]{1,0:T(8,128)(2,1)S(1)}, u32[]{:S(2)}, u32[]{:S(2)}) collective-permute-start(bf16[96,1024]{1,0:T(8,128)(2,1)S(1)} %get-tuple-element.33), channel_id=1, source_target_pairs={{0,16},{4,12},{8,24},{12,4},{16,0},{20,28},{24,8},{28,20},{1,17},{... | collective-permute-start | bytes 589832 | tf_op jit(solution)/shard_map/ppermute | solution.py:373
  24.8 9.5 %collective-permute-start.3 = (bf16[96,1024]{1,0:T(8,128)(2,1)S(1)}, bf16[96,1024]{1,0:T(8,128)(2,1)S(1)}, u32[]{:S(2)}, u32[]{:S(2)}) collective-permute-start(bf16[96,1024]{1,0:T(8,128)(2,1)S(1)} %get-tuple-element.31), channel_id=1, source_target_pairs={{0,24},{4,28},{8,16},{12,20},{16,8},{20,12},{24,0},{28,4},{1,25},{... | collective-permute-start | bytes 589832 | tf_op jit(solution)/shard_map/ppermute | solution.py:373
  25.6 4.0 %collective-permute-start.10 = (f32[8,128]{1,0:T(8,128)S(1)}, f32[8,128]{1,0:T(8,128)S(1)}, u32[]{:S(2)}, u32[]{:S(2)}) collective-permute-start(f32[8,128]{1,0:T(8,128)S(1)} %get-tuple-element.37), channel_id=1, source_target_pairs={{0,16},{4,12},{8,24},{12,4},{16,0},{20,28},{24,8},{28,20},{1,17},{... | collective-permute-start | bytes 12296 | tf_op jit(solution)/shard_map/ppermute | solution.py:373
  26.7 7.5 %collective-permute-start.9 = (f32[8,128]{1,0:T(8,128)S(1)}, f32[8,128]{1,0:T(8,128)S(1)}, u32[]{:S(2)}, u32[]{:S(2)}) collective-permute-start(f32[8,128]{1,0:T(8,128)S(1)} %get-tuple-element.36), channel_id=1, source_target_pairs={{0,8},{4,20},{8,0},{12,28},{16,24},{20,4},{24,16},{28,12},{1,9},{5... | collective-permute-start | bytes 12296 | tf_op jit(solution)/shard_map/ppermute | solution.py:373
  29.5 4.7 %collective-permute-start.8 = (f32[8,128]{1,0:T(8,128)S(1)}, f32[8,128]{1,0:T(8,128)S(1)}, u32[]{:S(2)}, u32[]{:S(2)}) collective-permute-start(f32[8,128]{1,0:T(8,128)S(1)} %get-tuple-element.35), channel_id=1, source_target_pairs={{0,24},{4,28},{8,16},{12,20},{16,8},{20,12},{24,0},{28,4},{1,25},{... | collective-permute-start | bytes 12296 | tf_op jit(solution)/shard_map/ppermute | solution.py:373
  36.4 11.8 %collective-permute-start.13 = (bf16[96,1024]{1,0:T(8,128)(2,1)S(1)}, bf16[96,1024]{1,0:T(8,128)(2,1)S(1)}, u32[]{:S(2)}, u32[]{:S(2)}) collective-permute-start(bf16[96,1024]{1,0:T(8,128)(2,1)S(1)} %get-tuple-element.41), channel_id=1, source_target_pairs={{0,1},{1,3},{3,2},{2,0},{4,5},{5,7},{7,6},{6,4},{8,9},{9,11},{11,1... | collective-permute-start | bytes 589832 | tf_op jit(solution)/shard_map/ppermute | solution.py:382
  39.1 11.8 %collective-permute-start.11 = (bf16[96,1024]{1,0:T(8,128)(2,1)S(1)}, bf16[96,1024]{1,0:T(8,128)(2,1)S(1)}, u32[]{:S(2)}, u32[]{:S(2)}) collective-permute-start(bf16[96,1024]{1,0:T(8,128)(2,1)S(1)} %get-tuple-element.39), channel_id=1, source_target_pairs={{0,3},{3,0},{4,7},{7,4},{8,11},{11,8},{12,15},{15,12},{16,19},{19,... | collective-permute-start | bytes 589832 | tf_op jit(solution)/shard_map/ppermute | solution.py:383
  39.7 13.1 %collective-permute-start.12 = (bf16[96,1024]{1,0:T(8,128)(2,1)S(1)}, bf16[96,1024]{1,0:T(8,128)(2,1)S(1)}, u32[]{:S(2)}, u32[]{:S(2)}) collective-permute-start(bf16[96,1024]{1,0:T(8,128)(2,1)S(1)} %get-tuple-element.40), channel_id=1, source_target_pairs={{0,1},{1,0},{2,3},{3,2},{4,5},{5,4},{6,7},{7,6},{8,9},{9,8},{10,11... | collective-permute-start | bytes 589832 | tf_op jit(solution)/shard_map/ppermute | solution.py:373
  48.3 9.2 %collective-permute-start.14 = (bf16[96,1024]{1,0:T(8,128)(2,1)S(1)}, bf16[96,1024]{1,0:T(8,128)(2,1)S(1)}, u32[]{:S(2)}, u32[]{:S(2)}) collective-permute-start(bf16[96,1024]{1,0:T(8,128)(2,1)S(1)} %add_convert_fusion.1), channel_id=1, source_target_pairs={{1,2},{2,1},{5,6},{6,5},{9,10},{10,9},{13,14},{14,13},{17,18},{18,... | collective-permute-start | bytes 589832 | tf_op jit(solution)/shard_map/ppermute | solution.py:386

commit v11 on v8

--- a/solution.py
+++ b/solution.py
@@ -416,7 +416,6 @@
     near, across = turns[:2]
     first, second = (near, across), (across, near)
     rest = [(turn, turn) for turn in turns[2:]]
-    stored, kv = lax.optimization_barrier((stored, kv))
     stored_other, kv_other = (swap(value, "seq", 1, seq_count) for value in (stored, kv))
     queries = {turn: swap(query, "seq", turn, seq_count) for turn in (first, second)}
     cache, key_pos, late = merge(

time: 53.7 us -> 53.3 us (level)
  starting transfers between devices: 17.4 us -> 16.2 us
    ppermute x9, waiting for transfers between devices: 5.62 us -> 7.52 us  [swap(): lax.ppermute(value, axis, [(at, at ^ (odd if at & 1 else even)) for at in...]
    ppermute x9, starting transfers between devices: 12.2 us -> 11 us  [swap(): lax.ppermute(value, axis, [(at, at ^ (odd if at & 1 else even)) for at in...]
    ppermute x1, waiting for transfers between devices: 4.1 us -> 3.21 us  [sum_heads(): step = lax.ppermute(blocks[2], 'head', [(0, 1), (1, 3), (3, 2), (2, 0)])]
    ppermute x1, waiting for transfers between devices: 4.1 us -> 3.53 us  [sum_heads(): middle = lax.ppermute(both, 'head', [(1, 2), (2, 1)])]
  transfers between devices with their start and end apart: 12 -> 12, of which waited for: 6 -> 6; matrix products, arithmetic and copies ran while one was open for 1% -> 1% of each run, Pallas kernels for 21% -> 34%
where the time goes in v11:
time: 53.3 us; the launch traced here: 52.8 us
  Pallas kernels  20 us (38%)
  starting transfers between devices  16.2 us (30%)
  waiting for transfers between devices  14.3 us (27%)
  other arithmetic  0.86 us (2%)
  between operations  0.79 us (1%)
  local copies, waits for them, and re-layouts  0.7 us (1%)
    ppermute x9, starting transfers between devices, swap(): lax.ppermute(value, axis, [(at, at ^ (odd if at & 1 else even)) for at in...  11 us
    pallas_call x4, Pallas kernels, attend(): pl.pallas_call(functools.partial(attend_kernel, partners, len(earlier)),...  9.43 us
    ppermute x9, waiting for transfers between devices, swap(): lax.ppermute(value, axis, [(at, at ^ (odd if at & 1 else even)) for at in...  7.52 us
    pallas_call x1, Pallas kernels, project(): pl.pallas_call(functools.partial(project_kernel, width), out_shape=(jax.S...  6.47 us
    ppermute x1, waiting for transfers between devices, sum_heads(): middle = lax.ppermute(both, 'head', [(1, 2), (2, 1)])  3.53 us
    ppermute x1, waiting for transfers between devices, sum_heads(): step = lax.ppermute(blocks[2], 'head', [(0, 1), (1, 3), (3, 2), (2, 0)])  3.21 us
    ppermute x1, starting transfers between devices, sum_heads(): step = lax.ppermute(blocks[2], 'head', [(0, 1), (1, 3), (3, 2), (2, 0)])  2.64 us
    pallas_call x1, Pallas kernels, finish(): pl.pallas_call(functools.partial(finish_kernel, len(parts), size), out_sh...  2.17 us
  transfers between devices with their start and end apart: 12, of which 6 were waited for; matrix products, arithmetic and copies ran while one was open for 1% of the time, Pallas kernels for 34%

profile of v11, /device:TPU:8, one launch (start us, length us, event | category | flops | bytes accessed | tf_op | source)
XLA Modules:
  0.0 52.8 jit_solution(4970100280332268964)
XLA Ops:
  0.6 0.1 collective-permute-start
  0.7 6.5 %project.1 = (bf16[96,1024]{1,0:T(8,128)(2,1)S(1)}, bf16[96,512]{1,0:T(8,128)(2,1)S(1)}, s32[8,128]{1,0:T(8,128)S(1)}) custom-call(bf16[96,4096]{1,0:T(8,128)(2,1)} %hidden_any.1, f32[1,4096]{1,0:T(1,128)} %bitcast.6, s32[768]{0:T(1024)} %selected_any.1, f32[1,128]{1,0:T(1,128)} %constant.10.clone.freq_any, bf16[4096,1024]{1,0:T(8,128)(2,1)} %wq_any.1, ...), custom_call_target="tpu_custom_call" | custom-call | flops 1207959552 | bytes 13369344 | tf_op jit(solution)/shard_map/project/pallas_call | solution.py:103
  7.2 0.5 %collective-permute-start.1 = (bf16[96,512]{1,0:T(8,128)(2,1)S(1)}, bf16[96,512]{1,0:T(8,128)(2,1)S(1)}, u32[]{:S(2)}, u32[]{:S(2)}) collective-permute-start(bf16[96,512]{1,0:T(8,128)(2,1)S(1)} %get-tuple-element.15.kv), channel_id=1, source_target_pairs={{0,4},{4,0},{8,12},{12,8},{16,20},{20,16},{24,28},{28,24},{1,5},{5... | collective-permute-start | bytes 294920 | tf_op jit(solution)/shard_map/ppermute | solution.py:385
  7.8 1.5 %collective-permute-start.5 = (bf16[96,1024]{1,0:T(8,128)(2,1)S(1)}, bf16[96,1024]{1,0:T(8,128)(2,1)S(1)}, u32[]{:S(2)}, u32[]{:S(2)}) collective-permute-start(bf16[96,1024]{1,0:T(8,128)(2,1)S(1)} %get-tuple-element.16.query.refs_3_), channel_id=1, source_target_pairs={{0,8},{4,20},{8,0},{12,28},{16,24},{20,4},{24,16},{28,12},{1,9},{5... | collective-permute-start | bytes 589832 | tf_op jit(solution)/shard_map/ppermute | solution.py:385
  9.3 1.5 %collective-permute-start.4 = (bf16[96,1024]{1,0:T(8,128)(2,1)S(1)}, bf16[96,1024]{1,0:T(8,128)(2,1)S(1)}, u32[]{:S(2)}, u32[]{:S(2)}) collective-permute-start(bf16[96,1024]{1,0:T(8,128)(2,1)S(1)} %get-tuple-element.16.query.refs_3_), channel_id=1, source_target_pairs={{0,16},{4,12},{8,24},{12,4},{16,0},{20,28},{24,8},{28,20},{1,17},{... | collective-permute-start | bytes 589832 | tf_op jit(solution)/shard_map/ppermute | solution.py:385
  10.8 0.0 collective-permute-done.1.kv_other
  10.8 0.0 collective-permute-done.stored_other
  10.8 0.0 slice-start
  10.8 1.9 %merge.1 = (bf16[2,1024,512]{2,1,0:T(8,128)(2,1)S(1)}, f32[2048,128]{1,0:T(8,128)S(1)}, bf16[96,1024]{1,0:T(8,128)(2,1)S(1)}) custom-call(s32[2]{0:T(128)S(1)} %copy-done.1, s32[2]{0:T(128)S(1)} %copy-done.2, s32[8,128]{1,0:T(8,128)S(1)} %get-tuple-element.14.selected.refs_2_, bf16[4096,128]{1,0:T(8,128)(2,1)S(1)} %bitcast.5, ...), custom_call_target="tpu_custom_call" | custom-call | flops 1000 | bytes 1000 | tf_op jit(solution)/shard_map/merge/pallas_call | solution.py:194
  12.7 0.5 %collective-permute-start.2 = (bf16[96,1024]{1,0:T(8,128)(2,1)S(1)}, bf16[96,1024]{1,0:T(8,128)(2,1)S(1)}, u32[]{:S(2)}, u32[]{:S(2)}) collective-permute-start(bf16[96,1024]{1,0:T(8,128)(2,1)S(1)} %get-tuple-element.19), channel_id=1, source_target_pairs={{0,24},{4,28},{8,16},{12,20},{16,8},{20,12},{24,0},{28,4},{1,25},{... | collective-permute-start | bytes 589832 | tf_op jit(solution)/shard_map/ppermute | solution.py:385
  13.2 2.0 %collective-permute-done.5.refs_3_ = bf16[96,1024]{1,0:T(8,128)(2,1)S(1)} collective-permute-done((bf16[96,1024]{1,0:T(8,128)(2,1)S(1)}, bf16[96,1024]{1,0:T(8,128)(2,1)S(1)}, u32[]{:S(2)}, u32[]{:S(2)}) %collective-permute-start.5) | collective-permute-done | bytes 196640 | tf_op jit(solution)/shard_map/ppermute | solution.py:385
  15.3 2.3 %attend.6.refs_4_ = bf16[96,1152]{1,0:T(8,128)(2,1)S(1)} custom-call(bf16[2,1024,512]{2,1,0:T(8,128)(2,1)S(1)} %get-tuple-element.17.refs_0_, f32[2048,128]{1,0:T(8,128)S(1)} %get-tuple-element.18.refs_1_, s32[8,128]{1,0:T(8,128)S(1)} %get-tuple-element.14.selected.refs_2_, bf16[96,1024]{1,0:T(8,128)(2,1)S(1)} %collective-permute-done.5.refs_3_), custom_call_target="tpu_custom_call" | custom-call | flops 1000 | bytes 1000 | tf_op jit(solution)/shard_map/attend/pallas_call | solution.py:312
  17.6 0.0 slice-start.1
  17.6 2.3 %attend.7 = (bf16[96,1152]{1,0:T(8,128)(2,1)S(1)}, bf16[96,1152]{1,0:T(8,128)(2,1)S(1)}) custom-call(bf16[2,1024,512]{2,1,0:T(8,128)(2,1)S(1)} %get-tuple-element.17.refs_0_, f32[2048,128]{1,0:T(8,128)S(1)} %get-tuple-element.18.refs_1_, s32[8,128]{1,0:T(8,128)S(1)} %get-tuple-element.14.selected.refs_2_, ...), custom_call_target="tpu_custom_call" | custom-call | flops 1000 | bytes 1000 | tf_op jit(solution)/shard_map/attend/pallas_call | solution.py:312
  19.9 1.6 %collective-permute-start.6 = (bf16[96,1152]{1,0:T(8,128)(2,1)S(1)}, bf16[96,1152]{1,0:T(8,128)(2,1)S(1)}, u32[]{:S(2)}, u32[]{:S(2)}) collective-permute-start(bf16[96,1152]{1,0:T(8,128)(2,1)S(1)} %get-tuple-element.20), channel_id=1, source_target_pairs={{0,8},{4,20},{8,0},{12,28},{16,24},{20,4},{24,16},{28,12},{1,9},{5... | collective-permute-start | bytes 663560 | tf_op jit(solution)/shard_map/ppermute | solution.py:385
  21.5 1.7 %collective-permute-start.7 = (bf16[96,1152]{1,0:T(8,128)(2,1)S(1)}, bf16[96,1152]{1,0:T(8,128)(2,1)S(1)}, u32[]{:S(2)}, u32[]{:S(2)}) collective-permute-start(bf16[96,1152]{1,0:T(8,128)(2,1)S(1)} %get-tuple-element.21), channel_id=1, source_target_pairs={{0,16},{4,12},{8,24},{12,4},{16,0},{20,28},{24,8},{28,20},{1,17},{... | collective-permute-start | bytes 663560 | tf_op jit(solution)/shard_map/ppermute | solution.py:385
  23.2 0.0 collective-permute-done.2.refs_3_
  23.2 2.3 %attend.5 = bf16[96,1152]{1,0:T(8,128)(2,1)S(1)} custom-call(bf16[2,1024,512]{2,1,0:T(8,128)(2,1)S(1)} %get-tuple-element.17.refs_0_, f32[2048,128]{1,0:T(8,128)S(1)} %get-tuple-element.18.refs_1_, s32[8,128]{1,0:T(8,128)S(1)} %get-tuple-element.14.selected.refs_2_, bf16[96,1024]{1,0:T(8,128)(2,1)S(1)} %collective-permute-done.2.refs_3_), custom_call_target="tpu_custom_call" | custom-call | flops 1000 | bytes 1000 | tf_op jit(solution)/shard_map/attend/pallas_call | solution.py:312
  25.5 0.3 collective-permute-start.3
  25.9 2.5 %attend.4.refs_0_ = bf16[96,1152]{1,0:T(8,128)(2,1)S(1)} custom-call(bf16[2,1024,512]{2,1,0:T(8,128)(2,1)S(1)} %get-tuple-element.17.refs_0_, f32[2048,128]{1,0:T(8,128)S(1)} %get-tuple-element.18.refs_1_, s32[8,128]{1,0:T(8,128)S(1)} %get-tuple-element.14.selected.refs_2_, bf16[96,1024]{1,0:T(8,128)(2,1)S(1)} %get-tuple-element.16.query.refs_3_), custom_call_target="tpu_custom_call" | custom-call | flops 1000 | bytes 1000 | tf_op jit(solution)/shard_map/attend/pallas_call | solution.py:312
  28.4 3.0 %collective-permute-done.7.refs_3_ = bf16[96,1152]{1,0:T(8,128)(2,1)S(1)} collective-permute-done((bf16[96,1152]{1,0:T(8,128)(2,1)S(1)}, bf16[96,1152]{1,0:T(8,128)(2,1)S(1)}, u32[]{:S(2)}, u32[]{:S(2)}) %collective-permute-start.7) | collective-permute-done | bytes 221216 | tf_op jit(solution)/shard_map/ppermute | solution.py:385
  31.4 1.0 %collective-permute-done.3.refs_1_ = bf16[96,1152]{1,0:T(8,128)(2,1)S(1)} collective-permute-done((bf16[96,1152]{1,0:T(8,128)(2,1)S(1)}, bf16[96,1152]{1,0:T(8,128)(2,1)S(1)}, u32[]{:S(2)}, u32[]{:S(2)}) %collective-permute-start.3) | collective-permute-done | bytes 221216 | tf_op jit(solution)/shard_map/ppermute | solution.py:385
  32.4 2.2 %finish.1 = (f32[96,1024]{1,0:T(8,128)S(1)}, bf16[96,1024]{1,0:T(8,128)(2,1)S(1)}, bf16[96,1024]{1,0:T(8,128)(2,1)S(1)}, bf16[96,1024]{1,0:T(8,128)(2,1)S(1)}) custom-call(bf16[96,1152]{1,0:T(8,128)(2,1)S(1)} %attend.4.refs_0_, bf16[96,1152]{1,0:T(8,128)(2,1)S(1)} %collective-permute-done.3.refs_1_, bf16[96,1152]{1,0:T(8,128)(2,1)S(1)} %collective-permute-done.6.refs_2_, ...), custom_call_target="tpu_custom_call" | custom-call | flops 805306368 | bytes 8388608 | tf_op jit(solution)/shard_map/finish/pallas_call | solution.py:367
  34.6 2.6 %collective-permute-start.10 = (bf16[96,1024]{1,0:T(8,128)(2,1)S(1)}, bf16[96,1024]{1,0:T(8,128)(2,1)S(1)}, u32[]{:S(2)}, u32[]{:S(2)}) collective-permute-start(bf16[96,1024]{1,0:T(8,128)(2,1)S(1)} %get-tuple-element.25), channel_id=1, source_target_pairs={{0,1},{1,3},{3,2},{2,0},{4,5},{5,7},{7,6},{6,4},{8,9},{9,11},{11,1... | collective-permute-start | bytes 589832 | tf_op jit(solution)/shard_map/ppermute | solution.py:396
  37.3 0.7 %collective-permute-start.8 = (bf16[96,1024]{1,0:T(8,128)(2,1)S(1)}, bf16[96,1024]{1,0:T(8,128)(2,1)S(1)}, u32[]{:S(2)}, u32[]{:S(2)}) collective-permute-start(bf16[96,1024]{1,0:T(8,128)(2,1)S(1)} %get-tuple-element.23), channel_id=1, source_target_pairs={{0,3},{3,0},{4,7},{7,4},{8,11},{11,8},{12,15},{15,12},{16,19},{19,... | collective-permute-start | bytes 589832 | tf_op jit(solution)/shard_map/ppermute | solution.py:394
  37.9 3.2 %collective-permute-start.9 = (bf16[96,1024]{1,0:T(8,128)(2,1)S(1)}, bf16[96,1024]{1,0:T(8,128)(2,1)S(1)}, u32[]{:S(2)}, u32[]{:S(2)}) collective-permute-start(bf16[96,1024]{1,0:T(8,128)(2,1)S(1)} %get-tuple-element.24), channel_id=1, source_target_pairs={{0,1},{1,0},{2,3},{3,2},{4,5},{5,4},{6,7},{7,6},{8,9},{9,8},{10,11... | collective-permute-start | bytes 589832 | tf_op jit(solution)/shard_map/ppermute | solution.py:385
  41.1 3.2 %collective-permute-done.10 = bf16[96,1024]{1,0:T(8,128)(2,1)S(1)} collective-permute-done((bf16[96,1024]{1,0:T(8,128)(2,1)S(1)}, bf16[96,1024]{1,0:T(8,128)(2,1)S(1)}, u32[]{:S(2)}, u32[]{:S(2)}) %collective-permute-start.10) | collective-permute-done | bytes 196640 | tf_op jit(solution)/shard_map/ppermute | solution.py:396
  44.4 1.9 %collective-permute-start.11 = (bf16[96,1024]{1,0:T(8,128)(2,1)S(1)}, bf16[96,1024]{1,0:T(8,128)(2,1)S(1)}, u32[]{:S(2)}, u32[]{:S(2)}) collective-permute-start(bf16[96,1024]{1,0:T(8,128)(2,1)S(1)} %add_convert_fusion.1), channel_id=1, source_target_pairs={{1,2},{2,1},{5,6},{6,5},{9,10},{10,9},{13,14},{14,13},{17,18},{18,... | collective-permute-start | bytes 589832 | tf_op jit(solution)/shard_map/ppermute | solution.py:398
  46.3 0.7 %reshape.15 = bf16[96,2,2,128]{3,2,1,0:T(2,128)(2,1)} reshape(bf16[96,512]{1,0:T(8,128)(2,1)S(1)} %get-tuple-element.15.kv) | data formatting | bytes 196608 | tf_op jit(solution)/shard_map/reshape | solution.py:434
  47.0 1.4 %collective-permute-done.9 = bf16[96,1024]{1,0:T(8,128)(2,1)S(1)} collective-permute-done((bf16[96,1024]{1,0:T(8,128)(2,1)S(1)}, bf16[96,1024]{1,0:T(8,128)(2,1)S(1)}, u32[]{:S(2)}, u32[]{:S(2)}) %collective-permute-start.9) | collective-permute-done | bytes 196640 | tf_op jit(solution)/shard_map/ppermute | solution.py:385
  48.4 3.5 %collective-permute-done.11 = bf16[96,1024]{1,0:T(8,128)(2,1)S(1)} collective-permute-done((bf16[96,1024]{1,0:T(8,128)(2,1)S(1)}, bf16[96,1024]{1,0:T(8,128)(2,1)S(1)}, u32[]{:S(2)}, u32[]{:S(2)}) %collective-permute-start.11) | collective-permute-done | bytes 196640 | tf_op jit(solution)/shard_map/ppermute | solution.py:398
  52.0 0.8 %add_convert_fusion = bf16[96,1024]{1,0:T(8,128)(2,1)} fusion(bf16[96,1024]{1,0:T(8,128)(2,1)S(1)} %collective-permute-done.9, f32[96,1024]{1,0:T(8,128)S(1)} %get-tuple-element.22, bf16[96,1024]{1,0:T(8,128)(2,1)S(1)} %collective-permute-done.8, bf16[96,1024]{1,0:T(8,128)(2,1)S(1)} %collective-permute-done.10, ...), kind=kLoop, calls=%fused_computation | loop fusion | flops 786432 | bytes 1376257 | tf_op jit(solution)/shard_map/convert_element_type | solution.py:403
  (13 shorter events, 0.1 us)
Async XLA Ops:
  0.6 10.1 %collective-permute-start = (bf16[4096,128]{1,0:T(8,128)(2,1)}, bf16[4096,128]{1,0:T(8,128)(2,1)S(1)}, u32[]{:S(2)}, u32[]{:S(2)}) collective-permute-start(bf16[4096,128]{1,0:T(8,128)(2,1)} %bitcast.4), channel_id=1, source_target_pairs={{0,4},{4,0},{8,12},{12,8},{16,20},{20,16},{24,28},{28,24},{1,5},{5... | collective-permute-start | bytes 3145736 | tf_op jit(solution)/shard_map/ppermute | solution.py:385
  0.7 10.1 %copy-start = (bf16[1024,2,2,128]{3,2,1,0:T(2,128)(2,1)S(1)}, bf16[1024,2,2,128]{3,2,1,0:T(2,128)(2,1)}, u32[]{:S(2)}) copy-start(bf16[1024,2,2,128]{3,2,1,0:T(2,128)(2,1)} %param.17) | copy-start | bytes 3145732
  0.7 10.1 %copy-start.1 = (s32[2]{0:T(128)S(1)}, s32[2]{0:T(128)}, u32[]{:S(2)}) copy-start(s32[2]{0:T(128)} %order.1) | copy-start | bytes 28
  0.7 10.1 %copy-start.2 = (s32[2]{0:T(128)S(1)}, s32[2]{0:T(128)}, u32[]{:S(2)}) copy-start(s32[2]{0:T(128)} %slot.1) | copy-start | bytes 28
  7.2 3.6 %collective-permute-start.1 = (bf16[96,512]{1,0:T(8,128)(2,1)S(1)}, bf16[96,512]{1,0:T(8,128)(2,1)S(1)}, u32[]{:S(2)}, u32[]{:S(2)}) collective-permute-start(bf16[96,512]{1,0:T(8,128)(2,1)S(1)} %get-tuple-element.15.kv), channel_id=1, source_target_pairs={{0,4},{4,0},{8,12},{12,8},{16,20},{20,16},{24,28},{28,24},{1,5},{5... | collective-permute-start | bytes 294920 | tf_op jit(solution)/shard_map/ppermute | solution.py:385
  7.8 7.5 %collective-permute-start.5 = (bf16[96,1024]{1,0:T(8,128)(2,1)S(1)}, bf16[96,1024]{1,0:T(8,128)(2,1)S(1)}, u32[]{:S(2)}, u32[]{:S(2)}) collective-permute-start(bf16[96,1024]{1,0:T(8,128)(2,1)S(1)} %get-tuple-element.16.query.refs_3_), channel_id=1, source_target_pairs={{0,8},{4,20},{8,0},{12,28},{16,24},{20,4},{24,16},{28,12},{1,9},{5... | collective-permute-start | bytes 589832 | tf_op jit(solution)/shard_map/ppermute | solution.py:385
  9.3 8.3 %collective-permute-start.4 = (bf16[96,1024]{1,0:T(8,128)(2,1)S(1)}, bf16[96,1024]{1,0:T(8,128)(2,1)S(1)}, u32[]{:S(2)}, u32[]{:S(2)}) collective-permute-start(bf16[96,1024]{1,0:T(8,128)(2,1)S(1)} %get-tuple-element.16.query.refs_3_), channel_id=1, source_target_pairs={{0,16},{4,12},{8,24},{12,4},{16,0},{20,28},{24,8},{28,20},{1,17},{... | collective-permute-start | bytes 589832 | tf_op jit(solution)/shard_map/ppermute | solution.py:385
  10.8 21.6 %slice-start = ((s8[8388608]{0:T(1024)(128)(4,1)}), s8[4194304]{0:T(1024)(128)(4,1)S(1)}, s32[]{:S(2)}) async-start(s8[8388608]{0:T(1024)(128)(4,1)} %bitcast.2), calls=%async_computation | async-start | bytes 8388608
  12.7 10.5 %collective-permute-start.2 = (bf16[96,1024]{1,0:T(8,128)(2,1)S(1)}, bf16[96,1024]{1,0:T(8,128)(2,1)S(1)}, u32[]{:S(2)}, u32[]{:S(2)}) collective-permute-start(bf16[96,1024]{1,0:T(8,128)(2,1)S(1)} %get-tuple-element.19), channel_id=1, source_target_pairs={{0,24},{4,28},{8,16},{12,20},{16,8},{20,12},{24,0},{28,4},{1,25},{... | collective-permute-start | bytes 589832 | tf_op jit(solution)/shard_map/ppermute | solution.py:385
  17.6 14.8 %slice-start.1 = ((s8[8388608]{0:T(1024)(128)(4,1)}), s8[4194304]{0:T(1024)(128)(4,1)S(1)}, s32[]{:S(2)}) async-start(s8[8388608]{0:T(1024)(128)(4,1)} %bitcast.2), calls=%async_computation.1 | async-start | bytes 8388608
  19.9 8.4 %collective-permute-start.6 = (bf16[96,1152]{1,0:T(8,128)(2,1)S(1)}, bf16[96,1152]{1,0:T(8,128)(2,1)S(1)}, u32[]{:S(2)}, u32[]{:S(2)}) collective-permute-start(bf16[96,1152]{1,0:T(8,128)(2,1)S(1)} %get-tuple-element.20), channel_id=1, source_target_pairs={{0,8},{4,20},{8,0},{12,28},{16,24},{20,4},{24,16},{28,12},{1,9},{5... | collective-permute-start | bytes 663560 | tf_op jit(solution)/shard_map/ppermute | solution.py:385
  21.5 9.9 %collective-permute-start.7 = (bf16[96,1152]{1,0:T(8,128)(2,1)S(1)}, bf16[96,1152]{1,0:T(8,128)(2,1)S(1)}, u32[]{:S(2)}, u32[]{:S(2)}) collective-permute-start(bf16[96,1152]{1,0:T(8,128)(2,1)S(1)} %get-tuple-element.21), channel_id=1, source_target_pairs={{0,16},{4,12},{8,24},{12,4},{16,0},{20,28},{24,8},{28,20},{1,17},{... | collective-permute-start | bytes 663560 | tf_op jit(solution)/shard_map/ppermute | solution.py:385
  25.5 6.9 %collective-permute-start.3 = (bf16[96,1152]{1,0:T(8,128)(2,1)S(1)}, bf16[96,1152]{1,0:T(8,128)(2,1)S(1)}, u32[]{:S(2)}, u32[]{:S(2)}) collective-permute-start(bf16[96,1152]{1,0:T(8,128)(2,1)S(1)} %attend.5), channel_id=1, source_target_pairs={{0,24},{4,28},{8,16},{12,20},{16,8},{20,12},{24,0},{28,4},{1,25},{... | collective-permute-start | bytes 663560 | tf_op jit(solution)/shard_map/ppermute | solution.py:385
  34.6 9.7 %collective-permute-start.10 = (bf16[96,1024]{1,0:T(8,128)(2,1)S(1)}, bf16[96,1024]{1,0:T(8,128)(2,1)S(1)}, u32[]{:S(2)}, u32[]{:S(2)}) collective-permute-start(bf16[96,1024]{1,0:T(8,128)(2,1)S(1)} %get-tuple-element.25), channel_id=1, source_target_pairs={{0,1},{1,3},{3,2},{2,0},{4,5},{5,7},{7,6},{6,4},{8,9},{9,11},{11,1... | collective-permute-start | bytes 589832 | tf_op jit(solution)/shard_map/ppermute | solution.py:396
  37.3 9.7 %collective-permute-start.8 = (bf16[96,1024]{1,0:T(8,128)(2,1)S(1)}, bf16[96,1024]{1,0:T(8,128)(2,1)S(1)}, u32[]{:S(2)}, u32[]{:S(2)}) collective-permute-start(bf16[96,1024]{1,0:T(8,128)(2,1)S(1)} %get-tuple-element.23), channel_id=1, source_target_pairs={{0,3},{3,0},{4,7},{7,4},{8,11},{11,8},{12,15},{15,12},{16,19},{19,... | collective-permute-start | bytes 589832 | tf_op jit(solution)/shard_map/ppermute | solution.py:394
  37.9 10.5 %collective-permute-start.9 = (bf16[96,1024]{1,0:T(8,128)(2,1)S(1)}, bf16[96,1024]{1,0:T(8,128)(2,1)S(1)}, u32[]{:S(2)}, u32[]{:S(2)}) collective-permute-start(bf16[96,1024]{1,0:T(8,128)(2,1)S(1)} %get-tuple-element.24), channel_id=1, source_target_pairs={{0,1},{1,0},{2,3},{3,2},{4,5},{5,4},{6,7},{7,6},{8,9},{9,8},{10,11... | collective-permute-start | bytes 589832 | tf_op jit(solution)/shard_map/ppermute | solution.py:385
  44.4 7.6 %collective-permute-start.11 = (bf16[96,1024]{1,0:T(8,128)(2,1)S(1)}, bf16[96,1024]{1,0:T(8,128)(2,1)S(1)}, u32[]{:S(2)}, u32[]{:S(2)}) collective-permute-start(bf16[96,1024]{1,0:T(8,128)(2,1)S(1)} %add_convert_fusion.1), channel_id=1, source_target_pairs={{1,2},{2,1},{5,6},{6,5},{9,10},{10,9},{13,14},{14,13},{17,18},{18,... | collective-permute-start | bytes 589832 | tf_op jit(solution)/shard_map/ppermute | solution.py:398

commit v12 on v11

--- a/solution.py
+++ b/solution.py
@@ -326,15 +326,25 @@
     return list(out)
 
 
-def finish_kernel(count, size, *refs):
+def multiply(context, weights, turns, outs, size):
+    width = weights.shape[1] // size
+    step = 256 if width % 256 == 0 else width
+    me = lax.axis_index("head")
+    for turn, out in zip(turns, outs):
+        start = (me ^ turn) * width
+        for at in range(0, width, step):
+            part = weights[:, pl.ds(pl.multiple_of(start + at, step), step)]
+            out[:, at : at + step] = jnp.dot(
+                context[...], part, preferred_element_type=f32
+            ).astype(out.dtype)
+
+
+def finish_kernel(count, turns, size, *refs):
     parts = refs[:count]
     weights = refs[count]
-    outs = refs[count + 1 : count + 1 + size]
-    (context,) = refs[count + 1 + size :]
+    context = refs[count + 1]
     feat = context.shape[1]
     heads = feat // HEAD_DIM
-    width = weights.shape[1] // size
-    me = lax.axis_index("head")
     tails = [part[:, feat : feat + LANES].astype(f32) for part in parts]
     for head in range(heads):
         levels = []
@@ -349,35 +359,43 @@
             jnp.add, [(share / whole) * part[:, span].astype(f32) for share, part in zip(shares, parts)]
         )
         context[:, span] = mixed.astype(bf16)
-    for turn in range(size):
-        start = (me ^ turn) * width
-        step = 256 if width % 256 == 0 else width
-        for at in range(0, width, step):
-            part = weights[:, pl.ds(pl.multiple_of(start + at, step), step)]
-            outs[turn][:, at : at + step] = jnp.dot(
-                context[...], part, preferred_element_type=f32
-            ).astype(outs[turn].dtype)
+    multiply(context, weights, turns, refs[count + 2 :], size)
+
+
+def more_kernel(turns, size, context, weights, *outs):
+    multiply(context, weights, turns, outs, size)
 
 
 def finish(parts, w_out, size):
     rows = parts[0].shape[0]
     feat, cols = w_out.shape
-    width = cols // size
     vmem = pl.BlockSpec(memory_space=pltpu.VMEM)
-    return pl.pallas_call(
-        functools.partial(finish_kernel, len(parts), size),
-        out_shape=[jax.ShapeDtypeStruct((rows, width), f32 if turn == 0 else bf16) for turn in range(size)],
+    options = dict(
+        compiler_params=pltpu.CompilerParams(vmem_limit_bytes=24 * MIB),
+        cost_estimate=pl.CostEstimate(flops=1000, bytes_accessed=1000, transcendentals=0),
+    )
+    early, later = tuple(range(2, size)), (1, 0)
+
+    def shape(turn):
+        return jax.ShapeDtypeStruct((rows, cols // size), bf16 if turn else f32)
+
+    context, *some = pl.pallas_call(
+        functools.partial(finish_kernel, len(parts), early, size),
+        out_shape=[jax.ShapeDtypeStruct((rows, feat), bf16)] + [shape(turn) for turn in early],
         in_specs=[vmem] * (len(parts) + 1),
-        out_specs=[vmem] * size,
-        scratch_shapes=[
-            pltpu.VMEM((rows, feat), bf16),
-        ],
-        compiler_params=pltpu.CompilerParams(vmem_limit_bytes=24 * MIB),
-        cost_estimate=pl.CostEstimate(
-            flops=2 * rows * feat * cols, bytes_accessed=2 * feat * cols, transcendentals=0
-        ),
+        out_specs=[vmem] * (1 + len(early)),
         name="finish",
+        **options,
     )(*parts, w_out)
+    others = pl.pallas_call(
+        functools.partial(more_kernel, later, size),
+        out_shape=[shape(turn) for turn in later],
+        in_specs=[vmem] * 2,
+        out_specs=[vmem] * len(later),
+        name="more",
+        **options,
+    )(context, w_out)
+    return dict(zip(early + later, some + list(others)))
 
 
 def swap(value, axis, turn, size):

time: 53.3 us -> 52.2 us (0.979)
  starting transfers between devices: 16.2 us -> 13.1 us
  waiting for transfers between devices: 14.3 us -> 15.8 us
    ppermute x9, starting transfers between devices: 11 us -> 7.85 us  [swap(): lax.ppermute(value, axis, [(at, at ^ (odd if at & 1 else even)) for at in...]
    ppermute x1, waiting for transfers between devices: 3.21 us -> 4.77 us  [sum_heads(): step = lax.ppermute(blocks[2], 'head', [(0, 1), (1, 3), (3, 2), (2, 0)])]
    ppermute x1, waiting for transfers between devices: 3.53 us -> 4.96 us  [sum_heads(): middle = lax.ppermute(both, 'head', [(1, 2), (2, 1)])]
    ppermute x9, waiting for transfers between devices: 7.52 us -> 6.09 us  [swap(): lax.ppermute(value, axis, [(at, at ^ (odd if at & 1 else even)) for at in...]
    pallas_call x1 -> x2, Pallas kernels: 2.17 us -> 2.33 us  [the longest x1 1.49 us: finish(): pl.pallas_call(functools.partial(finish_kernel, len(parts), early, size),...]
  transfers between devices with their start and end apart: 12 -> 12, of which waited for: 6 -> 5; matrix products, arithmetic and copies ran while one was open for 1% -> 1% of each run, Pallas kernels for 34% -> 36%
where the time goes in v12:
time: 52.2 us; the launch traced here: 51.4 us
  Pallas kernels  20.1 us (39%)
  waiting for transfers between devices  15.8 us (30%)
  starting transfers between devices  13.1 us (25%)
  other arithmetic  0.86 us (2%)
  between operations  0.8 us (2%)
  local copies, waits for them, and re-layouts  0.7 us (1%)
    pallas_call x4, Pallas kernels, attend(): pl.pallas_call(functools.partial(attend_kernel, partners, len(earlier)),...  9.43 us
    ppermute x9, starting transfers between devices, swap(): lax.ppermute(value, axis, [(at, at ^ (odd if at & 1 else even)) for at in...  7.85 us
    pallas_call x1, Pallas kernels, project(): pl.pallas_call(functools.partial(project_kernel, width), out_shape=(jax.S...  6.47 us
    ppermute x9, waiting for transfers between devices, swap(): lax.ppermute(value, axis, [(at, at ^ (odd if at & 1 else even)) for at in...  6.09 us
    ppermute x1, waiting for transfers between devices, sum_heads(): middle = lax.ppermute(both, 'head', [(1, 2), (2, 1)])  4.96 us
    ppermute x1, waiting for transfers between devices, sum_heads(): step = lax.ppermute(blocks[2], 'head', [(0, 1), (1, 3), (3, 2), (2, 0)])  4.77 us
    ppermute x1, starting transfers between devices, sum_heads(): step = lax.ppermute(blocks[2], 'head', [(0, 1), (1, 3), (3, 2), (2, 0)])  2.64 us
    ppermute x1, starting transfers between devices, sum_heads(): middle = lax.ppermute(both, 'head', [(1, 2), (2, 1)])  1.92 us
  transfers between devices with their start and end apart: 12, of which 5 were waited for; matrix products, arithmetic and copies ran while one was open for 1% of the time, Pallas kernels for 36%

profile of v12, /device:TPU:8, one launch (start us, length us, event | category | flops | bytes accessed | tf_op | source)
XLA Modules:
  0.0 51.4 jit_solution(3179823841746586992)
XLA Ops:
  0.6 0.1 collective-permute-start
  0.7 6.5 %project.1 = (bf16[96,1024]{1,0:T(8,128)(2,1)S(1)}, bf16[96,512]{1,0:T(8,128)(2,1)S(1)}, s32[8,128]{1,0:T(8,128)S(1)}) custom-call(bf16[96,4096]{1,0:T(8,128)(2,1)} %hidden_any.1, f32[1,4096]{1,0:T(1,128)} %bitcast.6, s32[768]{0:T(1024)} %selected_any.1, f32[1,128]{1,0:T(1,128)} %constant.10.clone.freq_any, bf16[4096,1024]{1,0:T(8,128)(2,1)} %wq_any.1, ...), custom_call_target="tpu_custom_call" | custom-call | flops 1207959552 | bytes 13369344 | tf_op jit(solution)/shard_map/project/pallas_call | solution.py:103
  7.2 0.5 %collective-permute-start.1 = (bf16[96,512]{1,0:T(8,128)(2,1)S(1)}, bf16[96,512]{1,0:T(8,128)(2,1)S(1)}, u32[]{:S(2)}, u32[]{:S(2)}) collective-permute-start(bf16[96,512]{1,0:T(8,128)(2,1)S(1)} %get-tuple-element.16.kv), channel_id=1, source_target_pairs={{0,4},{4,0},{8,12},{12,8},{16,20},{20,16},{24,28},{28,24},{1,5},{5... | collective-permute-start | bytes 294920 | tf_op jit(solution)/shard_map/ppermute | solution.py:403
  7.8 1.5 %collective-permute-start.5 = (bf16[96,1024]{1,0:T(8,128)(2,1)S(1)}, bf16[96,1024]{1,0:T(8,128)(2,1)S(1)}, u32[]{:S(2)}, u32[]{:S(2)}) collective-permute-start(bf16[96,1024]{1,0:T(8,128)(2,1)S(1)} %get-tuple-element.17.query.refs_3_), channel_id=1, source_target_pairs={{0,8},{4,20},{8,0},{12,28},{16,24},{20,4},{24,16},{28,12},{1,9},{5... | collective-permute-start | bytes 589832 | tf_op jit(solution)/shard_map/ppermute | solution.py:403
  9.3 1.5 %collective-permute-start.4 = (bf16[96,1024]{1,0:T(8,128)(2,1)S(1)}, bf16[96,1024]{1,0:T(8,128)(2,1)S(1)}, u32[]{:S(2)}, u32[]{:S(2)}) collective-permute-start(bf16[96,1024]{1,0:T(8,128)(2,1)S(1)} %get-tuple-element.17.query.refs_3_), channel_id=1, source_target_pairs={{0,16},{4,12},{8,24},{12,4},{16,0},{20,28},{24,8},{28,20},{1,17},{... | collective-permute-start | bytes 589832 | tf_op jit(solution)/shard_map/ppermute | solution.py:403
  10.8 0.0 slice-start
  10.8 1.9 %merge.1 = (bf16[2,1024,512]{2,1,0:T(8,128)(2,1)S(1)}, f32[2048,128]{1,0:T(8,128)S(1)}, bf16[96,1024]{1,0:T(8,128)(2,1)S(1)}) custom-call(s32[2]{0:T(128)S(1)} %copy-done.1, s32[2]{0:T(128)S(1)} %copy-done.2, s32[8,128]{1,0:T(8,128)S(1)} %get-tuple-element.15.selected.refs_2_, bf16[4096,128]{1,0:T(8,128)(2,1)S(1)} %bitcast.5, ...), custom_call_target="tpu_custom_call" | custom-call | flops 1000 | bytes 1000 | tf_op jit(solution)/shard_map/merge/pallas_call | solution.py:194
  12.7 0.5 %collective-permute-start.2 = (bf16[96,1024]{1,0:T(8,128)(2,1)S(1)}, bf16[96,1024]{1,0:T(8,128)(2,1)S(1)}, u32[]{:S(2)}, u32[]{:S(2)}) collective-permute-start(bf16[96,1024]{1,0:T(8,128)(2,1)S(1)} %get-tuple-element.20), channel_id=1, source_target_pairs={{0,24},{4,28},{8,16},{12,20},{16,8},{20,12},{24,0},{28,4},{1,25},{... | collective-permute-start | bytes 589832 | tf_op jit(solution)/shard_map/ppermute | solution.py:403
  13.2 2.0 %collective-permute-done.5.refs_3_ = bf16[96,1024]{1,0:T(8,128)(2,1)S(1)} collective-permute-done((bf16[96,1024]{1,0:T(8,128)(2,1)S(1)}, bf16[96,1024]{1,0:T(8,128)(2,1)S(1)}, u32[]{:S(2)}, u32[]{:S(2)}) %collective-permute-start.5) | collective-permute-done | bytes 196640 | tf_op jit(solution)/shard_map/ppermute | solution.py:403
  15.3 2.3 %attend.6.refs_4_ = bf16[96,1152]{1,0:T(8,128)(2,1)S(1)} custom-call(bf16[2,1024,512]{2,1,0:T(8,128)(2,1)S(1)} %get-tuple-element.18.refs_0_, f32[2048,128]{1,0:T(8,128)S(1)} %get-tuple-element.19.refs_1_, s32[8,128]{1,0:T(8,128)S(1)} %get-tuple-element.15.selected.refs_2_, bf16[96,1024]{1,0:T(8,128)(2,1)S(1)} %collective-permute-done.5.refs_3_), custom_call_target="tpu_custom_call" | custom-call | flops 1000 | bytes 1000 | tf_op jit(solution)/shard_map/attend/pallas_call | solution.py:312
  17.6 0.0 slice-start.1
  17.6 2.3 %attend.7 = (bf16[96,1152]{1,0:T(8,128)(2,1)S(1)}, bf16[96,1152]{1,0:T(8,128)(2,1)S(1)}) custom-call(bf16[2,1024,512]{2,1,0:T(8,128)(2,1)S(1)} %get-tuple-element.18.refs_0_, f32[2048,128]{1,0:T(8,128)S(1)} %get-tuple-element.19.refs_1_, s32[8,128]{1,0:T(8,128)S(1)} %get-tuple-element.15.selected.refs_2_, ...), custom_call_target="tpu_custom_call" | custom-call | flops 1000 | bytes 1000 | tf_op jit(solution)/shard_map/attend/pallas_call | solution.py:312
  19.9 1.6 %collective-permute-start.6 = (bf16[96,1152]{1,0:T(8,128)(2,1)S(1)}, bf16[96,1152]{1,0:T(8,128)(2,1)S(1)}, u32[]{:S(2)}, u32[]{:S(2)}) collective-permute-start(bf16[96,1152]{1,0:T(8,128)(2,1)S(1)} %get-tuple-element.21), channel_id=1, source_target_pairs={{0,8},{4,20},{8,0},{12,28},{16,24},{20,4},{24,16},{28,12},{1,9},{5... | collective-permute-start | bytes 663560 | tf_op jit(solution)/shard_map/ppermute | solution.py:403
  21.5 1.7 %collective-permute-start.7 = (bf16[96,1152]{1,0:T(8,128)(2,1)S(1)}, bf16[96,1152]{1,0:T(8,128)(2,1)S(1)}, u32[]{:S(2)}, u32[]{:S(2)}) collective-permute-start(bf16[96,1152]{1,0:T(8,128)(2,1)S(1)} %get-tuple-element.22), channel_id=1, source_target_pairs={{0,16},{4,12},{8,24},{12,4},{16,0},{20,28},{24,8},{28,20},{1,17},{... | collective-permute-start | bytes 663560 | tf_op jit(solution)/shard_map/ppermute | solution.py:403
  23.2 0.0 collective-permute-done.2.refs_3_
  23.2 2.3 %attend.5 = bf16[96,1152]{1,0:T(8,128)(2,1)S(1)} custom-call(bf16[2,1024,512]{2,1,0:T(8,128)(2,1)S(1)} %get-tuple-element.18.refs_0_, f32[2048,128]{1,0:T(8,128)S(1)} %get-tuple-element.19.refs_1_, s32[8,128]{1,0:T(8,128)S(1)} %get-tuple-element.15.selected.refs_2_, bf16[96,1024]{1,0:T(8,128)(2,1)S(1)} %collective-permute-done.2.refs_3_), custom_call_target="tpu_custom_call" | custom-call | flops 1000 | bytes 1000 | tf_op jit(solution)/shard_map/attend/pallas_call | solution.py:312
  25.5 0.3 collective-permute-start.3
  25.9 2.5 %attend.4.refs_0_ = bf16[96,1152]{1,0:T(8,128)(2,1)S(1)} custom-call(bf16[2,1024,512]{2,1,0:T(8,128)(2,1)S(1)} %get-tuple-element.18.refs_0_, f32[2048,128]{1,0:T(8,128)S(1)} %get-tuple-element.19.refs_1_, s32[8,128]{1,0:T(8,128)S(1)} %get-tuple-element.15.selected.refs_2_, bf16[96,1024]{1,0:T(8,128)(2,1)S(1)} %get-tuple-element.17.query.refs_3_), custom_call_target="tpu_custom_call" | custom-call | flops 1000 | bytes 1000 | tf_op jit(solution)/shard_map/attend/pallas_call | solution.py:312
  28.4 3.0 %collective-permute-done.7.refs_3_ = bf16[96,1152]{1,0:T(8,128)(2,1)S(1)} collective-permute-done((bf16[96,1152]{1,0:T(8,128)(2,1)S(1)}, bf16[96,1152]{1,0:T(8,128)(2,1)S(1)}, u32[]{:S(2)}, u32[]{:S(2)}) %collective-permute-start.7) | collective-permute-done | bytes 221216 | tf_op jit(solution)/shard_map/ppermute | solution.py:403
  31.4 1.0 %collective-permute-done.3.refs_1_ = bf16[96,1152]{1,0:T(8,128)(2,1)S(1)} collective-permute-done((bf16[96,1152]{1,0:T(8,128)(2,1)S(1)}, bf16[96,1152]{1,0:T(8,128)(2,1)S(1)}, u32[]{:S(2)}, u32[]{:S(2)}) %collective-permute-start.3) | collective-permute-done | bytes 221216 | tf_op jit(solution)/shard_map/ppermute | solution.py:403
  32.4 1.5 %finish.1 = (bf16[96,1024]{1,0:T(8,128)(2,1)S(1)}, bf16[96,1024]{1,0:T(8,128)(2,1)S(1)}, bf16[96,1024]{1,0:T(8,128)(2,1)S(1)}) custom-call(bf16[96,1152]{1,0:T(8,128)(2,1)S(1)} %attend.4.refs_0_, bf16[96,1152]{1,0:T(8,128)(2,1)S(1)} %collective-permute-done.3.refs_1_, bf16[96,1152]{1,0:T(8,128)(2,1)S(1)} %collective-permute-done.6.refs_2_, ...), custom_call_target="tpu_custom_call" | custom-call | flops 1000 | bytes 1000 | tf_op jit(solution)/shard_map/finish/pallas_call | solution.py:382
  33.9 2.6 %collective-permute-start.10 = (bf16[96,1024]{1,0:T(8,128)(2,1)S(1)}, bf16[96,1024]{1,0:T(8,128)(2,1)S(1)}, u32[]{:S(2)}, u32[]{:S(2)}) collective-permute-start(bf16[96,1024]{1,0:T(8,128)(2,1)S(1)} %get-tuple-element.27), channel_id=1, source_target_pairs={{0,1},{1,3},{3,2},{2,0},{4,5},{5,7},{7,6},{6,4},{8,9},{9,11},{11,1... | collective-permute-start | bytes 589832 | tf_op jit(solution)/shard_map/ppermute | solution.py:414
  36.6 0.8 %more.1 = (bf16[96,1024]{1,0:T(8,128)(2,1)S(1)}, f32[96,1024]{1,0:T(8,128)S(1)}) custom-call(bf16[96,1024]{1,0:T(8,128)(2,1)S(1)} %get-tuple-element.23.context, bf16[1024,4096]{1,0:T(8,128)(2,1)S(1)} %bitcast.3), custom_call_target="tpu_custom_call" | custom-call | flops 1000 | bytes 1000 | tf_op jit(solution)/shard_map/more/pallas_call | solution.py:390
  37.4 0.1 collective-permute-start.9
  37.5 0.7 %collective-permute-start.8 = (bf16[96,1024]{1,0:T(8,128)(2,1)S(1)}, bf16[96,1024]{1,0:T(8,128)(2,1)S(1)}, u32[]{:S(2)}, u32[]{:S(2)}) collective-permute-start(bf16[96,1024]{1,0:T(8,128)(2,1)S(1)} %get-tuple-element.25), channel_id=1, source_target_pairs={{0,3},{3,0},{4,7},{7,4},{8,11},{11,8},{12,15},{15,12},{16,19},{19,... | collective-permute-start | bytes 589832 | tf_op jit(solution)/shard_map/ppermute | solution.py:412
  38.2 4.8 %collective-permute-done.10 = bf16[96,1024]{1,0:T(8,128)(2,1)S(1)} collective-permute-done((bf16[96,1024]{1,0:T(8,128)(2,1)S(1)}, bf16[96,1024]{1,0:T(8,128)(2,1)S(1)}, u32[]{:S(2)}, u32[]{:S(2)}) %collective-permute-start.10) | collective-permute-done | bytes 196640 | tf_op jit(solution)/shard_map/ppermute | solution.py:414
  43.0 1.9 %collective-permute-start.11 = (bf16[96,1024]{1,0:T(8,128)(2,1)S(1)}, bf16[96,1024]{1,0:T(8,128)(2,1)S(1)}, u32[]{:S(2)}, u32[]{:S(2)}) collective-permute-start(bf16[96,1024]{1,0:T(8,128)(2,1)S(1)} %add_convert_fusion.1), channel_id=1, source_target_pairs={{1,2},{2,1},{5,6},{6,5},{9,10},{10,9},{13,14},{14,13},{17,18},{18,... | collective-permute-start | bytes 589832 | tf_op jit(solution)/shard_map/ppermute | solution.py:416
  44.9 0.7 %reshape.15 = bf16[96,2,2,128]{3,2,1,0:T(2,128)(2,1)} reshape(bf16[96,512]{1,0:T(8,128)(2,1)S(1)} %get-tuple-element.16.kv) | data formatting | bytes 196608 | tf_op jit(solution)/shard_map/reshape | solution.py:452
  45.6 0.0 collective-permute-done.9
  45.6 0.0 collective-permute-done.8
  45.6 5.0 %collective-permute-done.11 = bf16[96,1024]{1,0:T(8,128)(2,1)S(1)} collective-permute-done((bf16[96,1024]{1,0:T(8,128)(2,1)S(1)}, bf16[96,1024]{1,0:T(8,128)(2,1)S(1)}, u32[]{:S(2)}, u32[]{:S(2)}) %collective-permute-start.11) | collective-permute-done | bytes 196640 | tf_op jit(solution)/shard_map/ppermute | solution.py:416
  50.6 0.8 %add_convert_fusion = bf16[96,1024]{1,0:T(8,128)(2,1)} fusion(bf16[96,1024]{1,0:T(8,128)(2,1)S(1)} %collective-permute-done.9, f32[96,1024]{1,0:T(8,128)S(1)} %get-tuple-element.24, bf16[96,1024]{1,0:T(8,128)(2,1)S(1)} %collective-permute-done.8, bf16[96,1024]{1,0:T(8,128)(2,1)S(1)} %collective-permute-done.10, ...), kind=kLoop, calls=%fused_computation | loop fusion | flops 786432 | bytes 1376257 | tf_op jit(solution)/shard_map/convert_element_type | solution.py:421
  (14 shorter events, 0.1 us)
Async XLA Ops:
  0.6 10.1 %collective-permute-start = (bf16[4096,128]{1,0:T(8,128)(2,1)}, bf16[4096,128]{1,0:T(8,128)(2,1)S(1)}, u32[]{:S(2)}, u32[]{:S(2)}) collective-permute-start(bf16[4096,128]{1,0:T(8,128)(2,1)} %bitcast.4), channel_id=1, source_target_pairs={{0,4},{4,0},{8,12},{12,8},{16,20},{20,16},{24,28},{28,24},{1,5},{5... | collective-permute-start | bytes 3145736 | tf_op jit(solution)/shard_map/ppermute | solution.py:403
  0.7 10.1 %copy-start = (bf16[1024,2,2,128]{3,2,1,0:T(2,128)(2,1)S(1)}, bf16[1024,2,2,128]{3,2,1,0:T(2,128)(2,1)}, u32[]{:S(2)}) copy-start(bf16[1024,2,2,128]{3,2,1,0:T(2,128)(2,1)} %param.17) | copy-start | bytes 3145732
  0.7 10.1 %copy-start.1 = (s32[2]{0:T(128)S(1)}, s32[2]{0:T(128)}, u32[]{:S(2)}) copy-start(s32[2]{0:T(128)} %order.1) | copy-start | bytes 28
  0.7 10.1 %copy-start.2 = (s32[2]{0:T(128)S(1)}, s32[2]{0:T(128)}, u32[]{:S(2)}) copy-start(s32[2]{0:T(128)} %slot.1) | copy-start | bytes 28
  7.2 3.6 %collective-permute-start.1 = (bf16[96,512]{1,0:T(8,128)(2,1)S(1)}, bf16[96,512]{1,0:T(8,128)(2,1)S(1)}, u32[]{:S(2)}, u32[]{:S(2)}) collective-permute-start(bf16[96,512]{1,0:T(8,128)(2,1)S(1)} %get-tuple-element.16.kv), channel_id=1, source_target_pairs={{0,4},{4,0},{8,12},{12,8},{16,20},{20,16},{24,28},{28,24},{1,5},{5... | collective-permute-start | bytes 294920 | tf_op jit(solution)/shard_map/ppermute | solution.py:403
  7.8 7.5 %collective-permute-start.5 = (bf16[96,1024]{1,0:T(8,128)(2,1)S(1)}, bf16[96,1024]{1,0:T(8,128)(2,1)S(1)}, u32[]{:S(2)}, u32[]{:S(2)}) collective-permute-start(bf16[96,1024]{1,0:T(8,128)(2,1)S(1)} %get-tuple-element.17.query.refs_3_), channel_id=1, source_target_pairs={{0,8},{4,20},{8,0},{12,28},{16,24},{20,4},{24,16},{28,12},{1,9},{5... | collective-permute-start | bytes 589832 | tf_op jit(solution)/shard_map/ppermute | solution.py:403
  9.3 8.3 %collective-permute-start.4 = (bf16[96,1024]{1,0:T(8,128)(2,1)S(1)}, bf16[96,1024]{1,0:T(8,128)(2,1)S(1)}, u32[]{:S(2)}, u32[]{:S(2)}) collective-permute-start(bf16[96,1024]{1,0:T(8,128)(2,1)S(1)} %get-tuple-element.17.query.refs_3_), channel_id=1, source_target_pairs={{0,16},{4,12},{8,24},{12,4},{16,0},{20,28},{24,8},{28,20},{1,17},{... | collective-permute-start | bytes 589832 | tf_op jit(solution)/shard_map/ppermute | solution.py:403
  10.8 21.6 %slice-start = ((s8[8388608]{0:T(1024)(128)(4,1)}), s8[4194304]{0:T(1024)(128)(4,1)S(1)}, s32[]{:S(2)}) async-start(s8[8388608]{0:T(1024)(128)(4,1)} %bitcast.2), calls=%async_computation | async-start | bytes 8388608
  12.7 10.5 %collective-permute-start.2 = (bf16[96,1024]{1,0:T(8,128)(2,1)S(1)}, bf16[96,1024]{1,0:T(8,128)(2,1)S(1)}, u32[]{:S(2)}, u32[]{:S(2)}) collective-permute-start(bf16[96,1024]{1,0:T(8,128)(2,1)S(1)} %get-tuple-element.20), channel_id=1, source_target_pairs={{0,24},{4,28},{8,16},{12,20},{16,8},{20,12},{24,0},{28,4},{1,25},{... | collective-permute-start | bytes 589832 | tf_op jit(solution)/shard_map/ppermute | solution.py:403
  17.6 14.8 %slice-start.1 = ((s8[8388608]{0:T(1024)(128)(4,1)}), s8[4194304]{0:T(1024)(128)(4,1)S(1)}, s32[]{:S(2)}) async-start(s8[8388608]{0:T(1024)(128)(4,1)} %bitcast.2), calls=%async_computation.1 | async-start | bytes 8388608
  19.9 8.4 %collective-permute-start.6 = (bf16[96,1152]{1,0:T(8,128)(2,1)S(1)}, bf16[96,1152]{1,0:T(8,128)(2,1)S(1)}, u32[]{:S(2)}, u32[]{:S(2)}) collective-permute-start(bf16[96,1152]{1,0:T(8,128)(2,1)S(1)} %get-tuple-element.21), channel_id=1, source_target_pairs={{0,8},{4,20},{8,0},{12,28},{16,24},{20,4},{24,16},{28,12},{1,9},{5... | collective-permute-start | bytes 663560 | tf_op jit(solution)/shard_map/ppermute | solution.py:403
  21.5 9.9 %collective-permute-start.7 = (bf16[96,1152]{1,0:T(8,128)(2,1)S(1)}, bf16[96,1152]{1,0:T(8,128)(2,1)S(1)}, u32[]{:S(2)}, u32[]{:S(2)}) collective-permute-start(bf16[96,1152]{1,0:T(8,128)(2,1)S(1)} %get-tuple-element.22), channel_id=1, source_target_pairs={{0,16},{4,12},{8,24},{12,4},{16,0},{20,28},{24,8},{28,20},{1,17},{... | collective-permute-start | bytes 663560 | tf_op jit(solution)/shard_map/ppermute | solution.py:403
  25.5 6.9 %collective-permute-start.3 = (bf16[96,1152]{1,0:T(8,128)(2,1)S(1)}, bf16[96,1152]{1,0:T(8,128)(2,1)S(1)}, u32[]{:S(2)}, u32[]{:S(2)}) collective-permute-start(bf16[96,1152]{1,0:T(8,128)(2,1)S(1)} %attend.5), channel_id=1, source_target_pairs={{0,24},{4,28},{8,16},{12,20},{16,8},{20,12},{24,0},{28,4},{1,25},{... | collective-permute-start | bytes 663560 | tf_op jit(solution)/shard_map/ppermute | solution.py:403
  33.9 9.0 %collective-permute-start.10 = (bf16[96,1024]{1,0:T(8,128)(2,1)S(1)}, bf16[96,1024]{1,0:T(8,128)(2,1)S(1)}, u32[]{:S(2)}, u32[]{:S(2)}) collective-permute-start(bf16[96,1024]{1,0:T(8,128)(2,1)S(1)} %get-tuple-element.27), channel_id=1, source_target_pairs={{0,1},{1,3},{3,2},{2,0},{4,5},{5,7},{7,6},{6,4},{8,9},{9,11},{11,1... | collective-permute-start | bytes 589832 | tf_op jit(solution)/shard_map/ppermute | solution.py:414
  37.4 8.2 %collective-permute-start.9 = (bf16[96,1024]{1,0:T(8,128)(2,1)S(1)}, bf16[96,1024]{1,0:T(8,128)(2,1)S(1)}, u32[]{:S(2)}, u32[]{:S(2)}) collective-permute-start(bf16[96,1024]{1,0:T(8,128)(2,1)S(1)} %get-tuple-element.26), channel_id=1, source_target_pairs={{0,1},{1,0},{2,3},{3,2},{4,5},{5,4},{6,7},{7,6},{8,9},{9,8},{10,11... | collective-permute-start | bytes 589832 | tf_op jit(solution)/shard_map/ppermute | solution.py:403
  37.5 8.1 %collective-permute-start.8 = (bf16[96,1024]{1,0:T(8,128)(2,1)S(1)}, bf16[96,1024]{1,0:T(8,128)(2,1)S(1)}, u32[]{:S(2)}, u32[]{:S(2)}) collective-permute-start(bf16[96,1024]{1,0:T(8,128)(2,1)S(1)} %get-tuple-element.25), channel_id=1, source_target_pairs={{0,3},{3,0},{4,7},{7,4},{8,11},{11,8},{12,15},{15,12},{16,19},{19,... | collective-permute-start | bytes 589832 | tf_op jit(solution)/shard_map/ppermute | solution.py:412
  43.0 7.6 %collective-permute-start.11 = (bf16[96,1024]{1,0:T(8,128)(2,1)S(1)}, bf16[96,1024]{1,0:T(8,128)(2,1)S(1)}, u32[]{:S(2)}, u32[]{:S(2)}) collective-permute-start(bf16[96,1024]{1,0:T(8,128)(2,1)S(1)} %add_convert_fusion.1), channel_id=1, source_target_pairs={{1,2},{2,1},{5,6},{6,5},{9,10},{10,9},{13,14},{14,13},{17,18},{18,... | collective-permute-start | bytes 589832 | tf_op jit(solution)/shard_map/ppermute | solution.py:416

commit v13 on v12

--- a/solution.py
+++ b/solution.py
@@ -374,7 +374,7 @@
         compiler_params=pltpu.CompilerParams(vmem_limit_bytes=24 * MIB),
         cost_estimate=pl.CostEstimate(flops=1000, bytes_accessed=1000, transcendentals=0),
     )
-    early, later = tuple(range(2, size)), (1, 0)
+    early, later = (2,), tuple(turn for turn in (3, 1, 0) if turn < size)
 
     def shape(turn):
         return jax.ShapeDtypeStruct((rows, cols // size), bf16 if turn else f32)

time: 52.2 us -> 51 us (0.977)
  waiting for transfers between devices: 15.8 us -> 11.3 us
  starting transfers between devices: 13.1 us -> 16.9 us
    ppermute x1, waiting for transfers between devices: 4.77 us -> 0.98 us  [sum_heads(): step = lax.ppermute(blocks[2], 'head', [(0, 1), (1, 3), (3, 2), (2, 0)])]
    ppermute x9, starting transfers between devices: 7.85 us -> 11 us  [swap(): lax.ppermute(value, axis, [(at, at ^ (odd if at & 1 else even)) for at in...]
    ppermute x1, waiting for transfers between devices: 4.96 us -> 2.13 us  [sum_heads(): middle = lax.ppermute(both, 'head', [(1, 2), (2, 1)])]
    ppermute x9, waiting for transfers between devices: 6.09 us -> 8.22 us  [swap(): lax.ppermute(value, axis, [(at, at ^ (odd if at & 1 else even)) for at in...]
    ppermute x1, starting transfers between devices: 1.92 us -> 2.61 us  [sum_heads(): middle = lax.ppermute(both, 'head', [(1, 2), (2, 1)])]
  transfers between devices with their start and end apart: 12 -> 12, of which waited for: 5 -> 6; matrix products, arithmetic and copies ran while one was open for 1% -> 1% of each run, Pallas kernels for 36% -> 37%
where the time goes in v13:
time: 51 us; the launch traced here: 50.7 us
  Pallas kernels  20.1 us (39%)
  starting transfers between devices  16.9 us (33%)
  waiting for transfers between devices  11.3 us (22%)
  other arithmetic  0.86 us (2%)
  between operations  0.79 us (2%)
  local copies, waits for them, and re-layouts  0.7 us (1%)
    ppermute x9, starting transfers between devices, swap(): lax.ppermute(value, axis, [(at, at ^ (odd if at & 1 else even)) for at in...  11 us
    pallas_call x4, Pallas kernels, attend(): pl.pallas_call(functools.partial(attend_kernel, partners, len(earlier)),...  9.43 us
    ppermute x9, waiting for transfers between devices, swap(): lax.ppermute(value, axis, [(at, at ^ (odd if at & 1 else even)) for at in...  8.22 us
    pallas_call x1, Pallas kernels, project(): pl.pallas_call(functools.partial(project_kernel, width), out_shape=(jax.S...  6.47 us
    ppermute x1, starting transfers between devices, sum_heads(): step = lax.ppermute(blocks[2], 'head', [(0, 1), (1, 3), (3, 2), (2, 0)])  2.64 us
    ppermute x1, starting transfers between devices, sum_heads(): middle = lax.ppermute(both, 'head', [(1, 2), (2, 1)])  2.61 us
    ppermute x1, waiting for transfers between devices, sum_heads(): middle = lax.ppermute(both, 'head', [(1, 2), (2, 1)])  2.13 us
    pallas_call x1, Pallas kernels, merge(): pl.pallas_call(merge_kernel, out_shape=(jax.ShapeDtypeStruct((2, shard, c...  1.88 us
  transfers between devices with their start and end apart: 12, of which 6 were waited for; matrix products, arithmetic and copies ran while one was open for 1% of the time, Pallas kernels for 37%

profile of v13, /device:TPU:8, one launch (start us, length us, event | category | flops | bytes accessed | tf_op | source)
XLA Modules:
  0.0 50.7 jit_solution(1513390668434445458)
XLA Ops:
  0.6 0.1 collective-permute-start
  0.7 6.5 %project.1 = (bf16[96,1024]{1,0:T(8,128)(2,1)S(1)}, bf16[96,512]{1,0:T(8,128)(2,1)S(1)}, s32[8,128]{1,0:T(8,128)S(1)}) custom-call(bf16[96,4096]{1,0:T(8,128)(2,1)} %hidden_any.1, f32[1,4096]{1,0:T(1,128)} %bitcast.6, s32[768]{0:T(1024)} %selected_any.1, f32[1,128]{1,0:T(1,128)} %constant.10.clone.freq_any, bf16[4096,1024]{1,0:T(8,128)(2,1)} %wq_any.1, ...), custom_call_target="tpu_custom_call" | custom-call | flops 1207959552 | bytes 13369344 | tf_op jit(solution)/shard_map/project/pallas_call | solution.py:103
  7.2 0.5 %collective-permute-start.1 = (bf16[96,512]{1,0:T(8,128)(2,1)S(1)}, bf16[96,512]{1,0:T(8,128)(2,1)S(1)}, u32[]{:S(2)}, u32[]{:S(2)}) collective-permute-start(bf16[96,512]{1,0:T(8,128)(2,1)S(1)} %get-tuple-element.16.kv), channel_id=1, source_target_pairs={{0,4},{4,0},{8,12},{12,8},{16,20},{20,16},{24,28},{28,24},{1,5},{5... | collective-permute-start | bytes 294920 | tf_op jit(solution)/shard_map/ppermute | solution.py:403
  7.8 1.5 %collective-permute-start.5 = (bf16[96,1024]{1,0:T(8,128)(2,1)S(1)}, bf16[96,1024]{1,0:T(8,128)(2,1)S(1)}, u32[]{:S(2)}, u32[]{:S(2)}) collective-permute-start(bf16[96,1024]{1,0:T(8,128)(2,1)S(1)} %get-tuple-element.17.query.refs_3_), channel_id=1, source_target_pairs={{0,8},{4,20},{8,0},{12,28},{16,24},{20,4},{24,16},{28,12},{1,9},{5... | collective-permute-start | bytes 589832 | tf_op jit(solution)/shard_map/ppermute | solution.py:403
  9.3 1.5 %collective-permute-start.4 = (bf16[96,1024]{1,0:T(8,128)(2,1)S(1)}, bf16[96,1024]{1,0:T(8,128)(2,1)S(1)}, u32[]{:S(2)}, u32[]{:S(2)}) collective-permute-start(bf16[96,1024]{1,0:T(8,128)(2,1)S(1)} %get-tuple-element.17.query.refs_3_), channel_id=1, source_target_pairs={{0,16},{4,12},{8,24},{12,4},{16,0},{20,28},{24,8},{28,20},{1,17},{... | collective-permute-start | bytes 589832 | tf_op jit(solution)/shard_map/ppermute | solution.py:403
  10.8 0.0 collective-permute-done.1.kv_other
  10.8 0.0 collective-permute-done.stored_other
  10.8 0.0 slice-start
  10.8 1.9 %merge.1 = (bf16[2,1024,512]{2,1,0:T(8,128)(2,1)S(1)}, f32[2048,128]{1,0:T(8,128)S(1)}, bf16[96,1024]{1,0:T(8,128)(2,1)S(1)}) custom-call(s32[2]{0:T(128)S(1)} %copy-done.1, s32[2]{0:T(128)S(1)} %copy-done.2, s32[8,128]{1,0:T(8,128)S(1)} %get-tuple-element.15.selected.refs_2_, bf16[4096,128]{1,0:T(8,128)(2,1)S(1)} %bitcast.5, ...), custom_call_target="tpu_custom_call" | custom-call | flops 1000 | bytes 1000 | tf_op jit(solution)/shard_map/merge/pallas_call | solution.py:194
  12.7 0.5 %collective-permute-start.2 = (bf16[96,1024]{1,0:T(8,128)(2,1)S(1)}, bf16[96,1024]{1,0:T(8,128)(2,1)S(1)}, u32[]{:S(2)}, u32[]{:S(2)}) collective-permute-start(bf16[96,1024]{1,0:T(8,128)(2,1)S(1)} %get-tuple-element.20), channel_id=1, source_target_pairs={{0,24},{4,28},{8,16},{12,20},{16,8},{20,12},{24,0},{28,4},{1,25},{... | collective-permute-start | bytes 589832 | tf_op jit(solution)/shard_map/ppermute | solution.py:403
  13.2 2.0 %collective-permute-done.5.refs_3_ = bf16[96,1024]{1,0:T(8,128)(2,1)S(1)} collective-permute-done((bf16[96,1024]{1,0:T(8,128)(2,1)S(1)}, bf16[96,1024]{1,0:T(8,128)(2,1)S(1)}, u32[]{:S(2)}, u32[]{:S(2)}) %collective-permute-start.5) | collective-permute-done | bytes 196640 | tf_op jit(solution)/shard_map/ppermute | solution.py:403
  15.3 2.3 %attend.6.refs_4_ = bf16[96,1152]{1,0:T(8,128)(2,1)S(1)} custom-call(bf16[2,1024,512]{2,1,0:T(8,128)(2,1)S(1)} %get-tuple-element.18.refs_0_, f32[2048,128]{1,0:T(8,128)S(1)} %get-tuple-element.19.refs_1_, s32[8,128]{1,0:T(8,128)S(1)} %get-tuple-element.15.selected.refs_2_, bf16[96,1024]{1,0:T(8,128)(2,1)S(1)} %collective-permute-done.5.refs_3_), custom_call_target="tpu_custom_call" | custom-call | flops 1000 | bytes 1000 | tf_op jit(solution)/shard_map/attend/pallas_call | solution.py:312
  17.6 0.0 slice-start.1
  17.6 2.3 %attend.7 = (bf16[96,1152]{1,0:T(8,128)(2,1)S(1)}, bf16[96,1152]{1,0:T(8,128)(2,1)S(1)}) custom-call(bf16[2,1024,512]{2,1,0:T(8,128)(2,1)S(1)} %get-tuple-element.18.refs_0_, f32[2048,128]{1,0:T(8,128)S(1)} %get-tuple-element.19.refs_1_, s32[8,128]{1,0:T(8,128)S(1)} %get-tuple-element.15.selected.refs_2_, ...), custom_call_target="tpu_custom_call" | custom-call | flops 1000 | bytes 1000 | tf_op jit(solution)/shard_map/attend/pallas_call | solution.py:312
  19.9 1.6 %collective-permute-start.6 = (bf16[96,1152]{1,0:T(8,128)(2,1)S(1)}, bf16[96,1152]{1,0:T(8,128)(2,1)S(1)}, u32[]{:S(2)}, u32[]{:S(2)}) collective-permute-start(bf16[96,1152]{1,0:T(8,128)(2,1)S(1)} %get-tuple-element.21), channel_id=1, source_target_pairs={{0,8},{4,20},{8,0},{12,28},{16,24},{20,4},{24,16},{28,12},{1,9},{5... | collective-permute-start | bytes 663560 | tf_op jit(solution)/shard_map/ppermute | solution.py:403
  21.5 1.7 %collective-permute-start.7 = (bf16[96,1152]{1,0:T(8,128)(2,1)S(1)}, bf16[96,1152]{1,0:T(8,128)(2,1)S(1)}, u32[]{:S(2)}, u32[]{:S(2)}) collective-permute-start(bf16[96,1152]{1,0:T(8,128)(2,1)S(1)} %get-tuple-element.22), channel_id=1, source_target_pairs={{0,16},{4,12},{8,24},{12,4},{16,0},{20,28},{24,8},{28,20},{1,17},{... | collective-permute-start | bytes 663560 | tf_op jit(solution)/shard_map/ppermute | solution.py:403
  23.2 2.3 %attend.5 = bf16[96,1152]{1,0:T(8,128)(2,1)S(1)} custom-call(bf16[2,1024,512]{2,1,0:T(8,128)(2,1)S(1)} %get-tuple-element.18.refs_0_, f32[2048,128]{1,0:T(8,128)S(1)} %get-tuple-element.19.refs_1_, s32[8,128]{1,0:T(8,128)S(1)} %get-tuple-element.15.selected.refs_2_, bf16[96,1024]{1,0:T(8,128)(2,1)S(1)} %collective-permute-done.2.refs_3_), custom_call_target="tpu_custom_call" | custom-call | flops 1000 | bytes 1000 | tf_op jit(solution)/shard_map/attend/pallas_call | solution.py:312
  25.5 0.3 collective-permute-start.3
  25.9 2.5 %attend.4.refs_0_ = bf16[96,1152]{1,0:T(8,128)(2,1)S(1)} custom-call(bf16[2,1024,512]{2,1,0:T(8,128)(2,1)S(1)} %get-tuple-element.18.refs_0_, f32[2048,128]{1,0:T(8,128)S(1)} %get-tuple-element.19.refs_1_, s32[8,128]{1,0:T(8,128)S(1)} %get-tuple-element.15.selected.refs_2_, bf16[96,1024]{1,0:T(8,128)(2,1)S(1)} %get-tuple-element.17.query.refs_3_), custom_call_target="tpu_custom_call" | custom-call | flops 1000 | bytes 1000 | tf_op jit(solution)/shard_map/attend/pallas_call | solution.py:312
  28.4 3.0 %collective-permute-done.7.refs_3_ = bf16[96,1152]{1,0:T(8,128)(2,1)S(1)} collective-permute-done((bf16[96,1152]{1,0:T(8,128)(2,1)S(1)}, bf16[96,1152]{1,0:T(8,128)(2,1)S(1)}, u32[]{:S(2)}, u32[]{:S(2)}) %collective-permute-start.7) | collective-permute-done | bytes 221216 | tf_op jit(solution)/shard_map/ppermute | solution.py:403
  31.4 1.0 %collective-permute-done.3.refs_1_ = bf16[96,1152]{1,0:T(8,128)(2,1)S(1)} collective-permute-done((bf16[96,1152]{1,0:T(8,128)(2,1)S(1)}, bf16[96,1152]{1,0:T(8,128)(2,1)S(1)}, u32[]{:S(2)}, u32[]{:S(2)}) %collective-permute-start.3) | collective-permute-done | bytes 221216 | tf_op jit(solution)/shard_map/ppermute | solution.py:403
  32.4 1.1 %finish.1 = (bf16[96,1024]{1,0:T(8,128)(2,1)S(1)}, bf16[96,1024]{1,0:T(8,128)(2,1)S(1)}) custom-call(bf16[96,1152]{1,0:T(8,128)(2,1)S(1)} %attend.4.refs_0_, bf16[96,1152]{1,0:T(8,128)(2,1)S(1)} %collective-permute-done.3.refs_1_, bf16[96,1152]{1,0:T(8,128)(2,1)S(1)} %collective-permute-done.6.refs_2_, bf16[96,1152]{1,0:T(8,128)(2,1)S(1)} %collective-permute-done.7.refs_3_, ...), custom_call_target="tpu_custom_call" | custom-call | flops 1000 | bytes 1000 | tf_op jit(solution)/shard_map/finish/pallas_call | solution.py:382
  33.5 2.6 %collective-permute-start.10 = (bf16[96,1024]{1,0:T(8,128)(2,1)S(1)}, bf16[96,1024]{1,0:T(8,128)(2,1)S(1)}, u32[]{:S(2)}, u32[]{:S(2)}) collective-permute-start(bf16[96,1024]{1,0:T(8,128)(2,1)S(1)} %get-tuple-element.27), channel_id=1, source_target_pairs={{0,1},{1,3},{3,2},{2,0},{4,5},{5,7},{7,6},{6,4},{8,9},{9,11},{11,1... | collective-permute-start | bytes 589832 | tf_op jit(solution)/shard_map/ppermute | solution.py:414
  36.2 1.2 %more.1 = (bf16[96,1024]{1,0:T(8,128)(2,1)S(1)}, bf16[96,1024]{1,0:T(8,128)(2,1)S(1)}, f32[96,1024]{1,0:T(8,128)S(1)}) custom-call(bf16[96,1024]{1,0:T(8,128)(2,1)S(1)} %get-tuple-element.23.context, bf16[1024,4096]{1,0:T(8,128)(2,1)S(1)} %bitcast.3), custom_call_target="tpu_custom_call" | custom-call | flops 1000 | bytes 1000 | tf_op jit(solution)/shard_map/more/pallas_call | solution.py:390
  37.4 0.7 %collective-permute-start.8 = (bf16[96,1024]{1,0:T(8,128)(2,1)S(1)}, bf16[96,1024]{1,0:T(8,128)(2,1)S(1)}, u32[]{:S(2)}, u32[]{:S(2)}) collective-permute-start(bf16[96,1024]{1,0:T(8,128)(2,1)S(1)} %get-tuple-element.25), channel_id=1, source_target_pairs={{0,3},{3,0},{4,7},{7,4},{8,11},{11,8},{12,15},{15,12},{16,19},{19,... | collective-permute-start | bytes 589832 | tf_op jit(solution)/shard_map/ppermute | solution.py:412
  38.0 3.2 %collective-permute-start.9 = (bf16[96,1024]{1,0:T(8,128)(2,1)S(1)}, bf16[96,1024]{1,0:T(8,128)(2,1)S(1)}, u32[]{:S(2)}, u32[]{:S(2)}) collective-permute-start(bf16[96,1024]{1,0:T(8,128)(2,1)S(1)} %get-tuple-element.26), channel_id=1, source_target_pairs={{0,1},{1,0},{2,3},{3,2},{4,5},{5,4},{6,7},{7,6},{8,9},{9,8},{10,11... | collective-permute-start | bytes 589832 | tf_op jit(solution)/shard_map/ppermute | solution.py:403
  41.3 1.0 %collective-permute-done.10 = bf16[96,1024]{1,0:T(8,128)(2,1)S(1)} collective-permute-done((bf16[96,1024]{1,0:T(8,128)(2,1)S(1)}, bf16[96,1024]{1,0:T(8,128)(2,1)S(1)}, u32[]{:S(2)}, u32[]{:S(2)}) %collective-permute-start.10) | collective-permute-done | bytes 196640 | tf_op jit(solution)/shard_map/ppermute | solution.py:414
  42.3 2.6 %collective-permute-start.11 = (bf16[96,1024]{1,0:T(8,128)(2,1)S(1)}, bf16[96,1024]{1,0:T(8,128)(2,1)S(1)}, u32[]{:S(2)}, u32[]{:S(2)}) collective-permute-start(bf16[96,1024]{1,0:T(8,128)(2,1)S(1)} %add_convert_fusion.1), channel_id=1, source_target_pairs={{1,2},{2,1},{5,6},{6,5},{9,10},{10,9},{13,14},{14,13},{17,18},{18,... | collective-permute-start | bytes 589832 | tf_op jit(solution)/shard_map/ppermute | solution.py:416
  44.9 0.7 %reshape.15 = bf16[96,2,2,128]{3,2,1,0:T(2,128)(2,1)} reshape(bf16[96,512]{1,0:T(8,128)(2,1)S(1)} %get-tuple-element.16.kv) | data formatting | bytes 196608 | tf_op jit(solution)/shard_map/reshape | solution.py:452
  45.6 2.1 %collective-permute-done.9 = bf16[96,1024]{1,0:T(8,128)(2,1)S(1)} collective-permute-done((bf16[96,1024]{1,0:T(8,128)(2,1)S(1)}, bf16[96,1024]{1,0:T(8,128)(2,1)S(1)}, u32[]{:S(2)}, u32[]{:S(2)}) %collective-permute-start.9) | collective-permute-done | bytes 196640 | tf_op jit(solution)/shard_map/ppermute | solution.py:403
  47.7 2.1 %collective-permute-done.11 = bf16[96,1024]{1,0:T(8,128)(2,1)S(1)} collective-permute-done((bf16[96,1024]{1,0:T(8,128)(2,1)S(1)}, bf16[96,1024]{1,0:T(8,128)(2,1)S(1)}, u32[]{:S(2)}, u32[]{:S(2)}) %collective-permute-start.11) | collective-permute-done | bytes 196640 | tf_op jit(solution)/shard_map/ppermute | solution.py:416
  49.9 0.8 %add_convert_fusion = bf16[96,1024]{1,0:T(8,128)(2,1)} fusion(bf16[96,1024]{1,0:T(8,128)(2,1)S(1)} %collective-permute-done.9, f32[96,1024]{1,0:T(8,128)S(1)} %get-tuple-element.24, bf16[96,1024]{1,0:T(8,128)(2,1)S(1)} %collective-permute-done.8, bf16[96,1024]{1,0:T(8,128)(2,1)S(1)} %collective-permute-done.10, ...), kind=kLoop, calls=%fused_computation | loop fusion | flops 786432 | bytes 1376257 | tf_op jit(solution)/shard_map/convert_element_type | solution.py:421
  (14 shorter events, 0.1 us)
Async XLA Ops:
  0.6 10.1 %collective-permute-start = (bf16[4096,128]{1,0:T(8,128)(2,1)}, bf16[4096,128]{1,0:T(8,128)(2,1)S(1)}, u32[]{:S(2)}, u32[]{:S(2)}) collective-permute-start(bf16[4096,128]{1,0:T(8,128)(2,1)} %bitcast.4), channel_id=1, source_target_pairs={{0,4},{4,0},{8,12},{12,8},{16,20},{20,16},{24,28},{28,24},{1,5},{5... | collective-permute-start | bytes 3145736 | tf_op jit(solution)/shard_map/ppermute | solution.py:403
  0.7 10.1 %copy-start = (bf16[1024,2,2,128]{3,2,1,0:T(2,128)(2,1)S(1)}, bf16[1024,2,2,128]{3,2,1,0:T(2,128)(2,1)}, u32[]{:S(2)}) copy-start(bf16[1024,2,2,128]{3,2,1,0:T(2,128)(2,1)} %param.17) | copy-start | bytes 3145732
  0.7 10.1 %copy-start.1 = (s32[2]{0:T(128)S(1)}, s32[2]{0:T(128)}, u32[]{:S(2)}) copy-start(s32[2]{0:T(128)} %order.1) | copy-start | bytes 28
  0.7 10.1 %copy-start.2 = (s32[2]{0:T(128)S(1)}, s32[2]{0:T(128)}, u32[]{:S(2)}) copy-start(s32[2]{0:T(128)} %slot.1) | copy-start | bytes 28
  7.2 3.6 %collective-permute-start.1 = (bf16[96,512]{1,0:T(8,128)(2,1)S(1)}, bf16[96,512]{1,0:T(8,128)(2,1)S(1)}, u32[]{:S(2)}, u32[]{:S(2)}) collective-permute-start(bf16[96,512]{1,0:T(8,128)(2,1)S(1)} %get-tuple-element.16.kv), channel_id=1, source_target_pairs={{0,4},{4,0},{8,12},{12,8},{16,20},{20,16},{24,28},{28,24},{1,5},{5... | collective-permute-start | bytes 294920 | tf_op jit(solution)/shard_map/ppermute | solution.py:403
  7.8 7.5 %collective-permute-start.5 = (bf16[96,1024]{1,0:T(8,128)(2,1)S(1)}, bf16[96,1024]{1,0:T(8,128)(2,1)S(1)}, u32[]{:S(2)}, u32[]{:S(2)}) collective-permute-start(bf16[96,1024]{1,0:T(8,128)(2,1)S(1)} %get-tuple-element.17.query.refs_3_), channel_id=1, source_target_pairs={{0,8},{4,20},{8,0},{12,28},{16,24},{20,4},{24,16},{28,12},{1,9},{5... | collective-permute-start | bytes 589832 | tf_op jit(solution)/shard_map/ppermute | solution.py:403
  9.3 8.3 %collective-permute-start.4 = (bf16[96,1024]{1,0:T(8,128)(2,1)S(1)}, bf16[96,1024]{1,0:T(8,128)(2,1)S(1)}, u32[]{:S(2)}, u32[]{:S(2)}) collective-permute-start(bf16[96,1024]{1,0:T(8,128)(2,1)S(1)} %get-tuple-element.17.query.refs_3_), channel_id=1, source_target_pairs={{0,16},{4,12},{8,24},{12,4},{16,0},{20,28},{24,8},{28,20},{1,17},{... | collective-permute-start | bytes 589832 | tf_op jit(solution)/shard_map/ppermute | solution.py:403
  10.8 21.6 %slice-start = ((s8[8388608]{0:T(1024)(128)(4,1)}), s8[4194304]{0:T(1024)(128)(4,1)S(1)}, s32[]{:S(2)}) async-start(s8[8388608]{0:T(1024)(128)(4,1)} %bitcast.2), calls=%async_computation | async-start | bytes 8388608
  12.7 10.5 %collective-permute-start.2 = (bf16[96,1024]{1,0:T(8,128)(2,1)S(1)}, bf16[96,1024]{1,0:T(8,128)(2,1)S(1)}, u32[]{:S(2)}, u32[]{:S(2)}) collective-permute-start(bf16[96,1024]{1,0:T(8,128)(2,1)S(1)} %get-tuple-element.20), channel_id=1, source_target_pairs={{0,24},{4,28},{8,16},{12,20},{16,8},{20,12},{24,0},{28,4},{1,25},{... | collective-permute-start | bytes 589832 | tf_op jit(solution)/shard_map/ppermute | solution.py:403
  17.6 14.8 %slice-start.1 = ((s8[8388608]{0:T(1024)(128)(4,1)}), s8[4194304]{0:T(1024)(128)(4,1)S(1)}, s32[]{:S(2)}) async-start(s8[8388608]{0:T(1024)(128)(4,1)} %bitcast.2), calls=%async_computation.1 | async-start | bytes 8388608
  19.9 8.4 %collective-permute-start.6 = (bf16[96,1152]{1,0:T(8,128)(2,1)S(1)}, bf16[96,1152]{1,0:T(8,128)(2,1)S(1)}, u32[]{:S(2)}, u32[]{:S(2)}) collective-permute-start(bf16[96,1152]{1,0:T(8,128)(2,1)S(1)} %get-tuple-element.21), channel_id=1, source_target_pairs={{0,8},{4,20},{8,0},{12,28},{16,24},{20,4},{24,16},{28,12},{1,9},{5... | collective-permute-start | bytes 663560 | tf_op jit(solution)/shard_map/ppermute | solution.py:403
  21.5 9.9 %collective-permute-start.7 = (bf16[96,1152]{1,0:T(8,128)(2,1)S(1)}, bf16[96,1152]{1,0:T(8,128)(2,1)S(1)}, u32[]{:S(2)}, u32[]{:S(2)}) collective-permute-start(bf16[96,1152]{1,0:T(8,128)(2,1)S(1)} %get-tuple-element.22), channel_id=1, source_target_pairs={{0,16},{4,12},{8,24},{12,4},{16,0},{20,28},{24,8},{28,20},{1,17},{... | collective-permute-start | bytes 663560 | tf_op jit(solution)/shard_map/ppermute | solution.py:403
  25.5 6.9 %collective-permute-start.3 = (bf16[96,1152]{1,0:T(8,128)(2,1)S(1)}, bf16[96,1152]{1,0:T(8,128)(2,1)S(1)}, u32[]{:S(2)}, u32[]{:S(2)}) collective-permute-start(bf16[96,1152]{1,0:T(8,128)(2,1)S(1)} %attend.5), channel_id=1, source_target_pairs={{0,24},{4,28},{8,16},{12,20},{16,8},{20,12},{24,0},{28,4},{1,25},{... | collective-permute-start | bytes 663560 | tf_op jit(solution)/shard_map/ppermute | solution.py:403
  33.5 8.7 %collective-permute-start.10 = (bf16[96,1024]{1,0:T(8,128)(2,1)S(1)}, bf16[96,1024]{1,0:T(8,128)(2,1)S(1)}, u32[]{:S(2)}, u32[]{:S(2)}) collective-permute-start(bf16[96,1024]{1,0:T(8,128)(2,1)S(1)} %get-tuple-element.27), channel_id=1, source_target_pairs={{0,1},{1,3},{3,2},{2,0},{4,5},{5,7},{7,6},{6,4},{8,9},{9,11},{11,1... | collective-permute-start | bytes 589832 | tf_op jit(solution)/shard_map/ppermute | solution.py:414
  37.4 8.2 %collective-permute-start.8 = (bf16[96,1024]{1,0:T(8,128)(2,1)S(1)}, bf16[96,1024]{1,0:T(8,128)(2,1)S(1)}, u32[]{:S(2)}, u32[]{:S(2)}) collective-permute-start(bf16[96,1024]{1,0:T(8,128)(2,1)S(1)} %get-tuple-element.25), channel_id=1, source_target_pairs={{0,3},{3,0},{4,7},{7,4},{8,11},{11,8},{12,15},{15,12},{16,19},{19,... | collective-permute-start | bytes 589832 | tf_op jit(solution)/shard_map/ppermute | solution.py:412
  38.0 9.7 %collective-permute-start.9 = (bf16[96,1024]{1,0:T(8,128)(2,1)S(1)}, bf16[96,1024]{1,0:T(8,128)(2,1)S(1)}, u32[]{:S(2)}, u32[]{:S(2)}) collective-permute-start(bf16[96,1024]{1,0:T(8,128)(2,1)S(1)} %get-tuple-element.26), channel_id=1, source_target_pairs={{0,1},{1,0},{2,3},{3,2},{4,5},{5,4},{6,7},{7,6},{8,9},{9,8},{10,11... | collective-permute-start | bytes 589832 | tf_op jit(solution)/shard_map/ppermute | solution.py:403
  42.3 7.6 %collective-permute-start.11 = (bf16[96,1024]{1,0:T(8,128)(2,1)S(1)}, bf16[96,1024]{1,0:T(8,128)(2,1)S(1)}, u32[]{:S(2)}, u32[]{:S(2)}) collective-permute-start(bf16[96,1024]{1,0:T(8,128)(2,1)S(1)} %add_convert_fusion.1), channel_id=1, source_target_pairs={{1,2},{2,1},{5,6},{6,5},{9,10},{10,9},{13,14},{14,13},{17,18},{18,... | collective-permute-start | bytes 589832 | tf_op jit(solution)/shard_map/ppermute | solution.py:416

commit v14 on v13

--- a/solution.py
+++ b/solution.py
@@ -176,7 +176,9 @@
                 (places + block * shard).astype(f32),
             )
             slot_at = (at // step) % 2
-            wide[slot_at] = (stored, stored_other)[half][at * kinds : (at + step) * kinds, :].astype(f32)
+            wide[slot_at, 0 : step * kinds, :] = (stored, stored_other)[half][
+                at * kinds : (at + step) * kinds, :
+            ].astype(f32)
             for kind in range(kinds):
                 col = kind * LANES
                 cache[half, at : at + step, col : col + LANES] = jnp.where(
@@ -200,7 +202,7 @@
         ),
         in_specs=[smem, smem] + [vmem] * 6,
         out_specs=(vmem, vmem, vmem),
-        scratch_shapes=[pltpu.VMEM((2, 128 * cols // LANES, LANES), f32)],
+        scratch_shapes=[pltpu.VMEM((2, 128 * cols // LANES + 8, LANES), f32)],
         compiler_params=pltpu.CompilerParams(vmem_limit_bytes=16 * MIB),
         cost_estimate=pl.CostEstimate(flops=1000, bytes_accessed=1000, transcendentals=0),
         name="merge",

time: 51 us -> 51 us (level)
  no operation moved by 1% of the time
where the time goes in v14:
time: 51 us; the launch traced here: 50.7 us
  Pallas kernels  20.1 us (39%)
  starting transfers between devices  16.9 us (33%)
  waiting for transfers between devices  11.3 us (22%)
  other arithmetic  0.86 us (2%)
  between operations  0.79 us (2%)
  local copies, waits for them, and re-layouts  0.7 us (1%)
    ppermute x9, starting transfers between devices, swap(): lax.ppermute(value, axis, [(at, at ^ (odd if at & 1 else even)) for at in...  11 us
    pallas_call x4, Pallas kernels, attend(): pl.pallas_call(functools.partial(attend_kernel, partners, len(earlier)),...  9.43 us
    ppermute x9, waiting for transfers between devices, swap(): lax.ppermute(value, axis, [(at, at ^ (odd if at & 1 else even)) for at in...  8.23 us
    pallas_call x1, Pallas kernels, project(): pl.pallas_call(functools.partial(project_kernel, width), out_shape=(jax.S...  6.47 us
    ppermute x1, starting transfers between devices, sum_heads(): step = lax.ppermute(blocks[2], 'head', [(0, 1), (1, 3), (3, 2), (2, 0)])  2.64 us
    ppermute x1, starting transfers between devices, sum_heads(): middle = lax.ppermute(both, 'head', [(1, 2), (2, 1)])  2.61 us
    ppermute x1, waiting for transfers between devices, sum_heads(): middle = lax.ppermute(both, 'head', [(1, 2), (2, 1)])  2.13 us
    pallas_call x1, Pallas kernels, merge(): pl.pallas_call(merge_kernel, out_shape=(jax.ShapeDtypeStruct((2, shard, c...  1.88 us
  transfers between devices with their start and end apart: 12, of which 6 were waited for; matrix products, arithmetic and copies ran while one was open for 1% of the time, Pallas kernels for 37%

profile of v14, /device:TPU:8, one launch (start us, length us, event | category | flops | bytes accessed | tf_op | source)
XLA Modules:
  0.0 50.7 jit_solution(8000772672432554231)
XLA Ops:
  0.6 0.1 collective-permute-start
  0.7 6.5 %project.1 = (bf16[96,1024]{1,0:T(8,128)(2,1)S(1)}, bf16[96,512]{1,0:T(8,128)(2,1)S(1)}, s32[8,128]{1,0:T(8,128)S(1)}) custom-call(bf16[96,4096]{1,0:T(8,128)(2,1)} %hidden_any.1, f32[1,4096]{1,0:T(1,128)} %bitcast.6, s32[768]{0:T(1024)} %selected_any.1, f32[1,128]{1,0:T(1,128)} %constant.10.clone.freq_any, bf16[4096,1024]{1,0:T(8,128)(2,1)} %wq_any.1, ...), custom_call_target="tpu_custom_call" | custom-call | flops 1207959552 | bytes 13369344 | tf_op jit(solution)/shard_map/project/pallas_call | solution.py:103
  7.2 0.5 %collective-permute-start.1 = (bf16[96,512]{1,0:T(8,128)(2,1)S(1)}, bf16[96,512]{1,0:T(8,128)(2,1)S(1)}, u32[]{:S(2)}, u32[]{:S(2)}) collective-permute-start(bf16[96,512]{1,0:T(8,128)(2,1)S(1)} %get-tuple-element.16.kv), channel_id=1, source_target_pairs={{0,4},{4,0},{8,12},{12,8},{16,20},{20,16},{24,28},{28,24},{1,5},{5... | collective-permute-start | bytes 294920 | tf_op jit(solution)/shard_map/ppermute | solution.py:405
  7.8 1.5 %collective-permute-start.5 = (bf16[96,1024]{1,0:T(8,128)(2,1)S(1)}, bf16[96,1024]{1,0:T(8,128)(2,1)S(1)}, u32[]{:S(2)}, u32[]{:S(2)}) collective-permute-start(bf16[96,1024]{1,0:T(8,128)(2,1)S(1)} %get-tuple-element.17.query.refs_3_), channel_id=1, source_target_pairs={{0,8},{4,20},{8,0},{12,28},{16,24},{20,4},{24,16},{28,12},{1,9},{5... | collective-permute-start | bytes 589832 | tf_op jit(solution)/shard_map/ppermute | solution.py:405
  9.3 1.5 %collective-permute-start.4 = (bf16[96,1024]{1,0:T(8,128)(2,1)S(1)}, bf16[96,1024]{1,0:T(8,128)(2,1)S(1)}, u32[]{:S(2)}, u32[]{:S(2)}) collective-permute-start(bf16[96,1024]{1,0:T(8,128)(2,1)S(1)} %get-tuple-element.17.query.refs_3_), channel_id=1, source_target_pairs={{0,16},{4,12},{8,24},{12,4},{16,0},{20,28},{24,8},{28,20},{1,17},{... | collective-permute-start | bytes 589832 | tf_op jit(solution)/shard_map/ppermute | solution.py:405
  10.8 0.0 collective-permute-done.1.kv_other
  10.8 0.0 collective-permute-done.stored_other
  10.8 0.0 slice-start
  10.8 1.9 %merge.1 = (bf16[2,1024,512]{2,1,0:T(8,128)(2,1)S(1)}, f32[2048,128]{1,0:T(8,128)S(1)}, bf16[96,1024]{1,0:T(8,128)(2,1)S(1)}) custom-call(s32[2]{0:T(128)S(1)} %copy-done.1, s32[2]{0:T(128)S(1)} %copy-done.2, s32[8,128]{1,0:T(8,128)S(1)} %get-tuple-element.15.selected.refs_2_, bf16[4096,128]{1,0:T(8,128)(2,1)S(1)} %bitcast.5, ...), custom_call_target="tpu_custom_call" | custom-call | flops 1000 | bytes 1000 | tf_op jit(solution)/shard_map/merge/pallas_call | solution.py:196
  12.7 0.5 %collective-permute-start.2 = (bf16[96,1024]{1,0:T(8,128)(2,1)S(1)}, bf16[96,1024]{1,0:T(8,128)(2,1)S(1)}, u32[]{:S(2)}, u32[]{:S(2)}) collective-permute-start(bf16[96,1024]{1,0:T(8,128)(2,1)S(1)} %get-tuple-element.20), channel_id=1, source_target_pairs={{0,24},{4,28},{8,16},{12,20},{16,8},{20,12},{24,0},{28,4},{1,25},{... | collective-permute-start | bytes 589832 | tf_op jit(solution)/shard_map/ppermute | solution.py:405
  13.2 2.0 %collective-permute-done.5.refs_3_ = bf16[96,1024]{1,0:T(8,128)(2,1)S(1)} collective-permute-done((bf16[96,1024]{1,0:T(8,128)(2,1)S(1)}, bf16[96,1024]{1,0:T(8,128)(2,1)S(1)}, u32[]{:S(2)}, u32[]{:S(2)}) %collective-permute-start.5) | collective-permute-done | bytes 196640 | tf_op jit(solution)/shard_map/ppermute | solution.py:405
  15.3 2.3 %attend.6.refs_4_ = bf16[96,1152]{1,0:T(8,128)(2,1)S(1)} custom-call(bf16[2,1024,512]{2,1,0:T(8,128)(2,1)S(1)} %get-tuple-element.18.refs_0_, f32[2048,128]{1,0:T(8,128)S(1)} %get-tuple-element.19.refs_1_, s32[8,128]{1,0:T(8,128)S(1)} %get-tuple-element.15.selected.refs_2_, bf16[96,1024]{1,0:T(8,128)(2,1)S(1)} %collective-permute-done.5.refs_3_), custom_call_target="tpu_custom_call" | custom-call | flops 1000 | bytes 1000 | tf_op jit(solution)/shard_map/attend/pallas_call | solution.py:314
  17.6 0.0 slice-start.1
  17.6 2.3 %attend.7 = (bf16[96,1152]{1,0:T(8,128)(2,1)S(1)}, bf16[96,1152]{1,0:T(8,128)(2,1)S(1)}) custom-call(bf16[2,1024,512]{2,1,0:T(8,128)(2,1)S(1)} %get-tuple-element.18.refs_0_, f32[2048,128]{1,0:T(8,128)S(1)} %get-tuple-element.19.refs_1_, s32[8,128]{1,0:T(8,128)S(1)} %get-tuple-element.15.selected.refs_2_, ...), custom_call_target="tpu_custom_call" | custom-call | flops 1000 | bytes 1000 | tf_op jit(solution)/shard_map/attend/pallas_call | solution.py:314
  19.9 1.6 %collective-permute-start.6 = (bf16[96,1152]{1,0:T(8,128)(2,1)S(1)}, bf16[96,1152]{1,0:T(8,128)(2,1)S(1)}, u32[]{:S(2)}, u32[]{:S(2)}) collective-permute-start(bf16[96,1152]{1,0:T(8,128)(2,1)S(1)} %get-tuple-element.21), channel_id=1, source_target_pairs={{0,8},{4,20},{8,0},{12,28},{16,24},{20,4},{24,16},{28,12},{1,9},{5... | collective-permute-start | bytes 663560 | tf_op jit(solution)/shard_map/ppermute | solution.py:405
  21.5 1.7 %collective-permute-start.7 = (bf16[96,1152]{1,0:T(8,128)(2,1)S(1)}, bf16[96,1152]{1,0:T(8,128)(2,1)S(1)}, u32[]{:S(2)}, u32[]{:S(2)}) collective-permute-start(bf16[96,1152]{1,0:T(8,128)(2,1)S(1)} %get-tuple-element.22), channel_id=1, source_target_pairs={{0,16},{4,12},{8,24},{12,4},{16,0},{20,28},{24,8},{28,20},{1,17},{... | collective-permute-start | bytes 663560 | tf_op jit(solution)/shard_map/ppermute | solution.py:405
  23.2 2.3 %attend.5 = bf16[96,1152]{1,0:T(8,128)(2,1)S(1)} custom-call(bf16[2,1024,512]{2,1,0:T(8,128)(2,1)S(1)} %get-tuple-element.18.refs_0_, f32[2048,128]{1,0:T(8,128)S(1)} %get-tuple-element.19.refs_1_, s32[8,128]{1,0:T(8,128)S(1)} %get-tuple-element.15.selected.refs_2_, bf16[96,1024]{1,0:T(8,128)(2,1)S(1)} %collective-permute-done.2.refs_3_), custom_call_target="tpu_custom_call" | custom-call | flops 1000 | bytes 1000 | tf_op jit(solution)/shard_map/attend/pallas_call | solution.py:314
  25.5 0.3 collective-permute-start.3
  25.9 2.5 %attend.4.refs_0_ = bf16[96,1152]{1,0:T(8,128)(2,1)S(1)} custom-call(bf16[2,1024,512]{2,1,0:T(8,128)(2,1)S(1)} %get-tuple-element.18.refs_0_, f32[2048,128]{1,0:T(8,128)S(1)} %get-tuple-element.19.refs_1_, s32[8,128]{1,0:T(8,128)S(1)} %get-tuple-element.15.selected.refs_2_, bf16[96,1024]{1,0:T(8,128)(2,1)S(1)} %get-tuple-element.17.query.refs_3_), custom_call_target="tpu_custom_call" | custom-call | flops 1000 | bytes 1000 | tf_op jit(solution)/shard_map/attend/pallas_call | solution.py:314
  28.4 3.0 %collective-permute-done.7.refs_3_ = bf16[96,1152]{1,0:T(8,128)(2,1)S(1)} collective-permute-done((bf16[96,1152]{1,0:T(8,128)(2,1)S(1)}, bf16[96,1152]{1,0:T(8,128)(2,1)S(1)}, u32[]{:S(2)}, u32[]{:S(2)}) %collective-permute-start.7) | collective-permute-done | bytes 221216 | tf_op jit(solution)/shard_map/ppermute | solution.py:405
  31.4 1.0 %collective-permute-done.3.refs_1_ = bf16[96,1152]{1,0:T(8,128)(2,1)S(1)} collective-permute-done((bf16[96,1152]{1,0:T(8,128)(2,1)S(1)}, bf16[96,1152]{1,0:T(8,128)(2,1)S(1)}, u32[]{:S(2)}, u32[]{:S(2)}) %collective-permute-start.3) | collective-permute-done | bytes 221216 | tf_op jit(solution)/shard_map/ppermute | solution.py:405
  32.4 1.1 %finish.1 = (bf16[96,1024]{1,0:T(8,128)(2,1)S(1)}, bf16[96,1024]{1,0:T(8,128)(2,1)S(1)}) custom-call(bf16[96,1152]{1,0:T(8,128)(2,1)S(1)} %attend.4.refs_0_, bf16[96,1152]{1,0:T(8,128)(2,1)S(1)} %collective-permute-done.3.refs_1_, bf16[96,1152]{1,0:T(8,128)(2,1)S(1)} %collective-permute-done.6.refs_2_, bf16[96,1152]{1,0:T(8,128)(2,1)S(1)} %collective-permute-done.7.refs_3_, ...), custom_call_target="tpu_custom_call" | custom-call | flops 1000 | bytes 1000 | tf_op jit(solution)/shard_map/finish/pallas_call | solution.py:384
  33.5 2.6 %collective-permute-start.10 = (bf16[96,1024]{1,0:T(8,128)(2,1)S(1)}, bf16[96,1024]{1,0:T(8,128)(2,1)S(1)}, u32[]{:S(2)}, u32[]{:S(2)}) collective-permute-start(bf16[96,1024]{1,0:T(8,128)(2,1)S(1)} %get-tuple-element.27), channel_id=1, source_target_pairs={{0,1},{1,3},{3,2},{2,0},{4,5},{5,7},{7,6},{6,4},{8,9},{9,11},{11,1... | collective-permute-start | bytes 589832 | tf_op jit(solution)/shard_map/ppermute | solution.py:416
  36.2 1.2 %more.1 = (bf16[96,1024]{1,0:T(8,128)(2,1)S(1)}, bf16[96,1024]{1,0:T(8,128)(2,1)S(1)}, f32[96,1024]{1,0:T(8,128)S(1)}) custom-call(bf16[96,1024]{1,0:T(8,128)(2,1)S(1)} %get-tuple-element.23.context, bf16[1024,4096]{1,0:T(8,128)(2,1)S(1)} %bitcast.3), custom_call_target="tpu_custom_call" | custom-call | flops 1000 | bytes 1000 | tf_op jit(solution)/shard_map/more/pallas_call | solution.py:392
  37.4 0.7 %collective-permute-start.8 = (bf16[96,1024]{1,0:T(8,128)(2,1)S(1)}, bf16[96,1024]{1,0:T(8,128)(2,1)S(1)}, u32[]{:S(2)}, u32[]{:S(2)}) collective-permute-start(bf16[96,1024]{1,0:T(8,128)(2,1)S(1)} %get-tuple-element.25), channel_id=1, source_target_pairs={{0,3},{3,0},{4,7},{7,4},{8,11},{11,8},{12,15},{15,12},{16,19},{19,... | collective-permute-start | bytes 589832 | tf_op jit(solution)/shard_map/ppermute | solution.py:414
  38.0 3.2 %collective-permute-start.9 = (bf16[96,1024]{1,0:T(8,128)(2,1)S(1)}, bf16[96,1024]{1,0:T(8,128)(2,1)S(1)}, u32[]{:S(2)}, u32[]{:S(2)}) collective-permute-start(bf16[96,1024]{1,0:T(8,128)(2,1)S(1)} %get-tuple-element.26), channel_id=1, source_target_pairs={{0,1},{1,0},{2,3},{3,2},{4,5},{5,4},{6,7},{7,6},{8,9},{9,8},{10,11... | collective-permute-start | bytes 589832 | tf_op jit(solution)/shard_map/ppermute | solution.py:405
  41.3 1.0 %collective-permute-done.10 = bf16[96,1024]{1,0:T(8,128)(2,1)S(1)} collective-permute-done((bf16[96,1024]{1,0:T(8,128)(2,1)S(1)}, bf16[96,1024]{1,0:T(8,128)(2,1)S(1)}, u32[]{:S(2)}, u32[]{:S(2)}) %collective-permute-start.10) | collective-permute-done | bytes 196640 | tf_op jit(solution)/shard_map/ppermute | solution.py:416
  42.3 2.6 %collective-permute-start.11 = (bf16[96,1024]{1,0:T(8,128)(2,1)S(1)}, bf16[96,1024]{1,0:T(8,128)(2,1)S(1)}, u32[]{:S(2)}, u32[]{:S(2)}) collective-permute-start(bf16[96,1024]{1,0:T(8,128)(2,1)S(1)} %add_convert_fusion.1), channel_id=1, source_target_pairs={{1,2},{2,1},{5,6},{6,5},{9,10},{10,9},{13,14},{14,13},{17,18},{18,... | collective-permute-start | bytes 589832 | tf_op jit(solution)/shard_map/ppermute | solution.py:418
  44.9 0.7 %reshape.15 = bf16[96,2,2,128]{3,2,1,0:T(2,128)(2,1)} reshape(bf16[96,512]{1,0:T(8,128)(2,1)S(1)} %get-tuple-element.16.kv) | data formatting | bytes 196608 | tf_op jit(solution)/shard_map/reshape | solution.py:454
  45.6 2.1 %collective-permute-done.9 = bf16[96,1024]{1,0:T(8,128)(2,1)S(1)} collective-permute-done((bf16[96,1024]{1,0:T(8,128)(2,1)S(1)}, bf16[96,1024]{1,0:T(8,128)(2,1)S(1)}, u32[]{:S(2)}, u32[]{:S(2)}) %collective-permute-start.9) | collective-permute-done | bytes 196640 | tf_op jit(solution)/shard_map/ppermute | solution.py:405
  47.7 2.1 %collective-permute-done.11 = bf16[96,1024]{1,0:T(8,128)(2,1)S(1)} collective-permute-done((bf16[96,1024]{1,0:T(8,128)(2,1)S(1)}, bf16[96,1024]{1,0:T(8,128)(2,1)S(1)}, u32[]{:S(2)}, u32[]{:S(2)}) %collective-permute-start.11) | collective-permute-done | bytes 196640 | tf_op jit(solution)/shard_map/ppermute | solution.py:418
  49.9 0.8 %add_convert_fusion = bf16[96,1024]{1,0:T(8,128)(2,1)} fusion(bf16[96,1024]{1,0:T(8,128)(2,1)S(1)} %collective-permute-done.9, f32[96,1024]{1,0:T(8,128)S(1)} %get-tuple-element.24, bf16[96,1024]{1,0:T(8,128)(2,1)S(1)} %collective-permute-done.8, bf16[96,1024]{1,0:T(8,128)(2,1)S(1)} %collective-permute-done.10, ...), kind=kLoop, calls=%fused_computation | loop fusion | flops 786432 | bytes 1376257 | tf_op jit(solution)/shard_map/convert_element_type | solution.py:423
  (14 shorter events, 0.1 us)
Async XLA Ops:
  0.6 10.1 %collective-permute-start = (bf16[4096,128]{1,0:T(8,128)(2,1)}, bf16[4096,128]{1,0:T(8,128)(2,1)S(1)}, u32[]{:S(2)}, u32[]{:S(2)}) collective-permute-start(bf16[4096,128]{1,0:T(8,128)(2,1)} %bitcast.4), channel_id=1, source_target_pairs={{0,4},{4,0},{8,12},{12,8},{16,20},{20,16},{24,28},{28,24},{1,5},{5... | collective-permute-start | bytes 3145736 | tf_op jit(solution)/shard_map/ppermute | solution.py:405
  0.7 10.1 %copy-start = (bf16[1024,2,2,128]{3,2,1,0:T(2,128)(2,1)S(1)}, bf16[1024,2,2,128]{3,2,1,0:T(2,128)(2,1)}, u32[]{:S(2)}) copy-start(bf16[1024,2,2,128]{3,2,1,0:T(2,128)(2,1)} %param.17) | copy-start | bytes 3145732
  0.7 10.1 %copy-start.1 = (s32[2]{0:T(128)S(1)}, s32[2]{0:T(128)}, u32[]{:S(2)}) copy-start(s32[2]{0:T(128)} %order.1) | copy-start | bytes 28
  0.7 10.1 %copy-start.2 = (s32[2]{0:T(128)S(1)}, s32[2]{0:T(128)}, u32[]{:S(2)}) copy-start(s32[2]{0:T(128)} %slot.1) | copy-start | bytes 28
  7.2 3.6 %collective-permute-start.1 = (bf16[96,512]{1,0:T(8,128)(2,1)S(1)}, bf16[96,512]{1,0:T(8,128)(2,1)S(1)}, u32[]{:S(2)}, u32[]{:S(2)}) collective-permute-start(bf16[96,512]{1,0:T(8,128)(2,1)S(1)} %get-tuple-element.16.kv), channel_id=1, source_target_pairs={{0,4},{4,0},{8,12},{12,8},{16,20},{20,16},{24,28},{28,24},{1,5},{5... | collective-permute-start | bytes 294920 | tf_op jit(solution)/shard_map/ppermute | solution.py:405
  7.8 7.5 %collective-permute-start.5 = (bf16[96,1024]{1,0:T(8,128)(2,1)S(1)}, bf16[96,1024]{1,0:T(8,128)(2,1)S(1)}, u32[]{:S(2)}, u32[]{:S(2)}) collective-permute-start(bf16[96,1024]{1,0:T(8,128)(2,1)S(1)} %get-tuple-element.17.query.refs_3_), channel_id=1, source_target_pairs={{0,8},{4,20},{8,0},{12,28},{16,24},{20,4},{24,16},{28,12},{1,9},{5... | collective-permute-start | bytes 589832 | tf_op jit(solution)/shard_map/ppermute | solution.py:405
  9.3 8.3 %collective-permute-start.4 = (bf16[96,1024]{1,0:T(8,128)(2,1)S(1)}, bf16[96,1024]{1,0:T(8,128)(2,1)S(1)}, u32[]{:S(2)}, u32[]{:S(2)}) collective-permute-start(bf16[96,1024]{1,0:T(8,128)(2,1)S(1)} %get-tuple-element.17.query.refs_3_), channel_id=1, source_target_pairs={{0,16},{4,12},{8,24},{12,4},{16,0},{20,28},{24,8},{28,20},{1,17},{... | collective-permute-start | bytes 589832 | tf_op jit(solution)/shard_map/ppermute | solution.py:405
  10.8 21.6 %slice-start = ((s8[8388608]{0:T(1024)(128)(4,1)}), s8[4194304]{0:T(1024)(128)(4,1)S(1)}, s32[]{:S(2)}) async-start(s8[8388608]{0:T(1024)(128)(4,1)} %bitcast.2), calls=%async_computation | async-start | bytes 8388608
  12.7 10.5 %collective-permute-start.2 = (bf16[96,1024]{1,0:T(8,128)(2,1)S(1)}, bf16[96,1024]{1,0:T(8,128)(2,1)S(1)}, u32[]{:S(2)}, u32[]{:S(2)}) collective-permute-start(bf16[96,1024]{1,0:T(8,128)(2,1)S(1)} %get-tuple-element.20), channel_id=1, source_target_pairs={{0,24},{4,28},{8,16},{12,20},{16,8},{20,12},{24,0},{28,4},{1,25},{... | collective-permute-start | bytes 589832 | tf_op jit(solution)/shard_map/ppermute | solution.py:405
  17.6 14.8 %slice-start.1 = ((s8[8388608]{0:T(1024)(128)(4,1)}), s8[4194304]{0:T(1024)(128)(4,1)S(1)}, s32[]{:S(2)}) async-start(s8[8388608]{0:T(1024)(128)(4,1)} %bitcast.2), calls=%async_computation.1 | async-start | bytes 8388608
  19.9 8.4 %collective-permute-start.6 = (bf16[96,1152]{1,0:T(8,128)(2,1)S(1)}, bf16[96,1152]{1,0:T(8,128)(2,1)S(1)}, u32[]{:S(2)}, u32[]{:S(2)}) collective-permute-start(bf16[96,1152]{1,0:T(8,128)(2,1)S(1)} %get-tuple-element.21), channel_id=1, source_target_pairs={{0,8},{4,20},{8,0},{12,28},{16,24},{20,4},{24,16},{28,12},{1,9},{5... | collective-permute-start | bytes 663560 | tf_op jit(solution)/shard_map/ppermute | solution.py:405
  21.5 9.9 %collective-permute-start.7 = (bf16[96,1152]{1,0:T(8,128)(2,1)S(1)}, bf16[96,1152]{1,0:T(8,128)(2,1)S(1)}, u32[]{:S(2)}, u32[]{:S(2)}) collective-permute-start(bf16[96,1152]{1,0:T(8,128)(2,1)S(1)} %get-tuple-element.22), channel_id=1, source_target_pairs={{0,16},{4,12},{8,24},{12,4},{16,0},{20,28},{24,8},{28,20},{1,17},{... | collective-permute-start | bytes 663560 | tf_op jit(solution)/shard_map/ppermute | solution.py:405
  25.5 6.9 %collective-permute-start.3 = (bf16[96,1152]{1,0:T(8,128)(2,1)S(1)}, bf16[96,1152]{1,0:T(8,128)(2,1)S(1)}, u32[]{:S(2)}, u32[]{:S(2)}) collective-permute-start(bf16[96,1152]{1,0:T(8,128)(2,1)S(1)} %attend.5), channel_id=1, source_target_pairs={{0,24},{4,28},{8,16},{12,20},{16,8},{20,12},{24,0},{28,4},{1,25},{... | collective-permute-start | bytes 663560 | tf_op jit(solution)/shard_map/ppermute | solution.py:405
  33.5 8.7 %collective-permute-start.10 = (bf16[96,1024]{1,0:T(8,128)(2,1)S(1)}, bf16[96,1024]{1,0:T(8,128)(2,1)S(1)}, u32[]{:S(2)}, u32[]{:S(2)}) collective-permute-start(bf16[96,1024]{1,0:T(8,128)(2,1)S(1)} %get-tuple-element.27), channel_id=1, source_target_pairs={{0,1},{1,3},{3,2},{2,0},{4,5},{5,7},{7,6},{6,4},{8,9},{9,11},{11,1... | collective-permute-start | bytes 589832 | tf_op jit(solution)/shard_map/ppermute | solution.py:416
  37.4 8.2 %collective-permute-start.8 = (bf16[96,1024]{1,0:T(8,128)(2,1)S(1)}, bf16[96,1024]{1,0:T(8,128)(2,1)S(1)}, u32[]{:S(2)}, u32[]{:S(2)}) collective-permute-start(bf16[96,1024]{1,0:T(8,128)(2,1)S(1)} %get-tuple-element.25), channel_id=1, source_target_pairs={{0,3},{3,0},{4,7},{7,4},{8,11},{11,8},{12,15},{15,12},{16,19},{19,... | collective-permute-start | bytes 589832 | tf_op jit(solution)/shard_map/ppermute | solution.py:414
  38.0 9.7 %collective-permute-start.9 = (bf16[96,1024]{1,0:T(8,128)(2,1)S(1)}, bf16[96,1024]{1,0:T(8,128)(2,1)S(1)}, u32[]{:S(2)}, u32[]{:S(2)}) collective-permute-start(bf16[96,1024]{1,0:T(8,128)(2,1)S(1)} %get-tuple-element.26), channel_id=1, source_target_pairs={{0,1},{1,0},{2,3},{3,2},{4,5},{5,4},{6,7},{7,6},{8,9},{9,8},{10,11... | collective-permute-start | bytes 589832 | tf_op jit(solution)/shard_map/ppermute | solution.py:405
  42.3 7.6 %collective-permute-start.11 = (bf16[96,1024]{1,0:T(8,128)(2,1)S(1)}, bf16[96,1024]{1,0:T(8,128)(2,1)S(1)}, u32[]{:S(2)}, u32[]{:S(2)}) collective-permute-start(bf16[96,1024]{1,0:T(8,128)(2,1)S(1)} %add_convert_fusion.1), channel_id=1, source_target_pairs={{1,2},{2,1},{5,6},{6,5},{9,10},{10,9},{13,14},{14,13},{17,18},{18,... | collective-permute-start | bytes 589832 | tf_op jit(solution)/shard_map/ppermute | solution.py:418
